TPU v7x, 32 devices: a whole 2x2x4 slice. The times are simulated.
32 devices in a mesh: fsdp: 4 (over y, core), ctx: 8 (over z, x).
Axes of the slice: x: 2, y: 2, z: 4, core: 2. Of those that a mesh axis runs over, the one named last changes fastest.
Arguments:
- hidden_in: bfloat16 [4, 1024, 2048], P('fsdp', 'ctx'), may hold values from -6 to 6
- segments: int32 [4, 1024], P('fsdp', 'ctx'), may hold values from -1 to 9, as said below
- block_pairs: int32 [16], replicated, may hold values from 0 to 15, as said below
- routes: int32 [4, 1024, 4], P('fsdp', 'ctx'), may hold values from 0 to 7, all different within a row; in each aligned block of 128 rows (0 to 127, 128 to 255, ..., all dimensions but the last counted through in order) at most 128 rows name the same one
- out_grad: bfloat16 [4, 1024, 2048], P('fsdp', 'ctx'), may hold values from -6 to 6
- norm_gain_attn: bfloat16 [2048], P(('fsdp', 'ctx')), may hold values from 0.5 to 1.5
- qkv_weight: bfloat16 [2048, 6144], P(('fsdp', 'ctx')), may hold values from -0.1875 to 0.1875
- qkv_bias: bfloat16 [6144], P(('fsdp', 'ctx')), may hold values from -1 to 1
- out_weight: bfloat16 [2048, 2048], P(('fsdp', 'ctx')), may hold values from -0.75 to 0.75
- norm_gain_ffn: bfloat16 [2048], P(('fsdp', 'ctx')), may hold values from 0.5 to 1.5
- router_weight: bfloat16 [2048, 8], P(('fsdp', 'ctx')), may hold values from -0.0625 to 0.0625
- shared_gate_weight: bfloat16 [2048], P(('fsdp', 'ctx')), may hold values from -0.125 to 0.125
- shared_in_weight: bfloat16 [2048, 11264], P(('fsdp', 'ctx')), may hold values from -0.125 to 0.125
- shared_out_weight: bfloat16 [5632, 2048], P(('fsdp', 'ctx')), may hold values from -0.15625 to 0.15625
- expert_in_weight: bfloat16 [8, 2048, 2816], P('ctx', 'fsdp'), may hold values from -0.125 to 0.125
- expert_out_weight: bfloat16 [8, 1408, 2048], P('ctx', 'fsdp'), may hold values from -0.875 to 0.875
Outputs:
- hidden_out: bfloat16 [4, 1024, 2048], P('fsdp', 'ctx')
- hidden_grad: float32 [4, 1024, 2048], P('fsdp', 'ctx')
- grad_norm_gain_attn: float32 [2048], P(('fsdp', 'ctx'))
- grad_qkv_weight: float32 [2048, 6144], P(('fsdp', 'ctx'))
- grad_qkv_bias: float32 [6144], P(('fsdp', 'ctx'))
- grad_out_weight: float32 [2048, 2048], P(('fsdp', 'ctx'))
- grad_norm_gain_ffn: float32 [2048], P(('fsdp', 'ctx'))
- grad_router_weight: float32 [2048, 8], P(('fsdp', 'ctx'))
- grad_shared_gate_weight: float32 [2048], P(('fsdp', 'ctx'))
- grad_shared_in_weight: float32 [2048, 11264], P(('fsdp', 'ctx'))
- grad_shared_out_weight: float32 [5632, 2048], P(('fsdp', 'ctx'))
- grad_expert_in_weight: float32 [8, 2048, 2816], P('ctx', 'fsdp')
- grad_expert_out_weight: float32 [8, 1408, 2048], P('ctx', 'fsdp')
Inputs may be any that keep to these rules, and one draw needn't show every extreme that they name: `segments`: read in the order of positions that block_pairs gives, the segment numbers of a row start at 0 and never fall; -1 marks padding, which ends every row. `block_pairs`: device c of ctx holds, in this order, the row blocks numbered by entries 2 c and 2 c + 1, each 64 consecutive positions; every block number appears once. `routes`: each token names 4 different experts; among the tokens of one device (aligned blocks of 128 tokens of the array) no expert is named more than 128 times.
All inputs are finite; a program needn't handle non-finite values.
Results may differ from a plain program's by a relative error of at most 0.015.
The roundings to bfloat16 on the way count: a program that leaves them out, or rounds other values in their place, can miss the bound.
Values may be sent and summed in bfloat16 or wider, within the bound.
A program may use at most 512 MiB of HBM per device.

v0:
```python
from functools import partial

import jax
import jax.numpy as jnp
from jax import lax
from jax.sharding import PartitionSpec as P

HD = 128


EPSILON = 1e-06
THETA = 1000000.0
heads_per_group = 4


def rms_scale(values, gain_vec):
    return (
        values * lax.rsqrt(jnp.mean(values * values, axis=-1, keepdims=True) + EPSILON) * gain_vec
    )


def rotate(values, positions):
    half_len = values.shape[-1] // 2
    frequency = THETA ** (-jnp.arange(half_len, dtype=jnp.float32) / half_len)
    angles = positions.astype(jnp.float32)[:, None] * frequency[None, :]
    cosine = jnp.cos(angles)[:, None, :]
    sine_part = jnp.sin(angles)[:, None, :]
    first_half = values[..., :half_len]
    second = values[..., half_len:]
    return jnp.concatenate(
        [first_half * cosine - second * sine_part, second * cosine + first_half * sine_part],
        axis=-1,
    )


def visible(query_pos, query_seg, key_pos, key_seg):
    same_doc = (key_seg[None, :] == query_seg[:, None]) & (query_seg[:, None] >= 0)
    causal = key_pos[None, :] <= query_pos[:, None]
    return same_doc & causal | (key_pos[None, :] == query_pos[:, None])


def swiglu_mix(gate_up, hidden_width):
    return jax.nn.silu(gate_up[..., :hidden_width]) * gate_up[..., hidden_width:]


def matmul_low(left, right):
    return jnp.dot(left, right, preferred_element_type=jnp.float32)


def local(
    hidden_in,
    segments,
    block_pairs,
    routes,
    out_grad,
    norm_gain_attn,
    qkv_weight,
    qkv_bias,
    out_weight,
    norm_gain_ffn,
    router_weight,
    shared_gate_weight,
    shared_in_weight,
    shared_out_weight,
    expert_in_weight,
    expert_out_weight,
):
    tokens_dev = hidden_in.shape[1]
    model_width = hidden_in.shape[2]
    block_len = tokens_dev // 2
    inputs = hidden_in.reshape(tokens_dev, model_width).astype(jnp.float32)
    seg_local = segments.reshape(tokens_dev)
    token_routes = routes.reshape(tokens_dev, -1)
    top_count = token_routes.shape[1]
    ctx_count = lax.axis_size("ctx")
    ctx_rank = lax.axis_index("ctx")
    offsets = jnp.arange(block_len, dtype=jnp.int32)
    all_positions = (
        block_pairs.reshape(ctx_count, 2)[:, :, None] * block_len + offsets[None, None, :]
    ).reshape(ctx_count * tokens_dev)
    my_positions = lax.dynamic_slice_in_dim(all_positions, ctx_rank * tokens_dev, tokens_dev, 0)
    gathered = (
        lax.all_gather(norm_gain_attn, ("fsdp", "ctx"), axis=0, tiled=True),
        lax.all_gather(qkv_weight, ("fsdp", "ctx"), axis=0, tiled=True),
        lax.all_gather(qkv_bias, ("fsdp", "ctx"), axis=0, tiled=True),
        lax.all_gather(out_weight, ("fsdp", "ctx"), axis=0, tiled=True),
        lax.all_gather(norm_gain_ffn, ("fsdp", "ctx"), axis=0, tiled=True),
        lax.all_gather(router_weight, ("fsdp", "ctx"), axis=0, tiled=True),
        lax.all_gather(shared_gate_weight, ("fsdp", "ctx"), axis=0, tiled=True),
        lax.all_gather(shared_in_weight, ("fsdp", "ctx"), axis=0, tiled=True),
        lax.all_gather(shared_out_weight, ("fsdp", "ctx"), axis=0, tiled=True),
    )
    (
        gain_attn,
        qkv_full,
        shift_full,
        out_full,
        gain_ffn,
        router_full,
        gate_full,
        inner_full,
        outer_full,
    ) = gathered
    gain_attn = gain_attn.astype(jnp.float32)
    gain_ffn = gain_ffn.astype(jnp.float32)
    heads_width = out_full.shape[0]
    head_count = heads_width // HD
    group_width = heads_per_group * HD
    group_count = head_count // heads_per_group
    normed = rms_scale(inputs, gain_attn).astype(jnp.bfloat16)
    projected = matmul_low(normed, qkv_full) + shift_full.astype(jnp.float32)
    query_pre = projected[:, :heads_width].reshape(tokens_dev, head_count, HD)
    key_pre = projected[:, heads_width : 2 * heads_width].reshape(tokens_dev, head_count, HD)

    def place_heads(query_in, key_in):
        return (rotate(query_in, my_positions) * HD ** (-0.5), rotate(key_in, my_positions))

    query_rot, key_rot = place_heads(query_pre, key_pre)
    query_low = query_rot.reshape(tokens_dev, heads_width).astype(jnp.bfloat16)
    key_low = key_rot.reshape(tokens_dev, heads_width).astype(jnp.bfloat16)
    value_low = projected[:, 2 * heads_width :].astype(jnp.bfloat16)
    keys_all, values_all, segs_all = (
        lax.all_gather(key_low, "ctx", axis=0, tiled=True),
        lax.all_gather(value_low, "ctx", axis=0, tiled=True),
        lax.all_gather(seg_local.astype(jnp.bfloat16), "ctx", axis=0, tiled=True),
    )
    allowed = visible(
        my_positions, seg_local.astype(jnp.float32), all_positions, segs_all.astype(jnp.float32)
    )

    def head_slice(matrix, group_index):
        return lax.dynamic_slice_in_dim(matrix, group_index * group_width, group_width, 1).reshape(
            matrix.shape[0], heads_per_group, HD
        )

    def forward_group(group_index):
        query_part = head_slice(query_low, group_index)
        key_part = head_slice(keys_all, group_index)
        value_part = head_slice(values_all, group_index)
        scores = jnp.einsum(
            "qhd,khd->hqk", query_part, key_part, preferred_element_type=jnp.float32
        )
        scores = jnp.where(allowed[None], scores, -1e30)
        highest = jnp.max(scores, axis=-1, keepdims=True)
        log_total = highest + jnp.log(jnp.sum(jnp.exp(scores - highest), axis=-1, keepdims=True))
        weights = jnp.exp(scores - log_total).astype(jnp.bfloat16)
        mixed = jnp.einsum("hqk,khd->qhd", weights, value_part, preferred_element_type=jnp.float32)
        return (mixed, log_total[..., 0])

    mixed_groups, log_totals = lax.map(forward_group, jnp.arange(group_count, dtype=jnp.int32))
    attended = (
        jnp.moveaxis(mixed_groups, 0, 1).reshape(tokens_dev, heads_width).astype(jnp.bfloat16)
    )
    middle = inputs + matmul_low(attended, out_full)
    normed_ffn = rms_scale(middle, gain_ffn).astype(jnp.bfloat16)
    logits = matmul_low(normed_ffn, router_full)
    router_probs = jax.nn.softmax(logits, axis=-1)
    expert_count = logits.shape[1]
    expert_ids = jnp.arange(expert_count, dtype=jnp.int32)
    chosen = (token_routes[:, :, None] == expert_ids[None, None, :]).astype(jnp.float32)
    gate_weights = jnp.sum(chosen * router_probs[:, None, :], axis=-1)
    capacity = 2 * tokens_dev * top_count // expert_count
    local_experts = expert_in_weight.shape[0]
    assigned = tokens_dev * top_count
    flat_routes = token_routes.reshape(assigned)
    onehot = (flat_routes[:, None] == expert_ids[None, :]).astype(jnp.int32)
    earlier = jnp.cumsum(onehot, axis=0) - onehot
    places = flat_routes * capacity + jnp.sum(earlier * onehot, axis=1)
    slot_source = (
        jnp.full((expert_count * capacity,), assigned, jnp.int32)
        .at[places]
        .set(jnp.arange(assigned, dtype=jnp.int32))
    )
    slot_token = slot_source // top_count
    padded_rows = jnp.concatenate([normed_ffn, jnp.zeros((1, model_width), jnp.bfloat16)], axis=0)
    outgoing = padded_rows[slot_token].reshape(ctx_count, local_experts * capacity, model_width)
    expert_inner, expert_outer = (
        lax.all_gather(expert_in_weight, "fsdp", axis=1, tiled=True),
        lax.all_gather(expert_out_weight, "fsdp", axis=1, tiled=True),
    )
    landed_tokens = lax.all_to_all(outgoing, "ctx", split_axis=0, concat_axis=0, tiled=True)
    incoming = landed_tokens.reshape(ctx_count, local_experts, capacity, model_width)
    expert_gu = jnp.einsum(
        "necd,edf->necf", incoming, expert_inner, preferred_element_type=jnp.float32
    )
    expert_width = expert_outer.shape[1]
    expert_hidden = swiglu_mix(expert_gu, expert_width).astype(jnp.bfloat16)
    expert_result = jnp.einsum(
        "necf,efd->necd", expert_hidden, expert_outer, preferred_element_type=jnp.float32
    ).astype(jnp.bfloat16)
    returned = lax.all_to_all(
        expert_result.reshape(ctx_count, local_experts * capacity, model_width),
        "ctx",
        split_axis=0,
        concat_axis=0,
        tiled=True,
    )
    picked = (
        returned.reshape(expert_count * capacity, model_width)[places]
        .reshape(tokens_dev, top_count, model_width)
        .astype(jnp.float32)
    )
    routed = jnp.sum(gate_weights[:, :, None] * picked, axis=1)
    upstream = out_grad.reshape(tokens_dev, model_width).astype(jnp.float32)
    shared_gu = matmul_low(normed_ffn, inner_full)
    shared_width = outer_full.shape[0]
    shared_hidden = swiglu_mix(shared_gu, shared_width).astype(jnp.bfloat16)
    shared_out = matmul_low(shared_hidden, outer_full)
    gate_value = jax.nn.sigmoid(matmul_low(normed_ffn, gate_full))
    output = middle + gate_value[:, None] * shared_out + routed
    hidden_out = output.astype(jnp.bfloat16).reshape(1, tokens_dev, model_width)
    gain_ffn, router_full, gate_full, inner_full, outer_full = (
        lax.all_gather(norm_gain_ffn, ("fsdp", "ctx"), axis=0, tiled=True),
        lax.all_gather(router_weight, ("fsdp", "ctx"), axis=0, tiled=True),
        lax.all_gather(shared_gate_weight, ("fsdp", "ctx"), axis=0, tiled=True),
        lax.all_gather(shared_in_weight, ("fsdp", "ctx"), axis=0, tiled=True),
        lax.all_gather(shared_out_weight, ("fsdp", "ctx"), axis=0, tiled=True),
    )
    gain_ffn = gain_ffn.astype(jnp.float32)
    grad_shared_out = (gate_value[:, None] * upstream).astype(jnp.bfloat16)
    grad_outer = jnp.einsum(
        "tf,td->fd", shared_hidden, grad_shared_out, preferred_element_type=jnp.float32
    )
    grad_hidden = jnp.einsum(
        "td,fd->tf", grad_shared_out, outer_full, preferred_element_type=jnp.float32
    )
    unused_mix, mix_pull = jax.vjp(partial(swiglu_mix, hidden_width=shared_width), shared_gu)
    grad_shared_gu = mix_pull(grad_hidden)[0].astype(jnp.bfloat16)
    grad_inner = jnp.einsum(
        "td,tf->df", normed_ffn, grad_shared_gu, preferred_element_type=jnp.float32
    )
    grad_normed = jnp.einsum(
        "tf,df->td", grad_shared_gu, inner_full, preferred_element_type=jnp.float32
    )
    grad_gate_logit = (
        gate_value * (1.0 - gate_value) * jnp.sum(upstream * shared_out, axis=1)
    ).astype(jnp.bfloat16)
    grad_gate_vec = jnp.einsum(
        "td,t->d", normed_ffn, grad_gate_logit, preferred_element_type=jnp.float32
    )
    grad_normed = (
        grad_normed
        + grad_gate_logit.astype(jnp.float32)[:, None] * gate_full.astype(jnp.float32)[None, :]
    )
    grad_gates = jnp.sum(upstream[:, None, :] * picked, axis=2)
    grad_choice_probs = jnp.sum(chosen * grad_gates[:, :, None], axis=1)
    grad_logits = (
        router_probs
        * (grad_choice_probs - jnp.sum(router_probs * grad_choice_probs, axis=1, keepdims=True))
    ).astype(jnp.bfloat16)
    grad_router = jnp.einsum(
        "td,te->de", normed_ffn, grad_logits, preferred_element_type=jnp.float32
    )
    grad_normed = grad_normed + jnp.einsum(
        "te,de->td", grad_logits, router_full, preferred_element_type=jnp.float32
    )
    grad_slots = (
        (gate_weights[:, :, None] * upstream[:, None, :])
        .astype(jnp.bfloat16)
        .reshape(assigned, model_width)
    )
    padded_grads = jnp.concatenate([grad_slots, jnp.zeros((1, model_width), jnp.bfloat16)], axis=0)
    grad_outgoing = padded_grads[slot_source].reshape(
        ctx_count, local_experts * capacity, model_width
    )
    grad_incoming = lax.all_to_all(
        grad_outgoing, "ctx", split_axis=0, concat_axis=0, tiled=True
    ).reshape(ctx_count, local_experts, capacity, model_width)
    grad_expert_hidden = jnp.einsum(
        "necd,efd->necf", grad_incoming, expert_outer, preferred_element_type=jnp.float32
    )
    grad_expert_outer = jnp.einsum(
        "necf,necd->efd", expert_hidden, grad_incoming, preferred_element_type=jnp.float32
    )
    unused_mix, expert_pull = jax.vjp(partial(swiglu_mix, hidden_width=expert_width), expert_gu)
    grad_expert_gu = expert_pull(grad_expert_hidden)[0].astype(jnp.bfloat16)
    grad_expert_inner = jnp.einsum(
        "necd,necf->edf", incoming, grad_expert_gu, preferred_element_type=jnp.float32
    )
    grad_expert_rows = jnp.einsum(
        "necf,edf->necd", grad_expert_gu, expert_inner, preferred_element_type=jnp.float32
    ).astype(jnp.bfloat16)
    grad_returned = lax.all_to_all(
        grad_expert_rows.reshape(ctx_count, local_experts * capacity, model_width),
        "ctx",
        split_axis=0,
        concat_axis=0,
        tiled=True,
    )
    grad_picked = grad_returned.reshape(expert_count * capacity, model_width)[places].reshape(
        tokens_dev, top_count, model_width
    )
    grad_normed = grad_normed + jnp.sum(grad_picked.astype(jnp.float32), axis=1)
    sum_expert_inner, sum_expert_outer = (
        lax.psum_scatter(
            grad_expert_inner.astype(jnp.bfloat16), "fsdp", scatter_dimension=1, tiled=True
        ).astype(jnp.float32),
        lax.psum_scatter(
            grad_expert_outer.astype(jnp.bfloat16), "fsdp", scatter_dimension=1, tiled=True
        ).astype(jnp.float32),
    )
    unused_norm, norm_pull = jax.vjp(rms_scale, middle, gain_ffn)
    grad_middle_norm, grad_gain_ffn = norm_pull(grad_normed)
    grad_middle = upstream + grad_middle_norm
    sum_gain_ffn, sum_router, sum_gate_vec, sum_inner, sum_outer = (
        lax.psum_scatter(grad_gain_ffn, ("fsdp", "ctx"), scatter_dimension=0, tiled=True),
        lax.psum_scatter(grad_router, ("fsdp", "ctx"), scatter_dimension=0, tiled=True),
        lax.psum_scatter(grad_gate_vec, ("fsdp", "ctx"), scatter_dimension=0, tiled=True),
        lax.psum_scatter(grad_inner, ("fsdp", "ctx"), scatter_dimension=0, tiled=True),
        lax.psum_scatter(grad_outer, ("fsdp", "ctx"), scatter_dimension=0, tiled=True),
    )
    grad_branch = grad_middle.astype(jnp.bfloat16)
    grad_out_mat = jnp.einsum(
        "tc,td->cd", attended, grad_branch, preferred_element_type=jnp.float32
    )
    grad_attended = jnp.einsum(
        "td,cd->tc", grad_branch, out_full, preferred_element_type=jnp.float32
    ).astype(jnp.bfloat16)
    keys_again, values_again = (
        lax.all_gather(key_low, "ctx", axis=0, tiled=True),
        lax.all_gather(value_low, "ctx", axis=0, tiled=True),
    )

    def backward_group(group_index):
        query_part = head_slice(query_low, group_index)
        key_part = head_slice(keys_again, group_index)
        value_part = head_slice(values_again, group_index)
        grad_part = head_slice(grad_attended, group_index)
        log_total = lax.dynamic_index_in_dim(log_totals, group_index, 0, keepdims=False)
        scores = jnp.einsum(
            "qhd,khd->hqk", query_part, key_part, preferred_element_type=jnp.float32
        )
        scores = jnp.where(allowed[None], scores, -1e30)
        weights = jnp.exp(scores - log_total[..., None])
        grad_weights = jnp.einsum(
            "qhd,khd->hqk", grad_part, value_part, preferred_element_type=jnp.float32
        )
        offset_term = jnp.sum(weights * grad_weights, axis=-1, keepdims=True)
        grad_scores = (weights * (grad_weights - offset_term)).astype(jnp.bfloat16)
        grad_query = jnp.einsum(
            "hqk,khd->qhd", grad_scores, key_part, preferred_element_type=jnp.float32
        )
        grad_key = jnp.einsum(
            "hqk,qhd->khd", grad_scores, query_part, preferred_element_type=jnp.float32
        )
        grad_value = jnp.einsum(
            "hqk,qhd->khd",
            weights.astype(jnp.bfloat16),
            grad_part,
            preferred_element_type=jnp.float32,
        )
        return (grad_query, grad_key, grad_value)

    grad_queries, grad_keys, grad_values = lax.map(
        backward_group, jnp.arange(group_count, dtype=jnp.int32)
    )
    row_total = keys_again.shape[0]
    grad_key_rows = jnp.moveaxis(grad_keys, 0, 1).reshape(row_total, heads_width)
    grad_value_rows = jnp.moveaxis(grad_values, 0, 1).reshape(row_total, heads_width)
    key_share, value_share = (
        lax.psum_scatter(
            grad_key_rows.astype(jnp.bfloat16), "ctx", scatter_dimension=0, tiled=True
        ).astype(jnp.float32),
        lax.psum_scatter(
            grad_value_rows.astype(jnp.bfloat16), "ctx", scatter_dimension=0, tiled=True
        ).astype(jnp.float32),
    )
    grad_query_heads = jnp.moveaxis(grad_queries, 0, 1).reshape(tokens_dev, head_count, HD)
    unused_rot, rotate_pull = jax.vjp(place_heads, query_pre, key_pre)
    grad_query_pre, grad_key_pre = rotate_pull(
        (grad_query_heads, key_share.reshape(tokens_dev, head_count, HD))
    )
    grad_projected = jnp.concatenate(
        [
            grad_query_pre.reshape(tokens_dev, heads_width),
            grad_key_pre.reshape(tokens_dev, heads_width),
            value_share,
        ],
        axis=1,
    ).astype(jnp.bfloat16)
    grad_qkv = jnp.einsum("td,tc->dc", normed, grad_projected, preferred_element_type=jnp.float32)
    grad_shift = jnp.sum(grad_projected.astype(jnp.float32), axis=0)
    grad_normed_attn = jnp.einsum(
        "tc,dc->td", grad_projected, qkv_full, preferred_element_type=jnp.float32
    )
    unused_norm, first_pull = jax.vjp(rms_scale, inputs, gain_attn)
    grad_inputs_norm, grad_gain_attn = first_pull(grad_normed_attn)
    input_grad = grad_middle + grad_inputs_norm
    sum_gain_attn, sum_qkv, sum_shift, sum_out = (
        lax.psum_scatter(grad_gain_attn, ("fsdp", "ctx"), scatter_dimension=0, tiled=True),
        lax.psum_scatter(grad_qkv, ("fsdp", "ctx"), scatter_dimension=0, tiled=True),
        lax.psum_scatter(grad_shift, ("fsdp", "ctx"), scatter_dimension=0, tiled=True),
        lax.psum_scatter(grad_out_mat, ("fsdp", "ctx"), scatter_dimension=0, tiled=True),
    )
    return (
        hidden_out,
        input_grad.reshape(1, tokens_dev, model_width),
        sum_gain_attn,
        sum_qkv,
        sum_shift,
        sum_out,
        sum_gain_ffn,
        sum_router,
        sum_gate_vec,
        sum_inner,
        sum_outer,
        sum_expert_inner,
        sum_expert_outer,
    )


def solution(mesh):
    in_specs = (
        P("fsdp", "ctx", None),
        P("fsdp", "ctx"),
        P(),
        P("fsdp", "ctx", None),
        P("fsdp", "ctx", None),
        P(("fsdp", "ctx")),
        P(("fsdp", "ctx"), None),
        P(("fsdp", "ctx")),
        P(("fsdp", "ctx"), None),
        P(("fsdp", "ctx")),
        P(("fsdp", "ctx"), None),
        P(("fsdp", "ctx")),
        P(("fsdp", "ctx"), None),
        P(("fsdp", "ctx"), None),
        P("ctx", "fsdp", None),
        P("ctx", "fsdp", None),
    )
    out_specs = (
        P("fsdp", "ctx", None),
        P("fsdp", "ctx", None),
        P(("fsdp", "ctx")),
        P(("fsdp", "ctx"), None),
        P(("fsdp", "ctx")),
        P(("fsdp", "ctx"), None),
        P(("fsdp", "ctx")),
        P(("fsdp", "ctx"), None),
        P(("fsdp", "ctx")),
        P(("fsdp", "ctx"), None),
        P(("fsdp", "ctx"), None),
        P("ctx", "fsdp", None),
        P("ctx", "fsdp", None),
    )
    return jax.shard_map(local, mesh=mesh, in_specs=in_specs, out_specs=out_specs, check_vma=False)
```

profile of v0, /device:TPU:0, one launch (start us, length us, event | category | flops | bytes accessed | tf_op | source)
XLA Modules:
  0.0 5467.1 jit_solution(9482166103828676256)
XLA Ops:
  11.4 43.8 all-reduce.19
  56.5 113.4 %all-gather.11.cloned.1.call-done = bf16[2048,6144]{1,0:T(8,128)(2,1)} async-done(((bf16[64,6144]{1,0:T(8,128)(2,1)}), bf16[2048,6144]{1,0:T(8,128)(2,1)}) %all-gather.11.cloned.1.call-update) | async-done | bytes 25165840 | tf_op jit(solution)/shard_map/all_gather | solution.py:84
  212.2 40.6 all-gather.13.cloned.1.call-done
  259.2 69.5 %all-gather.15.cloned.1.call-done = bf16[1024,2048]{0,1:T(8,128)(2,1)} async-done(((bf16[128,2048]{0,1:T(8,128)(2,1)}), bf16[1024,2048]{0,1:T(8,128)(2,1)}) %all-gather.15.cloned.1.call-update) | async-done | bytes 4194320 | tf_op jit(solution)/shard_map/all_gather | solution.py:123
  328.7 23.2 while.30
  352.0 55.3 %all-gather.17.cloned.1.call-done = bf16[2048,2048]{1,0:T(8,128)(2,1)} async-done(((bf16[64,2048]{1,0:T(8,128)(2,1)}), bf16[2048,2048]{1,0:T(8,128)(2,1)}) %all-gather.17.cloned.1.call-update) | async-done | bytes 8388624 | tf_op jit(solution)/shard_map/all_gather | solution.py:86
  433.6 140.8 %all-gather.1 = bf16[32,64,8]{1,2,0:T(8,128)(2,1)S(1)} all-gather(bf16[1,64,8]{1,2,0:T(8,128)(2,1)S(1)} %bitcast.331), channel_id=1, replica_groups=mesh['fsdp'=4,'ctx'=8] {'fsdp','ctx'}, dimensions={0}, use_global_device_ids=true | all-gather | bytes 33792 | tf_op jit(solution)/shard_map/all_gather | solution.py:88
  607.8 152.5 %all-to-all-done.2 = bf16[8,128,2048]{2,1,0:T(8,128)(2,1)} async-done(((bf16[8,128,2048]{2,1,0:T(8,128)(2,1)}), bf16[8,128,2048]{2,1,0:T(8,128)(2,1)}, u32[]{:S(2)}, u32[]{:S(2)}) %all-to-all-start.2) | async-done | bytes 4194336 | tf_op jit(solution)/shard_map/all_to_all | solution.py:266
  815.4 134.4 %all-to-all-done.3 = bf16[8,128,2048]{2,1,0:T(8,128)(2,1)} async-done(((bf16[8,128,2048]{2,1,0:T(8,128)(2,1)}), bf16[8,128,2048]{2,1,0:T(8,128)(2,1)}, u32[]{:S(2)}, u32[]{:S(2)}) %all-to-all-start.3) | async-done | bytes 4194336 | tf_op jit(solution)/shard_map/all_to_all | solution.py:283
  965.2 128.2 %all-to-all-done.1 = bf16[8,128,2048]{2,1,0:T(8,128)(2,1)} async-done(((bf16[8,128,2048]{2,1,0:T(8,128)(2,1)}), bf16[8,128,2048]{2,1,0:T(8,128)(2,1)}, u32[]{:S(2)}, u32[]{:S(2)}) %all-to-all-start.1) | async-done | bytes 4194336 | tf_op jit(solution)/shard_map/all_to_all | solution.py:191
  1139.7 22.7 all-gather.21.cloned.1.call-done
  1190.4 22.7 convolution_add_fusion.3
  1223.8 69.1 %while.31 = (s32[]{:T(128)}, f32[4,128,4,128]{1,3,2,0:T(8,128)}, bf16[4,1024,4,128]{1,3,2,0:T(8,128)(2,1)}, bf16[4,1024,4,128]{1,3,2,0:T(8,128)(2,1)}, s32[4]{0:...) while((s32[]{:T(128)}, f32[4,128,4,128]{1,3,2,0:T(8,128)}, ...), condition=%wide.region_22.23_spmd.clone.clone, body=%wide.region_20.22_spmd.clone.sunk.clone | while | flops 676068864 | bytes 100421176 | solution.py:354
  1354.2 31.6 reduce-scatter.28.cloned.1.call-done
  1399.0 78.6 %reduce-scatter.30.cloned.1.call-done = bf16[128,2048]{1,0:T(8,128)(2,1)} async-done(((bf16[1024,2048]{1,0:T(8,128)(2,1)}), bf16[128,2048]{1,0:T(8,128)(2,1)}) %reduce-scatter.30.cloned.1.call-update) | async-done | bytes 524304
  1520.9 34.5 fusion.56
  1555.5 59.2 %reduce-scatter.32.cloned.1.call-done = f32[64,8]{1,0:T(8,128)} async-done(((f32[2048,8]{1,0:T(8,128)}), f32[64,8]{1,0:T(8,128)}) %reduce-scatter.32.cloned.1.call-update) | async-done | bytes 2064
  1616.1 52.4 reduce-scatter.26.cloned.1.call-done
  1671.7 91.5 %reduce-scatter.24.cloned.1.call-done = bf16[1,512,2816]{2,1,0:T(8,128)(2,1)} async-done(((bf16[1,2048,2816]{2,1,0:T(8,128)(2,1)}), bf16[1,512,2816]{2,1,0:T(8,128)(2,1)}) %reduce-scatter.24.cloned.1.call-update) | async-done | bytes 2883600 | tf_op jit(solution)/shard_map/reduce_scatter | solution.py:295
  1783.2 50.3 all-reduce.18
  1838.4 286.9 %reduce-scatter.18.cloned.1.call-done = f32[64,2048]{1,0:T(8,128)} async-done(((f32[2048,2048]{1,0:T(8,128)}), f32[64,2048]{1,0:T(8,128)}) %reduce-scatter.18.cloned.1.call-update) | async-done | bytes 524304 | tf_op jit(solution)/shard_map/reduce_scatter | solution.py:393
  2125.3 437.8 %reduce-scatter.16.cloned.1.call-done = f32[64,6144]{1,0:T(8,128)} async-done(((f32[2048,6144]{1,0:T(8,128)}), f32[64,6144]{1,0:T(8,128)}) %reduce-scatter.16.cloned.1.call-update) | async-done | bytes 1572880 | tf_op jit(solution)/shard_map/reduce_scatter | solution.py:391
  2563.1 969.1 %reduce-scatter.22.cloned.1.call-done = f32[176,2048]{1,0:T(8,128)} async-done(((f32[5632,2048]{1,0:T(8,128)}), f32[176,2048]{1,0:T(8,128)}) %reduce-scatter.22.cloned.1.call-update) | async-done | bytes 1441808 | tf_op jit(solution)/shard_map/reduce_scatter | solution.py:310
  3532.2 1927.9 %reduce-scatter.20.cloned.1.call-done = f32[64,11264]{1,0:T(8,128)} async-done(((f32[2048,11264]{1,0:T(8,128)}), f32[64,11264]{1,0:T(8,128)}) %reduce-scatter.20.cloned.1.call-update) | async-done | bytes 2883600 | tf_op jit(solution)/shard_map/reduce_scatter | solution.py:309
  (430 shorter events, 494.6 us)
Async XLA Ops:
  7.2 162.7 %all-gather.11.cloned.1.call-start = ((), (), s32[]{:S(2)}) async-start(), calls=%async_computation.13 | async-start | bytes 25952256 | tf_op jit(solution)/shard_map/all_gather | solution.py:84
  7.9 244.9 %all-gather.13.cloned.1.call-start = ((), (), s32[]{:S(2)}) async-start(), calls=%async_computation.14 | async-start | bytes 4718592 | tf_op jit(solution)/shard_map/all_gather | solution.py:124
  181.0 147.7 %all-gather.15.cloned.1.call-start = ((), (), s32[]{:S(2)}) async-start(), calls=%async_computation.15 | async-start | bytes 4718592 | tf_op jit(solution)/shard_map/all_gather | solution.py:123
  184.6 222.6 %all-gather.17.cloned.1.call-start = ((), (), s32[]{:S(2)}) async-start(), calls=%async_computation.16 | async-start | bytes 8650752 | tf_op jit(solution)/shard_map/all_gather | solution.py:86
  185.2 403.8 %all-gather.23.cloned.1.call-start = ((), (), s32[]{:S(2)}) async-start(), calls=%async_computation.19 | async-start | bytes 14417920 | tf_op jit(solution)/shard_map/all_gather | solution.py:178
  185.8 422.0 %all-gather.25.cloned.1.call-start = ((), (), s32[]{:S(2)}) async-start(), calls=%async_computation.20 | async-start | bytes 7208960 | tf_op jit(solution)/shard_map/all_gather | solution.py:179
  186.4 933.0 %all-gather.19.cloned.1.call-start = ((), (), s32[]{:S(2)}) async-start(), calls=%async_computation.17 | async-start | bytes 47579136 | tf_op jit(solution)/shard_map/all_gather | solution.py:90
  187.1 975.3 %all-gather.21.cloned.1.call-start = ((), (), s32[]{:S(2)}) async-start(), calls=%async_computation.18 | async-start | bytes 23789568 | tf_op jit(solution)/shard_map/all_gather | solution.py:91
  207.0 205.1 %copy-start.42 = (f32[2048]{0:T(1024)}, f32[2048]{0:T(1024)S(1)}, u32[]{:S(2)}) copy-start(f32[2048]{0:T(1024)S(1)} %convert_element_type.224) | copy-start | bytes 24580
  413.2 706.2 %copy-start = (bf16[128,2048]{1,0:T(8,128)(2,1)}, bf16[128,2048]{1,0:T(8,128)(2,1)S(1)}, u32[]{:S(2)}) copy-start(bf16[128,2048]{1,0:T(8,128)(2,1)S(1)} %multiply_convert_fusion.5) | copy-start | bytes 1572868
  419.2 164.8 %all-to-all-start = ((bf16[8,128,2048]{2,1,0:T(8,128)(2,1)}), bf16[8,128,2048]{2,1,0:T(8,128)(2,1)}, u32[]{:S(2)}, u32[]{:S(2)}) async-start(bf16[8,128,2048]{2,1,0:T(8,128)(2,1)} %bitcast.305), calls=%async_computation | async-start | bytes 8388608 | tf_op jit(solution)/shard_map/all_to_all | solution.py:181
  584.0 176.3 %all-to-all-start.2 = ((bf16[8,128,2048]{2,1,0:T(8,128)(2,1)}), bf16[8,128,2048]{2,1,0:T(8,128)(2,1)}, u32[]{:S(2)}, u32[]{:S(2)}) async-start(bf16[8,128,2048]{2,1,0:T(8,128)(2,1)} %bitcast.306), calls=%async_computation.2 | async-start | bytes 8388608 | tf_op jit(solution)/shard_map/all_to_all | solution.py:266
  796.7 153.1 %all-to-all-start.3 = ((bf16[8,128,2048]{2,1,0:T(8,128)(2,1)}), bf16[8,128,2048]{2,1,0:T(8,128)(2,1)}, u32[]{:S(2)}, u32[]{:S(2)}) async-start(bf16[8,128,2048]{2,1,0:T(8,128)(2,1)} %fusion.31), calls=%async_computation.3 | async-start | bytes 8388608 | tf_op jit(solution)/shard_map/all_to_all | solution.py:283
  815.4 139.2 %copy-start.54 = (bf16[2048]{0:T(1024)(128)(2,1)S(1)}, bf16[2048]{0:T(1024)(128)(2,1)}, u32[]{:S(2)}) copy-start(bf16[2048]{0:T(1024)(128)(2,1)} %get-tuple-element.375) | copy-start | bytes 12292
  949.8 143.6 %all-to-all-start.1 = ((bf16[8,128,2048]{2,1,0:T(8,128)(2,1)}), bf16[8,128,2048]{2,1,0:T(8,128)(2,1)}, u32[]{:S(2)}, u32[]{:S(2)}) async-start(bf16[8,128,2048]{2,1,0:T(8,128)(2,1)} %fusion.28), calls=%async_computation.1 | async-start | bytes 8388608 | tf_op jit(solution)/shard_map/all_to_all | solution.py:191
  954.4 431.4 %reduce-scatter.28.cloned.1.call-start = ((), (), s32[]{:S(2)}) async-start(), calls=%async_computation.27 | async-start | bytes 4718592
  1299.4 178.1 %reduce-scatter.30.cloned.1.call-start = ((), (), s32[]{:S(2)}) async-start(), calls=%async_computation.28 | async-start | bytes 4718592
  1306.0 308.6 %reduce-scatter.32.cloned.1.call-start = ((), (), s32[]{:S(2)}) async-start(), calls=%async_computation.29 | async-start | bytes 1081344
  1308.4 360.0 %reduce-scatter.26.cloned.1.call-start = ((), (), s32[]{:S(2)}) async-start(), calls=%async_computation.26 | async-start | bytes 7208960 | tf_op jit(solution)/shard_map/reduce_scatter | solution.py:298
  1319.3 444.0 %reduce-scatter.24.cloned.1.call-start = ((), (), s32[]{:S(2)}) async-start(), calls=%async_computation.25 | async-start | bytes 14417920 | tf_op jit(solution)/shard_map/reduce_scatter | solution.py:295
  1339.5 785.8 %reduce-scatter.18.cloned.1.call-start = ((), (), s32[]{:S(2)}) async-start(), calls=%async_computation.22 | async-start | bytes 17301504 | tf_op jit(solution)/shard_map/reduce_scatter | solution.py:393
  1349.1 1214.0 %reduce-scatter.16.cloned.1.call-start = ((), (), s32[]{:S(2)}) async-start(), calls=%async_computation.21 | async-start | bytes 51904512 | tf_op jit(solution)/shard_map/reduce_scatter | solution.py:391
  1500.3 2031.9 %reduce-scatter.22.cloned.1.call-start = ((), (), s32[]{:S(2)}) async-start(), calls=%async_computation.24 | async-start | bytes 47579136 | tf_op jit(solution)/shard_map/reduce_scatter | solution.py:310
  1520.6 3939.6 %reduce-scatter.20.cloned.1.call-start = ((), (), s32[]{:S(2)}) async-start(), calls=%async_computation.23 | async-start | bytes 95158272 | tf_op jit(solution)/shard_map/reduce_scatter | solution.py:309
  (81 other events, 2186.1 us)
Sparse Core Ops, SparseCore 0:
  11.0 158.8 all-gather.10
  181.1 71.5 all-gather.12
  255.4 73.2 all-gather.14
  331.6 75.6 all-gather.16
  408.6 74.7 all-gather.22
  484.9 43.4 all-gather.24
  531.2 409.8 all-gather.18
  944.0 218.3 all-gather.20
  1299.6 86.2 reduce-scatter.27
  1389.8 87.7 reduce-scatter.29
  1479.8 134.7 reduce-scatter.31
  1617.2 51.1 reduce-scatter.25
  1671.0 92.1 reduce-scatter.23
  1765.9 359.3 reduce-scatter.17
  2132.2 430.8 reduce-scatter.15
  2565.8 966.3 reduce-scatter.21
  3535.0 1925.1 reduce-scatter.19
where the time goes:
time: 5480 us; the launch traced here: 5470 us
  waiting for transfers between devices  4660 us (85%)
  matrix products  314 us (6%)
  blocking collectives  254 us (5%)
  local copies, waits for them, and re-layouts  147 us (3%)
    reduce_scatter x1, waiting for transfers between devices, local(): lax.psum_scatter(grad_inner, ('fsdp', 'ctx'), scatter_dimension=0, tiled=...  1930 us
    reduce_scatter x1, waiting for transfers between devices, local(): lax.psum_scatter(grad_outer, ('fsdp', 'ctx'), scatter_dimension=0, tiled=...  969 us
    reduce_scatter x1, waiting for transfers between devices, local(): lax.psum_scatter(grad_qkv, ('fsdp', 'ctx'), scatter_dimension=0, tiled=True)  438 us
    reduce_scatter x1, waiting for transfers between devices, local(): lax.psum_scatter(grad_out_mat, ('fsdp', 'ctx'), scatter_dimension=0, tile...  287 us
    unnamed x20, waiting for transfers between devices  173 us
    all_to_all x1, waiting for transfers between devices, local(): lax.all_to_all(grad_outgoing, 'ctx', split_axis=0, concat_axis=0, tiled=T...  153 us
    all_gather x1, blocking collectives, local(): lax.all_gather(router_weight, ('fsdp', 'ctx'), axis=0, tiled=True)  141 us
    all_to_all x1, waiting for transfers between devices, local(): lax.all_to_all(grad_expert_rows.reshape(ctx_count, local_experts * capaci...  134 us
  transfers between devices with their start and end apart: 21, of which 17 were waited for; matrix products, arithmetic and copies ran while one was open for 7% of the time, Pallas kernels for 0%

commit v1 on v0

--- a/solution.py
+++ b/solution.py
@@ -47,7 +47,7 @@
     return jnp.dot(left, right, preferred_element_type=jnp.float32)
 
 
-def local(
+def gathered_plan(
     hidden_in,
     segments,
     block_pairs,
@@ -409,6 +409,319 @@
     )
 
 
+def over(axis, array, dim=0):
+    return lax.all_gather(array, axis, axis=dim, tiled=True)
+
+
+def reduce_over(axis, array, dim=0):
+    return lax.psum_scatter(array, axis, scatter_dimension=dim, tiled=True)
+
+
+def exchange(array):
+    return lax.all_to_all(array, "ctx", split_axis=0, concat_axis=0, tiled=True)
+
+
+def transposed_dot(left, right):
+    return lax.dot_general(
+        left, right, (((0,), (0,)), ((), ())), preferred_element_type=jnp.float32
+    )
+
+
+def dot_transposed(left, right):
+    return lax.dot_general(
+        left, right, (((1,), (1,)), ((), ())), preferred_element_type=jnp.float32
+    )
+
+
+def split_plan(
+    hidden_in,
+    segments,
+    block_pairs,
+    routes,
+    out_grad,
+    norm_gain_attn,
+    qkv_weight,
+    qkv_bias,
+    out_weight,
+    norm_gain_ffn,
+    router_weight,
+    shared_gate_weight,
+    shared_in_weight,
+    shared_out_weight,
+    expert_in_weight,
+    expert_out_weight,
+):
+    low = jnp.bfloat16
+    full = jnp.float32
+    tokens_dev, width = hidden_in.shape[1:]
+    block_len = tokens_dev // 2
+    ctx_count = lax.axis_size("ctx")
+    fsdp_count = lax.axis_size("fsdp")
+    ctx_rank = lax.axis_index("ctx")
+    dev_count = ctx_count * fsdp_count
+    row_len = ctx_count * tokens_dev
+    head_count = width // HD
+    shard = qkv_weight.shape[0]
+    expert_count = router_weight.shape[1]
+    shared_shard = shared_out_weight.shape[0]
+    shared_width = fsdp_count * shared_shard
+    expert_width = expert_out_weight.shape[1] * fsdp_count
+    pair_rank = ctx_rank // 2
+    side = ctx_rank % 2
+    pairs = ctx_count // 2
+    head_order = [j + (p * 2 + t) * pairs for j in range(pairs) for p in range(2) for t in range(2)]
+
+    small = jnp.concatenate(
+        [
+            norm_gain_attn,
+            norm_gain_ffn,
+            shared_gate_weight,
+            router_weight.T.reshape(-1),
+            qkv_bias,
+        ]
+    )[None, :]
+    small_all = over(("fsdp", "ctx"), small)
+    gain_attn = small_all[:, :shard].reshape(width).astype(full)
+    gain_ffn = small_all[:, shard : 2 * shard].reshape(width).astype(full)
+    gate_full = small_all[:, 2 * shard : 3 * shard].reshape(width)
+    router_t = (
+        small_all[:, 3 * shard : (3 + expert_count) * shard]
+        .reshape(dev_count, expert_count, shard)
+        .transpose(1, 0, 2)
+        .reshape(expert_count, width)
+    )
+    bias_full = small_all[:, (3 + expert_count) * shard :].reshape(3, head_count, HD)
+    router_gate = jnp.concatenate([router_t, gate_full[None, :]], axis=0)
+    own_routes = routes.reshape(tokens_dev, -1)
+    own_seg = segments.reshape(1, tokens_dev)
+    numbers = over("ctx", jnp.concatenate([own_routes.T, own_seg], axis=0)[None])
+    row_seg = numbers[:, -1].reshape(row_len)
+    routed_here = jnp.any(numbers[:, :-1] == ctx_rank, axis=1).reshape(row_len)
+
+    qkv_parts = (
+        qkv_weight.reshape(shard, 3, head_count, HD)[:, :, jnp.array(head_order)]
+        .reshape(shard, 3, ctx_count, 2 * HD)
+        .transpose(2, 0, 1, 3)
+        .reshape(ctx_count, shard, 6 * HD)
+    )
+    qkv_c = over("fsdp", exchange(qkv_parts).reshape(ctx_count * shard, 6 * HD))
+    inner_parts = (
+        shared_in_weight.reshape(shard, 2, fsdp_count, ctx_count, shared_shard)
+        .transpose(3, 0, 1, 2, 4)
+        .reshape(ctx_count, shard, 2 * shared_width)
+    )
+    inner_c = over("fsdp", exchange(inner_parts).reshape(ctx_count * shard, 2 * shared_width))
+    outer_c = over("fsdp", shared_out_weight)
+    out_full = over(("fsdp", "ctx"), out_weight)
+    expert_inner = over("fsdp", expert_in_weight[0])
+    expert_outer = over("fsdp", expert_out_weight[0])
+    out_heads = out_full.reshape(head_count, HD, width)
+    my_heads = [pair_rank + (side * 2 + t) * pairs for t in range(2)]
+    out_c = jnp.concatenate(
+        [lax.dynamic_index_in_dim(out_heads, h, 0, keepdims=False) for h in my_heads], axis=0
+    )
+    bias_c = jnp.concatenate(
+        [lax.dynamic_index_in_dim(bias_full, h, 1, keepdims=False) for h in my_heads], axis=1
+    ).reshape(6 * HD)
+
+    offsets = jnp.arange(block_len, dtype=jnp.int32)
+    positions = (block_pairs[:, None] * block_len + offsets[None, :]).reshape(row_len)
+    own_inputs = hidden_in.reshape(tokens_dev, width)
+    inputs = own_inputs.astype(full)
+    row_inputs = over("ctx", own_inputs).astype(full)
+    row_upstream = over("ctx", out_grad.reshape(tokens_dev, width))
+    row_normed = rms_scale(row_inputs, gain_attn).astype(low)
+    projected = matmul_low(row_normed, qkv_c) + bias_c.astype(full)
+    query_pre = projected[:, : 2 * HD].reshape(row_len, 2, HD)
+    key_pre = projected[:, 2 * HD : 4 * HD].reshape(row_len, 2, HD)
+
+    def place_heads(query_in, key_in):
+        return (rotate(query_in, positions) * HD ** (-0.5), rotate(key_in, positions))
+
+    query_rot, key_rot = place_heads(query_pre, key_pre)
+    queries = query_rot.astype(low)
+    keys = key_rot.astype(low)
+    values = projected[:, 4 * HD :].reshape(row_len, 2, HD).astype(low)
+    seg_real = row_seg.astype(full)
+    allowed = visible(positions, seg_real, positions, seg_real)
+
+    def score_part():
+        scores = jnp.einsum("qhd,khd->hqk", queries, keys, preferred_element_type=full)
+        return jnp.where(allowed[None], scores, -1e30)
+
+    scores = score_part()
+    highest = jnp.max(scores, axis=-1, keepdims=True)
+    log_total = highest + jnp.log(jnp.sum(jnp.exp(scores - highest), axis=-1, keepdims=True))
+    probs = jnp.exp(scores - log_total)
+    attended_row = (
+        jnp.einsum("hqk,khd->qhd", probs.astype(low), values, preferred_element_type=full)
+        .astype(low)
+        .reshape(row_len, 2 * HD)
+    )
+    landed = exchange(attended_row.reshape(ctx_count, tokens_dev, 2 * HD))
+    places_of = [head_order.index(h) for h in range(head_count)]
+    attended = jnp.concatenate(
+        [landed[p // 2, :, (p % 2) * HD : (p % 2 + 1) * HD] for p in places_of], axis=1
+    )
+    middle = inputs + matmul_low(attended, out_full)
+    normed_ffn = rms_scale(middle, gain_ffn).astype(low)
+
+    row_ffn = over("ctx", normed_ffn)
+    row_logits = dot_transposed(row_ffn, router_gate)
+    row_probs = jax.nn.softmax(row_logits[:, :expert_count], axis=-1)
+    expert_ids = jnp.arange(expert_count, dtype=jnp.int32)
+    here = jnp.where(
+        routed_here, jnp.sum(jnp.where(expert_ids[None, :] == ctx_rank, row_probs, 0.0), axis=1), 0.0
+    )
+    row_gate = jax.nn.sigmoid(row_logits[:, expert_count])
+    expert_gu = matmul_low(row_ffn, expert_inner)
+    expert_hidden = swiglu_mix(expert_gu, expert_width).astype(low)
+    expert_result = matmul_low(expert_hidden, expert_outer).astype(low).astype(full)
+    shared_gu = matmul_low(row_ffn, inner_c)
+    shared_hidden = swiglu_mix(shared_gu, shared_width).astype(low)
+    shared_out = matmul_low(shared_hidden, outer_c)
+    upstream_row = row_upstream.astype(full)
+    out_part = (row_gate[:, None] * shared_out + here[:, None] * expert_result).astype(low)
+    gate_dot = jnp.sum(upstream_row * shared_out, axis=1)
+    expert_dot = jnp.where(routed_here, jnp.sum(upstream_row * expert_result, axis=1), 0.0)
+    own_dots = exchange(
+        jnp.stack([gate_dot, expert_dot]).reshape(2, ctx_count, tokens_dev).transpose(1, 0, 2)
+    )
+    output = middle + reduce_over("ctx", out_part).astype(full)
+    hidden_out = output.astype(low).reshape(1, tokens_dev, width)
+
+    grad_shared_out = (row_gate[:, None] * upstream_row).astype(low)
+    grad_buffers = (here[:, None] * upstream_row).astype(low)
+    grad_hidden = dot_transposed(grad_shared_out, outer_c)
+    unused_mix, mix_pull = jax.vjp(partial(swiglu_mix, hidden_width=shared_width), shared_gu)
+    grad_shared_gu = mix_pull(grad_hidden)[0].astype(low)
+    grad_expert_hidden = dot_transposed(grad_buffers, expert_outer)
+    unused_mix, expert_pull = jax.vjp(partial(swiglu_mix, hidden_width=expert_width), expert_gu)
+    grad_expert_gu = expert_pull(grad_expert_hidden)[0].astype(low)
+    grad_rows = dot_transposed(grad_expert_gu, expert_inner).astype(low).astype(full)
+    grad_ffn_part = (dot_transposed(grad_shared_gu, inner_c) + grad_rows).astype(low)
+    grad_normed = reduce_over("ctx", grad_ffn_part).astype(full)
+    sum_expert_inner = reduce_over("fsdp", transposed_dot(row_ffn, grad_expert_gu).astype(low))
+    sum_expert_outer = reduce_over("fsdp", transposed_dot(expert_hidden, grad_buffers).astype(low))
+    sum_outer = reduce_over("fsdp", transposed_dot(shared_hidden, grad_shared_out).astype(low))
+    sum_inner_c = reduce_over("fsdp", transposed_dot(row_ffn, grad_shared_gu).astype(low))
+    sum_inner = (
+        exchange(sum_inner_c.reshape(ctx_count, shard, 2 * shared_width))
+        .reshape(ctx_count, shard, 2, fsdp_count, shared_shard)
+        .transpose(1, 2, 3, 0, 4)
+        .reshape(shard, 2 * fsdp_count * ctx_count * shared_shard)
+    )
+
+    own_logits = dot_transposed(normed_ffn, router_gate)
+    router_probs = jax.nn.softmax(own_logits[:, :expert_count], axis=-1)
+    gate_value = jax.nn.sigmoid(own_logits[:, expert_count])
+    grad_gate_logit = gate_value * (1.0 - gate_value) * jnp.sum(own_dots[:, 0], axis=0)
+    grad_choice = own_dots[:, 1].T
+    grad_logits = router_probs * (
+        grad_choice - jnp.sum(router_probs * grad_choice, axis=1, keepdims=True)
+    )
+    grad_small = jnp.concatenate([grad_logits, grad_gate_logit[:, None]], axis=1).astype(low)
+    grad_router_gate = transposed_dot(grad_small, normed_ffn)
+    grad_normed = grad_normed + matmul_low(grad_small, router_gate)
+    unused_norm, norm_pull = jax.vjp(rms_scale, middle, gain_ffn)
+    grad_middle_norm, grad_gain_ffn = norm_pull(grad_normed)
+    grad_middle = out_grad.reshape(tokens_dev, width).astype(full) + grad_middle_norm
+
+    row_branch = over("ctx", grad_middle.astype(low))
+    grad_attended = dot_transposed(row_branch, out_c).astype(low).reshape(row_len, 2, HD)
+    grad_out_c = transposed_dot(attended_row, row_branch).astype(low).reshape(2, HD, width)
+    padded_out = jnp.concatenate(
+        [jnp.where(side == p, grad_out_c, jnp.zeros_like(grad_out_c)) for p in range(2)], axis=0
+    )
+    pair_out = reduce_over("fsdp", padded_out).reshape(2, shard, width)
+    kept = lax.dynamic_index_in_dim(pair_out, side, 0, keepdims=False)
+    given = lax.dynamic_index_in_dim(pair_out, 1 - side, 0, keepdims=False)
+    taken = lax.ppermute(given, "ctx", [(i, i ^ 1) for i in range(ctx_count)])
+    sum_out = kept.astype(full) + taken.astype(full)
+
+    grad_probs = jnp.einsum("qhd,khd->hqk", grad_attended, values, preferred_element_type=full)
+    weights = jnp.exp(score_part() - log_total)
+    offset_term = jnp.sum(weights * grad_probs, axis=-1, keepdims=True)
+    grad_scores = (weights * (grad_probs - offset_term)).astype(low)
+    grad_queries = jnp.einsum("hqk,khd->qhd", grad_scores, keys, preferred_element_type=full)
+    grad_keys = jnp.einsum("hqk,qhd->khd", grad_scores, queries, preferred_element_type=full)
+    grad_values = jnp.einsum(
+        "hqk,qhd->khd", weights.astype(low), grad_attended, preferred_element_type=full
+    )
+    unused_rot, rotate_pull = jax.vjp(place_heads, query_pre, key_pre)
+    grad_query_pre, grad_key_pre = rotate_pull((grad_queries, grad_keys))
+    grad_projected = jnp.concatenate(
+        [
+            grad_query_pre.reshape(row_len, 2 * HD),
+            grad_key_pre.reshape(row_len, 2 * HD),
+            grad_values.reshape(row_len, 2 * HD),
+        ],
+        axis=1,
+    ).astype(low)
+    grad_attn_part = dot_transposed(grad_projected, qkv_c).astype(low)
+    grad_normed_attn = reduce_over("ctx", grad_attn_part).astype(full)
+    sum_qkv_c = reduce_over("fsdp", transposed_dot(row_normed, grad_projected).astype(low))
+    sum_qkv = (
+        exchange(sum_qkv_c.reshape(ctx_count, shard, 6 * HD))
+        .reshape(ctx_count, shard, 3, 2, HD)
+        .transpose(1, 2, 0, 3, 4)
+        .reshape(shard, 3, head_count, HD)[:, :, jnp.array(places_of)]
+        .reshape(shard, 3 * width)
+    )
+    grad_bias_c = jnp.sum(grad_projected.astype(full), axis=0).reshape(3, 1, 2, HD)
+    mine = (jnp.arange(ctx_count) == ctx_rank)[None, :, None, None]
+    grad_bias = (
+        jnp.where(mine, grad_bias_c, 0.0)
+        .reshape(3, head_count, HD)[:, jnp.array(places_of)]
+        .reshape(dev_count, -1)
+    )
+    unused_norm, first_pull = jax.vjp(rms_scale, inputs, gain_attn)
+    grad_inputs_norm, grad_gain_attn = first_pull(grad_normed_attn)
+    input_grad = grad_middle + grad_inputs_norm
+    small_grads = jnp.concatenate(
+        [
+            grad_gain_attn.reshape(dev_count, shard),
+            grad_gain_ffn.reshape(dev_count, shard),
+            grad_router_gate.reshape(expert_count + 1, dev_count, shard)
+            .transpose(1, 0, 2)
+            .reshape(dev_count, (expert_count + 1) * shard),
+            grad_bias,
+        ],
+        axis=1,
+    )
+    sums = reduce_over(("fsdp", "ctx"), small_grads)[0]
+    sum_router = sums[2 * shard : (2 + expert_count) * shard].reshape(expert_count, shard).T
+    return (
+        hidden_out,
+        input_grad.reshape(1, tokens_dev, width),
+        sums[:shard],
+        sum_qkv.astype(full),
+        sums[(3 + expert_count) * shard :],
+        sum_out,
+        sums[shard : 2 * shard],
+        sum_router,
+        sums[(2 + expert_count) * shard : (3 + expert_count) * shard],
+        sum_inner.astype(full),
+        sum_outer.astype(full),
+        sum_expert_inner.astype(full)[None],
+        sum_expert_outer.astype(full)[None],
+    )
+
+
+def local(*arrays):
+    width = arrays[0].shape[2]
+    ctx_count = lax.axis_size("ctx")
+    shard = arrays[6].shape[0]
+    fits = (
+        width == 2 * ctx_count * HD
+        and 2 * shard == HD
+        and ctx_count % 2 == 0
+        and lax.axis_size("fsdp") * ctx_count * shard == width
+        and arrays[14].shape[0] == 1
+    )
+    return split_plan(*arrays) if fits else gathered_plan(*arrays)
+
+
 def solution(mesh):
     in_specs = (
         P("fsdp", "ctx", None),

time: 5480 us -> 1430 us (0.26)
  waiting for transfers between devices: 4660 us -> 834 us
  matrix products: 314 us -> 212 us
  local copies, waits for them, and re-layouts: 147 us -> 81.9 us
    reduce_scatter x6 -> x9, waiting for transfers between devices: 3770 us -> 412 us  [reduce_over(): return lax.psum_scatter(array, axis, scatter_dimension=dim, tiled=True)]
    all_to_all x4, waiting for transfers between devices: 415 us -> 25.7 us  [exchange(): return lax.all_to_all(array, 'ctx', split_axis=0, concat_axis=0, tiled=True)]
    dot_general x44 -> x21, matrix products: 265 us -> 151 us  [the longest x8 70.8 us: dot_transposed(): lax.dot_general(left, right, (((1,), (1,)), ((), ())), preferred_element_...]
    all_to_all x0 -> x2, blocking collectives: none -> 110 us  [exchange(): return lax.all_to_all(array, 'ctx', split_axis=0, concat_axis=0, tiled=True)]
    unnamed x2 -> x0, blocking collectives: 94.1 us -> none
    all_gather x2, blocking collectives: 159 us -> 97.3 us  [over(): return lax.all_gather(array, axis, axis=dim, tiled=True)]
    unnamed x20 -> x21, waiting for transfers between devices: 173 us -> 128 us
    all_gather x8 -> x10, waiting for transfers between devices: 301 us -> 268 us  [over(): return lax.all_gather(array, axis, axis=dim, tiled=True)]
  transfers between devices with their start and end apart: 21 -> 25, of which waited for: 17 -> 18; matrix products, arithmetic and copies ran while one was open for 7% -> 21% of each run, Pallas kernels for 0% -> 0%
where the time goes in v1:
time: 1430 us; the launch traced here: 1420 us
  waiting for transfers between devices  834 us (58%)
  matrix products  212 us (15%)
  blocking collectives  208 us (15%)
  local copies, waits for them, and re-layouts  81.9 us (6%)
  other arithmetic  47.1 us (3%)
  starting transfers between devices  21.5 us (2%)
  between operations  16 us (1%)
    reduce_scatter x9, waiting for transfers between devices, reduce_over(): return lax.psum_scatter(array, axis, scatter_dimension=dim, tiled=True)  412 us
    all_gather x10, waiting for transfers between devices, over(): return lax.all_gather(array, axis, axis=dim, tiled=True)  268 us
    unnamed x21, waiting for transfers between devices  128 us
    all_to_all x2, blocking collectives, exchange(): return lax.all_to_all(array, 'ctx', split_axis=0, concat_axis=0, tiled=True)  110 us
    all_gather x2, blocking collectives, over(): return lax.all_gather(array, axis, axis=dim, tiled=True)  97.3 us
    dot_general x8, matrix products, dot_transposed(): lax.dot_general(left, right, (((1,), (1,)), ((), ())), preferred_element_...  70.8 us
    dot_general x7, matrix products, transposed_dot(): lax.dot_general(left, right, (((0,), (0,)), ((), ())), preferred_element_...  61.4 us
    dot_general x7, matrix products, matmul_low(): return jnp.dot(left, right, preferred_element_type=jnp.float32)  60.3 us
  transfers between devices with their start and end apart: 25, of which 18 were waited for; matrix products, arithmetic and copies ran while one was open for 21% of the time, Pallas kernels for 0%

profile of v1, /device:TPU:0, one launch (start us, length us, event | category | flops | bytes accessed | tf_op | source)
XLA Modules:
  0.0 1419.4 jit_solution(13169767724963702494)
XLA Ops:
  13.1 44.1 %all_to_all.30 = bf16[8,64,768]{2,1,0:T(8,128)(2,1)} all-to-all(bf16[8,64,768]{2,1,0:T(8,128)(2,1)S(1)} %reshape.501), channel_id=1, replica_groups=mesh['fsdp'=4,'ctx'=8] {'ctx'}, dimensions={0} | all-to-all | bytes 1572864 | tf_op jit(solution)/shard_map/all_to_all | solution.py:421
  58.2 66.9 %all-gather.6 = bf16[32,1,896]{2,1,0:T(2,128)(2,1)S(1)} all-gather(bf16[1,1,896]{2,1,0:T(2,128)(2,1)S(1)} %reshape.576), channel_id=3, replica_groups=mesh['fsdp'=4,'ctx'=8] {'fsdp','ctx'}, dimensions={0}, use_global_device_ids=true | all-gather | bytes 59136 | tf_op jit(solution)/shard_map/all_gather | solution.py:413
  125.7 30.4 %all-gather.7 = s32[8,5,128]{2,1,0:T(8,128)S(1)} all-gather(s32[1,5,128]{2,1,0:T(8,128)S(1)} %add_bitcast_fusion), channel_id=4, replica_groups=mesh['fsdp'=4,'ctx'=8] {'ctx'}, dimensions={0}, use_global_device_ids=true | all-gather | bytes 23040 | tf_op jit(solution)/shard_map/all_gather | solution.py:413
  199.7 19.1 %all-to-all-done.1 = bf16[8,128,256]{2,1,0:T(8,128)(2,1)S(1)} async-done(((bf16[8,128,256]{2,1,0:T(8,128)(2,1)}), bf16[8,128,256]{2,1,0:T(8,128)(2,1)S(1)}, u32[]{:S(2)}, u32[]{:S(2)}) %all-to-all-start.1) | async-done | bytes 524320 | tf_op jit(solution)/shard_map/all_to_all | solution.py:421
  238.6 66.1 %all_to_all.31 = bf16[8,64,1408]{2,1,0:T(8,128)(2,1)} all-to-all(bf16[8,64,1408]{2,1,0:T(8,128)(2,1)S(1)} %reshape.510), channel_id=1, replica_groups=mesh['fsdp'=4,'ctx'=8] {'ctx'}, dimensions={0} | all-to-all | bytes 2883584 | tf_op jit(solution)/shard_map/all_to_all | solution.py:421
  306.1 14.1 all-gather.23.cloned.1.call-done
  323.7 72.9 %all-gather.33.cloned.1.call-done = bf16[1,2048,2816]{2,1,0:T(8,128)(2,1)} async-done(((bf16[1,512,2816]{2,1,0:T(8,128)(2,1)}), bf16[1,2048,2816]{2,1,0:T(8,128)(2,1)}) %all-gather.33.cloned.1.call-update) | async-done | bytes 11534352 | tf_op jit(solution)/shard_map/all_gather | solution.py:413
  396.6 18.9 %fusion.2 = f32[1024,2816]{1,0:T(8,128)} fusion(bf16[1024,2048]{1,0:T(8,128)(2,1)} %all-gather.23.cloned.1.call-done, bf16[1,2048,2816]{2,1,0:T(8,128)(2,1)} %all-gather.33.cloned.1.call-done), kind=kOutput, calls=%fused_computation.9 | convolution fusion | flops 11811160064 | bytes 27262976 | tf_op jit(solution)/shard_map/dot_general | solution.py:47
  415.6 56.5 %all-gather.37.cloned.1.call-done = bf16[1,1024,2048]{2,1,0:T(8,128)(2,1)} async-done(((bf16[1,128,2048]{2,1,0:T(8,128)(2,1)}), bf16[1,1024,2048]{2,1,0:T(8,128)(2,1)}) %all-gather.37.cloned.1.call-update) | async-done | bytes 4194320 | tf_op jit(solution)/shard_map/all_gather | solution.py:413
  472.0 43.3 %all-gather.35.cloned.1.call-done = bf16[1,1408,2048]{2,1,0:T(8,128)(2,1)} async-done(((bf16[1,352,2048]{2,1,0:T(8,128)(2,1)}), bf16[1,1408,2048]{2,1,0:T(8,128)(2,1)}) %all-gather.35.cloned.1.call-update) | async-done | bytes 5767184 | tf_op jit(solution)/shard_map/all_gather | solution.py:413
  515.3 17.7 %fusion.46 = (f32[1024,1408]{1,0:T(8,128)}, f32[1024,1408]{1,0:T(8,128)}, bf16[1024,1408]{1,0:T(8,128)(2,1)}) fusion(f32[1024,2816]{1,0:T(8,128)} %fusion.2, bf16[1,1408,2048]{2,1,0:T(8,128)(2,1)} %all-gather.35.cloned.1.call-done, bf16[1,1024,2048]{2,1,0:T(8,128)(2,1)} %all-gather.37.cloned.1.call-done, f32[1024]{0:T(1024)S(1)} %bitcast_select_fusion.2), kind=kOutput, calls=%fused_computation.116 | convolution fusion | flops 5932056576 | bytes 35917824 | tf_op jit(solution)/shard_map/dot_general | solution.py:431
  533.0 27.3 %all-gather.25.cloned.1.call-done = bf16[2048,1408]{1,0:T(8,128)(2,1)} async-done(((bf16[512,1408]{1,0:T(8,128)(2,1)}), bf16[2048,1408]{1,0:T(8,128)(2,1)}) %all-gather.25.cloned.1.call-update) | async-done | bytes 5767184 | tf_op jit(solution)/shard_map/all_gather | solution.py:413
  572.0 19.7 %fusion = bf16[1024,2048]{1,0:T(8,128)(2,1)} fusion(bf16[1,2048,2816]{2,1,0:T(8,128)(2,1)} %all-gather.33.cloned.1.call-done, f32[1024,1408]{1,0:T(8,128)} %get-tuple-element.20, f32[1024,1408]{1,0:T(8,128)} %get-tuple-element.19), kind=kOutput, calls=%fused_computation.7 | convolution fusion | flops 11816927232 | bytes 27262976 | tf_op jit(solution)/shard_map/dot_general | solution.py:431
  643.9 57.5 %reduce-scatter.12.cloned.1.call-done = bf16[128,2048]{1,0:T(8,128)(2,1)} async-done(((bf16[1024,2048]{1,0:T(8,128)(2,1)}), bf16[128,2048]{1,0:T(8,128)(2,1)}) %reduce-scatter.12.cloned.1.call-update) | async-done | bytes 524304 | tf_op jit(solution)/shard_map/reduce_scatter | solution.py:417
  704.3 12.3 convolution_convert_fusion.2
  724.4 53.1 %all-gather.29.cloned.1.call-done = bf16[1024,2048]{1,0:T(8,128)(2,1)} async-done(((bf16[128,2048]{1,0:T(8,128)(2,1)}), bf16[1024,2048]{1,0:T(8,128)(2,1)}) %all-gather.29.cloned.1.call-update) | async-done | bytes 4194320 | tf_op jit(solution)/shard_map/all_gather | solution.py:413
  833.9 20.3 %convolution_convert_fusion = bf16[2048,2816]{1,0:T(8,128)(2,1)} fusion(bf16[1024,2048]{1,0:T(8,128)(2,1)} %all-gather.23.cloned.1.call-done, f32[1024,1408]{1,0:T(8,128)} %get-tuple-element.20, f32[1024,1408]{1,0:T(8,128)} %get-tuple-element.19), kind=kOutput, calls=%fused_computation.12 | convolution fusion | flops 11822694400 | bytes 27262976 | tf_op jit(solution)/shard_map/dot_general | solution.py:425
  875.1 31.6 %reduce-scatter.18.cloned.1.call-done = bf16[1,128,2048]{2,1,0:T(8,128)(2,1)} async-done(((bf16[4,128,2048]{2,1,0:T(8,128)(2,1)}), bf16[1,128,2048]{2,1,0:T(8,128)(2,1)}) %reduce-scatter.18.cloned.1.call-update) | async-done | bytes 524304 | tf_op jit(solution)/shard_map/reduce_scatter | solution.py:417
  909.2 54.8 %reduce-scatter.26.cloned.1.call-done = bf16[352,2048]{1,0:T(8,128)(2,1)} async-done(((bf16[1408,2048]{1,0:T(8,128)(2,1)}), bf16[352,2048]{1,0:T(8,128)(2,1)}) %reduce-scatter.26.cloned.1.call-update) | async-done | bytes 1441808 | tf_op jit(solution)/shard_map/reduce_scatter | solution.py:417
  990.3 14.2 %reduce-scatter.16.cloned.1.call-done = bf16[512,768]{1,0:T(8,128)(2,1)} async-done(((bf16[2048,768]{1,0:T(8,128)(2,1)}), bf16[512,768]{1,0:T(8,128)(2,1)}) %reduce-scatter.16.cloned.1.call-update) | async-done | bytes 786448 | tf_op jit(solution)/shard_map/reduce_scatter | solution.py:417
  1012.0 87.2 %reduce-scatter.24.cloned.1.call-done = bf16[512,2816]{1,0:T(8,128)(2,1)} async-done(((bf16[2048,2816]{1,0:T(8,128)(2,1)}), bf16[512,2816]{1,0:T(8,128)(2,1)}) %reduce-scatter.24.cloned.1.call-update) | async-done | bytes 2883600 | tf_op jit(solution)/shard_map/reduce_scatter | solution.py:417
  1116.0 74.6 %reduce-scatter.14.cloned.1.call-done = bf16[128,2048]{1,0:T(8,128)(2,1)} async-done(((bf16[1024,2048]{1,0:T(8,128)(2,1)}), bf16[128,2048]{1,0:T(8,128)(2,1)}) %reduce-scatter.14.cloned.1.call-update) | async-done | bytes 524304 | tf_op jit(solution)/shard_map/reduce_scatter | solution.py:417
  1193.0 89.3 %reduce-scatter.10.cloned.1.call-done = bf16[128,2048]{1,0:T(8,128)(2,1)} async-done(((bf16[1024,2048]{1,0:T(8,128)(2,1)}), bf16[128,2048]{1,0:T(8,128)(2,1)}) %reduce-scatter.10.cloned.1.call-update) | async-done | bytes 524304 | tf_op jit(solution)/shard_map/reduce_scatter | solution.py:417
  1285.2 123.0 %all-reduce.11.cloned.1.call-done = f32[32,896]{1,0:T(8,128)} async-done(((f32[32,896]{1,0:T(8,128)}), f32[32,896]{1,0:T(8,128)}) %all-reduce.11.cloned.1.call-update) | async-done | bytes 114704
  (372 shorter events, 288.5 us)
Async XLA Ops:
  7.2 154.5 %all-gather.31.cloned.1.call-start = ((), (), s32[]{:S(2)}) async-start(), calls=%async_computation.30 | async-start | bytes 4718592 | tf_op jit(solution)/shard_map/all_gather | solution.py:413
  7.9 157.3 %all-gather.19.cloned.1.call-start = ((), (), s32[]{:S(2)}) async-start(), calls=%async_computation.15 | async-start | bytes 3932160 | tf_op jit(solution)/shard_map/all_gather | solution.py:413
  57.2 162.8 %all-gather.21.cloned.1.call-start = ((), (), s32[]{:S(2)}) async-start(), calls=%async_computation.16 | async-start | bytes 8650752 | tf_op jit(solution)/shard_map/all_gather | solution.py:413
  195.9 22.9 %all-to-all-start.1 = ((bf16[8,128,256]{2,1,0:T(8,128)(2,1)}), bf16[8,128,256]{2,1,0:T(8,128)(2,1)S(1)}, u32[]{:S(2)}, u32[]{:S(2)}) async-start(bf16[8,128,256]{2,1,0:T(8,128)(2,1)} %copy.165), calls=%async_computation.1 | async-start | bytes 1048576 | tf_op jit(solution)/shard_map/all_to_all | solution.py:421
  199.4 120.8 %all-gather.23.cloned.1.call-start = ((), (), s32[]{:S(2)}) async-start(), calls=%async_computation.17 | async-start | bytes 4718592 | tf_op jit(solution)/shard_map/all_gather | solution.py:413
  226.7 169.9 %all-gather.33.cloned.1.call-start = ((), (), s32[]{:S(2)}) async-start(), calls=%async_computation.31 | async-start | bytes 14417920 | tf_op jit(solution)/shard_map/all_gather | solution.py:413
  227.3 244.7 %all-gather.37.cloned.1.call-start = ((), (), s32[]{:S(2)}) async-start(), calls=%async_computation.33 | async-start | bytes 4718592 | tf_op jit(solution)/shard_map/all_gather | solution.py:413
  227.9 287.4 %all-gather.35.cloned.1.call-start = ((), (), s32[]{:S(2)}) async-start(), calls=%async_computation.32 | async-start | bytes 7208960 | tf_op jit(solution)/shard_map/all_gather | solution.py:413
  228.6 331.7 %all-gather.25.cloned.1.call-start = ((), (), s32[]{:S(2)}) async-start(), calls=%async_computation.18 | async-start | bytes 7208960 | tf_op jit(solution)/shard_map/all_gather | solution.py:413
  304.8 287.0 %all-gather.27.cloned.1.call-start = ((), (), s32[]{:S(2)}) async-start(), calls=%async_computation.19 | async-start | bytes 3604480 | tf_op jit(solution)/shard_map/all_gather | solution.py:413
  305.5 395.9 %reduce-scatter.12.cloned.1.call-start = ((), (), s32[]{:S(2)}) async-start(), calls=%async_computation.21 | async-start | bytes 4718592 | tf_op jit(solution)/shard_map/reduce_scatter | solution.py:417
  637.2 140.3 %all-gather.29.cloned.1.call-start = ((), (), s32[]{:S(2)}) async-start(), calls=%async_computation.22 | async-start | bytes 4718592 | tf_op jit(solution)/shard_map/all_gather | solution.py:413
  704.2 159.6 %reduce-scatter.20.cloned.1.call-start = ((), (), s32[]{:S(2)}) async-start(), calls=%async_computation.26 | async-start | bytes 7208960 | tf_op jit(solution)/shard_map/reduce_scatter | solution.py:417
  716.6 156.1 %reduce-scatter.22.cloned.1.call-start = ((), (), s32[]{:S(2)}) async-start(), calls=%async_computation.27 | async-start | bytes 3604480 | tf_op jit(solution)/shard_map/reduce_scatter | solution.py:417
  724.4 182.3 %reduce-scatter.18.cloned.1.call-start = ((), (), s32[]{:S(2)}) async-start(), calls=%async_computation.25 | async-start | bytes 2621440 | tf_op jit(solution)/shard_map/reduce_scatter | solution.py:417
  782.6 181.3 %reduce-scatter.26.cloned.1.call-start = ((), (), s32[]{:S(2)}) async-start(), calls=%async_computation.29 | async-start | bytes 7208960 | tf_op jit(solution)/shard_map/reduce_scatter | solution.py:417
  794.4 210.1 %reduce-scatter.16.cloned.1.call-start = ((), (), s32[]{:S(2)}) async-start(), calls=%async_computation.24 | async-start | bytes 3932160 | tf_op jit(solution)/shard_map/reduce_scatter | solution.py:417
  833.8 265.4 %reduce-scatter.24.cloned.1.call-start = ((), (), s32[]{:S(2)}) async-start(), calls=%async_computation.28 | async-start | bytes 14417920 | tf_op jit(solution)/shard_map/reduce_scatter | solution.py:417
  854.2 336.4 %reduce-scatter.14.cloned.1.call-start = ((), (), s32[]{:S(2)}) async-start(), calls=%async_computation.23 | async-start | bytes 4718592 | tf_op jit(solution)/shard_map/reduce_scatter | solution.py:417
  863.0 419.3 %reduce-scatter.10.cloned.1.call-start = ((), (), s32[]{:S(2)}) async-start(), calls=%async_computation.20 | async-start | bytes 4718592 | tf_op jit(solution)/shard_map/reduce_scatter | solution.py:417
  863.8 103.5 %all-to-all-start.5 = ((bf16[8,64,1408]{2,1,0:T(8,128)(2,1)}), bf16[8,64,1408]{2,1,0:T(8,128)(2,1)}, u32[]{:S(2)}, u32[]{:S(2)}) async-start(bf16[8,64,1408]{2,1,0:T(8,128)(2,1)} %bitcast.292), calls=%async_computation.11 | async-start | bytes 2883584 | tf_op jit(solution)/shard_map/all_to_all | solution.py:421
  907.7 102.4 %collective-permute-start = (bf16[64,2048]{1,0:T(8,128)(2,1)S(1)}, bf16[64,2048]{1,0:T(8,128)(2,1)}, u32[]{:S(2)}, u32[]{:S(2)}) collective-permute-start(bf16[64,2048]{1,0:T(8,128)(2,1)S(1)} %dynamic-slice_bitcast_fusion.2), channel_id=1, source_target_pairs={{0,1},{1,0},{2,3},{3,2},{4,5},{5,4},{6,7},{7,6},{8,9},{9,8},{10,11... | collective-permute-start | bytes 786440 | tf_op jit(solution)/shard_map/ppermute | solution.py:639
  1004.5 99.4 %all-to-all-start.4 = ((bf16[8,64,768]{2,1,0:T(8,128)(2,1)}), bf16[8,64,768]{2,1,0:T(8,128)(2,1)}, u32[]{:S(2)}, u32[]{:S(2)}) async-start(bf16[8,64,768]{2,1,0:T(8,128)(2,1)} %bitcast.297), calls=%async_computation.8 | async-start | bytes 1572864 | tf_op jit(solution)/shard_map/all_to_all | solution.py:421
  1010.0 398.2 %all-reduce.11.cloned.1.call-start = ((), (), s32[]{:S(2)}) async-start(), calls=%async_computation.34 | async-start | bytes 229376
  (78 other events, 2519.7 us)
Sparse Core Ops, SparseCore 0:
  10.1 92.5 all-gather.30
  104.3 27.0 all-gather.18
  134.4 85.5 all-gather.20
  226.8 93.2 all-gather.22
  321.6 75.0 all-gather.32
  398.6 73.3 all-gather.36
  473.6 41.6 all-gather.34
  516.9 43.3 all-gather.24
  561.9 27.0 all-gather.26
  613.1 88.2 reduce-scatter.11
  704.3 73.1 all-gather.28
  780.1 53.1 reduce-scatter.19
  836.3 36.3 reduce-scatter.21
  875.2 31.4 reduce-scatter.17
  909.1 54.8 reduce-scatter.25
  966.5 37.9 reduce-scatter.15
  1007.0 92.1 reduce-scatter.23
  1102.7 87.8 reduce-scatter.13
  1194.6 87.6 reduce-scatter.9
  1287.7 120.4 all-reduce.10

commit v2 on v1

--- a/solution.py
+++ b/solution.py
@@ -1,8 +1,10 @@
-from functools import partial
+import functools
 
 import jax
 import jax.numpy as jnp
 from jax import lax
+from jax.experimental import pallas as pl
+from jax.experimental.pallas import tpu as pltpu
 from jax.sharding import PartitionSpec as P
 
 HD = 128
@@ -224,7 +226,7 @@
     grad_hidden = jnp.einsum(
         "td,fd->tf", grad_shared_out, outer_full, preferred_element_type=jnp.float32
     )
-    unused_mix, mix_pull = jax.vjp(partial(swiglu_mix, hidden_width=shared_width), shared_gu)
+    unused_mix, mix_pull = jax.vjp(functools.partial(swiglu_mix, hidden_width=shared_width), shared_gu)
     grad_shared_gu = mix_pull(grad_hidden)[0].astype(jnp.bfloat16)
     grad_inner = jnp.einsum(
         "td,tf->df", normed_ffn, grad_shared_gu, preferred_element_type=jnp.float32
@@ -272,7 +274,7 @@
     grad_expert_outer = jnp.einsum(
         "necf,necd->efd", expert_hidden, grad_incoming, preferred_element_type=jnp.float32
     )
-    unused_mix, expert_pull = jax.vjp(partial(swiglu_mix, hidden_width=expert_width), expert_gu)
+    unused_mix, expert_pull = jax.vjp(functools.partial(swiglu_mix, hidden_width=expert_width), expert_gu)
     grad_expert_gu = expert_pull(grad_expert_hidden)[0].astype(jnp.bfloat16)
     grad_expert_inner = jnp.einsum(
         "necd,necf->edf", incoming, grad_expert_gu, preferred_element_type=jnp.float32
@@ -407,6 +409,649 @@
         sum_expert_inner,
         sum_expert_outer,
     )
+
+
+MESH = pl.DeviceIdType.MESH
+ANY = pl.BlockSpec(memory_space=pl.ANY)
+VMEM = pl.BlockSpec(memory_space=pltpu.VMEM)
+
+
+def remote(source, target, send_sem, recv_sem, **place):
+    return pltpu.make_async_remote_copy(
+        src_ref=source,
+        dst_ref=target,
+        send_sem=send_sem,
+        recv_sem=recv_sem,
+        device_id=place,
+        device_id_type=MESH,
+    )
+
+
+def line_place():
+    here = lax.axis_index("ctx")
+    line = here % 2
+    return here, here // 2, line, here + 1 - 2 * line
+
+
+def greet_line(last, here, level, side):
+    barrier = pltpu.get_barrier_semaphore()
+    pl.semaphore_signal(barrier, inc=1, device_id={"ctx": side}, device_id_type=MESH)
+
+    @pl.when(level < last)
+    def up():
+        pl.semaphore_signal(barrier, inc=1, device_id={"ctx": here + 2}, device_id_type=MESH)
+
+    @pl.when(level > 0)
+    def down():
+        pl.semaphore_signal(barrier, inc=1, device_id={"ctx": here - 2}, device_id_type=MESH)
+
+    ends = jnp.where(level < last, 1, 0) + jnp.where(level > 0, 1, 0)
+    pl.semaphore_wait(barrier, 1 + ends)
+
+
+def line_copy(rows_ref, block, way, target, sems, source=None):
+    send_sem, recv_sem = sems
+    return remote(
+        rows_ref.at[block] if source is None else source,
+        rows_ref.at[block],
+        send_sem.at[block, way],
+        recv_sem.at[block],
+        ctx=target,
+    )
+
+
+def line_start(rows_ref, own_ref, sems, place, last):
+    here, level, line, side = place
+
+    @pl.when(level < last)
+    def up():
+        line_copy(rows_ref, here, 0, here + 2, sems, own_ref).start()
+
+    @pl.when(level > 0)
+    def down():
+        line_copy(rows_ref, here, 1, here - 2, sems, own_ref).start()
+
+    line_copy(rows_ref, here, 2, side, sems, own_ref).start()
+
+
+def line_step(rows_ref, sems, place, last, step):
+    here, level, line, side = place
+
+    @pl.when(level >= step)
+    def from_below():
+        block = here - 2 * step
+        line_copy(rows_ref, block, 0, side, sems).wait_recv()
+
+        @pl.when(level < last)
+        def on():
+            line_copy(rows_ref, block, 0, here + 2, sems).start()
+
+        line_copy(rows_ref, block, 2, side, sems).start()
+
+    @pl.when(level + step <= last)
+    def from_above():
+        block = here + 2 * step
+        line_copy(rows_ref, block, 1, side, sems).wait_recv()
+
+        @pl.when(level > 0)
+        def on():
+            line_copy(rows_ref, block, 1, here - 2, sems).start()
+
+        line_copy(rows_ref, block, 2, side, sems).start()
+
+
+def line_finish(rows_ref, sems, place, last):
+    here, level, line, side = place
+    for other in range(last + 1):
+        block = 2 * other + line
+        line_copy(rows_ref, 2 * other + 1 - line, 2, side, sems).wait_recv()
+        line_copy(rows_ref, block, 2, side, sems).wait_send()
+
+        @pl.when((other <= level) & (level < last))
+        def up():
+            line_copy(rows_ref, block, 0, side, sems).wait_send()
+
+        @pl.when((other >= level) & (level > 0))
+        def down():
+            line_copy(rows_ref, block, 1, side, sems).wait_send()
+
+
+def gather_kernel(last, count, *refs):
+    owns, rows = refs[:count], refs[count : 2 * count]
+    keep_sem = refs[2 * count]
+    place = line_place()
+    here, level, line, side = place
+    sems = [(refs[2 * count + 1 + 2 * i], refs[2 * count + 2 + 2 * i]) for i in range(count)]
+    greet_line(last, here, level, side)
+    keeps = [
+        pltpu.make_async_copy(owns[i], rows[i].at[here], keep_sem.at[i]) for i in range(count)
+    ]
+    for i in range(count):
+        line_start(rows[i], owns[i], sems[i], place, last)
+        keeps[i].start()
+    for i in range(count):
+        for step in range(1, last + 1):
+            line_step(rows[i], sems[i], place, last, step)
+    for i in range(count):
+        line_finish(rows[i], sems[i], place, last)
+        keeps[i].wait()
+
+
+def line_gather(ctx_count, call_id, *arrays):
+    count = len(arrays)
+    return pl.pallas_call(
+        functools.partial(gather_kernel, ctx_count // 2 - 1, count),
+        out_shape=[jax.ShapeDtypeStruct((ctx_count,) + a.shape, a.dtype) for a in arrays],
+        in_specs=[ANY] * count,
+        out_specs=[ANY] * count,
+        scratch_shapes=[pltpu.SemaphoreType.DMA((count,))]
+        + [
+            pltpu.SemaphoreType.DMA((ctx_count, 3)),
+            pltpu.SemaphoreType.DMA((ctx_count,)),
+        ]
+        * count,
+        compiler_params=pltpu.CompilerParams(collective_id=call_id, has_side_effects=True),
+        name="line_gather",
+    )(*arrays)
+
+
+ROWS_STEP = 16
+
+
+def add_rows(target, pieces, row_count):
+    def one(index, carry):
+        rows = pl.ds(pl.multiple_of(index * ROWS_STEP, ROWS_STEP), ROWS_STEP)
+        total = pieces[0][rows, :].astype(jnp.float32)
+        for piece in pieces[1:]:
+            total = total + piece[rows, :].astype(jnp.float32)
+        target[rows, :] = total.astype(target.dtype)
+        return carry
+
+    lax.fori_loop(0, row_count // ROWS_STEP, one, 0)
+
+
+def scatter_turns(last, part, total, crossed, rising, falling, sums, *sems):
+    cross_send, cross_recv, move_send, rise_recv, fall_recv = sems
+    here, level, line, side = line_place()
+    row_count = total.shape[0]
+
+    def turn(k):
+        middle = (level > 0) & (level < last)
+        swapped = k + jnp.where(middle, (0, 0, 1, -1)[k], 0)
+        return jnp.where(level * 2 < last, last - swapped, swapped)
+
+    def cross(goal):
+        return remote(
+            part.at[2 * goal + 1 - line],
+            crossed.at[goal],
+            cross_send.at[goal],
+            cross_recv.at[goal],
+            ctx=side,
+        )
+
+    def rise(goal):
+        return remote(
+            sums.at[goal], rising.at[goal], move_send.at[goal], rise_recv.at[goal], ctx=here + 2
+        )
+
+    def fall(goal):
+        return remote(
+            sums.at[goal], falling.at[goal], move_send.at[goal], fall_recv.at[goal], ctx=here - 2
+        )
+
+    for k in range(last + 1):
+        cross(turn(k)).start()
+    for k in range(last + 1):
+        yield k
+        goal = turn(k)
+        mine = part.at[2 * goal + line]
+        cross(goal).wait_recv()
+
+        @pl.when(goal > level)
+        def upward():
+            @pl.when(level > 0)
+            def joined():
+                rise(goal).wait_recv()
+                add_rows(sums.at[goal], (mine, crossed.at[goal], rising.at[goal]), row_count)
+
+            @pl.when(level == 0)
+            def first():
+                add_rows(sums.at[goal], (mine, crossed.at[goal]), row_count)
+
+            rise(goal).start()
+
+        @pl.when(goal < level)
+        def downward():
+            @pl.when(level < last)
+            def joined():
+                fall(goal).wait_recv()
+                add_rows(sums.at[goal], (mine, crossed.at[goal], falling.at[goal]), row_count)
+
+            @pl.when(level == last)
+            def first():
+                add_rows(sums.at[goal], (mine, crossed.at[goal]), row_count)
+
+            fall(goal).start()
+
+        @pl.when(goal == level)
+        def here_at_last():
+            @pl.when(level > 0)
+            def from_below():
+                rise(goal).wait_recv()
+
+            @pl.when(level < last)
+            def from_above():
+                fall(goal).wait_recv()
+
+            @pl.when(level == 0)
+            def bottom():
+                add_rows(total, (mine, crossed.at[goal], falling.at[goal]), row_count)
+
+            @pl.when(level == last)
+            def top():
+                add_rows(total, (mine, crossed.at[goal], rising.at[goal]), row_count)
+
+            @pl.when((level > 0) & (level < last))
+            def between():
+                add_rows(
+                    total,
+                    (mine, crossed.at[goal], rising.at[goal], falling.at[goal]),
+                    row_count,
+                )
+
+    for goal in range(last + 1):
+        cross(goal).wait_send()
+
+        @pl.when(goal != level)
+        def sent():
+            rise(goal).wait_send()
+
+
+def scatter_kernel(last, count, *refs):
+    parts, totals = refs[:count], refs[count : 2 * count]
+    slots, sems = refs[2 * count : 6 * count], refs[6 * count :]
+    here, level, line, side = line_place()
+    greet_line(last, here, level, side)
+    turns = [
+        scatter_turns(
+            last, parts[i], totals[i], *slots[4 * i : 4 * i + 4], *sems[5 * i : 5 * i + 5]
+        )
+        for i in range(count)
+    ]
+    for each in turns:
+        next(each)
+    for each in turns:
+        for step in each:
+            pass
+
+
+def line_scatter(ctx_count, call_id, *parts):
+    rows, width = parts[0].shape[1:]
+    count = len(parts)
+    half = ctx_count // 2
+    dma = pltpu.SemaphoreType.DMA((half,))
+    slots = pltpu.VMEM((half, rows, width), parts[0].dtype)
+    return pl.pallas_call(
+        functools.partial(scatter_kernel, half - 1, count),
+        out_shape=[jax.ShapeDtypeStruct((rows, width), jnp.float32)] * count,
+        in_specs=[VMEM] * count,
+        out_specs=[VMEM] * count,
+        scratch_shapes=[slots] * (4 * count) + [dma] * (5 * count),
+        compiler_params=pltpu.CompilerParams(
+            collective_id=call_id, has_side_effects=True, vmem_limit_bytes=48 * 2**20
+        ),
+        name="line_scatter",
+    )(*parts)
+
+
+def fsdp_place():
+    here = lax.axis_index("fsdp")
+    beside = here + 1 - 2 * (here % 2)
+    return here, beside, (here + 2) % 4, (beside + 2) % 4
+
+
+def greet_all(ctx_count):
+    barrier = pltpu.get_barrier_semaphore()
+    here = lax.axis_index("ctx")
+    group = lax.axis_index("fsdp")
+    for k in range(1, ctx_count):
+        pl.semaphore_signal(
+            barrier, inc=1, device_id={"ctx": (here + k) % ctx_count}, device_id_type=MESH
+        )
+    for k in range(1, 4):
+        pl.semaphore_signal(barrier, inc=1, device_id={"fsdp": (group + k) % 4}, device_id_type=MESH)
+    pl.semaphore_wait(barrier, ctx_count + 2)
+
+
+def share_start(blocks, sems):
+    send_sem, recv_sem = sems
+    here, beside, across, corner = fsdp_place()
+    for way, target in ((0, across), (1, beside)):
+        remote(
+            blocks.at[here], blocks.at[here], send_sem.at[way], recv_sem.at[here], fsdp=target
+        ).start()
+
+
+def share_step(blocks, sems):
+    send_sem, recv_sem = sems
+    here, beside, across, corner = fsdp_place()
+    copy = remote(
+        blocks.at[across], blocks.at[across], send_sem.at[2], recv_sem.at[across], fsdp=beside
+    )
+    copy.wait_recv()
+    copy.start()
+
+
+def share_finish(blocks, sems):
+    send_sem, recv_sem = sems
+    here, beside, across, corner = fsdp_place()
+    for way, block in ((0, beside), (1, corner)):
+        copy = remote(
+            blocks.at[block], blocks.at[block], send_sem.at[way], recv_sem.at[block], fsdp=beside
+        )
+        copy.wait_recv()
+        copy.wait_send()
+    remote(
+        blocks.at[here], blocks.at[here], send_sem.at[2], recv_sem.at[here], fsdp=beside
+    ).wait_send()
+
+
+def spread(pieces, landing, sems, ctx_count):
+    send_sem, recv_sem = sems
+    here = lax.axis_index("ctx")
+
+    def copy(k, peer, source):
+        return remote(pieces(peer), landing(source), send_sem.at[k], recv_sem.at[k], ctx=peer)
+
+    starts = [copy(k, (here + k) % ctx_count, here) for k in range(1, ctx_count)]
+    waits = [
+        copy(k, (here + k) % ctx_count, (here + ctx_count - k) % ctx_count)
+        for k in range(1, ctx_count)
+    ]
+    return starts, waits
+
+
+def opening_kernel(
+    ctx_count,
+    own,
+    qkv_own,
+    out_own,
+    small_own,
+    number_own,
+    rows,
+    qkv,
+    out_pair,
+    small,
+    numbers,
+    keep_sem,
+    pair_send,
+    pair_recv,
+    row_send,
+    row_recv,
+    *sems,
+):
+    last = ctx_count // 2 - 1
+    place = line_place()
+    here, level, line, side = place
+    group = lax.axis_index("fsdp")
+    sems = [(sems[2 * i], sems[2 * i + 1]) for i in range(6)]
+    qkv_spread, small_spread, number_spread, qkv_share, out_share, small_share = sems
+    row_sems = (row_send, row_recv)
+    greet_all(ctx_count)
+    qkv_start, qkv_wait = spread(
+        lambda peer: qkv_own.at[peer], lambda source: qkv.at[group, source], qkv_spread, ctx_count
+    )
+    small_start, small_wait = spread(
+        lambda peer: small_own, lambda source: small.at[group, source], small_spread, ctx_count
+    )
+    number_start, number_wait = spread(
+        lambda peer: number_own, lambda source: numbers.at[source], number_spread, ctx_count
+    )
+    for copy in qkv_start + small_start + number_start:
+        copy.start()
+    line_start(rows, own, row_sems, place, last)
+    pair = remote(
+        out_own, out_pair.at[group, line], pair_send.at[0], pair_recv.at[0], ctx=side
+    )
+    pair.start()
+    keeps = [
+        pltpu.make_async_copy(source, target, keep_sem.at[i])
+        for i, (source, target) in enumerate(
+            (
+                (qkv_own.at[here], qkv.at[group, here]),
+                (out_own, out_pair.at[group, line]),
+                (small_own, small.at[group, here]),
+                (number_own, numbers.at[here]),
+                (own, rows.at[here]),
+            )
+        )
+    ]
+    for copy in keeps:
+        copy.start()
+    line_step(rows, row_sems, place, last, 1)
+    for copy in small_wait + qkv_wait:
+        copy.wait_recv()
+    keeps[2].wait()
+    keeps[0].wait()
+    share_start(small, small_share)
+    share_start(qkv, qkv_share)
+    remote(
+        out_own, out_pair.at[group, 1 - line], pair_send.at[0], pair_recv.at[0], ctx=side
+    ).wait_recv()
+    keeps[1].wait()
+    share_start(out_pair, out_share)
+    line_step(rows, row_sems, place, last, 2)
+    share_step(small, small_share)
+    share_step(qkv, qkv_share)
+    for step in range(3, last + 1):
+        line_step(rows, row_sems, place, last, step)
+    share_step(out_pair, out_share)
+    line_finish(rows, row_sems, place, last)
+    for copy in number_wait:
+        copy.wait_recv()
+    for copy in qkv_start + small_start + number_start:
+        copy.wait_send()
+    pair.wait_send()
+    share_finish(small, small_share)
+    share_finish(qkv, qkv_share)
+    share_finish(out_pair, out_share)
+    keeps[3].wait()
+    keeps[4].wait()
+
+
+def opening(ctx_count, call_id, own, qkv_own, out_own, small_own, number_own):
+    def out(lead, array):
+        return jax.ShapeDtypeStruct(lead + array.shape, array.dtype)
+
+    dma = pltpu.SemaphoreType.DMA
+    return pl.pallas_call(
+        functools.partial(opening_kernel, ctx_count),
+        out_shape=[
+            out((ctx_count,), own),
+            out((4,), qkv_own),
+            out((4, 2), out_own),
+            out((4, ctx_count), small_own),
+            out((ctx_count,), number_own),
+        ],
+        in_specs=[ANY] * 5,
+        out_specs=[ANY] * 5,
+        scratch_shapes=[
+            dma((5,)),
+            dma((1,)),
+            dma((1,)),
+            dma((ctx_count, 3)),
+            dma((ctx_count,)),
+        ]
+        + [dma((ctx_count,))] * 6
+        + [dma((3,)), dma((4,))] * 3,
+        compiler_params=pltpu.CompilerParams(collective_id=call_id, has_side_effects=True),
+        name="opening",
+    )(own, qkv_own, out_own, small_own, number_own)
+
+
+def group_reduce(blocks, beside_in, pair_sums, across_in, settled, sems):
+    core_send, core_recv, far_send, far_recv = sems
+    group, beside, across, corner = fsdp_place()
+    rows = settled.shape[0]
+
+    def core_copy(slot, block):
+        return remote(
+            blocks.at[block],
+            beside_in.at[slot],
+            core_send.at[slot],
+            core_recv.at[slot],
+            fsdp=beside,
+        )
+
+    far = remote(pair_sums.at[1], across_in, far_send.at[0], far_recv.at[0], fsdp=across)
+    core_copy(1, corner).start()
+    core_copy(0, beside).start()
+    yield
+    core_copy(1, corner).wait_recv()
+    add_rows(pair_sums.at[1], (blocks.at[across], beside_in.at[1]), rows)
+    far.start()
+    core_copy(0, beside).wait_recv()
+    add_rows(pair_sums.at[0], (blocks.at[group], beside_in.at[0]), rows)
+    yield
+    far.wait_recv()
+    add_rows(settled, (pair_sums.at[0], across_in), rows)
+    yield
+    core_copy(1, corner).wait_send()
+    core_copy(0, beside).wait_send()
+    far.wait_send()
+    yield
+
+
+def closing_kernel(ctx_count, part, weight, pair, small, *refs):
+    total, landed, pair_total, small_total = refs[:4]
+    line_slots, weight_slots, pair_slots = refs[4:8], refs[8:12], refs[12:16]
+    pair_in, small_in, small_sums, small_across = refs[16:20]
+    line_sems, weight_sems, pair_sems = refs[20:25], refs[25:29], refs[29:33]
+    keep_sem, half_send, half_recv = refs[33:36]
+    weight_spread, small_spread, (group_send, group_recv) = refs[36:38], refs[38:40], refs[40:42]
+    here, level, line, side = line_place()
+    group = lax.axis_index("fsdp")
+    greet_all(ctx_count)
+    turns = scatter_turns(ctx_count // 2 - 1, part, total, *line_slots, *line_sems)
+    settled, pair_settled = weight_slots[3], pair_slots[3]
+    weight_steps = group_reduce(weight, *weight_slots, weight_sems)
+    pair_steps = group_reduce(pair, *pair_slots, pair_sems)
+    next(weight_steps)
+    next(turns)
+    small_start, small_wait = spread(
+        lambda peer: small.at[:, peer], lambda source: small_in.at[source], small_spread, ctx_count
+    )
+    for copy in small_start:
+        copy.start()
+    next(weight_steps)
+    next(pair_steps)
+    next(turns)
+    next(pair_steps)
+    for copy in small_wait:
+        copy.wait_recv()
+    small_sum = small[:, here]
+    for k in range(1, ctx_count):
+        small_sum = small_sum + small_in[(here + k) % ctx_count]
+    small_sums[...] = small_sum
+    group_copies = [
+        remote(
+            small_sums.at[(group + k) % 4],
+            small_across.at[k],
+            group_send.at[k],
+            group_recv.at[k],
+            fsdp=(group + k) % 4,
+        )
+        for k in range(1, 4)
+    ]
+    for copy in group_copies:
+        copy.start()
+    next(weight_steps)
+    piece = settled.shape[0] // ctx_count
+    weight_start, weight_wait = spread(
+        lambda peer: settled.at[pl.ds(pl.multiple_of(peer * piece, piece), piece)],
+        lambda source: landed.at[source],
+        weight_spread,
+        ctx_count,
+    )
+    for copy in weight_start:
+        copy.start()
+    keep = pltpu.make_async_copy(
+        settled.at[pl.ds(pl.multiple_of(here * piece, piece), piece)],
+        landed.at[here],
+        keep_sem.at[0],
+    )
+    keep.start()
+    next(turns)
+    next(pair_steps)
+    half = pair_total.shape[0]
+    half_copy = remote(
+        pair_settled.at[pl.ds(pl.multiple_of((1 - line) * half, half), half)],
+        pair_in,
+        half_send.at[0],
+        half_recv.at[0],
+        ctx=side,
+    )
+    half_copy.start()
+    for copy in group_copies:
+        copy.wait_recv()
+    small_total[...] = small_sums[group] + small_across[1] + small_across[2] + small_across[3]
+    for step in turns:
+        pass
+    half_copy.wait_recv()
+    kept = pair_settled.at[pl.ds(pl.multiple_of(line * half, half), half)]
+    add_rows(pair_total, (kept, pair_in), half)
+    for copy in weight_wait:
+        copy.wait_recv()
+    for copy in weight_start + small_start + group_copies:
+        copy.wait_send()
+    half_copy.wait_send()
+    next(weight_steps)
+    next(pair_steps)
+    keep.wait()
+
+
+def closing(ctx_count, call_id, part, weight, pair, small):
+    rows, width = part.shape[1:]
+    half = ctx_count // 2
+    dma = pltpu.SemaphoreType.DMA
+    slots = pltpu.VMEM((half, rows, width), part.dtype)
+
+    def group_slots(array):
+        one = pltpu.VMEM(array.shape[1:], array.dtype)
+        two = pltpu.VMEM((2,) + array.shape[1:], array.dtype)
+        return [two, two, one, one]
+
+    block, columns = weight.shape[1:]
+    pair_half = (pair.shape[1] // 2, pair.shape[2])
+    return pl.pallas_call(
+        functools.partial(closing_kernel, ctx_count),
+        out_shape=[
+            jax.ShapeDtypeStruct((rows, width), jnp.float32),
+            jax.ShapeDtypeStruct((ctx_count, block // ctx_count, columns), weight.dtype),
+            jax.ShapeDtypeStruct(pair_half, jnp.float32),
+            jax.ShapeDtypeStruct(small.shape[2:], small.dtype),
+        ],
+        in_specs=[VMEM] * 4,
+        out_specs=[VMEM] * 4,
+        scratch_shapes=[slots] * 4
+        + group_slots(weight)
+        + group_slots(pair)
+        + [
+            pltpu.VMEM(pair_half, pair.dtype),
+            pltpu.VMEM((ctx_count, 4) + small.shape[2:], small.dtype),
+            pltpu.VMEM((4,) + small.shape[2:], small.dtype),
+            pltpu.VMEM((4,) + small.shape[2:], small.dtype),
+        ]
+        + [dma((half,))] * 5
+        + [dma((2,)), dma((2,)), dma((1,)), dma((1,))] * 2
+        + [dma((1,))] * 3
+        + [dma((ctx_count,))] * 4
+        + [dma((4,))] * 2,
+        compiler_params=pltpu.CompilerParams(
+            collective_id=call_id, has_side_effects=True, vmem_limit_bytes=48 * 2**20
+        ),
+        name="closing",
+    )(part, weight, pair, small)
 
 
 def over(axis, array, dim=0):
@@ -479,8 +1124,29 @@
             router_weight.T.reshape(-1),
             qkv_bias,
         ]
-    )[None, :]
-    small_all = over(("fsdp", "ctx"), small)
+    )
+    small_count = small.shape[0]
+    small = jnp.pad(small, (0, 16 * HD - small_count)).reshape(16, HD)
+    own_numbers = jnp.concatenate(
+        [routes.reshape(tokens_dev, -1).T, segments.reshape(1, tokens_dev)], axis=0
+    )
+    number_count = own_numbers.shape[0]
+    own_numbers = jnp.pad(own_numbers, ((0, 8 - number_count), (0, 0)))
+    qkv_parts = (
+        qkv_weight.reshape(shard, 3, head_count, HD)[:, :, jnp.array(head_order)]
+        .reshape(shard, 3, ctx_count, 2 * HD)
+        .transpose(2, 0, 1, 3)
+        .reshape(ctx_count, shard, 6 * HD)
+    )
+    own_inputs = hidden_in.reshape(tokens_dev, width)
+    row_inputs, qkv_c, out_pair, small_all, numbers = opening(
+        ctx_count, 1, own_inputs, qkv_parts, out_weight, small, own_numbers
+    )
+    qkv_c = qkv_c.reshape(width, 6 * HD)
+    out_c = lax.dynamic_index_in_dim(
+        out_pair.reshape(2, 2 * HD, width), side, 0, keepdims=False
+    )
+    small_all = small_all.reshape(dev_count, 16 * HD)
     gain_attn = small_all[:, :shard].reshape(width).astype(full)
     gain_ffn = small_all[:, shard : 2 * shard].reshape(width).astype(full)
     gate_full = small_all[:, 2 * shard : 3 * shard].reshape(width)
@@ -490,46 +1156,33 @@
         .transpose(1, 0, 2)
         .reshape(expert_count, width)
     )
-    bias_full = small_all[:, (3 + expert_count) * shard :].reshape(3, head_count, HD)
+    bias_full = small_all[:, (3 + expert_count) * shard : small_count].reshape(3, head_count, HD)
     router_gate = jnp.concatenate([router_t, gate_full[None, :]], axis=0)
-    own_routes = routes.reshape(tokens_dev, -1)
-    own_seg = segments.reshape(1, tokens_dev)
-    numbers = over("ctx", jnp.concatenate([own_routes.T, own_seg], axis=0)[None])
-    row_seg = numbers[:, -1].reshape(row_len)
-    routed_here = jnp.any(numbers[:, :-1] == ctx_rank, axis=1).reshape(row_len)
-
-    qkv_parts = (
-        qkv_weight.reshape(shard, 3, head_count, HD)[:, :, jnp.array(head_order)]
-        .reshape(shard, 3, ctx_count, 2 * HD)
-        .transpose(2, 0, 1, 3)
-        .reshape(ctx_count, shard, 6 * HD)
-    )
-    qkv_c = over("fsdp", exchange(qkv_parts).reshape(ctx_count * shard, 6 * HD))
+    row_seg = numbers[:, number_count - 1].reshape(row_len)
+    routed_here = jnp.any(numbers[:, : number_count - 1] == ctx_rank, axis=1).reshape(row_len)
+
+    shared_in_weight, numbers = lax.optimization_barrier((shared_in_weight, numbers))
     inner_parts = (
         shared_in_weight.reshape(shard, 2, fsdp_count, ctx_count, shared_shard)
         .transpose(3, 0, 1, 2, 4)
         .reshape(ctx_count, shard, 2 * shared_width)
     )
-    inner_c = over("fsdp", exchange(inner_parts).reshape(ctx_count * shard, 2 * shared_width))
-    outer_c = over("fsdp", shared_out_weight)
-    out_full = over(("fsdp", "ctx"), out_weight)
     expert_inner = over("fsdp", expert_in_weight[0])
     expert_outer = over("fsdp", expert_out_weight[0])
-    out_heads = out_full.reshape(head_count, HD, width)
+    outer_c = over("fsdp", shared_out_weight)
+    inner_parts = exchange(inner_parts).reshape(ctx_count * shard, 2 * shared_width)
+    inner_parts, late_grad = lax.optimization_barrier((inner_parts, out_grad))
+    inner_c = over("fsdp", inner_parts)
     my_heads = [pair_rank + (side * 2 + t) * pairs for t in range(2)]
-    out_c = jnp.concatenate(
-        [lax.dynamic_index_in_dim(out_heads, h, 0, keepdims=False) for h in my_heads], axis=0
-    )
     bias_c = jnp.concatenate(
         [lax.dynamic_index_in_dim(bias_full, h, 1, keepdims=False) for h in my_heads], axis=1
     ).reshape(6 * HD)
 
     offsets = jnp.arange(block_len, dtype=jnp.int32)
     positions = (block_pairs[:, None] * block_len + offsets[None, :]).reshape(row_len)
-    own_inputs = hidden_in.reshape(tokens_dev, width)
     inputs = own_inputs.astype(full)
-    row_inputs = over("ctx", own_inputs).astype(full)
-    row_upstream = over("ctx", out_grad.reshape(tokens_dev, width))
+    row_inputs = row_inputs.reshape(row_len, width).astype(full)
+    row_upstream = over("ctx", late_grad.reshape(tokens_dev, width))
     row_normed = rms_scale(row_inputs, gain_attn).astype(low)
     projected = matmul_low(row_normed, qkv_c) + bias_c.astype(full)
     query_pre = projected[:, : 2 * HD].reshape(row_len, 2, HD)
@@ -558,15 +1211,13 @@
         .astype(low)
         .reshape(row_len, 2 * HD)
     )
-    landed = exchange(attended_row.reshape(ctx_count, tokens_dev, 2 * HD))
-    places_of = [head_order.index(h) for h in range(head_count)]
-    attended = jnp.concatenate(
-        [landed[p // 2, :, (p % 2) * HD : (p % 2 + 1) * HD] for p in places_of], axis=1
-    )
-    middle = inputs + matmul_low(attended, out_full)
+    branch_part = matmul_low(attended_row, out_c).astype(low)
+    (branch,) = line_scatter(ctx_count, 2, branch_part.reshape(ctx_count, tokens_dev, width))
+    middle = inputs + branch
     normed_ffn = rms_scale(middle, gain_ffn).astype(low)
 
-    row_ffn = over("ctx", normed_ffn)
+    (row_ffn,) = line_gather(ctx_count, 3, normed_ffn)
+    row_ffn = row_ffn.reshape(row_len, width)
     row_logits = dot_transposed(row_ffn, router_gate)
     row_probs = jax.nn.softmax(row_logits[:, :expert_count], axis=-1)
     expert_ids = jnp.arange(expert_count, dtype=jnp.int32)
@@ -577,9 +1228,11 @@
     expert_gu = matmul_low(row_ffn, expert_inner)
     expert_hidden = swiglu_mix(expert_gu, expert_width).astype(low)
     expert_result = matmul_low(expert_hidden, expert_outer).astype(low).astype(full)
-    shared_gu = matmul_low(row_ffn, inner_c)
+    row_shared, expert_result = lax.optimization_barrier((row_ffn, expert_result))
+    shared_gu = matmul_low(row_shared, inner_c)
     shared_hidden = swiglu_mix(shared_gu, shared_width).astype(low)
     shared_out = matmul_low(shared_hidden, outer_c)
+    row_upstream, shared_out = lax.optimization_barrier((row_upstream, shared_out))
     upstream_row = row_upstream.astype(full)
     out_part = (row_gate[:, None] * shared_out + here[:, None] * expert_result).astype(low)
     gate_dot = jnp.sum(upstream_row * shared_out, axis=1)
@@ -587,24 +1240,42 @@
     own_dots = exchange(
         jnp.stack([gate_dot, expert_dot]).reshape(2, ctx_count, tokens_dev).transpose(1, 0, 2)
     )
-    output = middle + reduce_over("ctx", out_part).astype(full)
-    hidden_out = output.astype(low).reshape(1, tokens_dev, width)
 
     grad_shared_out = (row_gate[:, None] * upstream_row).astype(low)
     grad_buffers = (here[:, None] * upstream_row).astype(low)
     grad_hidden = dot_transposed(grad_shared_out, outer_c)
-    unused_mix, mix_pull = jax.vjp(partial(swiglu_mix, hidden_width=shared_width), shared_gu)
+    unused_mix, mix_pull = jax.vjp(functools.partial(swiglu_mix, hidden_width=shared_width), shared_gu)
     grad_shared_gu = mix_pull(grad_hidden)[0].astype(low)
     grad_expert_hidden = dot_transposed(grad_buffers, expert_outer)
-    unused_mix, expert_pull = jax.vjp(partial(swiglu_mix, hidden_width=expert_width), expert_gu)
+    unused_mix, expert_pull = jax.vjp(functools.partial(swiglu_mix, hidden_width=expert_width), expert_gu)
     grad_expert_gu = expert_pull(grad_expert_hidden)[0].astype(low)
     grad_rows = dot_transposed(grad_expert_gu, expert_inner).astype(low).astype(full)
     grad_ffn_part = (dot_transposed(grad_shared_gu, inner_c) + grad_rows).astype(low)
-    grad_normed = reduce_over("ctx", grad_ffn_part).astype(full)
-    sum_expert_inner = reduce_over("fsdp", transposed_dot(row_ffn, grad_expert_gu).astype(low))
-    sum_expert_outer = reduce_over("fsdp", transposed_dot(expert_hidden, grad_buffers).astype(low))
-    sum_outer = reduce_over("fsdp", transposed_dot(shared_hidden, grad_shared_out).astype(low))
-    sum_inner_c = reduce_over("fsdp", transposed_dot(row_ffn, grad_shared_gu).astype(low))
+    grad_expert_outer = transposed_dot(expert_hidden, grad_buffers).astype(low)
+    grad_expert_inner = transposed_dot(row_ffn, grad_expert_gu).astype(low)
+    grad_outer = transposed_dot(shared_hidden, grad_shared_out).astype(low)
+    grad_inner = transposed_dot(row_ffn, grad_shared_gu).astype(low)
+    (
+        grad_ffn_part,
+        out_part,
+        grad_expert_outer,
+        grad_expert_inner,
+        grad_outer,
+        grad_inner,
+    ) = lax.optimization_barrier(
+        (grad_ffn_part, out_part, grad_expert_outer, grad_expert_inner, grad_outer, grad_inner)
+    )
+    sum_expert_outer = reduce_over("fsdp", grad_expert_outer)
+    sum_expert_inner = reduce_over("fsdp", grad_expert_inner)
+    sum_outer = reduce_over("fsdp", grad_outer)
+    sum_inner_c = reduce_over("fsdp", grad_inner)
+    grad_normed, out_sum = line_scatter(
+        ctx_count,
+        4,
+        grad_ffn_part.reshape(ctx_count, tokens_dev, width),
+        out_part.reshape(ctx_count, tokens_dev, width),
+    )
+    hidden_out = (middle + out_sum).astype(low).reshape(1, tokens_dev, width)
     sum_inner = (
         exchange(sum_inner_c.reshape(ctx_count, shard, 2 * shared_width))
         .reshape(ctx_count, shard, 2, fsdp_count, shared_shard)
@@ -627,17 +1298,13 @@
     grad_middle_norm, grad_gain_ffn = norm_pull(grad_normed)
     grad_middle = out_grad.reshape(tokens_dev, width).astype(full) + grad_middle_norm
 
-    row_branch = over("ctx", grad_middle.astype(low))
+    (row_branch,) = line_gather(ctx_count, 3, grad_middle.astype(low))
+    row_branch = row_branch.reshape(row_len, width)
     grad_attended = dot_transposed(row_branch, out_c).astype(low).reshape(row_len, 2, HD)
     grad_out_c = transposed_dot(attended_row, row_branch).astype(low).reshape(2, HD, width)
     padded_out = jnp.concatenate(
         [jnp.where(side == p, grad_out_c, jnp.zeros_like(grad_out_c)) for p in range(2)], axis=0
     )
-    pair_out = reduce_over("fsdp", padded_out).reshape(2, shard, width)
-    kept = lax.dynamic_index_in_dim(pair_out, side, 0, keepdims=False)
-    given = lax.dynamic_index_in_dim(pair_out, 1 - side, 0, keepdims=False)
-    taken = lax.ppermute(given, "ctx", [(i, i ^ 1) for i in range(ctx_count)])
-    sum_out = kept.astype(full) + taken.astype(full)
 
     grad_probs = jnp.einsum("qhd,khd->hqk", grad_attended, values, preferred_element_type=full)
     weights = jnp.exp(score_part() - log_total)
@@ -658,26 +1325,19 @@
         ],
         axis=1,
     ).astype(low)
-    grad_attn_part = dot_transposed(grad_projected, qkv_c).astype(low)
-    grad_normed_attn = reduce_over("ctx", grad_attn_part).astype(full)
-    sum_qkv_c = reduce_over("fsdp", transposed_dot(row_normed, grad_projected).astype(low))
-    sum_qkv = (
-        exchange(sum_qkv_c.reshape(ctx_count, shard, 6 * HD))
-        .reshape(ctx_count, shard, 3, 2, HD)
-        .transpose(1, 2, 0, 3, 4)
-        .reshape(shard, 3, head_count, HD)[:, :, jnp.array(places_of)]
-        .reshape(shard, 3 * width)
-    )
+    grad_attn_part = dot_transposed(grad_projected, qkv_c)
+    row_scaled = row_inputs * lax.rsqrt(
+        jnp.mean(row_inputs * row_inputs, axis=-1, keepdims=True) + EPSILON
+    )
+    grad_gain_attn = jnp.sum(grad_attn_part * row_scaled, axis=0)
     grad_bias_c = jnp.sum(grad_projected.astype(full), axis=0).reshape(3, 1, 2, HD)
     mine = (jnp.arange(ctx_count) == ctx_rank)[None, :, None, None]
+    places_of = [head_order.index(h) for h in range(head_count)]
     grad_bias = (
         jnp.where(mine, grad_bias_c, 0.0)
         .reshape(3, head_count, HD)[:, jnp.array(places_of)]
         .reshape(dev_count, -1)
     )
-    unused_norm, first_pull = jax.vjp(rms_scale, inputs, gain_attn)
-    grad_inputs_norm, grad_gain_attn = first_pull(grad_normed_attn)
-    input_grad = grad_middle + grad_inputs_norm
     small_grads = jnp.concatenate(
         [
             grad_gain_attn.reshape(dev_count, shard),
@@ -689,7 +1349,25 @@
         ],
         axis=1,
     )
-    sums = reduce_over(("fsdp", "ctx"), small_grads)[0]
+    small_grads = jnp.pad(small_grads, ((0, 0), (0, 8 * HD - small_count)))
+    grad_qkv_c = transposed_dot(row_normed, grad_projected).astype(low)
+    grad_normed_attn, sum_qkv_c, sum_out, sums = closing(
+        ctx_count,
+        5,
+        grad_attn_part.astype(low).reshape(ctx_count, tokens_dev, width),
+        grad_qkv_c.reshape(fsdp_count, ctx_count * shard, 6 * HD),
+        padded_out,
+        small_grads.reshape(fsdp_count, ctx_count, 8, HD),
+    )
+    sums = sums.reshape(8 * HD)[:small_count]
+    sum_qkv = (
+        sum_qkv_c.reshape(ctx_count, shard, 3, 2, HD)
+        .transpose(1, 2, 0, 3, 4)
+        .reshape(shard, 3, head_count, HD)[:, :, jnp.array(places_of)]
+        .reshape(shard, 3 * width)
+    )
+    unused_norm, first_pull = jax.vjp(lambda v: rms_scale(v, gain_attn), inputs)
+    input_grad = grad_middle + first_pull(grad_normed_attn)[0]
     sum_router = sums[2 * shard : (2 + expert_count) * shard].reshape(expert_count, shard).T
     return (
         hidden_out,

time: 1430 us -> 880 us (0.62)
  waiting for transfers between devices: 834 us -> 17.7 us
  Pallas kernels: 0 us -> 434 us
  blocking collectives: 208 us -> 42.9 us
    pallas_call x0 -> x6, Pallas kernels: none -> 434 us  [the longest x2 147 us: line_scatter(): pl.pallas_call(functools.partial(scatter_kernel, half - 1, count), out_sh...]
    reduce_scatter x9 -> x4, waiting for transfers between devices: 412 us -> 0.01 us  [reduce_over(): return lax.psum_scatter(array, axis, scatter_dimension=dim, tiled=True)]
    all_gather x10 -> x5, waiting for transfers between devices: 268 us -> 13.7 us  [over(): return lax.all_gather(array, axis, axis=dim, tiled=True)]
    unnamed x21 -> x9, waiting for transfers between devices: 128 us -> 4.02 us
    all_gather x2 -> x0, blocking collectives: 97.3 us -> none  [over(): return lax.all_gather(array, axis, axis=dim, tiled=True)]
    all_to_all x2 -> x1, blocking collectives: 110 us -> 42.9 us  [exchange(): return lax.all_to_all(array, 'ctx', split_axis=0, concat_axis=0, tiled=True)]
    all_to_all x4 -> x2, waiting for transfers between devices: 25.7 us -> 0.01 us  [exchange(): return lax.all_to_all(array, 'ctx', split_axis=0, concat_axis=0, tiled=True)]
  transfers between devices with their start and end apart: 25 -> 11, of which waited for: 18 -> 1; matrix products, arithmetic and copies ran while one was open for 21% -> 25% of each run, Pallas kernels for 0% -> 50%
where the time goes in v2:
time: 880 us; the launch traced here: 870 us
  Pallas kernels  434 us (49%)
  matrix products  212 us (24%)
  local copies, waits for them, and re-layouts  80.6 us (9%)
  other arithmetic  59.6 us (7%)
  blocking collectives  42.9 us (5%)
  waiting for transfers between devices  17.7 us (2%)
  between operations  15.5 us (2%)
    pallas_call x2, Pallas kernels, line_scatter(): pl.pallas_call(functools.partial(scatter_kernel, half - 1, count), out_sh...  147 us
    pallas_call x1, Pallas kernels, closing(): pl.pallas_call(functools.partial(closing_kernel, ctx_count), out_shape=[j...  99.1 us
    pallas_call x1, Pallas kernels, opening(): pl.pallas_call(functools.partial(opening_kernel, ctx_count), out_shape=[o...  95.8 us
    pallas_call x2, Pallas kernels, line_gather(): pl.pallas_call(functools.partial(gather_kernel, ctx_count // 2 - 1, count...  91.7 us
    dot_general x8, matrix products, dot_transposed(): lax.dot_general(left, right, (((1,), (1,)), ((), ())), preferred_element_...  76.2 us
    dot_general x7, matrix products, transposed_dot(): lax.dot_general(left, right, (((0,), (0,)), ((), ())), preferred_element_...  57.7 us
    dot_general x7, matrix products, matmul_low(): return jnp.dot(left, right, preferred_element_type=jnp.float32)  53.5 us
    all_to_all x1, blocking collectives, exchange(): return lax.all_to_all(array, 'ctx', split_axis=0, concat_axis=0, tiled=True)  42.9 us
  transfers between devices with their start and end apart: 11, of which 1 were waited for; matrix products, arithmetic and copies ran while one was open for 25% of the time, Pallas kernels for 50%

profile of v2, /device:TPU:0, one launch (start us, length us, event | category | flops | bytes accessed | tf_op | source)
XLA Modules:
  0.0 869.7 jit_solution(5566638667515670981)
XLA Ops:
  14.2 95.8 %opening.1 = (bf16[8,128,2048]{2,1,0:T(8,128)(2,1)}, bf16[4,8,64,768]{3,2,1,0:T(8,128)(2,1)}, bf16[4,2,64,2048]{3,2,1,0:T(8,128)(2,1)}, bf16[4,8,16,128]{3,2,1,0:T(8,128)(2,1)}, s32[8,8,128]{2,1,0:T(8,128)}) custom-call(bf16[128,2048]{1,0:T(8,128)(2,1)} %bitcast.202, bf16[8,64,768]{2,1,0:T(8,128)(2,1)} %reshape.541.qkv_own, bf16[64,2048]{1,0:T(8,128)(2,1)} %out_own.1, ...), custom_call_target="tpu_custom_call" | custom-call | tf_op jit(solution)/shard_map/opening/pallas_call | solution.py:867
  119.8 42.9 %all_to_all.15 = bf16[8,64,1408]{2,1,0:T(8,128)(2,1)} all-to-all(bf16[8,64,1408]{2,1,0:T(8,128)(2,1)S(1)} %reshape.555), channel_id=1, replica_groups=mesh['fsdp'=4,'ctx'=8] {'ctx'}, dimensions={0} | all-to-all | bytes 2883584 | tf_op jit(solution)/shard_map/all_to_all | solution.py:1066
  205.2 47.9 %line_scatter.2 = f32[128,2048]{1,0:T(8,128)S(1)} custom-call(bf16[8,128,2048]{2,1,0:T(8,128)(2,1)S(1)} %bitcast.191), custom_call_target="tpu_custom_call" | custom-call | tf_op jit(solution)/shard_map/line_scatter/pallas_call | solution.py:694
  255.6 45.7 %line_gather.2 = bf16[8,128,2048]{2,1,0:T(8,128)(2,1)} custom-call(bf16[128,2048]{1,0:T(8,128)(2,1)} %multiply_convert_fusion.5.refs_0_), custom_call_target="tpu_custom_call" | custom-call | tf_op jit(solution)/shard_map/line_gather/pallas_call | solution.py:542
  306.1 17.2 %fusion.2 = f32[1024,2816]{1,0:T(8,128)S(1)} fusion(bf16[1024,2048]{1,0:T(8,128)(2,1)} %bitcast.195, bf16[1,2048,2816]{2,1,0:T(8,128)(2,1)} %all-gather.13.cloned.1.call-done), kind=kOutput, calls=%fused_computation.9 | convolution fusion | flops 11811160064 | bytes 27262976 | tf_op jit(solution)/shard_map/dot_general | solution.py:49
  329.4 10.6 %convert_convert_fusion = f32[1024,2048]{1,0:T(8,128)} fusion(bf16[1024,1408]{1,0:T(8,128)(2,1)S(1)} %multiply_convert_fusion.3, bf16[1,1408,2048]{2,1,0:T(8,128)(2,1)} %all-gather.15.cloned.1.call-done), kind=kOutput, calls=%fused_computation.45 | convolution fusion | flops 5909774336 | bytes 17039360 | tf_op jit(solution)/shard_map/dot_general | solution.py:49
  340.0 10.6 %fusion.80 = f32[1024,1408]{1,0:T(8,128)S(1)} fusion(bf16[1024,2048]{1,0:T(8,128)(2,1)} %bitcast.196, bf16[2048,1408]{1,0:T(8,128)(2,1)} %all-gather.9.cloned.1.call-done), kind=kOutput, calls=%fused_computation.201 | convolution fusion | flops 5905580032 | bytes 15728640 | tf_op jit(solution)/shard_map/dot_general | solution.py:49
  355.4 9.0 %fusion.82 = f32[1024,2048]{1,0:T(8,128)} fusion(bf16[1024,704]{1,0:T(8,128)(2,1)} %multiply_convert_fusion.4, bf16[704,2048]{1,0:T(8,128)(2,1)} %all-gather.11.cloned.1.call-done), kind=kOutput, calls=%fused_computation.203 | convolution fusion | flops 2952790016 | bytes 12713984 | tf_op jit(solution)/shard_map/dot_general | solution.py:49
  364.4 13.6 %all-gather.17.cloned.1.call-done = bf16[1,1024,2048]{2,1,0:T(8,128)(2,1)} async-done(((bf16[1,128,2048]{2,1,0:T(8,128)(2,1)}), bf16[1,1024,2048]{2,1,0:T(8,128)(2,1)}) %all-gather.17.cloned.1.call-update) | async-done | bytes 4194320 | tf_op jit(solution)/shard_map/all_gather | solution.py:1058
  378.0 7.7 convolution_convert_fusion.5
  385.7 11.1 %convolution_convert_fusion.2 = bf16[1408,2048]{1,0:T(8,128)(2,1)} fusion(bf16[1024,1408]{1,0:T(8,128)(2,1)S(1)} %multiply_convert_fusion.3, bf16[1024,2048]{1,0:T(8,128)(2,1)} %bitcast.213, f32[1024]{0:T(1024)S(1)} %bitcast_select_fusion.2), kind=kOutput, calls=%fused_computation.30 | convolution fusion | flops 5914755072 | bytes 12849152 | tf_op jit(solution)/shard_map/dot_general | solution.py:1070
  396.8 10.8 %fusion.6 = (f32[1024]{0:T(1024)S(1)}, f32[1024]{0:T(1024)S(1)}, bf16[1024,2048]{1,0:T(8,128)(2,1)}) fusion(f32[1024,2048]{1,0:T(8,128)} %fusion.82, bf16[1024,2048]{1,0:T(8,128)(2,1)} %bitcast.214, f32[1024,2048]{1,0:T(8,128)} %convert_convert_fusion, f32[1024]{0:T(1024)S(1)} %bitcast_select_fusion.2, f32[1024]{0:T(1024)S(1)} %bitcast.255), kind=kLoop, calls=%fused_computation.16 | loop fusion | flops 18872320 | bytes 25182208 | tf_op jit(solution)/shard_map/reduce_sum | solution.py:1238
  407.6 7.1 fusion.39
  417.4 8.8 %convolution_convert_fusion.1 = bf16[2048,1408]{1,0:T(8,128)(2,1)} fusion(bf16[1024,2048]{1,0:T(8,128)(2,1)S(1)} %bitcast.197, f32[1024,704]{1,0:T(8,128)S(1)} %get-tuple-element.73, f32[1024,704]{1,0:T(8,128)S(1)} %get-tuple-element.72), kind=kOutput, calls=%fused_computation.29 | convolution fusion | flops 5911347200 | bytes 15728640 | tf_op jit(solution)/shard_map/dot_general | solution.py:1070
  426.2 17.0 %fusion.37 = (f32[1024,1408]{1,0:T(8,128)}, f32[1024,1408]{1,0:T(8,128)}) fusion(f32[1024,2816]{1,0:T(8,128)} %copy-done.8, bf16[1,1408,2048]{2,1,0:T(8,128)(2,1)} %all-gather.15.cloned.1.call-done, bf16[1024,2048]{1,0:T(8,128)(2,1)} %bitcast.215, f32[1024]{0:T(1024)S(1)} %bitcast_select_fusion.2), kind=kOutput, calls=%fused_computation.110 | convolution fusion | flops 5929172992 | bytes 33034240 | tf_op jit(solution)/shard_map/dot_general | solution.py:1076
  443.2 19.3 %convolution_convert_fusion = bf16[2048,2816]{1,0:T(8,128)(2,1)} fusion(bf16[1024,2048]{1,0:T(8,128)(2,1)S(1)} %bitcast.198, f32[1024,1408]{1,0:T(8,128)} %get-tuple-element.70, f32[1024,1408]{1,0:T(8,128)} %get-tuple-element.69), kind=kOutput, calls=%fused_computation.12 | convolution fusion | flops 11822694400 | bytes 27262976 | tf_op jit(solution)/shard_map/dot_general | solution.py:1070
  462.5 19.4 %fusion = bf16[1024,2048]{1,0:T(8,128)(2,1)} fusion(bf16[1,2048,2816]{2,1,0:T(8,128)(2,1)} %all-gather.13.cloned.1.call-done, f32[1024,1408]{1,0:T(8,128)} %get-tuple-element.70, f32[1024,1408]{1,0:T(8,128)} %get-tuple-element.69), kind=kOutput, calls=%fused_computation.7 | convolution fusion | flops 11816927232 | bytes 27262976 | tf_op jit(solution)/shard_map/dot_general | solution.py:1076
  481.9 11.7 %add_convert_fusion.2 = bf16[1024,2048]{1,0:T(8,128)(2,1)} fusion(bf16[1024,2048]{1,0:T(8,128)(2,1)} %fusion, bf16[2048,1408]{1,0:T(8,128)(2,1)} %all-gather.9.cloned.1.call-done, f32[1024,704]{1,0:T(8,128)} %copy-done.75, f32[1024,704]{1,0:T(8,128)S(1)} %copy-done.74), kind=kOutput, calls=%fused_computation.24 | convolution fusion | flops 5914755072 | bytes 19922944 | tf_op jit(solution)/shard_map/dot_general | solution.py:1076
  501.1 99.4 %line_scatter.3 = (f32[128,2048]{1,0:T(8,128)S(1)}, f32[128,2048]{1,0:T(8,128)S(1)}) custom-call(bf16[8,128,2048]{2,1,0:T(8,128)(2,1)} %bitcast.208, bf16[8,128,2048]{2,1,0:T(8,128)(2,1)} %bitcast.200), custom_call_target="tpu_custom_call" | custom-call | tf_op jit(solution)/shard_map/line_scatter/pallas_call | solution.py:694
  608.2 46.0 %line_gather.3 = bf16[8,128,2048]{2,1,0:T(8,128)(2,1)} custom-call(bf16[128,2048]{1,0:T(8,128)(2,1)} %fusion.73.refs_0_), custom_call_target="tpu_custom_call" | custom-call | tf_op jit(solution)/shard_map/line_gather/pallas_call | solution.py:542
  659.7 6.9 multiply_reduce_fusion.1
  691.1 12.0 %multiply_reduce_fusion = (f32[2048]{0:T(1024)S(1)}, bf16[1024,2048]{1,0:T(8,128)(2,1)}, bf16[1024,2048]{1,0:T(8,128)(2,1)}) fusion(bf16[8,128,2048]{2,1,0:T(8,128)(2,1)} %get-tuple-element.37, f32[1024]{0:T(1024)S(1)} %copy-done.53, f32[2048]{0:T(1024)S(1)} %copy-done.41, bf16[2048,768]{1,0:T(8,128)(2,1)} %bitcast.261, bf16[1024,256]{0,1:T(8,128)(2,1)} %bitcast.239, ...), kind=kOutput, calls=%fused_computation.19 | convolution fusion | flops 3240622080 | bytes 17321984 | tf_op jit(solution)/shard_map/dot_general | solution.py:1076
  718.7 99.1 %closing.1 = (f32[128,2048]{1,0:T(8,128)S(1)}, bf16[8,64,768]{2,1,0:T(8,128)(2,1)S(1)}, f32[64,2048]{1,0:T(8,128)S(1)}, f32[8,128]{1,0:T(8,128)S(1)}) custom-call(bf16[8,128,2048]{2,1,0:T(8,128)(2,1)} %bitcast.205, bf16[4,512,768]{2,1,0:T(8,128)(2,1)} %bitcast.221, bf16[4,128,2048]{2,1,0:T(8,128)(2,1)S(1)} %pad_maximum_fusion.pair, f32[4,8,8,128]{3,2,1,0:T(8,128)S(1)} %copy.198), custom_call_target="tpu_custom_call" | custom-call | tf_op jit(solution)/shard_map/closing/pallas_call | solution.py:1026
  837.0 8.4 reshape.591
  (324 shorter events, 176.4 us)
Async XLA Ops:
  7.2 298.6 %all-gather.13.cloned.1.call-start = ((), (), s32[]{:S(2)}) async-start(), calls=%async_computation.13 | async-start | bytes 14417920 | tf_op jit(solution)/shard_map/all_gather | solution.py:1058
  7.9 321.4 %all-gather.15.cloned.1.call-start = ((), (), s32[]{:S(2)}) async-start(), calls=%async_computation.14 | async-start | bytes 7208960 | tf_op jit(solution)/shard_map/all_gather | solution.py:1058
  8.7 331.3 %all-gather.9.cloned.1.call-start = ((), (), s32[]{:S(2)}) async-start(), calls=%async_computation.7 | async-start | bytes 7208960 | tf_op jit(solution)/shard_map/all_gather | solution.py:1058
  9.9 100.1 %copy-start.29 = (bf16[64,11264]{1,0:T(8,128)(2,1)S(1)}, bf16[64,11264]{1,0:T(8,128)(2,1)}, u32[]{:S(2)}) copy-start(bf16[64,11264]{1,0:T(8,128)(2,1)} %param.31) | copy-start | bytes 4325380
  119.8 43.7 %copy-start.43 = (bf16[4,8,16,128]{3,2,1,0:T(8,128)(2,1)S(1)}, bf16[4,8,16,128]{3,2,1,0:T(8,128)(2,1)}, u32[]{:S(2)}) copy-start(bf16[4,8,16,128]{3,2,1,0:T(8,128)(2,1)} %get-tuple-element.38) | copy-start | bytes 393220
  162.7 192.7 %all-gather.11.cloned.1.call-start = ((), (), s32[]{:S(2)}) async-start(), calls=%async_computation.8 | async-start | bytes 3604480 | tf_op jit(solution)/shard_map/all_gather | solution.py:1058
  163.3 214.8 %all-gather.17.cloned.1.call-start = ((), (), s32[]{:S(2)}) async-start(), calls=%async_computation.15 | async-start | bytes 4718592 | tf_op jit(solution)/shard_map/all_gather | solution.py:1058
  186.5 11.4 %copy-start.1 = (pred[1024,1024]{0,1:T(8,128)(4,1)}, pred[1024,1024]{0,1:T(8,128)(4,1)S(1)}, u32[]{:S(2)}) copy-start(pred[1024,1024]{0,1:T(8,128)(4,1)S(1)} %compare_or_fusion) | copy-start | bytes 3145732
  203.9 49.2 %copy-start.30 = (bf16[2,128,1024]{2,1,0:T(8,128)(2,1)}, bf16[2,128,1024]{2,1,0:T(8,128)(2,1)S(1)}, u32[]{:S(2)}) copy-start(bf16[2,128,1024]{2,1,0:T(8,128)(2,1)S(1)} %convolution_convert_fusion.8) | copy-start | bytes 1572868
  205.2 48.3 %copy-start.11 = (bf16[1,128,2048]{2,1,0:T(8,128)(2,1)S(1)}, bf16[1,128,2048]{2,1,0:T(8,128)(2,1)}, u32[]{:S(2)}) copy-start(bf16[1,128,2048]{2,1,0:T(8,128)(2,1)} %param.19) | copy-start | bytes 1572868
  253.1 48.3 %copy-start.38 = (f32[2048]{0:T(1024)}, f32[2048]{0:T(1024)S(1)}, u32[]{:S(2)}) copy-start(f32[2048]{0:T(1024)S(1)} %reshape.584) | copy-start | bytes 24580
  255.6 49.8 %copy-start.47 = (s32[8,8,128]{2,1,0:T(8,128)S(1)}, s32[8,8,128]{2,1,0:T(8,128)}, u32[]{:S(2)}) copy-start(s32[8,8,128]{2,1,0:T(8,128)} %get-tuple-element.40) | copy-start | bytes 98308
  305.7 407.3 %reduce-scatter.5.cloned.1.call-start = ((), (), s32[]{:S(2)}) async-start(), calls=%async_computation.9 | async-start | bytes 7208960 | tf_op jit(solution)/shard_map/reduce_scatter | solution.py:1062
  396.8 10.8 %copy-start.24 = (bf16[1,1024,2048]{2,1,0:T(8,128)(2,1)S(1)}, bf16[1,1024,2048]{2,1,0:T(8,128)(2,1)}, u32[]{:S(2)}) copy-start(bf16[1,1024,2048]{2,1,0:T(8,128)(2,1)} %all-gather.17.cloned.1.call-done) | copy-start | bytes 12582916
  396.8 10.8 %copy-start.70 = (bf16[704,2048]{1,0:T(8,128)(2,1)S(1)}, bf16[704,2048]{1,0:T(8,128)(2,1)}, u32[]{:S(2)}) copy-start(bf16[704,2048]{1,0:T(8,128)(2,1)} %all-gather.11.cloned.1.call-done) | copy-start | bytes 8650756
  426.2 17.0 %copy-start.6 = (bf16[8,128,2048]{2,1,0:T(8,128)(2,1)S(1)}, bf16[8,128,2048]{2,1,0:T(8,128)(2,1)}, u32[]{:S(2)}) copy-start(bf16[8,128,2048]{2,1,0:T(8,128)(2,1)} %line_gather.2) | copy-start | bytes 12582916
  462.5 19.4 %copy-start.74 = (f32[1024,704]{1,0:T(8,128)S(1)}, f32[1024,704]{1,0:T(8,128)}, u32[]{:S(2)}) copy-start(f32[1024,704]{1,0:T(8,128)} %copy-done.73) | copy-start | bytes 8650756
  493.6 337.8 %reduce-scatter.7.cloned.1.call-start = ((), (), s32[]{:S(2)}) async-start(), calls=%async_computation.10 | async-start | bytes 3604480 | tf_op jit(solution)/shard_map/reduce_scatter | solution.py:1062
  494.3 339.4 %reduce-scatter.11.cloned.1.call-start = ((), (), s32[]{:S(2)}) async-start(), calls=%async_computation.12 | async-start | bytes 7208960 | tf_op jit(solution)/shard_map/reduce_scatter | solution.py:1062
  495.1 362.3 %reduce-scatter.9.cloned.1.call-start = ((), (), s32[]{:S(2)}) async-start(), calls=%async_computation.11 | async-start | bytes 14417920 | tf_op jit(solution)/shard_map/reduce_scatter | solution.py:1062
  497.0 103.5 %all-to-all-start.1 = ((f32[8,2,128]{2,1,0:T(2,128)}), f32[8,2,128]{2,1,0:T(2,128)S(1)}, u32[]{:S(2)}, u32[]{:S(2)}) async-start(f32[8,2,128]{2,1,0:T(2,128)} %copy.145), calls=%async_computation.1 | async-start | bytes 16384 | tf_op jit(solution)/shard_map/all_to_all | solution.py:1066
  501.1 102.7 %copy-start.4 = (f32[128,2048]{1,0:T(8,128)S(1)}, f32[128,2048]{1,0:T(8,128)}, u32[]{:S(2)}) copy-start(f32[128,2048]{1,0:T(8,128)} %copy-done.3) | copy-start | bytes 3145732
  605.7 53.9 %copy-start.54 = (f32[128]{0:T(128)}, f32[128]{0:T(128)S(1)}, u32[]{:S(2)}) copy-start(f32[128]{0:T(128)S(1)} %multiply_multiply_fusion.1) | copy-start | bytes 1540
  713.0 124.0 %all-to-all-start.2 = ((bf16[8,64,1408]{2,1,0:T(8,128)(2,1)}), bf16[8,64,1408]{2,1,0:T(8,128)(2,1)}, u32[]{:S(2)}, u32[]{:S(2)}) async-start(bf16[8,64,1408]{2,1,0:T(8,128)(2,1)} %bitcast.231), calls=%async_computation.3 | async-start | bytes 2883584 | tf_op jit(solution)/shard_map/all_to_all | solution.py:1066
  (65 other events, 242.7 us)
Sparse Core Ops, SparseCore 0:
  9.6 107.6 all-gather.12
  118.8 43.3 all-gather.14
  163.8 43.3 all-gather.8
  208.7 27.0 all-gather.10
  305.8 72.1 all-gather.16
  493.7 53.1 reduce-scatter.4
  550.2 36.3 reduce-scatter.6
  589.1 54.8 reduce-scatter.10
  646.7 99.1 reduce-scatter.8

commit v3 on v2

--- a/solution.py
+++ b/solution.py
@@ -433,7 +433,7 @@
     return here, here // 2, line, here + 1 - 2 * line
 
 
-def greet_line(last, here, level, side):
+def greet_line(last, here, level, side, others=0):
     barrier = pltpu.get_barrier_semaphore()
     pl.semaphore_signal(barrier, inc=1, device_id={"ctx": side}, device_id_type=MESH)
 
@@ -446,7 +446,7 @@
         pl.semaphore_signal(barrier, inc=1, device_id={"ctx": here - 2}, device_id_type=MESH)
 
     ends = jnp.where(level < last, 1, 0) + jnp.where(level > 0, 1, 0)
-    pl.semaphore_wait(barrier, 1 + ends)
+    pl.semaphore_wait(barrier, 1 + others + ends)
 
 
 def line_copy(rows_ref, block, way, target, sems, source=None):
@@ -516,45 +516,6 @@
             line_copy(rows_ref, block, 1, side, sems).wait_send()
 
 
-def gather_kernel(last, count, *refs):
-    owns, rows = refs[:count], refs[count : 2 * count]
-    keep_sem = refs[2 * count]
-    place = line_place()
-    here, level, line, side = place
-    sems = [(refs[2 * count + 1 + 2 * i], refs[2 * count + 2 + 2 * i]) for i in range(count)]
-    greet_line(last, here, level, side)
-    keeps = [
-        pltpu.make_async_copy(owns[i], rows[i].at[here], keep_sem.at[i]) for i in range(count)
-    ]
-    for i in range(count):
-        line_start(rows[i], owns[i], sems[i], place, last)
-        keeps[i].start()
-    for i in range(count):
-        for step in range(1, last + 1):
-            line_step(rows[i], sems[i], place, last, step)
-    for i in range(count):
-        line_finish(rows[i], sems[i], place, last)
-        keeps[i].wait()
-
-
-def line_gather(ctx_count, call_id, *arrays):
-    count = len(arrays)
-    return pl.pallas_call(
-        functools.partial(gather_kernel, ctx_count // 2 - 1, count),
-        out_shape=[jax.ShapeDtypeStruct((ctx_count,) + a.shape, a.dtype) for a in arrays],
-        in_specs=[ANY] * count,
-        out_specs=[ANY] * count,
-        scratch_shapes=[pltpu.SemaphoreType.DMA((count,))]
-        + [
-            pltpu.SemaphoreType.DMA((ctx_count, 3)),
-            pltpu.SemaphoreType.DMA((ctx_count,)),
-        ]
-        * count,
-        compiler_params=pltpu.CompilerParams(collective_id=call_id, has_side_effects=True),
-        name="line_gather",
-    )(*arrays)
-
-
 ROWS_STEP = 16
 
 
@@ -599,13 +560,15 @@
             sums.at[goal], falling.at[goal], move_send.at[goal], fall_recv.at[goal], ctx=here - 2
         )
 
-    for k in range(last + 1):
+    for k in range(min(2, last + 1)):
         cross(turn(k)).start()
     for k in range(last + 1):
         yield k
         goal = turn(k)
         mine = part.at[2 * goal + line]
         cross(goal).wait_recv()
+        if k + 2 <= last:
+            cross(turn(k + 2)).start()
 
         @pl.when(goal > level)
         def upward():
@@ -723,13 +686,12 @@
     pl.semaphore_wait(barrier, ctx_count + 2)
 
 
-def share_start(blocks, sems):
+def share_start(blocks, sems, own=None):
     send_sem, recv_sem = sems
     here, beside, across, corner = fsdp_place()
+    source = blocks.at[here] if own is None else own
     for way, target in ((0, across), (1, beside)):
-        remote(
-            blocks.at[here], blocks.at[here], send_sem.at[way], recv_sem.at[here], fsdp=target
-        ).start()
+        remote(source, blocks.at[here], send_sem.at[way], recv_sem.at[here], fsdp=target).start()
 
 
 def share_step(blocks, sems):
@@ -769,6 +731,64 @@
         for k in range(1, ctx_count)
     ]
     return starts, waits
+
+
+def greet_near(last, here, level, side):
+    barrier = pltpu.get_barrier_semaphore()
+    group = lax.axis_index("fsdp")
+    for k in range(1, 4):
+        pl.semaphore_signal(barrier, inc=1, device_id={"fsdp": (group + k) % 4}, device_id_type=MESH)
+    greet_line(last, here, level, side, 3)
+
+
+def gather_kernel(last, shared_count, *refs):
+    total = 1 + shared_count
+    owns, rows, keep_sem = refs[:total], refs[total : 2 * total], refs[2 * total]
+    refs = refs[2 * total + 1 :]
+    place = line_place()
+    here, level, line, side = place
+    sems = [(refs[2 * i], refs[2 * i + 1]) for i in range(total)]
+    group = lax.axis_index("fsdp")
+    if shared_count:
+        greet_near(last, here, level, side)
+    else:
+        greet_line(last, here, level, side)
+    line_start(rows[0], owns[0], sems[0], place, last)
+    for i in range(1, total):
+        share_start(rows[i], sems[i], owns[i])
+    keeps = [
+        pltpu.make_async_copy(
+            owns[i], rows[i].at[group if i else here], keep_sem.at[i]
+        )
+        for i in range(total)
+    ]
+    for copy in keeps:
+        copy.start()
+    for step in range(1, last + 1):
+        line_step(rows[0], sems[0], place, last, step)
+    for i in range(1, total):
+        share_step(rows[i], sems[i])
+    line_finish(rows[0], sems[0], place, last)
+    for i in range(1, total):
+        share_finish(rows[i], sems[i])
+    for copy in keeps:
+        copy.wait()
+
+
+def line_gather(ctx_count, call_id, own, *shared):
+    count = len(shared)
+    dma = pltpu.SemaphoreType.DMA
+    return pl.pallas_call(
+        functools.partial(gather_kernel, ctx_count // 2 - 1, count),
+        out_shape=[jax.ShapeDtypeStruct((ctx_count,) + own.shape, own.dtype)]
+        + [jax.ShapeDtypeStruct((4,) + a.shape, a.dtype) for a in shared],
+        in_specs=[VMEM] * (1 + count),
+        out_specs=[ANY] * (1 + count),
+        scratch_shapes=[dma((1 + count,)), dma((ctx_count, 3)), dma((ctx_count,))]
+        + [dma((3,)), dma((4,))] * count,
+        compiler_params=pltpu.CompilerParams(collective_id=call_id, has_side_effects=True),
+        name="line_gather",
+    )(own, *shared)
 
 
 def opening_kernel(
@@ -788,14 +808,16 @@
     pair_recv,
     row_send,
     row_recv,
+    share_send,
+    share_recv,
     *sems,
 ):
     last = ctx_count // 2 - 1
     place = line_place()
     here, level, line, side = place
-    group = lax.axis_index("fsdp")
-    sems = [(sems[2 * i], sems[2 * i + 1]) for i in range(6)]
-    qkv_spread, small_spread, number_spread, qkv_share, out_share, small_share = sems
+    group, beside, across, corner = fsdp_place()
+    sems = [(sems[2 * i], sems[2 * i + 1]) for i in range(5)]
+    qkv_spread, small_spread, number_spread, out_share, small_share = sems
     row_sems = (row_send, row_recv)
     greet_all(ctx_count)
     qkv_start, qkv_wait = spread(
@@ -807,9 +829,25 @@
     number_start, number_wait = spread(
         lambda peer: number_own, lambda source: numbers.at[source], number_spread, ctx_count
     )
-    for copy in qkv_start + small_start + number_start:
+
+    def piece_copy(way, owner, k, target, first=False):
+        source = (here + ctx_count - k) % ctx_count
+        return remote(
+            qkv_own.at[here] if first else qkv.at[owner, source],
+            qkv.at[owner, source],
+            share_send.at[way, k],
+            share_recv.at[owner, k],
+            fsdp=target,
+        )
+
+    def piece_on(k):
+        piece_copy(0, group, k, across, k == 0).start()
+        piece_copy(1, group, k, beside, k == 0).start()
+
+    for copy in small_start + number_start + qkv_start:
         copy.start()
     line_start(rows, own, row_sems, place, last)
+    piece_on(0)
     pair = remote(
         out_own, out_pair.at[group, line], pair_send.at[0], pair_recv.at[0], ctx=side
     )
@@ -828,21 +866,24 @@
     ]
     for copy in keeps:
         copy.start()
-    line_step(rows, row_sems, place, last, 1)
-    for copy in small_wait + qkv_wait:
+    for copy in small_wait:
         copy.wait_recv()
     keeps[2].wait()
-    keeps[0].wait()
     share_start(small, small_share)
-    share_start(qkv, qkv_share)
+    line_step(rows, row_sems, place, last, 1)
+    for k in range(1, ctx_count):
+        qkv_wait[k - 1].wait_recv()
+        piece_on(k)
     remote(
         out_own, out_pair.at[group, 1 - line], pair_send.at[0], pair_recv.at[0], ctx=side
     ).wait_recv()
     keeps[1].wait()
     share_start(out_pair, out_share)
     line_step(rows, row_sems, place, last, 2)
+    for k in range(ctx_count):
+        piece_copy(0, across, k, across).wait_recv()
+        piece_copy(2, across, k, beside).start()
     share_step(small, small_share)
-    share_step(qkv, qkv_share)
     for step in range(3, last + 1):
         line_step(rows, row_sems, place, last, step)
     share_step(out_pair, out_share)
@@ -852,11 +893,15 @@
     for copy in qkv_start + small_start + number_start:
         copy.wait_send()
     pair.wait_send()
+    for k in range(ctx_count):
+        piece_copy(1, beside, k, beside).wait_recv()
+        piece_copy(2, corner, k, beside).wait_recv()
+        for way in range(3):
+            piece_copy(way, group, k, beside).wait_send()
     share_finish(small, small_share)
-    share_finish(qkv, qkv_share)
     share_finish(out_pair, out_share)
-    keeps[3].wait()
-    keeps[4].wait()
+    for i in (0, 3, 4):
+        keeps[i].wait()
 
 
 def opening(ctx_count, call_id, own, qkv_own, out_own, small_own, number_own):
@@ -873,7 +918,7 @@
             out((4, ctx_count), small_own),
             out((ctx_count,), number_own),
         ],
-        in_specs=[ANY] * 5,
+        in_specs=[VMEM] * 5,
         out_specs=[ANY] * 5,
         scratch_shapes=[
             dma((5,)),
@@ -881,9 +926,11 @@
             dma((1,)),
             dma((ctx_count, 3)),
             dma((ctx_count,)),
+            dma((3, ctx_count)),
+            dma((4, ctx_count)),
         ]
         + [dma((ctx_count,))] * 6
-        + [dma((3,)), dma((4,))] * 3,
+        + [dma((3,)), dma((4,))] * 2,
         compiler_params=pltpu.CompilerParams(collective_id=call_id, has_side_effects=True),
         name="opening",
     )(own, qkv_own, out_own, small_own, number_own)
@@ -936,13 +983,13 @@
     settled, pair_settled = weight_slots[3], pair_slots[3]
     weight_steps = group_reduce(weight, *weight_slots, weight_sems)
     pair_steps = group_reduce(pair, *pair_slots, pair_sems)
+    small_start, small_wait = spread(
+        lambda peer: small.at[:, peer], lambda source: small_in.at[source], small_spread, ctx_count
+    )
+    for copy in small_start:
+        copy.start()
     next(weight_steps)
     next(turns)
-    small_start, small_wait = spread(
-        lambda peer: small.at[:, peer], lambda source: small_in.at[source], small_spread, ctx_count
-    )
-    for copy in small_start:
-        copy.start()
     next(weight_steps)
     next(pair_steps)
     next(turns)
@@ -1052,6 +1099,50 @@
         ),
         name="closing",
     )(part, weight, pair, small)
+
+
+def deal_kernel(pieces, weight, dealt):
+    ctx_count = dealt.shape[0]
+    width = dealt.shape[2] // pieces
+    for c in range(ctx_count):
+        dealt[c] = jnp.concatenate(
+            [
+                weight[:, (q * ctx_count + c) * width : (q * ctx_count + c + 1) * width]
+                for q in range(pieces)
+            ],
+            axis=1,
+        )
+
+
+def deal_columns(weight, ctx_count, pieces):
+    rows, columns = weight.shape
+    return pl.pallas_call(
+        functools.partial(deal_kernel, pieces),
+        out_shape=jax.ShapeDtypeStruct((ctx_count, rows, columns // ctx_count), weight.dtype),
+        name="deal_columns",
+    )(weight)
+
+
+def collect_kernel(pieces, dealt, whole):
+    ctx_count = dealt.shape[0]
+    width = dealt.shape[2] // pieces
+    whole[...] = jnp.concatenate(
+        [
+            dealt[c, :, q * width : (q + 1) * width]
+            for q in range(pieces)
+            for c in range(ctx_count)
+        ],
+        axis=1,
+    ).astype(whole.dtype)
+
+
+def collect_columns(dealt, pieces):
+    ctx_count, rows, columns = dealt.shape
+    return pl.pallas_call(
+        functools.partial(collect_kernel, pieces),
+        out_shape=jax.ShapeDtypeStruct((rows, columns * ctx_count), jnp.float32),
+        name="collect_columns",
+    )(dealt)
 
 
 def over(axis, array, dim=0):
@@ -1162,17 +1253,10 @@
     routed_here = jnp.any(numbers[:, : number_count - 1] == ctx_rank, axis=1).reshape(row_len)
 
     shared_in_weight, numbers = lax.optimization_barrier((shared_in_weight, numbers))
-    inner_parts = (
-        shared_in_weight.reshape(shard, 2, fsdp_count, ctx_count, shared_shard)
-        .transpose(3, 0, 1, 2, 4)
-        .reshape(ctx_count, shard, 2 * shared_width)
-    )
+    inner_parts = deal_columns(shared_in_weight, ctx_count, 2 * fsdp_count)
     expert_inner = over("fsdp", expert_in_weight[0])
     expert_outer = over("fsdp", expert_out_weight[0])
-    outer_c = over("fsdp", shared_out_weight)
-    inner_parts = exchange(inner_parts).reshape(ctx_count * shard, 2 * shared_width)
-    inner_parts, late_grad = lax.optimization_barrier((inner_parts, out_grad))
-    inner_c = over("fsdp", inner_parts)
+    inner_parts = exchange(inner_parts)
     my_heads = [pair_rank + (side * 2 + t) * pairs for t in range(2)]
     bias_c = jnp.concatenate(
         [lax.dynamic_index_in_dim(bias_full, h, 1, keepdims=False) for h in my_heads], axis=1
@@ -1182,7 +1266,7 @@
     positions = (block_pairs[:, None] * block_len + offsets[None, :]).reshape(row_len)
     inputs = own_inputs.astype(full)
     row_inputs = row_inputs.reshape(row_len, width).astype(full)
-    row_upstream = over("ctx", late_grad.reshape(tokens_dev, width))
+    row_upstream = over("ctx", out_grad.reshape(tokens_dev, width))
     row_normed = rms_scale(row_inputs, gain_attn).astype(low)
     projected = matmul_low(row_normed, qkv_c) + bias_c.astype(full)
     query_pre = projected[:, : 2 * HD].reshape(row_len, 2, HD)
@@ -1211,13 +1295,22 @@
         .astype(low)
         .reshape(row_len, 2 * HD)
     )
+    attended_row, inner_parts = lax.optimization_barrier((attended_row, inner_parts))
     branch_part = matmul_low(attended_row, out_c).astype(low)
     (branch,) = line_scatter(ctx_count, 2, branch_part.reshape(ctx_count, tokens_dev, width))
     middle = inputs + branch
     normed_ffn = rms_scale(middle, gain_ffn).astype(low)
 
-    (row_ffn,) = line_gather(ctx_count, 3, normed_ffn)
+    row_ffn, inner_c, outer_c = line_gather(
+        ctx_count,
+        4,
+        normed_ffn,
+        inner_parts.reshape(ctx_count * shard, 2 * shared_width),
+        shared_out_weight,
+    )
     row_ffn = row_ffn.reshape(row_len, width)
+    inner_c = inner_c.reshape(width, 2 * shared_width)
+    outer_c = outer_c.reshape(shared_width, width)
     row_logits = dot_transposed(row_ffn, router_gate)
     row_probs = jax.nn.softmax(row_logits[:, :expert_count], axis=-1)
     expert_ids = jnp.arange(expert_count, dtype=jnp.int32)
@@ -1226,13 +1319,13 @@
     )
     row_gate = jax.nn.sigmoid(row_logits[:, expert_count])
     expert_gu = matmul_low(row_ffn, expert_inner)
+    row_upstream, expert_gu = lax.optimization_barrier((row_upstream, expert_gu))
     expert_hidden = swiglu_mix(expert_gu, expert_width).astype(low)
     expert_result = matmul_low(expert_hidden, expert_outer).astype(low).astype(full)
     row_shared, expert_result = lax.optimization_barrier((row_ffn, expert_result))
     shared_gu = matmul_low(row_shared, inner_c)
     shared_hidden = swiglu_mix(shared_gu, shared_width).astype(low)
     shared_out = matmul_low(shared_hidden, outer_c)
-    row_upstream, shared_out = lax.optimization_barrier((row_upstream, shared_out))
     upstream_row = row_upstream.astype(full)
     out_part = (row_gate[:, None] * shared_out + here[:, None] * expert_result).astype(low)
     gate_dot = jnp.sum(upstream_row * shared_out, axis=1)
@@ -1251,36 +1344,32 @@
     grad_expert_gu = expert_pull(grad_expert_hidden)[0].astype(low)
     grad_rows = dot_transposed(grad_expert_gu, expert_inner).astype(low).astype(full)
     grad_ffn_part = (dot_transposed(grad_shared_gu, inner_c) + grad_rows).astype(low)
+    out_sum = reduce_over("ctx", out_part).astype(full)
+    hidden_out = (middle + out_sum).astype(low)
     grad_expert_outer = transposed_dot(expert_hidden, grad_buffers).astype(low)
     grad_expert_inner = transposed_dot(row_ffn, grad_expert_gu).astype(low)
     grad_outer = transposed_dot(shared_hidden, grad_shared_out).astype(low)
     grad_inner = transposed_dot(row_ffn, grad_shared_gu).astype(low)
     (
         grad_ffn_part,
-        out_part,
+        hidden_out,
         grad_expert_outer,
         grad_expert_inner,
         grad_outer,
         grad_inner,
     ) = lax.optimization_barrier(
-        (grad_ffn_part, out_part, grad_expert_outer, grad_expert_inner, grad_outer, grad_inner)
+        (grad_ffn_part, hidden_out, grad_expert_outer, grad_expert_inner, grad_outer, grad_inner)
     )
     sum_expert_outer = reduce_over("fsdp", grad_expert_outer)
     sum_expert_inner = reduce_over("fsdp", grad_expert_inner)
     sum_outer = reduce_over("fsdp", grad_outer)
     sum_inner_c = reduce_over("fsdp", grad_inner)
-    grad_normed, out_sum = line_scatter(
-        ctx_count,
-        4,
-        grad_ffn_part.reshape(ctx_count, tokens_dev, width),
-        out_part.reshape(ctx_count, tokens_dev, width),
-    )
-    hidden_out = (middle + out_sum).astype(low).reshape(1, tokens_dev, width)
-    sum_inner = (
-        exchange(sum_inner_c.reshape(ctx_count, shard, 2 * shared_width))
-        .reshape(ctx_count, shard, 2, fsdp_count, shared_shard)
-        .transpose(1, 2, 3, 0, 4)
-        .reshape(shard, 2 * fsdp_count * ctx_count * shared_shard)
+    (grad_normed,) = line_scatter(
+        ctx_count, 2, grad_ffn_part.reshape(ctx_count, tokens_dev, width)
+    )
+    hidden_out = hidden_out.reshape(1, tokens_dev, width)
+    sum_inner = collect_columns(
+        exchange(sum_inner_c.reshape(ctx_count, shard, 2 * shared_width)), 2 * fsdp_count
     )
 
     own_logits = dot_transposed(normed_ffn, router_gate)
@@ -1379,7 +1468,7 @@
         sums[shard : 2 * shard],
         sum_router,
         sums[(2 + expert_count) * shard : (3 + expert_count) * shard],
-        sum_inner.astype(full),
+        sum_inner,
         sum_outer.astype(full),
         sum_expert_inner.astype(full)[None],
         sum_expert_outer.astype(full)[None],

time: 880 us -> 811 us (0.922)
  blocking collectives: 42.9 us -> 0 us
  local copies, waits for them, and re-layouts: 80.6 us -> 46.8 us
  waiting for transfers between devices: 17.7 us -> 34 us
  starting transfers between devices: 8.14 us -> 17 us
    all_to_all x1 -> x0, blocking collectives: 42.9 us -> none  [exchange(): return lax.all_to_all(array, 'ctx', split_axis=0, concat_axis=0, tiled=True)]
    pallas_call x2, Pallas kernels: 91.7 us -> 121 us  [line_gather(): pl.pallas_call(functools.partial(gather_kernel, ctx_count // 2 - 1, count...]
    reduce_scatter x4 -> x5, waiting for transfers between devices: 0.01 us -> 23.5 us  [reduce_over(): return lax.psum_scatter(array, axis, scatter_dimension=dim, tiled=True)]
    pallas_call x2, Pallas kernels: 147 us -> 125 us  [line_scatter(): pl.pallas_call(functools.partial(scatter_kernel, half - 1, count), out_sh...]
    convert_element_type x3 -> x0, local copies, waits for them, and re-layouts: 20.4 us -> none  [split_plan(): sum_inner.astype(full)]
    pallas_call x1, Pallas kernels: 99.1 us -> 84.1 us  [closing(): pl.pallas_call(functools.partial(closing_kernel, ctx_count), out_shape=[j...]
    all_gather x5 -> x3, waiting for transfers between devices: 13.7 us -> 0.02 us  [over(): return lax.all_gather(array, axis, axis=dim, tiled=True)]
    reduce_sum x1 -> x0, other arithmetic: 10.8 us -> none  [split_plan(): gate_dot = jnp.sum(upstream_row * shared_out, axis=1)]
  transfers between devices with their start and end apart: 11 -> 11, of which waited for: 1 -> 2; matrix products, arithmetic and copies ran while one was open for 25% -> 28% of each run, Pallas kernels for 50% -> 53%
where the time goes in v3:
time: 811 us; the launch traced here: 805 us
  Pallas kernels  428 us (53%)
  matrix products  211 us (26%)
  other arithmetic  52.1 us (6%)
  local copies, waits for them, and re-layouts  46.8 us (6%)
  waiting for transfers between devices  34 us (4%)
  starting transfers between devices  17 us (2%)
  between operations  15.6 us (2%)
    pallas_call x2, Pallas kernels, line_scatter(): pl.pallas_call(functools.partial(scatter_kernel, half - 1, count), out_sh...  125 us
    pallas_call x2, Pallas kernels, line_gather(): pl.pallas_call(functools.partial(gather_kernel, ctx_count // 2 - 1, count...  121 us
    pallas_call x1, Pallas kernels, opening(): pl.pallas_call(functools.partial(opening_kernel, ctx_count), out_shape=[o...  91.7 us
    pallas_call x1, Pallas kernels, closing(): pl.pallas_call(functools.partial(closing_kernel, ctx_count), out_shape=[j...  84.1 us
    dot_general x8, matrix products, dot_transposed(): lax.dot_general(left, right, (((1,), (1,)), ((), ())), preferred_element_...  74.7 us
    dot_general x7, matrix products, transposed_dot(): lax.dot_general(left, right, (((0,), (0,)), ((), ())), preferred_element_...  59.1 us
    dot_general x7, matrix products, matmul_low(): return jnp.dot(left, right, preferred_element_type=jnp.float32)  57.2 us
    reduce_scatter x5, waiting for transfers between devices, reduce_over(): return lax.psum_scatter(array, axis, scatter_dimension=dim, tiled=True)  23.5 us
  transfers between devices with their start and end apart: 11, of which 2 were waited for; matrix products, arithmetic and copies ran while one was open for 28% of the time, Pallas kernels for 53%

profile of v3, /device:TPU:0, one launch (start us, length us, event | category | flops | bytes accessed | tf_op | source)
XLA Modules:
  0.0 804.5 jit_solution(17604547378347142286)
XLA Ops:
  15.3 91.7 %opening.1 = (bf16[8,128,2048]{2,1,0:T(8,128)(2,1)}, bf16[4,8,64,768]{3,2,1,0:T(8,128)(2,1)}, bf16[4,2,64,2048]{3,2,1,0:T(8,128)(2,1)}, bf16[4,8,16,128]{3,2,1,0:T(8,128)(2,1)}, s32[8,8,128]{2,1,0:T(8,128)}) custom-call(bf16[128,2048]{1,0:T(8,128)(2,1)} %bitcast.187, bf16[8,64,768]{2,1,0:T(8,128)(2,1)} %reshape.530.qkv_own, bf16[64,2048]{1,0:T(8,128)(2,1)} %out_own.1, ...), custom_call_target="tpu_custom_call" | custom-call | tf_op jit(solution)/shard_map/opening/pallas_call | solution.py:912
  110.1 7.8 all-to-all-start
  173.1 78.4 %line_scatter.2 = f32[128,2048]{1,0:T(8,128)S(1)} custom-call(bf16[8,128,2048]{2,1,0:T(8,128)(2,1)S(1)} %bitcast.183), custom_call_target="tpu_custom_call" | custom-call | tf_op jit(solution)/shard_map/line_scatter/pallas_call | solution.py:657
  253.7 74.2 %line_gather.2 = (bf16[8,128,2048]{2,1,0:T(8,128)(2,1)}, bf16[4,512,1408]{2,1,0:T(8,128)(2,1)}, bf16[4,176,2048]{2,1,0:T(8,128)(2,1)}) custom-call(bf16[128,2048]{1,0:T(8,128)(2,1)} %multiply_convert_fusion.5.refs_0_, bf16[512,1408]{1,0:T(8,128)(2,1)} %bitcast.194, bf16[176,2048]{1,0:T(8,128)(2,1)} %refs_2_.1), custom_call_target="tpu_custom_call" | custom-call | tf_op jit(solution)/shard_map/line_gather/pallas_call | solution.py:781
  331.5 19.1 %fusion.2 = f32[1024,2816]{1,0:T(8,128)} fusion(bf16[1024,2048]{1,0:T(8,128)(2,1)} %bitcast.189, bf16[1,2048,2816]{2,1,0:T(8,128)(2,1)} %all-gather.9.cloned.1.call-done), kind=kOutput, calls=%fused_computation.9 | convolution fusion | flops 11811160064 | bytes 27262976 | tf_op jit(solution)/shard_map/dot_general | solution.py:49
  350.6 17.1 %fusion.37 = (f32[1024,1408]{1,0:T(8,128)}, f32[1024,1408]{1,0:T(8,128)}, bf16[1024,1408]{1,0:T(8,128)(2,1)S(1)}) fusion(f32[1024,2816]{1,0:T(8,128)} %fusion.2, bf16[1,1408,2048]{2,1,0:T(8,128)(2,1)} %all-gather.11.cloned.1.call-done, bf16[1024,2048]{1,0:T(8,128)(2,1)} %bitcast.248, f32[1024]{0:T(1024)S(1)} %bitcast_select_fusion.2), kind=kOutput, calls=%fused_computation.108 | convolution fusion | flops 5932056576 | bytes 35917824 | tf_op jit(solution)/shard_map/dot_general | solution.py:1167
  367.8 11.1 %convolution_convert_fusion.2 = bf16[1408,2048]{1,0:T(8,128)(2,1)} fusion(bf16[1024,1408]{1,0:T(8,128)(2,1)S(1)} %get-tuple-element.74, bf16[1024,2048]{1,0:T(8,128)(2,1)} %bitcast.249, f32[1024]{0:T(1024)S(1)} %bitcast_select_fusion.2), kind=kOutput, calls=%fused_computation.30 | convolution fusion | flops 5914755072 | bytes 12849152 | tf_op jit(solution)/shard_map/dot_general | solution.py:1161
  378.9 11.0 %convert_convert_fusion = f32[1024,2048]{1,0:T(8,128)} fusion(bf16[1024,1408]{1,0:T(8,128)(2,1)S(1)} %get-tuple-element.74, bf16[1,1408,2048]{2,1,0:T(8,128)(2,1)} %all-gather.11.cloned.1.call-done), kind=kOutput, calls=%fused_computation.44 | convolution fusion | flops 5909774336 | bytes 17039360 | tf_op jit(solution)/shard_map/dot_general | solution.py:49
  390.0 9.3 %fusion.79 = f32[1024,1408]{1,0:T(8,128)S(1)} fusion(bf16[1024,2048]{1,0:T(8,128)(2,1)S(1)} %bitcast.192, bf16[2048,1408]{1,0:T(8,128)(2,1)} %bitcast.246), kind=kOutput, calls=%fused_computation.198 | convolution fusion | flops 5905580032 | bytes 15728640 | tf_op jit(solution)/shard_map/dot_general | solution.py:49
  399.3 6.3 fusion.38
  410.4 10.4 %fusion.6 = (f32[1024]{0:T(1024)S(1)}, f32[1024]{0:T(1024)S(1)}, bf16[1024,2048]{1,0:T(8,128)(2,1)}) fusion(bf16[1024,2048]{1,0:T(8,128)(2,1)} %bitcast.250, f32[1024,2048]{1,0:T(8,128)} %convert_convert_fusion, f32[1024]{0:T(1024)S(1)} %bitcast_select_fusion.2, f32[1024]{0:T(1024)S(1)} %bitcast.242, bf16[1024,704]{1,0:T(8,128)(2,1)S(1)} %get-tuple-element.79, ...), kind=kOutput, calls=%fused_computation.16 | convolution fusion | flops 2971662336 | bytes 21118976 | tf_op jit(solution)/shard_map/dot_general | solution.py:49
  420.9 12.4 %convolution_convert_fusion.1 = bf16[2048,1408]{1,0:T(8,128)(2,1)} fusion(bf16[1024,2048]{1,0:T(8,128)(2,1)} %bitcast.190, f32[1024,704]{1,0:T(8,128)} %get-tuple-element.76, f32[1024,704]{1,0:T(8,128)} %get-tuple-element.75), kind=kOutput, calls=%fused_computation.29 | convolution fusion | flops 5911347200 | bytes 15728640 | tf_op jit(solution)/shard_map/dot_general | solution.py:1161
  433.3 19.3 %fusion = bf16[1024,2048]{1,0:T(8,128)(2,1)} fusion(bf16[1,2048,2816]{2,1,0:T(8,128)(2,1)} %all-gather.9.cloned.1.call-done, f32[1024,1408]{1,0:T(8,128)} %get-tuple-element.72, f32[1024,1408]{1,0:T(8,128)} %get-tuple-element.71), kind=kOutput, calls=%fused_computation.7 | convolution fusion | flops 11816927232 | bytes 27262976 | tf_op jit(solution)/shard_map/dot_general | solution.py:1167
  452.6 12.8 %add_convert_fusion.2 = bf16[1024,2048]{1,0:T(8,128)(2,1)} fusion(bf16[1024,2048]{1,0:T(8,128)(2,1)} %fusion, bf16[2048,1408]{1,0:T(8,128)(2,1)} %bitcast.247, f32[1024,704]{1,0:T(8,128)} %get-tuple-element.76, f32[1024,704]{1,0:T(8,128)} %get-tuple-element.75), kind=kOutput, calls=%fused_computation.24 | convolution fusion | flops 5914755072 | bytes 19922944 | tf_op jit(solution)/shard_map/dot_general | solution.py:1167
  465.4 20.3 %convolution_convert_fusion = bf16[2048,2816]{1,0:T(8,128)(2,1)} fusion(bf16[1024,2048]{1,0:T(8,128)(2,1)} %bitcast.191, f32[1024,1408]{1,0:T(8,128)} %get-tuple-element.72, f32[1024,1408]{1,0:T(8,128)} %get-tuple-element.71), kind=kOutput, calls=%fused_computation.12 | convolution fusion | flops 11822694400 | bytes 27262976 | tf_op jit(solution)/shard_map/dot_general | solution.py:1161
  485.7 23.4 %reduce-scatter.6.cloned.1.call-done = bf16[128,2048]{1,0:T(8,128)(2,1)} async-done(((bf16[1024,2048]{1,0:T(8,128)(2,1)}), bf16[128,2048]{1,0:T(8,128)(2,1)}) %reduce-scatter.6.cloned.1.call-update) | async-done | bytes 524304 | tf_op jit(solution)/shard_map/reduce_scatter | solution.py:1153
  518.8 6.5 all-to-all-done.1
  528.0 46.6 %line_scatter.3 = f32[128,2048]{1,0:T(8,128)S(1)} custom-call(bf16[8,128,2048]{2,1,0:T(8,128)(2,1)S(1)} %bitcast.184), custom_call_target="tpu_custom_call" | custom-call | tf_op jit(solution)/shard_map/line_scatter/pallas_call | solution.py:657
  577.3 46.8 %line_gather.3 = bf16[8,128,2048]{2,1,0:T(8,128)(2,1)} custom-call(bf16[128,2048]{1,0:T(8,128)(2,1)} %fusion.72.refs_0_), custom_call_target="tpu_custom_call" | custom-call | tf_op jit(solution)/shard_map/line_gather/pallas_call | solution.py:781
  628.1 6.0 multiply_reduce_fusion.1
  649.3 5.9 convolution_convert_fusion.7
  657.3 11.7 %multiply_reduce_fusion = (f32[2048]{0:T(1024)S(1)}, bf16[1024,2048]{1,0:T(8,128)(2,1)}, bf16[1024,2048]{1,0:T(8,128)(2,1)}) fusion(bf16[8,128,2048]{2,1,0:T(8,128)(2,1)} %get-tuple-element.38, f32[1024]{0:T(1024)S(1)} %copy-done.46, f32[2048]{0:T(1024)S(1)} %copy-done.36, bf16[2048,768]{1,0:T(8,128)(2,1)} %bitcast.253, bf16[1024,256]{0,1:T(8,128)(2,1)} %bitcast.223, ...), kind=kOutput, calls=%fused_computation.19 | convolution fusion | flops 3240622080 | bytes 17321984 | tf_op jit(solution)/shard_map/dot_general | solution.py:1167
  669.3 5.4 broadcast_select_fusion.1
  685.4 84.1 %closing.1 = (f32[128,2048]{1,0:T(8,128)S(1)}, bf16[8,64,768]{2,1,0:T(8,128)(2,1)S(1)}, f32[64,2048]{1,0:T(8,128)S(1)}, f32[8,128]{1,0:T(8,128)S(1)}) custom-call(bf16[8,128,2048]{2,1,0:T(8,128)(2,1)} %bitcast.195, bf16[4,512,768]{2,1,0:T(8,128)(2,1)} %bitcast.205, bf16[4,128,2048]{2,1,0:T(8,128)(2,1)S(1)} %pad_maximum_fusion.pair, f32[4,8,8,128]{3,2,1,0:T(8,128)S(1)} %copy.185), custom_call_target="tpu_custom_call" | custom-call | tf_op jit(solution)/shard_map/closing/pallas_call | solution.py:1073
  (296 shorter events, 151.1 us)
Async XLA Ops:
  7.2 324.3 %all-gather.9.cloned.1.call-start = ((), (), s32[]{:S(2)}) async-start(), calls=%async_computation.14 | async-start | bytes 14417920 | tf_op jit(solution)/shard_map/all_gather | solution.py:1149
  7.9 342.7 %all-gather.7.cloned.1.call-start = ((), (), s32[]{:S(2)}) async-start(), calls=%async_computation.13 | async-start | bytes 4718592 | tf_op jit(solution)/shard_map/all_gather | solution.py:1149
  110.1 59.7 %all-to-all-start = ((bf16[8,64,1408]{2,1,0:T(8,128)(2,1)}), bf16[8,64,1408]{2,1,0:T(8,128)(2,1)S(1)}, u32[]{:S(2)}, u32[]{:S(2)}) async-start(bf16[8,64,1408]{2,1,0:T(8,128)(2,1)} %deal_columns.1), calls=%async_computation | async-start | bytes 2883584 | tf_op jit(solution)/shard_map/all_to_all | solution.py:1157
  117.8 232.8 %all-gather.11.cloned.1.call-start = ((), (), s32[]{:S(2)}) async-start(), calls=%async_computation.15 | async-start | bytes 7208960 | tf_op jit(solution)/shard_map/all_gather | solution.py:1149
  118.6 390.5 %reduce-scatter.6.cloned.1.call-start = ((), (), s32[]{:S(2)}) async-start(), calls=%async_computation.8 | async-start | bytes 4718592 | tf_op jit(solution)/shard_map/reduce_scatter | solution.py:1153
  148.5 103.3 %copy-start.33 = (f32[2048]{0:T(1024)}, f32[2048]{0:T(1024)S(1)}, u32[]{:S(2)}) copy-start(f32[2048]{0:T(1024)S(1)} %reshape.572) | copy-start | bytes 24580
  158.7 172.7 %copy-start.51 = (pred[8]{0:T(512)(128)(4,1)}, pred[8]{0:T(512)(128)(4,1)S(1)}, u32[]{:S(2)}) copy-start(pred[8]{0:T(512)(128)(4,1)S(1)} %iota_compare_fusion.1) | copy-start | bytes 28
  169.8 81.7 %copy-start.26 = (bf16[2,128,1024]{2,1,0:T(8,128)(2,1)}, bf16[2,128,1024]{2,1,0:T(8,128)(2,1)S(1)}, u32[]{:S(2)}) copy-start(bf16[2,128,1024]{2,1,0:T(8,128)(2,1)S(1)} %convolution_convert_fusion.8) | copy-start | bytes 1572868
  169.8 81.7 %copy-start.11 = (bf16[8,64,1408]{2,1,0:T(8,128)(2,1)}, bf16[8,64,1408]{2,1,0:T(8,128)(2,1)S(1)}, u32[]{:S(2)}) copy-start(bf16[8,64,1408]{2,1,0:T(8,128)(2,1)S(1)} %all-to-all-done) | copy-start | bytes 4325380
  173.0 78.5 %copy-start.7 = (bf16[1,128,2048]{2,1,0:T(8,128)(2,1)S(1)}, bf16[1,128,2048]{2,1,0:T(8,128)(2,1)}, u32[]{:S(2)}) copy-start(bf16[1,128,2048]{2,1,0:T(8,128)(2,1)} %param.19) | copy-start | bytes 1572868
  251.5 76.4 %copy-start.27 = (bf16[9,2048]{1,0:T(8,128)(2,1)S(1)}, bf16[9,2048]{1,0:T(8,128)(2,1)}, u32[]{:S(2)}) copy-start(bf16[9,2048]{1,0:T(8,128)(2,1)} %constant_dynamic-update-slice_fusion) | copy-start | bytes 110596
  251.7 79.5 %copy-start.59 = (f32[128]{0:T(128)}, f32[128]{0:T(128)S(1)}, u32[]{:S(2)}) copy-start(f32[128]{0:T(128)S(1)} %get-tuple-element.69) | copy-start | bytes 1540
  251.8 79.5 %copy-start.43 = (f32[128]{0:T(128)}, f32[128]{0:T(128)S(1)}, u32[]{:S(2)}) copy-start(f32[128]{0:T(128)S(1)} %fusion.58) | copy-start | bytes 1540
  253.7 77.8 %copy-start.41 = (pred[8,128]{1,0:T(8,128)(4,1)S(1)}, pred[8,128]{1,0:T(8,128)(4,1)}, u32[]{:S(2)}) copy-start(pred[8,128]{1,0:T(8,128)(4,1)} %fusion.44) | copy-start | bytes 3076
  420.9 258.7 %reduce-scatter.8.cloned.1.call-start = ((), (), s32[]{:S(2)}) async-start(), calls=%async_computation.9 | async-start | bytes 7208960 | tf_op jit(solution)/shard_map/reduce_scatter | solution.py:1153
  511.1 271.6 %reduce-scatter.10.cloned.1.call-start = ((), (), s32[]{:S(2)}) async-start(), calls=%async_computation.10 | async-start | bytes 3604480 | tf_op jit(solution)/shard_map/reduce_scatter | solution.py:1153
  511.7 273.4 %reduce-scatter.14.cloned.1.call-start = ((), (), s32[]{:S(2)}) async-start(), calls=%async_computation.12 | async-start | bytes 7208960 | tf_op jit(solution)/shard_map/reduce_scatter | solution.py:1153
  512.5 279.5 %reduce-scatter.12.cloned.1.call-start = ((), (), s32[]{:S(2)}) async-start(), calls=%async_computation.11 | async-start | bytes 14417920 | tf_op jit(solution)/shard_map/reduce_scatter | solution.py:1153
  513.2 61.4 %copy-start.34 = (f32[2048]{0:T(1024)S(1)}, f32[2048]{0:T(1024)}, u32[]{:S(2)}) copy-start(f32[2048]{0:T(1024)} %copy-done.33) | copy-start | bytes 24580
  513.2 61.4 %copy-start.44 = (f32[128]{0:T(128)S(1)}, f32[128]{0:T(128)}, u32[]{:S(2)}) copy-start(f32[128]{0:T(128)} %copy-done.43) | copy-start | bytes 1540
  514.4 10.9 %all-to-all-start.1 = ((f32[8,2,128]{2,1,0:T(2,128)}), f32[8,2,128]{2,1,0:T(2,128)S(1)}, u32[]{:S(2)}, u32[]{:S(2)}) async-start(f32[8,2,128]{2,1,0:T(2,128)} %copy.137), calls=%async_computation.2 | async-start | bytes 16384 | tf_op jit(solution)/shard_map/all_to_all | solution.py:1157
  528.0 47.2 %copy-start.60 = (f32[128]{0:T(128)S(1)}, f32[128]{0:T(128)}, u32[]{:S(2)}) copy-start(f32[128]{0:T(128)} %copy-done.59) | copy-start | bytes 1540
  528.0 48.1 %copy-start.20 = (bf16[1,128,2048]{2,1,0:T(8,128)(2,1)S(1)}, bf16[1,128,2048]{2,1,0:T(8,128)(2,1)}, u32[]{:S(2)}) copy-start(bf16[1,128,2048]{2,1,0:T(8,128)(2,1)} %param.23) | copy-start | bytes 1572868
  679.6 108.8 %all-to-all-start.2 = ((bf16[8,64,1408]{2,1,0:T(8,128)(2,1)}), bf16[8,64,1408]{2,1,0:T(8,128)(2,1)}, u32[]{:S(2)}, u32[]{:S(2)}) async-start(bf16[8,64,1408]{2,1,0:T(8,128)(2,1)} %bitcast.215), calls=%async_computation.4 | async-start | bytes 2883584 | tf_op jit(solution)/shard_map/all_to_all | solution.py:1157
  (55 other events, 275.6 us)
Sparse Core Ops, SparseCore 0:
  9.6 107.4 all-gather.8
  119.2 113.6 all-gather.6
  234.5 65.6 all-gather.10
  421.0 88.0 reduce-scatter.5
  511.7 54.6 reduce-scatter.7
  569.3 36.3 reduce-scatter.9
  608.3 54.8 reduce-scatter.13
  665.8 120.4 reduce-scatter.11

commit v4 on v3

--- a/solution.py
+++ b/solution.py
@@ -630,41 +630,59 @@
             rise(goal).wait_send()
 
 
-def scatter_kernel(last, count, *refs):
-    parts, totals = refs[:count], refs[count : 2 * count]
-    slots, sems = refs[2 * count : 6 * count], refs[6 * count :]
+def scatter_kernel(ctx_count, part, small, total, small_in, *refs):
+    greet_all(ctx_count)
+    here = lax.axis_index("ctx")
+    starts, waits = spread(
+        lambda peer: small.at[peer], lambda source: small_in.at[source], refs[9:11], ctx_count
+    )
+    for copy in starts:
+        copy.start()
+    small_in[here] = small[here]
+    for step in scatter_turns(ctx_count // 2 - 1, part, total, *refs[:9]):
+        pass
+    for copy in waits:
+        copy.wait_recv()
+    for copy in starts:
+        copy.wait_send()
+
+
+def line_scatter_kernel(last, part, total, *refs):
     here, level, line, side = line_place()
     greet_line(last, here, level, side)
-    turns = [
-        scatter_turns(
-            last, parts[i], totals[i], *slots[4 * i : 4 * i + 4], *sems[5 * i : 5 * i + 5]
-        )
-        for i in range(count)
-    ]
-    for each in turns:
-        next(each)
-    for each in turns:
-        for step in each:
-            pass
-
-
-def line_scatter(ctx_count, call_id, *parts):
-    rows, width = parts[0].shape[1:]
-    count = len(parts)
+    for step in scatter_turns(last, part, total, *refs):
+        pass
+
+
+def line_scatter(ctx_count, call_id, part, small=None):
+    rows, width = part.shape[1:]
     half = ctx_count // 2
     dma = pltpu.SemaphoreType.DMA((half,))
-    slots = pltpu.VMEM((half, rows, width), parts[0].dtype)
+    spread_dma = pltpu.SemaphoreType.DMA((ctx_count,))
+    slots = pltpu.VMEM((half, rows, width), part.dtype)
+    total = jax.ShapeDtypeStruct((rows, width), jnp.float32)
+    params = pltpu.CompilerParams(
+        collective_id=call_id, has_side_effects=True, vmem_limit_bytes=40 * 2**20
+    )
+    if small is None:
+        return pl.pallas_call(
+            functools.partial(line_scatter_kernel, half - 1),
+            out_shape=total,
+            in_specs=[VMEM],
+            out_specs=VMEM,
+            scratch_shapes=[slots] * 4 + [dma] * 5,
+            compiler_params=params,
+            name="line_scatter",
+        )(part)
     return pl.pallas_call(
-        functools.partial(scatter_kernel, half - 1, count),
-        out_shape=[jax.ShapeDtypeStruct((rows, width), jnp.float32)] * count,
-        in_specs=[VMEM] * count,
-        out_specs=[VMEM] * count,
-        scratch_shapes=[slots] * (4 * count) + [dma] * (5 * count),
-        compiler_params=pltpu.CompilerParams(
-            collective_id=call_id, has_side_effects=True, vmem_limit_bytes=48 * 2**20
-        ),
+        functools.partial(scatter_kernel, ctx_count),
+        out_shape=[total, jax.ShapeDtypeStruct(small.shape, small.dtype)],
+        in_specs=[VMEM] * 2,
+        out_specs=[VMEM] * 2,
+        scratch_shapes=[slots] * 4 + [dma] * 5 + [spread_dma] * 2,
+        compiler_params=params,
         name="line_scatter",
-    )(*parts)
+    )(part, small)
 
 
 def fsdp_place():
@@ -969,13 +987,19 @@
     yield
 
 
-def closing_kernel(ctx_count, part, weight, pair, small, *refs):
-    total, landed, pair_total, small_total = refs[:4]
-    line_slots, weight_slots, pair_slots = refs[4:8], refs[8:12], refs[12:16]
-    pair_in, small_in, small_sums, small_across = refs[16:20]
-    line_sems, weight_sems, pair_sems = refs[20:25], refs[25:29], refs[29:33]
-    keep_sem, half_send, half_recv = refs[33:36]
-    weight_spread, small_spread, (group_send, group_recv) = refs[36:38], refs[38:40], refs[40:42]
+def closing_kernel(ctx_count, part, weight, pair, plain, small, *refs):
+    total, landed, pair_total, plain_total, small_total = refs[:5]
+    line_slots, weight_slots, pair_slots, plain_slots = (
+        refs[5:9],
+        refs[9:13],
+        refs[13:17],
+        refs[17:20],
+    )
+    pair_in, small_in, small_sums, small_across = refs[20:24]
+    sems = refs[24:]
+    line_sems, weight_sems, pair_sems, plain_sems = sems[:5], sems[5:9], sems[9:13], sems[13:17]
+    keep_sem, half_send, half_recv = sems[17:20]
+    weight_spread, small_spread, (group_send, group_recv) = sems[20:22], sems[22:24], sems[24:26]
     here, level, line, side = line_place()
     group = lax.axis_index("fsdp")
     greet_all(ctx_count)
@@ -983,6 +1007,7 @@
     settled, pair_settled = weight_slots[3], pair_slots[3]
     weight_steps = group_reduce(weight, *weight_slots, weight_sems)
     pair_steps = group_reduce(pair, *pair_slots, pair_sems)
+    plain_steps = group_reduce(plain, *plain_slots, plain_total, plain_sems)
     small_start, small_wait = spread(
         lambda peer: small.at[:, peer], lambda source: small_in.at[source], small_spread, ctx_count
     )
@@ -994,6 +1019,7 @@
     next(pair_steps)
     next(turns)
     next(pair_steps)
+    next(plain_steps)
     for copy in small_wait:
         copy.wait_recv()
     small_sum = small[:, here]
@@ -1028,6 +1054,7 @@
         keep_sem.at[0],
     )
     keep.start()
+    next(plain_steps)
     next(turns)
     next(pair_steps)
     half = pair_total.shape[0]
@@ -1044,6 +1071,7 @@
     small_total[...] = small_sums[group] + small_across[1] + small_across[2] + small_across[3]
     for step in turns:
         pass
+    next(plain_steps)
     half_copy.wait_recv()
     kept = pair_settled.at[pl.ds(pl.multiple_of(line * half, half), half)]
     add_rows(pair_total, (kept, pair_in), half)
@@ -1054,10 +1082,11 @@
     half_copy.wait_send()
     next(weight_steps)
     next(pair_steps)
+    next(plain_steps)
     keep.wait()
 
 
-def closing(ctx_count, call_id, part, weight, pair, small):
+def closing(ctx_count, call_id, part, weight, pair, plain, small):
     rows, width = part.shape[1:]
     half = ctx_count // 2
     dma = pltpu.SemaphoreType.DMA
@@ -1076,13 +1105,15 @@
             jax.ShapeDtypeStruct((rows, width), jnp.float32),
             jax.ShapeDtypeStruct((ctx_count, block // ctx_count, columns), weight.dtype),
             jax.ShapeDtypeStruct(pair_half, jnp.float32),
+            jax.ShapeDtypeStruct(plain.shape[1:], jnp.float32),
             jax.ShapeDtypeStruct(small.shape[2:], small.dtype),
         ],
-        in_specs=[VMEM] * 4,
-        out_specs=[VMEM] * 4,
+        in_specs=[VMEM] * 5,
+        out_specs=[VMEM] * 5,
         scratch_shapes=[slots] * 4
         + group_slots(weight)
         + group_slots(pair)
+        + group_slots(plain)[:3]
         + [
             pltpu.VMEM(pair_half, pair.dtype),
             pltpu.VMEM((ctx_count, 4) + small.shape[2:], small.dtype),
@@ -1090,15 +1121,15 @@
             pltpu.VMEM((4,) + small.shape[2:], small.dtype),
         ]
         + [dma((half,))] * 5
-        + [dma((2,)), dma((2,)), dma((1,)), dma((1,))] * 2
+        + [dma((2,)), dma((2,)), dma((1,)), dma((1,))] * 3
         + [dma((1,))] * 3
         + [dma((ctx_count,))] * 4
         + [dma((4,))] * 2,
         compiler_params=pltpu.CompilerParams(
-            collective_id=call_id, has_side_effects=True, vmem_limit_bytes=48 * 2**20
+            collective_id=call_id, has_side_effects=True, vmem_limit_bytes=56 * 2**20
         ),
         name="closing",
-    )(part, weight, pair, small)
+    )(part, weight, pair, plain, small)
 
 
 def deal_kernel(pieces, weight, dealt):
@@ -1142,6 +1173,26 @@
         functools.partial(collect_kernel, pieces),
         out_shape=jax.ShapeDtypeStruct((rows, columns * ctx_count), jnp.float32),
         name="collect_columns",
+    )(dealt)
+
+
+def heads_kernel(order, dealt, whole):
+    pairs = dealt.shape[0] * 2
+    for place, head in enumerate(order):
+        for which in range(3):
+            column = (which * 2 + place % 2) * HD
+            target = (which * pairs + head) * HD
+            whole[:, target : target + HD] = dealt[
+                place // 2, :, column : column + HD
+            ].astype(whole.dtype)
+
+
+def collect_heads(dealt, order):
+    ctx_count, rows, columns = dealt.shape
+    return pl.pallas_call(
+        functools.partial(heads_kernel, order),
+        out_shape=jax.ShapeDtypeStruct((rows, columns * ctx_count), jnp.float32),
+        name="collect_heads",
     )(dealt)
 
 
@@ -1297,7 +1348,7 @@
     )
     attended_row, inner_parts = lax.optimization_barrier((attended_row, inner_parts))
     branch_part = matmul_low(attended_row, out_c).astype(low)
-    (branch,) = line_scatter(ctx_count, 2, branch_part.reshape(ctx_count, tokens_dev, width))
+    branch = line_scatter(ctx_count, 2, branch_part.reshape(ctx_count, tokens_dev, width))
     middle = inputs + branch
     normed_ffn = rms_scale(middle, gain_ffn).astype(low)
 
@@ -1330,47 +1381,46 @@
     out_part = (row_gate[:, None] * shared_out + here[:, None] * expert_result).astype(low)
     gate_dot = jnp.sum(upstream_row * shared_out, axis=1)
     expert_dot = jnp.where(routed_here, jnp.sum(upstream_row * expert_result, axis=1), 0.0)
-    own_dots = exchange(
-        jnp.stack([gate_dot, expert_dot]).reshape(2, ctx_count, tokens_dev).transpose(1, 0, 2)
-    )
-
+    out_landed = reduce_over("ctx", out_part)
+
+    upstream_row, out_part = lax.optimization_barrier((upstream_row, out_part))
+    grad_buffers = (here[:, None] * upstream_row).astype(low)
+    sum_expert_outer = reduce_over("fsdp", transposed_dot(expert_hidden, grad_buffers).astype(low))
+    grad_expert_hidden = dot_transposed(grad_buffers, expert_outer)
+    unused_mix, expert_pull = jax.vjp(
+        functools.partial(swiglu_mix, hidden_width=expert_width), expert_gu
+    )
+    grad_expert_gu = expert_pull(grad_expert_hidden)[0].astype(low)
+    grad_rows = dot_transposed(grad_expert_gu, expert_inner).astype(low)
+    upstream_row, grad_rows = lax.optimization_barrier((upstream_row, grad_rows))
     grad_shared_out = (row_gate[:, None] * upstream_row).astype(low)
-    grad_buffers = (here[:, None] * upstream_row).astype(low)
     grad_hidden = dot_transposed(grad_shared_out, outer_c)
-    unused_mix, mix_pull = jax.vjp(functools.partial(swiglu_mix, hidden_width=shared_width), shared_gu)
+    unused_mix, mix_pull = jax.vjp(
+        functools.partial(swiglu_mix, hidden_width=shared_width), shared_gu
+    )
     grad_shared_gu = mix_pull(grad_hidden)[0].astype(low)
-    grad_expert_hidden = dot_transposed(grad_buffers, expert_outer)
-    unused_mix, expert_pull = jax.vjp(functools.partial(swiglu_mix, hidden_width=expert_width), expert_gu)
-    grad_expert_gu = expert_pull(grad_expert_hidden)[0].astype(low)
-    grad_rows = dot_transposed(grad_expert_gu, expert_inner).astype(low).astype(full)
-    grad_ffn_part = (dot_transposed(grad_shared_gu, inner_c) + grad_rows).astype(low)
-    out_sum = reduce_over("ctx", out_part).astype(full)
-    hidden_out = (middle + out_sum).astype(low)
-    grad_expert_outer = transposed_dot(expert_hidden, grad_buffers).astype(low)
+    grad_inner = transposed_dot(row_ffn, grad_shared_gu).astype(low)
+    sum_inner_c = reduce_over("fsdp", grad_inner)
+    grad_outer = transposed_dot(shared_hidden, grad_shared_out).astype(low)
+    grad_ffn_part = (
+        dot_transposed(grad_shared_gu, inner_c) + grad_rows.astype(full)
+    ).astype(low)
+    grad_expert_gu, grad_ffn_part, grad_inner = lax.optimization_barrier(
+        (grad_expert_gu, grad_ffn_part, grad_inner)
+    )
     grad_expert_inner = transposed_dot(row_ffn, grad_expert_gu).astype(low)
-    grad_outer = transposed_dot(shared_hidden, grad_shared_out).astype(low)
-    grad_inner = transposed_dot(row_ffn, grad_shared_gu).astype(low)
-    (
-        grad_ffn_part,
-        hidden_out,
-        grad_expert_outer,
-        grad_expert_inner,
-        grad_outer,
-        grad_inner,
-    ) = lax.optimization_barrier(
-        (grad_ffn_part, hidden_out, grad_expert_outer, grad_expert_inner, grad_outer, grad_inner)
-    )
-    sum_expert_outer = reduce_over("fsdp", grad_expert_outer)
+    dots = jnp.stack([gate_dot, expert_dot]).reshape(2, ctx_count, tokens_dev).transpose(1, 0, 2)
+    grad_ffn_part, grad_expert_inner, grad_outer = lax.optimization_barrier(
+        (grad_ffn_part, grad_expert_inner, grad_outer)
+    )
     sum_expert_inner = reduce_over("fsdp", grad_expert_inner)
-    sum_outer = reduce_over("fsdp", grad_outer)
-    sum_inner_c = reduce_over("fsdp", grad_inner)
-    (grad_normed,) = line_scatter(
-        ctx_count, 2, grad_ffn_part.reshape(ctx_count, tokens_dev, width)
-    )
-    hidden_out = hidden_out.reshape(1, tokens_dev, width)
-    sum_inner = collect_columns(
-        exchange(sum_inner_c.reshape(ctx_count, shard, 2 * shared_width)), 2 * fsdp_count
-    )
+    grad_normed, own_dots = line_scatter(
+        ctx_count,
+        6,
+        grad_ffn_part.reshape(ctx_count, tokens_dev, width),
+        jnp.pad(dots, ((0, 0), (0, 6), (0, 0))),
+    )
+    hidden_out = (middle + out_landed.astype(full)).astype(low).reshape(1, tokens_dev, width)
 
     own_logits = dot_transposed(normed_ffn, router_gate)
     router_probs = jax.nn.softmax(own_logits[:, :expert_count], axis=-1)
@@ -1387,8 +1437,16 @@
     grad_middle_norm, grad_gain_ffn = norm_pull(grad_normed)
     grad_middle = out_grad.reshape(tokens_dev, width).astype(full) + grad_middle_norm
 
-    (row_branch,) = line_gather(ctx_count, 3, grad_middle.astype(low))
-    row_branch = row_branch.reshape(row_len, width)
+    grad_branch, sum_expert_outer, hidden_out = lax.optimization_barrier(
+        (grad_middle.astype(low), sum_expert_outer, hidden_out)
+    )
+    (row_branch,) = line_gather(ctx_count, 3, grad_branch)
+    row_branch, sum_inner_c = lax.optimization_barrier(
+        (row_branch.reshape(row_len, width), sum_inner_c)
+    )
+    sum_inner = collect_columns(
+        exchange(sum_inner_c.reshape(ctx_count, shard, 2 * shared_width)), 2 * fsdp_count
+    )
     grad_attended = dot_transposed(row_branch, out_c).astype(low).reshape(row_len, 2, HD)
     grad_out_c = transposed_dot(attended_row, row_branch).astype(low).reshape(2, HD, width)
     padded_out = jnp.concatenate(
@@ -1414,6 +1472,7 @@
         ],
         axis=1,
     ).astype(low)
+    grad_projected, sum_inner = lax.optimization_barrier((grad_projected, sum_inner))
     grad_attn_part = dot_transposed(grad_projected, qkv_c)
     row_scaled = row_inputs * lax.rsqrt(
         jnp.mean(row_inputs * row_inputs, axis=-1, keepdims=True) + EPSILON
@@ -1440,21 +1499,17 @@
     )
     small_grads = jnp.pad(small_grads, ((0, 0), (0, 8 * HD - small_count)))
     grad_qkv_c = transposed_dot(row_normed, grad_projected).astype(low)
-    grad_normed_attn, sum_qkv_c, sum_out, sums = closing(
+    grad_normed_attn, sum_qkv_c, sum_out, sum_outer, sums = closing(
         ctx_count,
         5,
         grad_attn_part.astype(low).reshape(ctx_count, tokens_dev, width),
         grad_qkv_c.reshape(fsdp_count, ctx_count * shard, 6 * HD),
         padded_out,
+        grad_outer.reshape(fsdp_count, shared_shard, width),
         small_grads.reshape(fsdp_count, ctx_count, 8, HD),
     )
     sums = sums.reshape(8 * HD)[:small_count]
-    sum_qkv = (
-        sum_qkv_c.reshape(ctx_count, shard, 3, 2, HD)
-        .transpose(1, 2, 0, 3, 4)
-        .reshape(shard, 3, head_count, HD)[:, :, jnp.array(places_of)]
-        .reshape(shard, 3 * width)
-    )
+    sum_qkv = collect_heads(sum_qkv_c, head_order)
     unused_norm, first_pull = jax.vjp(lambda v: rms_scale(v, gain_attn), inputs)
     input_grad = grad_middle + first_pull(grad_normed_attn)[0]
     sum_router = sums[2 * shard : (2 + expert_count) * shard].reshape(expert_count, shard).T
@@ -1462,14 +1517,14 @@
         hidden_out,
         input_grad.reshape(1, tokens_dev, width),
         sums[:shard],
-        sum_qkv.astype(full),
+        sum_qkv,
         sums[(3 + expert_count) * shard :],
         sum_out,
         sums[shard : 2 * shard],
         sum_router,
         sums[(2 + expert_count) * shard : (3 + expert_count) * shard],
         sum_inner,
-        sum_outer.astype(full),
+        sum_outer,
         sum_expert_inner.astype(full)[None],
         sum_expert_outer.astype(full)[None],
     )

time: 811 us -> 790 us (0.974)
  waiting for transfers between devices: 34 us -> 2.22 us
  other arithmetic: 52.1 us -> 65 us
  local copies, waits for them, and re-layouts: 46.8 us -> 58.4 us
  matrix products: 211 us -> 201 us
    reduce_scatter x5 -> x4, waiting for transfers between devices: 23.5 us -> 0.04 us  [reduce_over(): return lax.psum_scatter(array, axis, scatter_dimension=dim, tiled=True)]
    unnamed x147 -> x171, local copies, waits for them, and re-layouts: 20.2 us -> 32.1 us
    convert_element_type x4, other arithmetic: 6.82 us -> 16.8 us  [the longest x1 7.53 us: split_plan(): grad_expert_gu = expert_pull(grad_expert_hidden)[0].astype(low)]
    pallas_call x1, Pallas kernels: 84.1 us -> 75.2 us  [closing(): pl.pallas_call(functools.partial(closing_kernel, ctx_count), out_shape=[j...]
    pallas_call x2 -> x3, Pallas kernels: 125 us -> 132 us  [the longest x1 75.3 us: line_scatter(): pl.pallas_call(functools.partial(line_scatter_kernel, half - 1), out_shap...]
    all_to_all x3 -> x2, starting transfers between devices: 16.5 us -> 12.4 us  [exchange(): return lax.all_to_all(array, 'ctx', split_axis=0, concat_axis=0, tiled=True)]
  transfers between devices with their start and end apart: 11 -> 9, of which waited for: 2 -> 0; matrix products, arithmetic and copies ran while one was open for 28% -> 35% of each run, Pallas kernels for 53% -> 55%
where the time goes in v4:
time: 790 us; the launch traced here: 782 us
  Pallas kernels  427 us (54%)
  matrix products  201 us (25%)
  other arithmetic  65 us (8%)
  local copies, waits for them, and re-layouts  58.4 us (7%)
  between operations  15.7 us (2%)
  starting transfers between devices  12.7 us (2%)
    pallas_call x2, Pallas kernels, line_gather(): pl.pallas_call(functools.partial(gather_kernel, ctx_count // 2 - 1, count...  121 us
    pallas_call x1, Pallas kernels, opening(): pl.pallas_call(functools.partial(opening_kernel, ctx_count), out_shape=[o...  91.7 us
    dot_general x8, matrix products, dot_transposed(): lax.dot_general(left, right, (((1,), (1,)), ((), ())), preferred_element_...  76.2 us
    pallas_call x1, Pallas kernels, line_scatter(): pl.pallas_call(functools.partial(line_scatter_kernel, half - 1), out_shap...  75.3 us
    pallas_call x1, Pallas kernels, closing(): pl.pallas_call(functools.partial(closing_kernel, ctx_count), out_shape=[j...  75.2 us
    pallas_call x1, Pallas kernels, line_scatter(): pl.pallas_call(functools.partial(scatter_kernel, ctx_count), out_shape=[t...  54.2 us
    dot_general x7, matrix products, transposed_dot(): lax.dot_general(left, right, (((0,), (0,)), ((), ())), preferred_element_...  53.4 us
    dot_general x7, matrix products, matmul_low(): return jnp.dot(left, right, preferred_element_type=jnp.float32)  51.6 us
  transfers between devices with their start and end apart: 9, of which 0 were waited for; matrix products, arithmetic and copies ran while one was open for 35% of the time, Pallas kernels for 55%

profile of v4, /device:TPU:0, one launch (start us, length us, event | category | flops | bytes accessed | tf_op | source)
XLA Modules:
  0.0 782.2 jit_solution(7553772148203540301)
XLA Ops:
  15.3 91.7 %opening.1 = (bf16[8,128,2048]{2,1,0:T(8,128)(2,1)}, bf16[4,8,64,768]{3,2,1,0:T(8,128)(2,1)}, bf16[4,2,64,2048]{3,2,1,0:T(8,128)(2,1)}, bf16[4,8,16,128]{3,2,1,0:T(8,128)(2,1)}, s32[8,8,128]{2,1,0:T(8,128)}) custom-call(bf16[128,2048]{1,0:T(8,128)(2,1)} %bitcast.181, bf16[8,64,768]{2,1,0:T(8,128)(2,1)} %reshape.525.qkv_own, bf16[64,2048]{1,0:T(8,128)(2,1)} %out_own.1, ...), custom_call_target="tpu_custom_call" | custom-call | tf_op jit(solution)/shard_map/opening/pallas_call | solution.py:930
  110.1 7.9 %all-to-all-start = ((bf16[8,64,1408]{2,1,0:T(8,128)(2,1)}), bf16[8,64,1408]{2,1,0:T(8,128)(2,1)S(1)}, u32[]{:S(2)}, u32[]{:S(2)}) async-start(bf16[8,64,1408]{2,1,0:T(8,128)(2,1)} %deal_columns.1), calls=%async_computation | async-start | bytes 2883584 | tf_op jit(solution)/shard_map/all_to_all | solution.py:1208
  175.8 75.3 %line_scatter.2 = f32[128,2048]{1,0:T(8,128)S(1)} custom-call(bf16[8,128,2048]{2,1,0:T(8,128)(2,1)S(1)} %bitcast.177), custom_call_target="tpu_custom_call" | custom-call | tf_op jit(solution)/shard_map/line_scatter/pallas_call | solution.py:668
  253.3 74.2 %line_gather.2 = (bf16[8,128,2048]{2,1,0:T(8,128)(2,1)}, bf16[4,512,1408]{2,1,0:T(8,128)(2,1)}, bf16[4,176,2048]{2,1,0:T(8,128)(2,1)}) custom-call(bf16[128,2048]{1,0:T(8,128)(2,1)} %multiply_convert_fusion.7.refs_0_, bf16[512,1408]{1,0:T(8,128)(2,1)} %bitcast.189, bf16[176,2048]{1,0:T(8,128)(2,1)} %refs_2_.1), custom_call_target="tpu_custom_call" | custom-call | tf_op jit(solution)/shard_map/line_gather/pallas_call | solution.py:799
  331.2 19.2 %fusion.2 = f32[1024,2816]{1,0:T(8,128)} fusion(bf16[1024,2048]{1,0:T(8,128)(2,1)} %bitcast.185, bf16[1,2048,2816]{2,1,0:T(8,128)(2,1)} %all-gather.9.cloned.1.call-done), kind=kOutput, calls=%fused_computation.4 | convolution fusion | flops 11811160064 | bytes 27262976 | tf_op jit(solution)/shard_map/dot_general | solution.py:49
  355.6 8.8 %convert_convert_fusion = f32[1024,2048]{1,0:T(8,128)S(1)} fusion(bf16[1024,1408]{1,0:T(8,128)(2,1)S(1)} %multiply_convert_fusion.5, bf16[1,1408,2048]{2,1,0:T(8,128)(2,1)} %all-gather.11.cloned.1.call-done), kind=kOutput, calls=%fused_computation.39 | convolution fusion | flops 5909774336 | bytes 17039360 | tf_op jit(solution)/shard_map/dot_general | solution.py:49
  364.5 9.2 %fusion.73 = f32[1024,1408]{1,0:T(8,128)S(1)} fusion(bf16[1024,2048]{1,0:T(8,128)(2,1)S(1)} %bitcast.186, bf16[2048,1408]{1,0:T(8,128)(2,1)} %bitcast.237), kind=kOutput, calls=%fused_computation.191 | convolution fusion | flops 5905580032 | bytes 15728640 | tf_op jit(solution)/shard_map/dot_general | solution.py:49
  379.8 7.1 multiply_reduce_fusion.3
  393.4 8.3 %convolution_convert_fusion.1 = bf16[1408,2048]{1,0:T(8,128)(2,1)} fusion(bf16[1024,1408]{1,0:T(8,128)(2,1)S(1)} %multiply_convert_fusion.5, f32[1024,2048]{1,0:T(8,128)S(1)} %convert_element_type.214, f32[1024]{0:T(1024)S(1)} %bitcast_select_fusion.1), kind=kOutput, calls=%fused_computation.24 | convolution fusion | flops 5912657920 | bytes 17043456 | tf_op jit(solution)/shard_map/dot_general | solution.py:1212
  401.8 17.6 %fusion.31 = (f32[1024,1408]{1,0:T(8,128)}, f32[1024,1408]{1,0:T(8,128)}) fusion(f32[1024,2816]{1,0:T(8,128)} %fusion.2, bf16[1,1408,2048]{2,1,0:T(8,128)(2,1)} %all-gather.11.cloned.1.call-done, f32[1024,2048]{1,0:T(8,128)} %copy-done.6, f32[1024]{0:T(1024)S(1)} %bitcast_select_fusion.1), kind=kOutput, calls=%fused_computation.101 | convolution fusion | flops 5927075840 | bytes 37228544 | tf_op jit(solution)/shard_map/dot_general | solution.py:1218
  419.4 7.5 add_convert_fusion
  426.9 18.3 %fusion.12 = bf16[1024,2048]{1,0:T(8,128)(2,1)} fusion(bf16[1024,2816]{1,0:T(8,128)(2,1)} %add_convert_fusion, bf16[1,2048,2816]{2,1,0:T(8,128)(2,1)} %all-gather.9.cloned.1.call-done), kind=kOutput, calls=%fused_computation.41 | convolution fusion | flops 11813257216 | bytes 21495808 | tf_op jit(solution)/shard_map/dot_general | solution.py:1218
  445.3 7.3 fusion.33
  455.2 9.0 %convolution_convert_fusion.2 = bf16[2048,1408]{1,0:T(8,128)(2,1)} fusion(bf16[1024,2048]{1,0:T(8,128)(2,1)S(1)} %bitcast.187, f32[1024,704]{1,0:T(8,128)S(1)} %get-tuple-element.99, f32[1024,704]{1,0:T(8,128)S(1)} %get-tuple-element.98), kind=kOutput, calls=%fused_computation.25 | convolution fusion | flops 5911347200 | bytes 15728640 | tf_op jit(solution)/shard_map/dot_general | solution.py:1212
  464.3 13.2 %add_convert_fusion.1 = bf16[1024,2048]{1,0:T(8,128)(2,1)} fusion(bf16[1024,2048]{1,0:T(8,128)(2,1)} %fusion.12, bf16[2048,1408]{1,0:T(8,128)(2,1)} %bitcast.238, f32[1024,704]{1,0:T(8,128)} %copy-done.75, f32[1024,704]{1,0:T(8,128)} %copy-done.74), kind=kOutput, calls=%fused_computation.16 | convolution fusion | flops 5914755072 | bytes 19922944 | tf_op jit(solution)/shard_map/dot_general | solution.py:1218
  477.5 8.7 %convolution_convert_fusion.5 = bf16[704,2048]{1,0:T(8,128)(2,1)} fusion(bf16[1024,704]{1,0:T(8,128)(2,1)S(1)} %copy-done.33, f32[1024,2048]{1,0:T(8,128)} %copy-done.6, f32[1024]{0:T(1024)S(1)} %bitcast.233), kind=kOutput, calls=%fused_computation.44 | convolution fusion | flops 2958426112 | bytes 12718080 | tf_op jit(solution)/shard_map/dot_general | solution.py:1212
  486.1 18.0 %convolution_convert_fusion = bf16[2048,2816]{1,0:T(8,128)(2,1)} fusion(bf16[1024,2048]{1,0:T(8,128)(2,1)S(1)} %bitcast.188, bf16[1024,2816]{1,0:T(8,128)(2,1)} %add_convert_fusion), kind=kOutput, calls=%fused_computation.7 | convolution fusion | flops 11816927232 | bytes 21495808 | tf_op jit(solution)/shard_map/dot_general | solution.py:1212
  507.7 54.2 %line_scatter.3 = (f32[128,2048]{1,0:T(8,128)S(1)}, f32[8,8,128]{2,1,0:T(8,128)S(1)}) custom-call(bf16[8,128,2048]{2,1,0:T(8,128)(2,1)S(1)} %bitcast.178, f32[8,8,128]{2,1,0:T(8,128)S(1)} %pad.46.small), custom_call_target="tpu_custom_call" | custom-call | tf_op jit(solution)/shard_map/line_scatter/pallas_call | solution.py:677
  565.7 47.1 %line_gather.3 = bf16[8,128,2048]{2,1,0:T(8,128)(2,1)} custom-call(bf16[128,2048]{1,0:T(8,128)(2,1)} %get-tuple-element.74.refs_0_), custom_call_target="tpu_custom_call" | custom-call | tf_op jit(solution)/shard_map/line_gather/pallas_call | solution.py:799
  621.7 5.4 multiply_reduce_fusion.1
  643.6 6.3 convolution_convert_fusion.7
  662.2 12.0 %multiply_reduce_fusion = (f32[2048]{0:T(1024)S(1)}, bf16[1024,2048]{1,0:T(8,128)(2,1)}, bf16[1024,2048]{1,0:T(8,128)(2,1)}) fusion(bf16[8,128,2048]{2,1,0:T(8,128)(2,1)} %get-tuple-element.50, f32[1024]{0:T(1024)S(1)} %copy-done.57, f32[2048]{0:T(1024)S(1)} %copy-done.47, bf16[1024,768]{0,1:T(8,128)(2,1)} %pad_maximum_fusion.1, bf16[2048,768]{1,0:T(8,128)(2,1)} %bitcast.239), kind=kOutput, calls=%fused_computation.10 | convolution fusion | flops 3235903488 | bytes 17321984 | tf_op jit(solution)/shard_map/dot_general | solution.py:1218
  675.0 8.0 %convolution_convert_fusion.4 = bf16[2048,768]{1,0:T(8,128)(2,1)} fusion(bf16[1024,2048]{1,0:T(8,128)(2,1)} %get-tuple-element.102, bf16[1024,768]{0,1:T(8,128)(2,1)} %pad_maximum_fusion.1), kind=kOutput, calls=%fused_computation.43 | convolution fusion | flops 3222798336 | bytes 8912896 | tf_op jit(solution)/shard_map/dot_general | solution.py:1212
  683.0 75.2 %closing.1 = (f32[128,2048]{1,0:T(8,128)}, bf16[8,64,768]{2,1,0:T(8,128)(2,1)}, f32[64,2048]{1,0:T(8,128)}, f32[176,2048]{1,0:T(8,128)}, f32[8,128]{1,0:T(8,128)}) custom-call(bf16[8,128,2048]{2,1,0:T(8,128)(2,1)} %bitcast.192, bf16[4,512,768]{2,1,0:T(8,128)(2,1)} %bitcast.201, bf16[4,128,2048]{2,1,0:T(8,128)(2,1)} %pad_maximum_fusion.pair, ...), custom_call_target="tpu_custom_call" | custom-call | tf_op jit(solution)/shard_map/closing/pallas_call | solution.py:1102
  (315 shorter events, 157.2 us)
Async XLA Ops:
  7.2 324.0 %all-gather.9.cloned.1.call-start = ((), (), s32[]{:S(2)}) async-start(), calls=%async_computation.11 | async-start | bytes 14417920 | tf_op jit(solution)/shard_map/all_gather | solution.py:1200
  7.9 342.5 %all-gather.7.cloned.1.call-start = ((), (), s32[]{:S(2)}) async-start(), calls=%async_computation.10 | async-start | bytes 4718592 | tf_op jit(solution)/shard_map/all_gather | solution.py:1200
  110.1 62.5 %all-to-all-start = ((bf16[8,64,1408]{2,1,0:T(8,128)(2,1)}), bf16[8,64,1408]{2,1,0:T(8,128)(2,1)S(1)}, u32[]{:S(2)}, u32[]{:S(2)}) async-start(bf16[8,64,1408]{2,1,0:T(8,128)(2,1)} %deal_columns.1), calls=%async_computation | async-start | bytes 2883584 | tf_op jit(solution)/shard_map/all_to_all | solution.py:1208
  118.0 237.6 %all-gather.11.cloned.1.call-start = ((), (), s32[]{:S(2)}) async-start(), calls=%async_computation.12 | async-start | bytes 7208960 | tf_op jit(solution)/shard_map/all_gather | solution.py:1200
  118.7 444.4 %reduce-scatter.7.cloned.1.call-start = ((), (), s32[]{:S(2)}) async-start(), calls=%async_computation.7 | async-start | bytes 4718592 | tf_op jit(solution)/shard_map/reduce_scatter | solution.py:1204
  127.0 43.1 %copy-start.2 = (pred[1024,1024]{0,1:T(8,128)(4,1)}, pred[1024,1024]{0,1:T(8,128)(4,1)S(1)}, u32[]{:S(2)}) copy-start(pred[1024,1024]{0,1:T(8,128)(4,1)S(1)} %compare_or_fusion) | copy-start | bytes 3145732
  157.7 93.7 %copy-start.44 = (f32[2048]{0:T(1024)}, f32[2048]{0:T(1024)S(1)}, u32[]{:S(2)}) copy-start(f32[2048]{0:T(1024)S(1)} %reshape.565) | copy-start | bytes 24580
  172.5 78.6 %copy-start.36 = (bf16[2,128,1024]{2,1,0:T(8,128)(2,1)}, bf16[2,128,1024]{2,1,0:T(8,128)(2,1)S(1)}, u32[]{:S(2)}) copy-start(bf16[2,128,1024]{2,1,0:T(8,128)(2,1)S(1)} %convolution_convert_fusion.8) | copy-start | bytes 1572868
  172.5 78.6 %copy-start.14 = (bf16[8,64,1408]{2,1,0:T(8,128)(2,1)}, bf16[8,64,1408]{2,1,0:T(8,128)(2,1)S(1)}, u32[]{:S(2)}) copy-start(bf16[8,64,1408]{2,1,0:T(8,128)(2,1)S(1)} %all-to-all-done) | copy-start | bytes 4325380
  175.8 75.3 %copy-start.7 = (bf16[1,128,2048]{2,1,0:T(8,128)(2,1)S(1)}, bf16[1,128,2048]{2,1,0:T(8,128)(2,1)}, u32[]{:S(2)}) copy-start(bf16[1,128,2048]{2,1,0:T(8,128)(2,1)} %param.18) | copy-start | bytes 1572868
  251.1 76.4 %copy-start.39 = (bf16[9,2048]{1,0:T(8,128)(2,1)S(1)}, bf16[9,2048]{1,0:T(8,128)(2,1)}, u32[]{:S(2)}) copy-start(bf16[9,2048]{1,0:T(8,128)(2,1)} %copy-done.38) | copy-start | bytes 110596
  251.4 79.6 %copy-start.68 = (f32[128]{0:T(128)}, f32[128]{0:T(128)S(1)}, u32[]{:S(2)}) copy-start(f32[128]{0:T(128)S(1)} %get-tuple-element.93) | copy-start | bytes 1540
  253.3 77.7 %copy-start.60 = (pred[8]{0:T(512)(128)(4,1)S(1)}, pred[8]{0:T(512)(128)(4,1)}, u32[]{:S(2)}) copy-start(pred[8]{0:T(512)(128)(4,1)} %iota_compare_fusion.1) | copy-start | bytes 28
  253.3 77.8 %copy-start.52 = (pred[8,128]{1,0:T(8,128)(4,1)S(1)}, pred[8,128]{1,0:T(8,128)(4,1)}, u32[]{:S(2)}) copy-start(pred[8,128]{1,0:T(8,128)(4,1)} %fusion.39) | copy-start | bytes 3076
  386.9 178.8 %reduce-scatter.5.cloned.1.call-start = ((), (), s32[]{:S(2)}) async-start(), calls=%async_computation.6 | async-start | bytes 7208960 | tf_op jit(solution)/shard_map/reduce_scatter | solution.py:1204
  401.8 211.1 %reduce-scatter.9.cloned.1.call-start = ((), (), s32[]{:S(2)}) async-start(), calls=%async_computation.8 | async-start | bytes 7208960 | tf_op jit(solution)/shard_map/reduce_scatter | solution.py:1204
  419.4 25.9 %slice-start.2 = ((s8[5767168]{0:T(1024)(128)(4,1)}), s8[1572864]{0:T(1024)(128)(4,1)S(1)}, s32[]{:S(2)}) async-start(s8[5767168]{0:T(1024)(128)(4,1)} %bitcast.182), calls=%async_computation.15 | async-start | bytes 3145728
  464.3 304.1 %reduce-scatter.11.cloned.1.call-start = ((), (), s32[]{:S(2)}) async-start(), calls=%async_computation.9 | async-start | bytes 14417920 | tf_op jit(solution)/shard_map/reduce_scatter | solution.py:1204
  504.2 58.3 %copy-start.5 = (f32[128,2048]{1,0:T(8,128)S(1)}, f32[128,2048]{1,0:T(8,128)}, u32[]{:S(2)}) copy-start(f32[128,2048]{1,0:T(8,128)} %copy-done.4) | copy-start | bytes 3145732
  504.2 58.3 %copy-start.45 = (f32[2048]{0:T(1024)S(1)}, f32[2048]{0:T(1024)}, u32[]{:S(2)}) copy-start(f32[2048]{0:T(1024)} %copy-done.44) | copy-start | bytes 24580
  504.2 58.3 %copy-start.55 = (f32[128]{0:T(128)S(1)}, f32[128]{0:T(128)}, u32[]{:S(2)}) copy-start(f32[128]{0:T(128)} %copy-done.54) | copy-start | bytes 1540
  507.7 55.4 %copy-start.69 = (f32[128]{0:T(128)S(1)}, f32[128]{0:T(128)}, u32[]{:S(2)}) copy-start(f32[128]{0:T(128)} %copy-done.68) | copy-start | bytes 1540
  612.9 43.2 %all-to-all-start.1 = ((bf16[8,64,1408]{2,1,0:T(8,128)(2,1)}), bf16[8,64,1408]{2,1,0:T(8,128)(2,1)}, u32[]{:S(2)}, u32[]{:S(2)}) async-start(bf16[8,64,1408]{2,1,0:T(8,128)(2,1)} %bitcast.207), calls=%async_computation.4 | async-start | bytes 2883584 | tf_op jit(solution)/shard_map/all_to_all | solution.py:1208
  683.0 80.4 %copy-start.8 = (bf16[1,128,2048]{2,1,0:T(8,128)(2,1)S(1)}, bf16[1,128,2048]{2,1,0:T(8,128)(2,1)}, u32[]{:S(2)}) copy-start(bf16[1,128,2048]{2,1,0:T(8,128)(2,1)} %param.18) | copy-start | bytes 1572868
  (65 other events, 351.8 us)
Sparse Core Ops, SparseCore 0:
  9.6 107.4 all-gather.8
  119.2 112.2 all-gather.6
  233.1 65.9 all-gather.10
  387.1 87.9 reduce-scatter.6
  477.6 54.6 reduce-scatter.4
  535.2 54.8 reduce-scatter.8
  592.9 92.1 reduce-scatter.10

commit v5 on v4

--- a/solution.py
+++ b/solution.py
@@ -1132,6 +1132,269 @@
     )(part, weight, pair, plain, small)
 
 
+SPAN = 256
+
+
+def flat_dot(left, right):
+    return lax.dot_general(left, right, (((1,), (0,)), ((), ())), preferred_element_type=jnp.float32)
+
+
+def turned_dot(left, right):
+    return lax.dot_general(left, right, (((1,), (1,)), ((), ())), preferred_element_type=jnp.float32)
+
+
+def span_of(index, size=SPAN):
+    return pl.ds(pl.multiple_of(index * size, size), size)
+
+
+def scaled_rows(values):
+    return values * lax.rsqrt(jnp.mean(values * values, axis=-1, keepdims=True) + EPSILON)
+
+
+def attend_kernel(
+    inputs,
+    gain,
+    weight,
+    bias,
+    cosine,
+    sine,
+    columns,
+    lines,
+    out_weight,
+    normed,
+    queries,
+    keys,
+    values,
+    attended,
+    log_totals,
+    part,
+):
+    rows = inputs.shape[0]
+    low = jnp.bfloat16
+    heads = queries.shape[1] // HD
+
+    @pl.loop(0, rows // SPAN)
+    def project(index):
+        here = span_of(index)
+        unit = scaled_rows(inputs[here, :].astype(jnp.float32)) * gain[...]
+        normed[here, :] = unit.astype(low)
+        projected = flat_dot(normed[here, :], weight[...]) + bias[...]
+        turn, tilt = cosine[here, :], sine[here, :]
+        for head in range(heads):
+            own = slice(head * HD, (head + 1) * HD)
+            query = projected[:, own]
+            query = query * turn + pltpu.roll(query, HD // 2, 1) * tilt
+            queries[here, own] = (query * HD ** (-0.5)).astype(low)
+            key = projected[:, (heads + head) * HD : (heads + head + 1) * HD]
+            keys[here, own] = (key * turn + pltpu.roll(key, HD // 2, 1) * tilt).astype(low)
+            values[here, own] = projected[
+                :, (2 * heads + head) * HD : (2 * heads + head + 1) * HD
+            ].astype(low)
+
+    @pl.loop(0, rows // SPAN)
+    def attend(index):
+        here = span_of(index)
+        position, segment = columns[here, 0:1], columns[here, 1:2]
+        allowed = (lines[1:2, :] == segment) & (lines[0:1, :] <= position)
+        allowed = allowed | (lines[0:1, :] == position)
+        for head in range(heads):
+            own = slice(head * HD, (head + 1) * HD)
+            scores = turned_dot(queries[here, own], keys[:, own])
+            scores = jnp.where(allowed, scores, -1e30)
+            highest = jnp.max(scores, axis=1, keepdims=True)
+            weights = jnp.exp(scores - highest)
+            sums = jnp.sum(weights, axis=1, keepdims=True)
+            log_totals[here, head : head + 1] = highest + jnp.log(sums)
+            probs = (weights * (1.0 / sums)).astype(low)
+            attended[here, own] = flat_dot(probs, values[:, own]).astype(low)
+        part[here, :] = flat_dot(attended[here, :], out_weight[...]).astype(low)
+
+
+def attend(inputs, gain, weight, bias, cosine, sine, columns, lines, out_weight):
+    rows, width = inputs.shape
+    wide = out_weight.shape[0]
+    low = jnp.bfloat16
+    shape = jax.ShapeDtypeStruct
+    return pl.pallas_call(
+        attend_kernel,
+        out_shape=[shape((rows, width), low)]
+        + [shape((rows, wide), low)] * 4
+        + [shape((rows, wide // HD), jnp.float32), shape((rows, width), low)],
+        in_specs=[VMEM] * 9,
+        out_specs=[VMEM] * 7,
+        compiler_params=pltpu.CompilerParams(vmem_limit_bytes=40 * 2**20),
+        cost_estimate=pl.CostEstimate(
+            flops=2 * rows * width * 4 * wide + 4 * rows * rows * wide,
+            bytes_accessed=20 * 2**20,
+            transcendentals=rows * rows * wide // HD,
+        ),
+        name="attend",
+    )(inputs, gain, weight, bias, cosine, sine, columns, lines, out_weight)
+
+
+def attend_back_kernel(
+    branch,
+    out_weight,
+    queries,
+    keys,
+    values,
+    attended,
+    totals,
+    cosine,
+    sine,
+    columns,
+    lines,
+    inputs,
+    normed,
+    weight,
+    part,
+    grad_weight,
+    grad_out,
+    grad_bias,
+    grad_gain,
+    grads,
+    grad_attended,
+    grad_keys,
+    grad_values,
+    gain_sum,
+):
+    rows, width = branch.shape
+    low = jnp.bfloat16
+    full = jnp.float32
+    wide = queries.shape[1]
+    heads = wide // HD
+
+    @pl.loop(0, rows // SPAN)
+    def into_heads(index):
+        here = span_of(index)
+        grad_attended[here, :] = turned_dot(branch[here, :], out_weight[...]).astype(low)
+
+    for head in range(heads):
+        own = slice(head * HD, (head + 1) * HD)
+        grad_keys[...] = jnp.zeros_like(grad_keys)
+        grad_values[...] = jnp.zeros_like(grad_values)
+
+        @pl.loop(0, rows // SPAN)
+        def scores_back(index):
+            here = span_of(index)
+            position, segment = lines[0:1, here], lines[1:2, here]
+            allowed = (columns[:, 1:2] == segment) & (columns[:, 0:1] <= position)
+            allowed = allowed | (columns[:, 0:1] == position)
+            query, grad = queries[here, own], grad_attended[here, own]
+            scores = jnp.where(allowed, turned_dot(keys[:, own], query), -1e30)
+            probs = jnp.exp(scores - totals[head : head + 1, here])
+            grad_probs = turned_dot(values[:, own], grad)
+            delta = jnp.sum(probs * grad_probs, axis=0, keepdims=True)
+            grad_scores = (probs * (grad_probs - delta)).astype(low)
+            grad_keys[...] += flat_dot(grad_scores, query)
+            grad_values[...] += flat_dot(probs.astype(low), grad)
+            grad_query = flat_dot(grad_scores.T, keys[:, own]) * HD ** (-0.5)
+            grads[here, own] = (
+                grad_query * cosine[here, :] + pltpu.roll(grad_query * sine[here, :], HD // 2, 1)
+            ).astype(low)
+
+        @pl.loop(0, rows // SPAN)
+        def keys_back(index):
+            here = span_of(index)
+            grad_key = grad_keys[here, :]
+            grads[here, (heads + head) * HD : (heads + head + 1) * HD] = (
+                grad_key * cosine[here, :] + pltpu.roll(grad_key * sine[here, :], HD // 2, 1)
+            ).astype(low)
+            grads[here, (2 * heads + head) * HD : (2 * heads + head + 1) * HD] = grad_values[
+                here, :
+            ].astype(low)
+
+    gain_sum[...] = jnp.zeros_like(gain_sum)
+    grad_bias[...] = jnp.zeros_like(grad_bias)
+
+    @pl.loop(0, rows // SPAN)
+    def project_back(index):
+        here = span_of(index)
+        grad_rows = turned_dot(grads[here, :], weight[...])
+        part[here, :] = grad_rows.astype(low)
+        unit = scaled_rows(inputs[here, :].astype(full))
+        gain_sum[...] += jnp.sum(grad_rows * unit, axis=0, keepdims=True)
+        grad_bias[...] += jnp.sum(grads[here, :].astype(full), axis=0, keepdims=True)
+
+    grad_gain[...] = gain_sum[...]
+
+    @pl.loop(0, width // SPAN)
+    def weight_back(index):
+        here = span_of(index)
+        grad_weight[here, :] = flat_dot(normed[:, here].T, grads[...]).astype(low)
+
+    attended_turned = attended[...].T
+
+    @pl.loop(0, width // (2 * SPAN))
+    def out_back(index):
+        here = span_of(index, 2 * SPAN)
+        grad_out[:, here] = flat_dot(attended_turned, branch[:, here]).astype(low)
+
+
+def attend_back(
+    branch,
+    out_weight,
+    queries,
+    keys,
+    values,
+    attended,
+    totals,
+    cosine,
+    sine,
+    columns,
+    lines,
+    inputs,
+    normed,
+    weight,
+):
+    rows, width = branch.shape
+    wide = out_weight.shape[0]
+    low = jnp.bfloat16
+    full = jnp.float32
+    shape = jax.ShapeDtypeStruct
+    return pl.pallas_call(
+        attend_back_kernel,
+        out_shape=[
+            shape((rows, width), low),
+            shape(weight.shape, low),
+            shape((wide, width), low),
+            shape((1, 3 * wide), full),
+            shape((1, width), full),
+        ],
+        in_specs=[VMEM] * 14,
+        out_specs=[VMEM] * 5,
+        scratch_shapes=[
+            pltpu.VMEM((rows, 3 * wide), low),
+            pltpu.VMEM((rows, wide), low),
+            pltpu.VMEM((rows, HD), full),
+            pltpu.VMEM((rows, HD), full),
+            pltpu.VMEM((1, width), full),
+        ],
+        compiler_params=pltpu.CompilerParams(vmem_limit_bytes=56 * 2**20),
+        cost_estimate=pl.CostEstimate(
+            flops=2 * rows * width * 8 * wide + 10 * rows * rows * wide,
+            bytes_accessed=35 * 2**20,
+            transcendentals=rows * rows * wide // HD,
+        ),
+        name="attend_back",
+    )(
+        branch,
+        out_weight,
+        queries,
+        keys,
+        values,
+        attended,
+        totals,
+        cosine,
+        sine,
+        columns,
+        lines,
+        inputs,
+        normed,
+        weight,
+    )
+
+
 def deal_kernel(pieces, weight, dealt):
     ctx_count = dealt.shape[0]
     width = dealt.shape[2] // pieces
@@ -1247,6 +1510,7 @@
     ctx_rank = lax.axis_index("ctx")
     dev_count = ctx_count * fsdp_count
     row_len = ctx_count * tokens_dev
+    early = width * 3 // 8
     head_count = width // HD
     shard = qkv_weight.shape[0]
     expert_count = router_weight.shape[1]
@@ -1304,6 +1568,7 @@
     routed_here = jnp.any(numbers[:, : number_count - 1] == ctx_rank, axis=1).reshape(row_len)
 
     shared_in_weight, numbers = lax.optimization_barrier((shared_in_weight, numbers))
+    early_upstream = over("ctx", out_grad.reshape(tokens_dev, width)[:, :early])
     inner_parts = deal_columns(shared_in_weight, ctx_count, 2 * fsdp_count)
     expert_inner = over("fsdp", expert_in_weight[0])
     expert_outer = over("fsdp", expert_out_weight[0])
@@ -1316,38 +1581,32 @@
     offsets = jnp.arange(block_len, dtype=jnp.int32)
     positions = (block_pairs[:, None] * block_len + offsets[None, :]).reshape(row_len)
     inputs = own_inputs.astype(full)
-    row_inputs = row_inputs.reshape(row_len, width).astype(full)
-    row_upstream = over("ctx", out_grad.reshape(tokens_dev, width))
-    row_normed = rms_scale(row_inputs, gain_attn).astype(low)
-    projected = matmul_low(row_normed, qkv_c) + bias_c.astype(full)
-    query_pre = projected[:, : 2 * HD].reshape(row_len, 2, HD)
-    key_pre = projected[:, 2 * HD : 4 * HD].reshape(row_len, 2, HD)
-
-    def place_heads(query_in, key_in):
-        return (rotate(query_in, positions) * HD ** (-0.5), rotate(key_in, positions))
-
-    query_rot, key_rot = place_heads(query_pre, key_pre)
-    queries = query_rot.astype(low)
-    keys = key_rot.astype(low)
-    values = projected[:, 4 * HD :].reshape(row_len, 2, HD).astype(low)
-    seg_real = row_seg.astype(full)
-    allowed = visible(positions, seg_real, positions, seg_real)
-
-    def score_part():
-        scores = jnp.einsum("qhd,khd->hqk", queries, keys, preferred_element_type=full)
-        return jnp.where(allowed[None], scores, -1e30)
-
-    scores = score_part()
-    highest = jnp.max(scores, axis=-1, keepdims=True)
-    log_total = highest + jnp.log(jnp.sum(jnp.exp(scores - highest), axis=-1, keepdims=True))
-    probs = jnp.exp(scores - log_total)
-    attended_row = (
-        jnp.einsum("hqk,khd->qhd", probs.astype(low), values, preferred_element_type=full)
-        .astype(low)
-        .reshape(row_len, 2 * HD)
-    )
-    attended_row, inner_parts = lax.optimization_barrier((attended_row, inner_parts))
-    branch_part = matmul_low(attended_row, out_c).astype(low)
+    row_inputs = row_inputs.reshape(row_len, width)
+    half_len = HD // 2
+    frequency = THETA ** (-jnp.arange(half_len, dtype=full) / half_len)
+    places = positions.astype(full)
+    angles = places[:, None] * frequency[None, :]
+    cosine, sine = jnp.cos(angles), jnp.sin(angles)
+    cosine = jnp.concatenate([cosine, cosine], axis=1)
+    sine = jnp.concatenate([-sine, sine], axis=1)
+    key_seg = row_seg.astype(full)
+    query_seg = jnp.where(row_seg >= 0, key_seg, -2.0)
+    query_marks = jnp.stack([places, query_seg])
+    key_marks = jnp.stack([places, key_seg])
+    row_normed, queries, keys, values, attended_row, log_totals, branch_part = attend(
+        row_inputs,
+        gain_attn[None, :],
+        qkv_c,
+        bias_c.astype(full)[None, :],
+        cosine,
+        sine,
+        query_marks.T,
+        key_marks,
+        out_c,
+    )
+    branch_part, inner_parts, early_upstream = lax.optimization_barrier(
+        (branch_part, inner_parts, early_upstream)
+    )
     branch = line_scatter(ctx_count, 2, branch_part.reshape(ctx_count, tokens_dev, width))
     middle = inputs + branch
     normed_ffn = rms_scale(middle, gain_ffn).astype(low)
@@ -1360,6 +1619,8 @@
         shared_out_weight,
     )
     row_ffn = row_ffn.reshape(row_len, width)
+    row_ffn, late_grad = lax.optimization_barrier((row_ffn, out_grad))
+    late_upstream = over("ctx", late_grad.reshape(tokens_dev, width)[:, early:])
     inner_c = inner_c.reshape(width, 2 * shared_width)
     outer_c = outer_c.reshape(shared_width, width)
     row_logits = dot_transposed(row_ffn, router_gate)
@@ -1370,14 +1631,14 @@
     )
     row_gate = jax.nn.sigmoid(row_logits[:, expert_count])
     expert_gu = matmul_low(row_ffn, expert_inner)
-    row_upstream, expert_gu = lax.optimization_barrier((row_upstream, expert_gu))
     expert_hidden = swiglu_mix(expert_gu, expert_width).astype(low)
     expert_result = matmul_low(expert_hidden, expert_outer).astype(low).astype(full)
     row_shared, expert_result = lax.optimization_barrier((row_ffn, expert_result))
     shared_gu = matmul_low(row_shared, inner_c)
     shared_hidden = swiglu_mix(shared_gu, shared_width).astype(low)
     shared_out = matmul_low(shared_hidden, outer_c)
-    upstream_row = row_upstream.astype(full)
+    shared_out, late_upstream = lax.optimization_barrier((shared_out, late_upstream))
+    upstream_row = jnp.concatenate([early_upstream, late_upstream], axis=1).astype(full)
     out_part = (row_gate[:, None] * shared_out + here[:, None] * expert_result).astype(low)
     gate_dot = jnp.sum(upstream_row * shared_out, axis=1)
     expert_dot = jnp.where(routed_here, jnp.sum(upstream_row * expert_result, axis=1), 0.0)
@@ -1447,38 +1708,28 @@
     sum_inner = collect_columns(
         exchange(sum_inner_c.reshape(ctx_count, shard, 2 * shared_width)), 2 * fsdp_count
     )
-    grad_attended = dot_transposed(row_branch, out_c).astype(low).reshape(row_len, 2, HD)
-    grad_out_c = transposed_dot(attended_row, row_branch).astype(low).reshape(2, HD, width)
+    grad_attn_part, grad_qkv_c, grad_out_c, grad_bias_c, grad_gain_attn = attend_back(
+        row_branch,
+        out_c,
+        queries,
+        keys,
+        values,
+        attended_row,
+        log_totals.T,
+        cosine,
+        sine,
+        key_marks.T,
+        query_marks,
+        row_inputs,
+        row_normed,
+        qkv_c,
+    )
+    grad_out_c = grad_out_c.reshape(2, HD, width)
     padded_out = jnp.concatenate(
         [jnp.where(side == p, grad_out_c, jnp.zeros_like(grad_out_c)) for p in range(2)], axis=0
     )
-
-    grad_probs = jnp.einsum("qhd,khd->hqk", grad_attended, values, preferred_element_type=full)
-    weights = jnp.exp(score_part() - log_total)
-    offset_term = jnp.sum(weights * grad_probs, axis=-1, keepdims=True)
-    grad_scores = (weights * (grad_probs - offset_term)).astype(low)
-    grad_queries = jnp.einsum("hqk,khd->qhd", grad_scores, keys, preferred_element_type=full)
-    grad_keys = jnp.einsum("hqk,qhd->khd", grad_scores, queries, preferred_element_type=full)
-    grad_values = jnp.einsum(
-        "hqk,qhd->khd", weights.astype(low), grad_attended, preferred_element_type=full
-    )
-    unused_rot, rotate_pull = jax.vjp(place_heads, query_pre, key_pre)
-    grad_query_pre, grad_key_pre = rotate_pull((grad_queries, grad_keys))
-    grad_projected = jnp.concatenate(
-        [
-            grad_query_pre.reshape(row_len, 2 * HD),
-            grad_key_pre.reshape(row_len, 2 * HD),
-            grad_values.reshape(row_len, 2 * HD),
-        ],
-        axis=1,
-    ).astype(low)
-    grad_projected, sum_inner = lax.optimization_barrier((grad_projected, sum_inner))
-    grad_attn_part = dot_transposed(grad_projected, qkv_c)
-    row_scaled = row_inputs * lax.rsqrt(
-        jnp.mean(row_inputs * row_inputs, axis=-1, keepdims=True) + EPSILON
-    )
-    grad_gain_attn = jnp.sum(grad_attn_part * row_scaled, axis=0)
-    grad_bias_c = jnp.sum(grad_projected.astype(full), axis=0).reshape(3, 1, 2, HD)
+    grad_attn_part, sum_inner = lax.optimization_barrier((grad_attn_part, sum_inner))
+    grad_bias_c = grad_bias_c.reshape(3, 1, 2, HD)
     mine = (jnp.arange(ctx_count) == ctx_rank)[None, :, None, None]
     places_of = [head_order.index(h) for h in range(head_count)]
     grad_bias = (
@@ -1498,11 +1749,10 @@
         axis=1,
     )
     small_grads = jnp.pad(small_grads, ((0, 0), (0, 8 * HD - small_count)))
-    grad_qkv_c = transposed_dot(row_normed, grad_projected).astype(low)
     grad_normed_attn, sum_qkv_c, sum_out, sum_outer, sums = closing(
         ctx_count,
         5,
-        grad_attn_part.astype(low).reshape(ctx_count, tokens_dev, width),
+        grad_attn_part.reshape(ctx_count, tokens_dev, width),
         grad_qkv_c.reshape(fsdp_count, ctx_count * shard, 6 * HD),
         padded_out,
         grad_outer.reshape(fsdp_count, shared_shard, width),

time: 790 us -> 740 us (0.937)
  matrix products: 201 us -> 151 us
  other arithmetic: 65 us -> 49.8 us
  Pallas kernels: 427 us -> 435 us
    pallas_call x0 -> x2, Pallas kernels: none -> 52.5 us  [the longest x1 34.9 us: attend_back(): pl.pallas_call(attend_back_kernel, out_shape=[shape((rows, width), low),...]
    pallas_call x1, Pallas kernels: 75.3 us -> 49.1 us  [line_scatter(): pl.pallas_call(functools.partial(line_scatter_kernel, half - 1), out_shap...]
    pallas_call x2, Pallas kernels: 121 us -> 101 us  [line_gather(): pl.pallas_call(functools.partial(gather_kernel, ctx_count // 2 - 1, count...]
    dot_general x6 -> x0, matrix products: 20.2 us -> none  [the longest x1 6.3 us: split_plan(): jnp.einsum('hqk,qhd->khd', weights.astype(low), grad_attended, preferred_...]
    dot_general x8 -> x6, matrix products: 76.2 us -> 62.5 us  [dot_transposed(): lax.dot_general(left, right, (((1,), (1,)), ((), ())), preferred_element_...]
    dot_general x7 -> x5, matrix products: 53.4 us -> 44.1 us  [transposed_dot(): lax.dot_general(left, right, (((0,), (0,)), ((), ())), preferred_element_...]
    dot_general x7 -> x5, matrix products: 51.6 us -> 44.5 us  [matmul_low(): return jnp.dot(left, right, preferred_element_type=jnp.float32)]
    unnamed x171 -> x149, local copies, waits for them, and re-layouts: 32.1 us -> 30.7 us
  transfers between devices with their start and end apart: 9 -> 10, of which waited for: 0 -> 1; matrix products, arithmetic and copies ran while one was open for 35% -> 29% of each run, Pallas kernels for 55% -> 60%
where the time goes in v5:
time: 740 us; the launch traced here: 728 us
  Pallas kernels  435 us (59%)
  matrix products  151 us (20%)
  local copies, waits for them, and re-layouts  56 us (8%)
  other arithmetic  49.8 us (7%)
  between operations  15.3 us (2%)
  starting transfers between devices  15 us (2%)
    pallas_call x2, Pallas kernels, line_gather(): pl.pallas_call(functools.partial(gather_kernel, ctx_count // 2 - 1, count...  101 us
    pallas_call x1, Pallas kernels, opening(): pl.pallas_call(functools.partial(opening_kernel, ctx_count), out_shape=[o...  95.2 us
    pallas_call x1, Pallas kernels, closing(): pl.pallas_call(functools.partial(closing_kernel, ctx_count), out_shape=[j...  73.4 us
    dot_general x6, matrix products, dot_transposed(): lax.dot_general(left, right, (((1,), (1,)), ((), ())), preferred_element_...  62.5 us
    pallas_call x1, Pallas kernels, line_scatter(): pl.pallas_call(functools.partial(scatter_kernel, ctx_count), out_shape=[t...  54.5 us
    pallas_call x1, Pallas kernels, line_scatter(): pl.pallas_call(functools.partial(line_scatter_kernel, half - 1), out_shap...  49.1 us
    dot_general x5, matrix products, matmul_low(): return jnp.dot(left, right, preferred_element_type=jnp.float32)  44.5 us
    dot_general x5, matrix products, transposed_dot(): lax.dot_general(left, right, (((0,), (0,)), ((), ())), preferred_element_...  44.1 us
  transfers between devices with their start and end apart: 10, of which 1 were waited for; matrix products, arithmetic and copies ran while one was open for 29% of the time, Pallas kernels for 60%

profile of v5, /device:TPU:0, one launch (start us, length us, event | category | flops | bytes accessed | tf_op | source)
XLA Modules:
  0.0 728.0 jit_solution(14833846927262939285)
XLA Ops:
  15.9 95.2 %opening.1 = (bf16[8,128,2048]{2,1,0:T(8,128)(2,1)}, bf16[4,8,64,768]{3,2,1,0:T(8,128)(2,1)}, bf16[4,2,64,2048]{3,2,1,0:T(8,128)(2,1)}, bf16[4,8,16,128]{3,2,1,0:T(8,128)(2,1)}, s32[8,8,128]{2,1,0:T(8,128)}) custom-call(bf16[128,2048]{1,0:T(8,128)(2,1)} %bitcast.151, bf16[8,64,768]{2,1,0:T(8,128)(2,1)} %reshape.347.qkv_own, bf16[64,2048]{1,0:T(8,128)(2,1)} %out_own.1, ...), custom_call_target="tpu_custom_call" | custom-call | tf_op jit(solution)/shard_map/opening/pallas_call | solution.py:930
  114.2 10.9 %all-to-all-start = ((bf16[8,64,1408]{2,1,0:T(8,128)(2,1)}), bf16[8,64,1408]{2,1,0:T(8,128)(2,1)S(1)}, u32[]{:S(2)}, u32[]{:S(2)}) async-start(bf16[8,64,1408]{2,1,0:T(8,128)(2,1)} %deal_columns.1), calls=%async_computation | async-start | bytes 2883584 | tf_op jit(solution)/shard_map/all_to_all | solution.py:1471
  131.6 17.6 %attend.1 = (bf16[1024,2048]{1,0:T(8,128)(2,1)S(1)}, bf16[1024,256]{1,0:T(8,128)(2,1)S(1)}, bf16[1024,256]{1,0:T(8,128)(2,1)S(1)}, bf16[1024,256]{1,0:T(8,128)(2...) custom-call(bf16[1024,2048]{1,0:T(8,128)(2,1)} %bitcast.193, ...), custom_call_target="tpu_custom_call" | custom-call | flops 5368709120 | bytes 20971520 | tf_op jit(solution)/shard_map/attend/pallas_call | solution.py:1218
  162.5 49.1 %line_scatter.2 = f32[128,2048]{1,0:T(8,128)S(1)} custom-call(bf16[8,128,2048]{2,1,0:T(8,128)(2,1)S(1)} %bitcast.146), custom_call_target="tpu_custom_call" | custom-call | tf_op jit(solution)/shard_map/line_scatter/pallas_call | solution.py:668
  213.8 53.8 %line_gather.2 = (bf16[8,128,2048]{2,1,0:T(8,128)(2,1)}, bf16[4,512,1408]{2,1,0:T(8,128)(2,1)}, bf16[4,176,2048]{2,1,0:T(8,128)(2,1)}) custom-call(bf16[128,2048]{1,0:T(8,128)(2,1)} %multiply_convert_fusion.4.refs_0_, bf16[512,1408]{1,0:T(8,128)(2,1)} %bitcast.157, bf16[176,2048]{1,0:T(8,128)(2,1)} %refs_2_.1), custom_call_target="tpu_custom_call" | custom-call | tf_op jit(solution)/shard_map/line_gather/pallas_call | solution.py:799
  272.1 17.2 %fusion.2 = f32[1024,2816]{1,0:T(8,128)S(1)} fusion(bf16[1024,2048]{1,0:T(8,128)(2,1)} %bitcast.153, bf16[1,2048,2816]{2,1,0:T(8,128)(2,1)} %all-gather.11.cloned.1.call-done), kind=kOutput, calls=%fused_computation.4 | convolution fusion | flops 11811160064 | bytes 27262976 | tf_op jit(solution)/shard_map/dot_general | solution.py:49
  296.4 11.7 %convert_convert_fusion = f32[1024,2048]{1,0:T(8,128)} fusion(bf16[1024,1408]{1,0:T(8,128)(2,1)} %multiply_convert_fusion.2, bf16[1,1408,2048]{2,1,0:T(8,128)(2,1)} %all-gather.13.cloned.1.call-done), kind=kOutput, calls=%fused_computation.29 | convolution fusion | flops 5909774336 | bytes 17039360 | tf_op jit(solution)/shard_map/dot_general | solution.py:49
  308.1 9.2 %fusion.56 = f32[1024,1408]{1,0:T(8,128)S(1)} fusion(bf16[1024,2048]{1,0:T(8,128)(2,1)S(1)} %bitcast.154, bf16[2048,1408]{1,0:T(8,128)(2,1)} %bitcast.191), kind=kOutput, calls=%fused_computation.145 | convolution fusion | flops 5905580032 | bytes 15728640 | tf_op jit(solution)/shard_map/dot_general | solution.py:49
  321.7 5.9 fusion.57
  327.6 10.5 %multiply_reduce_fusion.1 = (f32[1024]{0:T(1024)}, f32[1024]{0:T(1024)}, bf16[1024,2048]{1,0:T(8,128)(2,1)}) fusion(f32[1024,2048]{1,0:T(8,128)} %fusion.57, bf16[1024,1280]{1,0:T(8,128)(2,1)} %all-gather.9.cloned.1.call-done, bf16[1024,768]{1,0:T(8,128)(2,1)S(1)} %copy-done.22, f32[1024,2048]{1,0:T(8,128)} %convert_convert_fusion, ...), kind=kLoop, calls=%fused_computation.10 | loop fusion | flops 25163776 | bytes 25182208 | tf_op jit(solution)/shard_map/reduce_sum | solution.py:1643
  344.6 8.3 %convolution_convert_fusion.1 = bf16[1408,2048]{1,0:T(8,128)(2,1)} fusion(bf16[1024,1408]{1,0:T(8,128)(2,1)S(1)} %copy-done.27, f32[1024,2048]{1,0:T(8,128)S(1)} %maximum_convert_fusion, f32[1024]{0:T(1024)S(1)} %bitcast_select_fusion.2), kind=kOutput, calls=%fused_computation.15 | convolution fusion | flops 5912657920 | bytes 17043456 | tf_op jit(solution)/shard_map/dot_general | solution.py:1475
  353.0 17.6 %fusion.24 = (f32[1024,1408]{1,0:T(8,128)}, f32[1024,1408]{1,0:T(8,128)}) fusion(f32[1024,2816]{1,0:T(8,128)} %copy-done.13, bf16[1,1408,2048]{2,1,0:T(8,128)(2,1)} %all-gather.13.cloned.1.call-done, f32[1024,2048]{1,0:T(8,128)} %copy-done.14, f32[1024]{0:T(1024)S(1)} %bitcast_select_fusion.2), kind=kOutput, calls=%fused_computation.62 | convolution fusion | flops 5927075840 | bytes 37228544 | tf_op jit(solution)/shard_map/dot_general | solution.py:1481
  370.7 7.5 %add_convert_fusion = bf16[1024,2816]{1,0:T(8,128)(2,1)} fusion(f32[1024,1408]{1,0:T(8,128)} %get-tuple-element.126, f32[1024,1408]{1,0:T(8,128)} %get-tuple-element.125), kind=kLoop, calls=%fused_computation.6 | loop fusion | flops 5767168 | bytes 17301504 | tf_op jit(solution)/shard_map/convert_element_type | solution.py:1654
  378.2 18.3 %fusion.11 = bf16[1024,2048]{1,0:T(8,128)(2,1)} fusion(bf16[1024,2816]{1,0:T(8,128)(2,1)} %add_convert_fusion, bf16[1,2048,2816]{2,1,0:T(8,128)(2,1)} %all-gather.11.cloned.1.call-done), kind=kOutput, calls=%fused_computation.30 | convolution fusion | flops 11813257216 | bytes 21495808 | tf_op jit(solution)/shard_map/dot_general | solution.py:1481
  396.5 9.8 %fusion.26 = (f32[1024,704]{1,0:T(8,128)S(1)}, f32[1024,704]{1,0:T(8,128)S(1)}) fusion(f32[1024,1408]{1,0:T(8,128)} %copy-done.18, bf16[704,2048]{1,0:T(8,128)(2,1)S(1)} %bitcast.196, f32[1024,2048]{1,0:T(8,128)} %copy-done.14, f32[1024]{0:T(1024)S(1)} %bitcast.182), kind=kOutput, calls=%fused_computation.66 | convolution fusion | flops 2965635072 | bytes 22810624 | tf_op jit(solution)/shard_map/dot_general | solution.py:1481
  409.0 9.0 %convolution_convert_fusion.2 = bf16[2048,1408]{1,0:T(8,128)(2,1)} fusion(bf16[1024,2048]{1,0:T(8,128)(2,1)S(1)} %bitcast.155, f32[1024,704]{1,0:T(8,128)S(1)} %get-tuple-element.129, f32[1024,704]{1,0:T(8,128)S(1)} %get-tuple-element.128), kind=kOutput, calls=%fused_computation.16 | convolution fusion | flops 5911347200 | bytes 15728640 | tf_op jit(solution)/shard_map/dot_general | solution.py:1475
  418.1 13.1 %add_convert_fusion.1 = bf16[1024,2048]{1,0:T(8,128)(2,1)} fusion(bf16[1024,2048]{1,0:T(8,128)(2,1)} %fusion.11, bf16[2048,1408]{1,0:T(8,128)(2,1)} %bitcast.192, f32[1024,704]{1,0:T(8,128)} %copy-done.70, f32[1024,704]{1,0:T(8,128)} %copy-done.69), kind=kOutput, calls=%fused_computation.11 | convolution fusion | flops 5914755072 | bytes 19922944 | tf_op jit(solution)/shard_map/dot_general | solution.py:1481
  431.2 9.4 %convolution_convert_fusion.3 = bf16[704,2048]{1,0:T(8,128)(2,1)} fusion(bf16[1024,704]{1,0:T(8,128)(2,1)S(1)} %copy-done.29, f32[1024,2048]{1,0:T(8,128)} %copy-done.14, f32[1024]{0:T(1024)S(1)} %bitcast.183), kind=kOutput, calls=%fused_computation.31 | convolution fusion | flops 2958426112 | bytes 12718080 | tf_op jit(solution)/shard_map/dot_general | solution.py:1475
  440.6 17.2 %convolution_convert_fusion = bf16[2048,2816]{1,0:T(8,128)(2,1)} fusion(bf16[1024,2048]{1,0:T(8,128)(2,1)S(1)} %bitcast.156, bf16[1024,2816]{1,0:T(8,128)(2,1)} %add_convert_fusion), kind=kOutput, calls=%fused_computation.7 | convolution fusion | flops 11816927232 | bytes 21495808 | tf_op jit(solution)/shard_map/dot_general | solution.py:1475
  463.7 54.5 %line_scatter.3 = (f32[128,2048]{1,0:T(8,128)S(1)}, f32[8,8,128]{2,1,0:T(8,128)S(1)}) custom-call(bf16[8,128,2048]{2,1,0:T(8,128)(2,1)S(1)} %bitcast.147, f32[8,8,128]{2,1,0:T(8,128)S(1)} %pad.34.small), custom_call_target="tpu_custom_call" | custom-call | tf_op jit(solution)/shard_map/line_scatter/pallas_call | solution.py:677
  523.1 47.3 %line_gather.3 = bf16[8,128,2048]{2,1,0:T(8,128)(2,1)} custom-call(bf16[128,2048]{1,0:T(8,128)(2,1)} %get-tuple-element.93.refs_0_), custom_call_target="tpu_custom_call" | custom-call | tf_op jit(solution)/shard_map/line_gather/pallas_call | solution.py:799
  574.3 34.9 %attend_back.1 = (bf16[1024,2048]{1,0:T(8,128)(2,1)}, bf16[2048,768]{1,0:T(8,128)(2,1)}, bf16[256,2048]{1,0:T(8,128)(2,1)}, f32[1,768]{1,0:T(1,128)}, f32[1,2048]{1,0:T(1,128)}) custom-call(bf16[1024,2048]{1,0:T(8,128)(2,1)} %bitcast.161, bf16[256,2048]{1,0:T(8,128)(2,1)} %copy-done.2, bf16[1024,256]{1,0:T(8,128)(2,1)} %copy-done.7, ...), custom_call_target="tpu_custom_call" | custom-call | flops 11274289152 | bytes 36700160 | tf_op jit(solution)/shard_map/attend_back/pallas_call | solution.py:1355
  630.6 73.4 %closing.1 = (f32[128,2048]{1,0:T(8,128)}, bf16[8,64,768]{2,1,0:T(8,128)(2,1)}, f32[64,2048]{1,0:T(8,128)}, f32[176,2048]{1,0:T(8,128)}, f32[8,128]{1,0:T(8,128)}) custom-call(bf16[8,128,2048]{2,1,0:T(8,128)(2,1)} %bitcast.160, bf16[4,512,768]{2,1,0:T(8,128)(2,1)} %bitcast.167, bf16[4,128,2048]{2,1,0:T(8,128)(2,1)} %pad_maximum_fusion.pair, ...), custom_call_target="tpu_custom_call" | custom-call | tf_op jit(solution)/shard_map/closing/pallas_call | solution.py:1102
  714.2 4.9 bitcast_convert_fusion
  (276 shorter events, 106.4 us)
Async XLA Ops:
  7.2 152.6 %all-gather.7.cloned.1.call-start = ((), (), s32[]{:S(2)}) async-start(), calls=%async_computation.6 | async-start | bytes 1769472 | tf_op jit(solution)/shard_map/all_gather | solution.py:1463
  9.0 263.1 %all-gather.11.cloned.1.call-start = ((), (), s32[]{:S(2)}) async-start(), calls=%async_computation.12 | async-start | bytes 14417920 | tf_op jit(solution)/shard_map/all_gather | solution.py:1463
  9.7 286.7 %all-gather.13.cloned.1.call-start = ((), (), s32[]{:S(2)}) async-start(), calls=%async_computation.13 | async-start | bytes 7208960 | tf_op jit(solution)/shard_map/all_gather | solution.py:1463
  14.5 111.0 %copy-start.68 = (s32[16]{0:T(128)S(1)}, s32[16]{0:T(128)}, u32[]{:S(2)}) copy-start(s32[16]{0:T(128)} %param.20) | copy-start | bytes 196
  114.2 45.6 %all-to-all-start = ((bf16[8,64,1408]{2,1,0:T(8,128)(2,1)}), bf16[8,64,1408]{2,1,0:T(8,128)(2,1)S(1)}, u32[]{:S(2)}, u32[]{:S(2)}) async-start(bf16[8,64,1408]{2,1,0:T(8,128)(2,1)} %deal_columns.1), calls=%async_computation | async-start | bytes 2883584 | tf_op jit(solution)/shard_map/all_to_all | solution.py:1471
  125.1 202.5 %all-gather.9.cloned.1.call-start = ((), (), s32[]{:S(2)}) async-start(), calls=%async_computation.7 | async-start | bytes 2949120 | tf_op jit(solution)/shard_map/all_gather | solution.py:1463
  126.9 85.0 %copy-start.36 = (f32[2048]{0:T(1024)}, f32[2048]{0:T(1024)S(1)}, u32[]{:S(2)}) copy-start(f32[2048]{0:T(1024)S(1)} %reshape.382) | copy-start | bytes 24580
  127.6 144.3 %copy-start.55 = (pred[8]{0:T(512)(128)(4,1)}, pred[8]{0:T(512)(128)(4,1)S(1)}, u32[]{:S(2)}) copy-start(pred[8]{0:T(512)(128)(4,1)S(1)} %iota_compare_fusion.1) | copy-start | bytes 28
  127.6 144.3 %copy-start.45 = (pred[8,128]{1,0:T(8,128)(4,1)}, pred[8,128]{1,0:T(8,128)(4,1)S(1)}, u32[]{:S(2)}) copy-start(pred[8,128]{1,0:T(8,128)(4,1)S(1)} %fusion.30) | copy-start | bytes 3076
  129.9 138.5 %copy-start.32 = (bf16[9,2048]{1,0:T(8,128)(2,1)}, bf16[9,2048]{1,0:T(8,128)(2,1)S(1)}, u32[]{:S(2)}) copy-start(bf16[9,2048]{1,0:T(8,128)(2,1)S(1)} %constant_dynamic-update-slice_fusion) | copy-start | bytes 110596
  131.6 80.0 %copy-start.15 = (bf16[1,128,2048]{2,1,0:T(8,128)(2,1)S(1)}, bf16[1,128,2048]{2,1,0:T(8,128)(2,1)}, u32[]{:S(2)}) copy-start(bf16[1,128,2048]{2,1,0:T(8,128)(2,1)} %param.18) | copy-start | bytes 1572868
  211.9 59.8 %copy-start.64 = (f32[128]{0:T(128)}, f32[128]{0:T(128)S(1)}, u32[]{:S(2)}) copy-start(f32[128]{0:T(128)S(1)} %get-tuple-element.123) | copy-start | bytes 1540
  211.9 59.8 %copy-start.47 = (f32[128]{0:T(128)}, f32[128]{0:T(128)S(1)}, u32[]{:S(2)}) copy-start(f32[128]{0:T(128)S(1)} %fusion.42) | copy-start | bytes 1540
  272.0 248.6 %reduce-scatter.7.cloned.1.call-start = ((), (), s32[]{:S(2)}) async-start(), calls=%async_computation.9 | async-start | bytes 4718592 | tf_op jit(solution)/shard_map/reduce_scatter | solution.py:1467
  338.2 185.0 %reduce-scatter.5.cloned.1.call-start = ((), (), s32[]{:S(2)}) async-start(), calls=%async_computation.8 | async-start | bytes 7208960 | tf_op jit(solution)/shard_map/reduce_scatter | solution.py:1467
  353.0 217.5 %reduce-scatter.9.cloned.1.call-start = ((), (), s32[]{:S(2)}) async-start(), calls=%async_computation.10 | async-start | bytes 7208960 | tf_op jit(solution)/shard_map/reduce_scatter | solution.py:1467
  418.0 296.2 %reduce-scatter.11.cloned.1.call-start = ((), (), s32[]{:S(2)}) async-start(), calls=%async_computation.11 | async-start | bytes 14417920 | tf_op jit(solution)/shard_map/reduce_scatter | solution.py:1467
  457.9 61.4 %copy-start.12 = (f32[128,2048]{1,0:T(8,128)S(1)}, f32[128,2048]{1,0:T(8,128)}, u32[]{:S(2)}) copy-start(f32[128,2048]{1,0:T(8,128)} %copy-done.11) | copy-start | bytes 3145732
  457.9 61.4 %copy-start.37 = (f32[2048]{0:T(1024)S(1)}, f32[2048]{0:T(1024)}, u32[]{:S(2)}) copy-start(f32[2048]{0:T(1024)} %copy-done.36) | copy-start | bytes 24580
  457.9 61.4 %copy-start.48 = (f32[128]{0:T(128)S(1)}, f32[128]{0:T(128)}, u32[]{:S(2)}) copy-start(f32[128]{0:T(128)} %copy-done.47) | copy-start | bytes 1540
  570.5 55.5 %all-to-all-start.1 = ((bf16[8,64,1408]{2,1,0:T(8,128)(2,1)}), bf16[8,64,1408]{2,1,0:T(8,128)(2,1)S(1)}, u32[]{:S(2)}, u32[]{:S(2)}) async-start(bf16[8,64,1408]{2,1,0:T(8,128)(2,1)} %bitcast.169), calls=%async_computation.4 | async-start | bytes 2883584 | tf_op jit(solution)/shard_map/all_to_all | solution.py:1471
  630.6 78.6 %copy-start.16 = (bf16[1,128,2048]{2,1,0:T(8,128)(2,1)S(1)}, bf16[1,128,2048]{2,1,0:T(8,128)(2,1)}, u32[]{:S(2)}) copy-start(bf16[1,128,2048]{2,1,0:T(8,128)(2,1)} %param.18) | copy-start | bytes 1572868
  630.6 80.7 %copy-start.49 = (f32[128]{0:T(128)S(1)}, f32[128]{0:T(128)}, u32[]{:S(2)}) copy-start(f32[128]{0:T(128)} %copy-done.47) | copy-start | bytes 1540
  630.6 80.7 %copy-start.52 = (f32[128]{0:T(128)S(1)}, f32[128]{0:T(128)}, u32[]{:S(2)}) copy-start(f32[128]{0:T(128)} %copy-done.51) | copy-start | bytes 1540
  (57 other events, 478.2 us)
Sparse Core Ops, SparseCore 0:
  10.8 62.0 all-gather.6
  74.4 78.1 all-gather.10
  154.1 53.2 all-gather.12
  272.1 53.8 all-gather.8
  338.3 87.3 reduce-scatter.6
  428.2 54.6 reduce-scatter.4
  486.0 54.8 reduce-scatter.8
  543.7 92.1 reduce-scatter.10

commit v6 on v5

--- a/solution.py
+++ b/solution.py
@@ -411,6 +411,21 @@
     )
 
 
+SPAN = 256
+
+
+def flat_dot(left, right):
+    return lax.dot_general(left, right, (((1,), (0,)), ((), ())), preferred_element_type=jnp.float32)
+
+
+def turned_dot(left, right):
+    return lax.dot_general(left, right, (((1,), (1,)), ((), ())), preferred_element_type=jnp.float32)
+
+
+def span_of(index, size=SPAN):
+    return pl.ds(pl.multiple_of(index * size, size), size)
+
+
 MESH = pl.DeviceIdType.MESH
 ANY = pl.BlockSpec(memory_space=pl.ANY)
 VMEM = pl.BlockSpec(memory_space=pltpu.VMEM)
@@ -630,7 +645,10 @@
             rise(goal).wait_send()
 
 
-def scatter_kernel(ctx_count, part, small, total, small_in, *refs):
+def scatter_kernel(
+    ctx_count, part, small, tokens, grads, total, small_in, weight_grad, *refs
+):
+    *refs, product, store_sem = refs
     greet_all(ctx_count)
     here = lax.axis_index("ctx")
     starts, waits = spread(
@@ -639,12 +657,30 @@
     for copy in starts:
         copy.start()
     small_in[here] = small[here]
-    for step in scatter_turns(ctx_count // 2 - 1, part, total, *refs[:9]):
-        pass
+    turns = scatter_turns(ctx_count // 2 - 1, part, total, *refs[:9])
+    next(turns)
+    pieces = ctx_count // 2
+    depth = tokens.shape[1] // pieces
+    stores = []
+    for piece in range(pieces):
+
+        @pl.loop(0, depth // SPAN)
+        def multiply(index):
+            here = pl.ds(pl.multiple_of(piece * depth + index * SPAN, SPAN), SPAN)
+            product[here, :] = flat_dot(tokens[:, here].T, grads[...]).astype(product.dtype)
+
+        rows = pl.ds(piece * depth, depth)
+        stores.append(
+            pltpu.make_async_copy(product.at[rows], weight_grad.at[rows], store_sem.at[piece])
+        )
+        stores[-1].start()
+        next(turns, None)
     for copy in waits:
         copy.wait_recv()
     for copy in starts:
         copy.wait_send()
+    for copy in stores:
+        copy.wait()
 
 
 def line_scatter_kernel(last, part, total, *refs):
@@ -654,7 +690,7 @@
         pass
 
 
-def line_scatter(ctx_count, call_id, part, small=None):
+def line_scatter(ctx_count, call_id, part, small=None, tokens=None, grads=None):
     rows, width = part.shape[1:]
     half = ctx_count // 2
     dma = pltpu.SemaphoreType.DMA((half,))
@@ -674,15 +710,26 @@
             compiler_params=params,
             name="line_scatter",
         )(part)
+    product = (tokens.shape[1], grads.shape[1])
+    params = pltpu.CompilerParams(
+        collective_id=call_id, has_side_effects=True, vmem_limit_bytes=56 * 2**20
+    )
     return pl.pallas_call(
         functools.partial(scatter_kernel, ctx_count),
-        out_shape=[total, jax.ShapeDtypeStruct(small.shape, small.dtype)],
-        in_specs=[VMEM] * 2,
-        out_specs=[VMEM] * 2,
-        scratch_shapes=[slots] * 4 + [dma] * 5 + [spread_dma] * 2,
+        out_shape=[
+            total,
+            jax.ShapeDtypeStruct(small.shape, small.dtype),
+            jax.ShapeDtypeStruct(product, part.dtype),
+        ],
+        in_specs=[VMEM] * 4,
+        out_specs=[VMEM] * 2 + [ANY],
+        scratch_shapes=[slots] * 4
+        + [dma] * 5
+        + [spread_dma] * 2
+        + [pltpu.VMEM(product, part.dtype), pltpu.SemaphoreType.DMA((half,))],
         compiler_params=params,
         name="line_scatter",
-    )(part, small)
+    )(part, small, tokens, grads)
 
 
 def fsdp_place():
@@ -791,6 +838,43 @@
         share_finish(rows[i], sems[i])
     for copy in keeps:
         copy.wait()
+
+
+def product_kernel(last, own, units, grads, rows, product, keep_sem, send_sem, recv_sem):
+    place = line_place()
+    here, level, line, side = place
+    sems = (send_sem, recv_sem)
+    greet_line(last, here, level, side)
+    line_start(rows, own, sems, place, last)
+    keep = pltpu.make_async_copy(own, rows.at[here], keep_sem.at[0])
+    keep.start()
+    turned = units[...].T
+    piece = grads.shape[1] // (last + 1)
+    for step in range(last + 1):
+        columns = pl.ds(step * piece, piece)
+        product[:, columns] = flat_dot(turned, grads[:, columns]).astype(product.dtype)
+        if step < last:
+            line_step(rows, sems, place, last, step + 1)
+    line_finish(rows, sems, place, last)
+    keep.wait()
+
+
+def product_gather(ctx_count, call_id, own, units, grads):
+    dma = pltpu.SemaphoreType.DMA
+    return pl.pallas_call(
+        functools.partial(product_kernel, ctx_count // 2 - 1),
+        out_shape=[
+            jax.ShapeDtypeStruct((ctx_count,) + own.shape, own.dtype),
+            jax.ShapeDtypeStruct((units.shape[1], grads.shape[1]), own.dtype),
+        ],
+        in_specs=[VMEM] * 3,
+        out_specs=[ANY, VMEM],
+        scratch_shapes=[dma((1,)), dma((ctx_count, 3)), dma((ctx_count,))],
+        compiler_params=pltpu.CompilerParams(
+            collective_id=call_id, has_side_effects=True, vmem_limit_bytes=32 * 2**20
+        ),
+        name="product_gather",
+    )(own, units, grads)
 
 
 def line_gather(ctx_count, call_id, own, *shared):
@@ -1130,21 +1214,6 @@
         ),
         name="closing",
     )(part, weight, pair, plain, small)
-
-
-SPAN = 256
-
-
-def flat_dot(left, right):
-    return lax.dot_general(left, right, (((1,), (0,)), ((), ())), preferred_element_type=jnp.float32)
-
-
-def turned_dot(left, right):
-    return lax.dot_general(left, right, (((1,), (1,)), ((), ())), preferred_element_type=jnp.float32)
-
-
-def span_of(index, size=SPAN):
-    return pl.ds(pl.multiple_of(index * size, size), size)
 
 
 def scaled_rows(values):
@@ -1567,11 +1636,13 @@
     row_seg = numbers[:, number_count - 1].reshape(row_len)
     routed_here = jnp.any(numbers[:, : number_count - 1] == ctx_rank, axis=1).reshape(row_len)
 
-    shared_in_weight, numbers = lax.optimization_barrier((shared_in_weight, numbers))
-    early_upstream = over("ctx", out_grad.reshape(tokens_dev, width)[:, :early])
+    expert_outer = over("fsdp", expert_out_weight[0])
+    shared_in_weight, early_grad, numbers, expert_outer = lax.optimization_barrier(
+        (shared_in_weight, out_grad, numbers, expert_outer)
+    )
+    early_upstream = over("ctx", early_grad.reshape(tokens_dev, width)[:, :early])
     inner_parts = deal_columns(shared_in_weight, ctx_count, 2 * fsdp_count)
     expert_inner = over("fsdp", expert_in_weight[0])
-    expert_outer = over("fsdp", expert_out_weight[0])
     inner_parts = exchange(inner_parts)
     my_heads = [pair_rank + (side * 2 + t) * pairs for t in range(2)]
     bias_c = jnp.concatenate(
@@ -1662,25 +1733,20 @@
     grad_shared_gu = mix_pull(grad_hidden)[0].astype(low)
     grad_inner = transposed_dot(row_ffn, grad_shared_gu).astype(low)
     sum_inner_c = reduce_over("fsdp", grad_inner)
-    grad_outer = transposed_dot(shared_hidden, grad_shared_out).astype(low)
     grad_ffn_part = (
         dot_transposed(grad_shared_gu, inner_c) + grad_rows.astype(full)
     ).astype(low)
-    grad_expert_gu, grad_ffn_part, grad_inner = lax.optimization_barrier(
-        (grad_expert_gu, grad_ffn_part, grad_inner)
-    )
-    grad_expert_inner = transposed_dot(row_ffn, grad_expert_gu).astype(low)
     dots = jnp.stack([gate_dot, expert_dot]).reshape(2, ctx_count, tokens_dev).transpose(1, 0, 2)
-    grad_ffn_part, grad_expert_inner, grad_outer = lax.optimization_barrier(
-        (grad_ffn_part, grad_expert_inner, grad_outer)
-    )
-    sum_expert_inner = reduce_over("fsdp", grad_expert_inner)
-    grad_normed, own_dots = line_scatter(
+    grad_ffn_part, grad_inner = lax.optimization_barrier((grad_ffn_part, grad_inner))
+    grad_normed, own_dots, grad_expert_inner = line_scatter(
         ctx_count,
         6,
         grad_ffn_part.reshape(ctx_count, tokens_dev, width),
         jnp.pad(dots, ((0, 0), (0, 6), (0, 0))),
-    )
+        row_ffn,
+        grad_expert_gu,
+    )
+    sum_expert_inner = reduce_over("fsdp", grad_expert_inner)
     hidden_out = (middle + out_landed.astype(full)).astype(low).reshape(1, tokens_dev, width)
 
     own_logits = dot_transposed(normed_ffn, router_gate)
@@ -1701,7 +1767,9 @@
     grad_branch, sum_expert_outer, hidden_out = lax.optimization_barrier(
         (grad_middle.astype(low), sum_expert_outer, hidden_out)
     )
-    (row_branch,) = line_gather(ctx_count, 3, grad_branch)
+    row_branch, grad_outer = product_gather(
+        ctx_count, 3, grad_branch, shared_hidden, grad_shared_out
+    )
     row_branch, sum_inner_c = lax.optimization_barrier(
         (row_branch.reshape(row_len, width), sum_inner_c)
     )
@@ -1734,7 +1802,8 @@
     places_of = [head_order.index(h) for h in range(head_count)]
     grad_bias = (
         jnp.where(mine, grad_bias_c, 0.0)
-        .reshape(3, head_count, HD)[:, jnp.array(places_of)]
+        .reshape(3, pairs, 2, 2, HD)
+        .transpose(0, 2, 3, 1, 4)
         .reshape(dev_count, -1)
     )
     small_grads = jnp.concatenate(

time: 740 us -> 737 us (level)
  matrix products: 151 us -> 125 us
  waiting for transfers between devices: 5.93 us -> 26.7 us
  Pallas kernels: 435 us -> 446 us
    pallas_call x0 -> x1, Pallas kernels: none -> 47 us  [product_gather(): pl.pallas_call(functools.partial(product_kernel, ctx_count // 2 - 1), out...]
    pallas_call x2 -> x1, Pallas kernels: 101 us -> 70.2 us  [line_gather(): pl.pallas_call(functools.partial(gather_kernel, ctx_count // 2 - 1, count...]
    dot_general x5 -> x3, matrix products: 44.1 us -> 18.9 us  [transposed_dot(): lax.dot_general(left, right, (((0,), (0,)), ((), ())), preferred_element_...]
    pallas_call x1, Pallas kernels: 95.2 us -> 75.8 us  [opening(): pl.pallas_call(functools.partial(opening_kernel, ctx_count), out_shape=[o...]
    all_to_all x2, waiting for transfers between devices: 4.39 us -> 21.1 us  [exchange(): return lax.all_to_all(array, 'ctx', split_axis=0, concat_axis=0, tiled=True)]
    all_to_all x2, starting transfers between devices: 14.7 us -> 7.15 us  [exchange(): return lax.all_to_all(array, 'ctx', split_axis=0, concat_axis=0, tiled=True)]
    unnamed x149 -> x131, local copies, waits for them, and re-layouts: 30.7 us -> 34.9 us
  transfers between devices with their start and end apart: 10 -> 10, of which waited for: 1 -> 3; matrix products, arithmetic and copies ran while one was open for 29% -> 25% of each run, Pallas kernels for 60% -> 61%
where the time goes in v6:
time: 737 us; the launch traced here: 726 us
  Pallas kernels  446 us (61%)
  matrix products  125 us (17%)
  other arithmetic  54 us (7%)
  local copies, waits for them, and re-layouts  52 us (7%)
  waiting for transfers between devices  26.7 us (4%)
  between operations  15.3 us (2%)
  starting transfers between devices  7.69 us (1%)
    pallas_call x1, Pallas kernels, closing(): pl.pallas_call(functools.partial(closing_kernel, ctx_count), out_shape=[j...  79.7 us
    pallas_call x1, Pallas kernels, opening(): pl.pallas_call(functools.partial(opening_kernel, ctx_count), out_shape=[o...  75.8 us
    pallas_call x1, Pallas kernels, line_gather(): pl.pallas_call(functools.partial(gather_kernel, ctx_count // 2 - 1, count...  70.2 us
    pallas_call x1, Pallas kernels, line_scatter(): pl.pallas_call(functools.partial(scatter_kernel, ctx_count), out_shape=[t...  61.4 us
    dot_general x6, matrix products, dot_transposed(): lax.dot_general(left, right, (((1,), (1,)), ((), ())), preferred_element_...  61.4 us
    pallas_call x1, Pallas kernels, line_scatter(): pl.pallas_call(functools.partial(line_scatter_kernel, half - 1), out_shap...  48.9 us
    pallas_call x1, Pallas kernels, product_gather(): pl.pallas_call(functools.partial(product_kernel, ctx_count // 2 - 1), out...  47 us
    dot_general x5, matrix products, matmul_low(): return jnp.dot(left, right, preferred_element_type=jnp.float32)  44.5 us
  transfers between devices with their start and end apart: 10, of which 3 were waited for; matrix products, arithmetic and copies ran while one was open for 25% of the time, Pallas kernels for 61%

profile of v6, /device:TPU:0, one launch (start us, length us, event | category | flops | bytes accessed | tf_op | source)
XLA Modules:
  0.0 726.2 jit_solution(9531966942967375235)
XLA Ops:
  14.6 75.8 %opening.1 = (bf16[8,128,2048]{2,1,0:T(8,128)(2,1)}, bf16[4,8,64,768]{3,2,1,0:T(8,128)(2,1)}, bf16[4,2,64,2048]{3,2,1,0:T(8,128)(2,1)}, bf16[4,8,16,128]{3,2,1,0:T(8,128)(2,1)}, s32[8,8,128]{2,1,0:T(8,128)}) custom-call(bf16[128,2048]{1,0:T(8,128)(2,1)} %bitcast.148, bf16[8,64,768]{2,1,0:T(8,128)(2,1)} %reshape.350.qkv_own, bf16[64,2048]{1,0:T(8,128)(2,1)} %out_own.1, ...), custom_call_target="tpu_custom_call" | custom-call | tf_op jit(solution)/shard_map/opening/pallas_call | solution.py:1014
  97.9 3.6 all-to-all-start
  107.4 17.6 %attend.1 = (bf16[1024,2048]{1,0:T(8,128)(2,1)S(1)}, bf16[1024,256]{1,0:T(8,128)(2,1)S(1)}, bf16[1024,256]{1,0:T(8,128)(2,1)S(1)}, bf16[1024,256]{1,0:T(8,128)(2...) custom-call(bf16[1024,2048]{1,0:T(8,128)(2,1)} %bitcast.186, ...), custom_call_target="tpu_custom_call" | custom-call | flops 5368709120 | bytes 20971520 | tf_op jit(solution)/shard_map/attend/pallas_call | solution.py:1287
  131.2 21.1 %all-to-all-done = bf16[8,64,1408]{2,1,0:T(8,128)(2,1)S(1)} async-done(((bf16[8,64,1408]{2,1,0:T(8,128)(2,1)}), bf16[8,64,1408]{2,1,0:T(8,128)(2,1)S(1)}, u32[]{:S(2)}, u32[]{:S(2)}) %all-to-all-start) | async-done | bytes 1441824 | tf_op jit(solution)/shard_map/all_to_all | solution.py:1540
  155.5 48.9 %line_scatter.2 = f32[128,2048]{1,0:T(8,128)S(1)} custom-call(bf16[8,128,2048]{2,1,0:T(8,128)(2,1)S(1)} %bitcast.137), custom_call_target="tpu_custom_call" | custom-call | tf_op jit(solution)/shard_map/line_scatter/pallas_call | solution.py:704
  206.5 70.2 %line_gather.1 = (bf16[8,128,2048]{2,1,0:T(8,128)(2,1)}, bf16[4,512,1408]{2,1,0:T(8,128)(2,1)}, bf16[4,176,2048]{2,1,0:T(8,128)(2,1)}) custom-call(bf16[128,2048]{1,0:T(8,128)(2,1)} %multiply_convert_fusion.4.refs_0_, bf16[512,1408]{1,0:T(8,128)(2,1)} %bitcast.149, bf16[176,2048]{1,0:T(8,128)(2,1)} %refs_2_.1), custom_call_target="tpu_custom_call" | custom-call | tf_op jit(solution)/shard_map/line_gather/pallas_call | solution.py:883
  281.4 17.2 %fusion.2 = f32[1024,2816]{1,0:T(8,128)S(1)} fusion(bf16[1024,2048]{1,0:T(8,128)(2,1)} %bitcast.144, bf16[1,2048,2816]{2,1,0:T(8,128)(2,1)} %all-gather.13.cloned.1.call-done), kind=kOutput, calls=%fused_computation.3 | convolution fusion | flops 11811160064 | bytes 27262976 | tf_op jit(solution)/shard_map/dot_general | solution.py:49
  303.9 11.9 %convert_convert_fusion = f32[1024,2048]{1,0:T(8,128)} fusion(bf16[1024,1408]{1,0:T(8,128)(2,1)S(1)} %multiply_convert_fusion.2, bf16[1408,2048]{1,0:T(8,128)(2,1)} %bitcast.180), kind=kOutput, calls=%fused_computation.23 | convolution fusion | flops 5909774336 | bytes 17039360 | tf_op jit(solution)/shard_map/dot_general | solution.py:49
  315.8 6.7 fusion.49
  326.8 6.1 fusion.51
  335.9 10.7 %multiply_reduce_fusion.1 = (f32[1024]{0:T(1024)S(1)}, f32[1024]{0:T(1024)S(1)}, bf16[1024,2048]{1,0:T(8,128)(2,1)}) fusion(f32[1024,2048]{1,0:T(8,128)} %fusion.51, bf16[1024,1280]{1,0:T(8,128)(2,1)} %all-gather.9.cloned.1.call-done, bf16[1024,768]{1,0:T(8,128)(2,1)} %all-gather.7.cloned.1.call-done, f32[1024,2048]{1,0:T(8,128)} %convert_convert_fusion, ...), kind=kLoop, calls=%fused_computation.8 | loop fusion | flops 25163776 | bytes 25182208 | tf_op jit(solution)/shard_map/reduce_sum | solution.py:1714
  353.6 8.3 %convolution_convert_fusion = bf16[1408,2048]{1,0:T(8,128)(2,1)} fusion(bf16[1024,1408]{1,0:T(8,128)(2,1)S(1)} %copy-done.29, f32[1024,2048]{1,0:T(8,128)S(1)} %maximum_convert_fusion, f32[1024]{0:T(1024)S(1)} %bitcast_select_fusion.1), kind=kOutput, calls=%fused_computation.13 | convolution fusion | flops 5912657920 | bytes 17043456 | tf_op jit(solution)/shard_map/dot_general | solution.py:1544
  362.0 17.8 %fusion.18 = (f32[1024,1408]{1,0:T(8,128)}, f32[1024,1408]{1,0:T(8,128)}) fusion(f32[1024,2816]{1,0:T(8,128)} %copy-done.19, bf16[1408,2048]{1,0:T(8,128)(2,1)} %bitcast.181, f32[1024,2048]{1,0:T(8,128)} %copy-done.14, f32[1024]{0:T(1024)S(1)} %bitcast_select_fusion.1), kind=kOutput, calls=%fused_computation.55 | convolution fusion | flops 5927075840 | bytes 37228544 | tf_op jit(solution)/shard_map/dot_general | solution.py:1550
  379.8 7.5 %add_convert_fusion.grads = bf16[1024,2816]{1,0:T(8,128)(2,1)} fusion(f32[1024,1408]{1,0:T(8,128)} %get-tuple-element.128, f32[1024,1408]{1,0:T(8,128)} %get-tuple-element.127), kind=kLoop, calls=%fused_computation.5 | loop fusion | flops 5767168 | bytes 17301504 | tf_op jit(solution)/shard_map/convert_element_type | solution.py:1725
  387.3 18.2 %fusion.7 = bf16[1024,2048]{1,0:T(8,128)(2,1)} fusion(bf16[1024,2816]{1,0:T(8,128)(2,1)} %add_convert_fusion.grads, bf16[1,2048,2816]{2,1,0:T(8,128)(2,1)} %all-gather.13.cloned.1.call-done), kind=kOutput, calls=%fused_computation.24 | convolution fusion | flops 11813257216 | bytes 21495808 | tf_op jit(solution)/shard_map/dot_general | solution.py:1550
  405.5 4.0 multiply_convert_fusion.grads
  409.7 8.1 %fusion.20 = (f32[1024,704]{1,0:T(8,128)S(1)}, f32[1024,704]{1,0:T(8,128)S(1)}) fusion(f32[1024,1408]{1,0:T(8,128)} %copy-done.23, bf16[1024,2048]{1,0:T(8,128)(2,1)S(1)} %multiply_convert_fusion.grads, bf16[704,2048]{1,0:T(8,128)(2,1)S(1)} %bitcast.189), kind=kOutput, calls=%fused_computation.59 | convolution fusion | flops 2961440768 | bytes 18612224 | tf_op jit(solution)/shard_map/dot_general | solution.py:1550
  420.5 9.3 %convolution_convert_fusion.1 = bf16[2048,1408]{1,0:T(8,128)(2,1)} fusion(bf16[1024,2048]{1,0:T(8,128)(2,1)S(1)} %bitcast.147, f32[1024,704]{1,0:T(8,128)S(1)} %get-tuple-element.131, f32[1024,704]{1,0:T(8,128)S(1)} %get-tuple-element.130), kind=kOutput, calls=%fused_computation.14 | convolution fusion | flops 5911347200 | bytes 15728640 | tf_op jit(solution)/shard_map/dot_general | solution.py:1544
  429.9 12.7 %add_convert_fusion.1 = bf16[1024,2048]{1,0:T(8,128)(2,1)} fusion(bf16[1024,2048]{1,0:T(8,128)(2,1)} %fusion.7, bf16[2048,1408]{1,0:T(8,128)(2,1)} %bitcast.182, f32[1024,704]{1,0:T(8,128)} %copy-done.59, f32[1024,704]{1,0:T(8,128)} %copy-done.58), kind=kOutput, calls=%fused_computation.9 | convolution fusion | flops 5914755072 | bytes 19922944 | tf_op jit(solution)/shard_map/dot_general | solution.py:1550
  443.3 61.4 %line_scatter.3 = (f32[128,2048]{1,0:T(8,128)}, f32[8,8,128]{2,1,0:T(8,128)}, bf16[2048,2816]{1,0:T(8,128)(2,1)}) custom-call(bf16[8,128,2048]{2,1,0:T(8,128)(2,1)} %bitcast.153, f32[8,8,128]{2,1,0:T(8,128)} %pad.34.small, bf16[1024,2048]{1,0:T(8,128)(2,1)} %bitcast.145, bf16[1024,2816]{1,0:T(8,128)(2,1)} %add_convert_fusion.grads), custom_call_target="tpu_custom_call" | custom-call | tf_op jit(solution)/shard_map/line_scatter/pallas_call | solution.py:717
  519.2 47.0 %product_gather.1 = (bf16[8,128,2048]{2,1,0:T(8,128)(2,1)S(1)}, bf16[704,2048]{1,0:T(8,128)(2,1)S(1)}) custom-call(bf16[128,2048]{1,0:T(8,128)(2,1)S(1)} %get-tuple-element.94.own, bf16[1024,704]{1,0:T(8,128)(2,1)S(1)} %multiply_convert_fusion.3.units, bf16[1024,2048]{1,0:T(8,128)(2,1)S(1)} %copy-done.1), custom_call_target="tpu_custom_call" | custom-call | tf_op jit(solution)/shard_map/product_gather/pallas_call | solution.py:864
  573.5 35.9 %attend_back.1 = (bf16[1024,2048]{1,0:T(8,128)(2,1)}, bf16[2048,768]{1,0:T(8,128)(2,1)}, bf16[256,2048]{1,0:T(8,128)(2,1)}, f32[1,768]{1,0:T(1,128)}, f32[1,2048]{1,0:T(1,128)}) custom-call(bf16[1024,2048]{1,0:T(8,128)(2,1)} %bitcast.140, bf16[256,2048]{1,0:T(8,128)(2,1)} %copy-done.4, bf16[1024,256]{1,0:T(8,128)(2,1)} %copy-done.10, ...), custom_call_target="tpu_custom_call" | custom-call | flops 11274289152 | bytes 36700160 | tf_op jit(solution)/shard_map/attend_back/pallas_call | solution.py:1424
  622.5 79.7 %closing.1 = (f32[128,2048]{1,0:T(8,128)}, bf16[8,64,768]{2,1,0:T(8,128)(2,1)}, f32[64,2048]{1,0:T(8,128)}, f32[176,2048]{1,0:T(8,128)}, f32[8,128]{1,0:T(8,128)}) custom-call(bf16[8,128,2048]{2,1,0:T(8,128)(2,1)} %bitcast.152, bf16[4,512,768]{2,1,0:T(8,128)(2,1)} %bitcast.159, bf16[4,128,2048]{2,1,0:T(8,128)(2,1)} %pad_maximum_fusion.pair, ...), custom_call_target="tpu_custom_call" | custom-call | tf_op jit(solution)/shard_map/closing/pallas_call | solution.py:1186
  712.4 4.9 bitcast_convert_fusion
  (254 shorter events, 106.4 us)
Async XLA Ops:
  7.2 83.2 %all-gather.11.cloned.1.call-start = ((), (), s32[]{:S(2)}) async-start(), calls=%async_computation.12 | async-start | bytes 7208960 | tf_op jit(solution)/shard_map/all_gather | solution.py:1532
  7.9 145.4 %all-gather.7.cloned.1.call-start = ((), (), s32[]{:S(2)}) async-start(), calls=%async_computation.6 | async-start | bytes 1769472 | tf_op jit(solution)/shard_map/all_gather | solution.py:1532
  11.0 82.9 %copy-start.57 = (s32[16]{0:T(128)S(1)}, s32[16]{0:T(128)}, u32[]{:S(2)}) copy-start(s32[16]{0:T(128)} %param.19) | copy-start | bytes 196
  92.0 189.3 %all-gather.13.cloned.1.call-start = ((), (), s32[]{:S(2)}) async-start(), calls=%async_computation.13 | async-start | bytes 14417920 | tf_op jit(solution)/shard_map/all_gather | solution.py:1532
  97.9 54.4 %all-to-all-start = ((bf16[8,64,1408]{2,1,0:T(8,128)(2,1)}), bf16[8,64,1408]{2,1,0:T(8,128)(2,1)S(1)}, u32[]{:S(2)}, u32[]{:S(2)}) async-start(bf16[8,64,1408]{2,1,0:T(8,128)(2,1)} %deal_columns.1), calls=%async_computation | async-start | bytes 2883584 | tf_op jit(solution)/shard_map/all_to_all | solution.py:1540
  101.5 234.5 %all-gather.9.cloned.1.call-start = ((), (), s32[]{:S(2)}) async-start(), calls=%async_computation.7 | async-start | bytes 2949120 | tf_op jit(solution)/shard_map/all_gather | solution.py:1532
  102.9 101.8 %copy-start.35 = (f32[2048]{0:T(1024)}, f32[2048]{0:T(1024)S(1)}, u32[]{:S(2)}) copy-start(f32[2048]{0:T(1024)S(1)} %reshape.386) | copy-start | bytes 24580
  103.3 177.7 %copy-start.41 = (pred[8,128]{1,0:T(8,128)(4,1)}, pred[8,128]{1,0:T(8,128)(4,1)S(1)}, u32[]{:S(2)}) copy-start(pred[8,128]{1,0:T(8,128)(4,1)S(1)} %fusion.24) | copy-start | bytes 3076
  105.6 171.9 %copy-start.32 = (bf16[9,2048]{1,0:T(8,128)(2,1)}, bf16[9,2048]{1,0:T(8,128)(2,1)S(1)}, u32[]{:S(2)}) copy-start(bf16[9,2048]{1,0:T(8,128)(2,1)S(1)} %constant_dynamic-update-slice_fusion) | copy-start | bytes 110596
  107.4 97.0 %copy-start.21 = (bf16[1,128,2048]{2,1,0:T(8,128)(2,1)S(1)}, bf16[1,128,2048]{2,1,0:T(8,128)(2,1)}, u32[]{:S(2)}) copy-start(bf16[1,128,2048]{2,1,0:T(8,128)(2,1)} %param.17) | copy-start | bytes 1572868
  152.3 54.3 %copy-start.25 = (bf16[8,64,1408]{2,1,0:T(8,128)(2,1)}, bf16[8,64,1408]{2,1,0:T(8,128)(2,1)S(1)}, u32[]{:S(2)}) copy-start(bf16[8,64,1408]{2,1,0:T(8,128)(2,1)S(1)} %all-to-all-done) | copy-start | bytes 4325380
  204.4 72.4 %copy-start.26 = (bf16[1,128,2048]{2,1,0:T(8,128)(2,1)S(1)}, bf16[1,128,2048]{2,1,0:T(8,128)(2,1)}, u32[]{:S(2)}) copy-start(bf16[1,128,2048]{2,1,0:T(8,128)(2,1)} %param.21) | copy-start | bytes 1572868
  204.6 76.2 %copy-start.53 = (f32[128]{0:T(128)}, f32[128]{0:T(128)S(1)}, u32[]{:S(2)}) copy-start(f32[128]{0:T(128)S(1)} %get-tuple-element.125) | copy-start | bytes 1540
  204.7 76.2 %copy-start.43 = (f32[128]{0:T(128)}, f32[128]{0:T(128)S(1)}, u32[]{:S(2)}) copy-start(f32[128]{0:T(128)S(1)} %fusion.36) | copy-start | bytes 1540
  281.1 232.8 %reduce-scatter.7.cloned.1.call-start = ((), (), s32[]{:S(2)}) async-start(), calls=%async_computation.9 | async-start | bytes 4718592 | tf_op jit(solution)/shard_map/reduce_scatter | solution.py:1536
  298.6 17.2 %slice-start = ((s8[5767168]{0:T(1024)(128)(4,1)}), s8[4194304]{0:T(1024)(128)(4,1)S(1)}, s32[]{:S(2)}) async-start(s8[5767168]{0:T(1024)(128)(4,1)} %bitcast.183), calls=%async_computation.14 | async-start | bytes 8388608
  303.9 11.9 %copy-start.17 = (bf16[8,128,2048]{2,1,0:T(8,128)(2,1)S(1)}, bf16[8,128,2048]{2,1,0:T(8,128)(2,1)}, u32[]{:S(2)}) copy-start(bf16[8,128,2048]{2,1,0:T(8,128)(2,1)} %get-tuple-element.76) | copy-start | bytes 12582916
  303.9 11.9 %slice-start.1 = ((s8[5767168]{0:T(1024)(128)(4,1)}), s8[1572864]{0:T(1024)(128)(4,1)S(1)}, s32[]{:S(2)}) async-start(s8[5767168]{0:T(1024)(128)(4,1)} %bitcast.183), calls=%async_computation.15 | async-start | bytes 3145728
  346.7 170.4 %reduce-scatter.5.cloned.1.call-start = ((), (), s32[]{:S(2)}) async-start(), calls=%async_computation.8 | async-start | bytes 7208960 | tf_op jit(solution)/shard_map/reduce_scatter | solution.py:1536
  361.9 208.0 %reduce-scatter.9.cloned.1.call-start = ((), (), s32[]{:S(2)}) async-start(), calls=%async_computation.10 | async-start | bytes 7208960 | tf_op jit(solution)/shard_map/reduce_scatter | solution.py:1536
  429.9 12.8 %copy-start.42 = (pred[8,128]{1,0:T(8,128)(4,1)S(1)}, pred[8,128]{1,0:T(8,128)(4,1)}, u32[]{:S(2)}) copy-start(pred[8,128]{1,0:T(8,128)(4,1)} %copy-done.41) | copy-start | bytes 3076
  429.9 282.5 %reduce-scatter.11.cloned.1.call-start = ((), (), s32[]{:S(2)}) async-start(), calls=%async_computation.11 | async-start | bytes 14417920 | tf_op jit(solution)/shard_map/reduce_scatter | solution.py:1536
  569.9 47.9 %all-to-all-start.1 = ((bf16[8,64,1408]{2,1,0:T(8,128)(2,1)}), bf16[8,64,1408]{2,1,0:T(8,128)(2,1)S(1)}, u32[]{:S(2)}, u32[]{:S(2)}) async-start(bf16[8,64,1408]{2,1,0:T(8,128)(2,1)} %bitcast.160), calls=%async_computation.4 | async-start | bytes 2883584 | tf_op jit(solution)/shard_map/all_to_all | solution.py:1540
  622.5 85.0 %copy-start.22 = (bf16[1,128,2048]{2,1,0:T(8,128)(2,1)S(1)}, bf16[1,128,2048]{2,1,0:T(8,128)(2,1)}, u32[]{:S(2)}) copy-start(bf16[1,128,2048]{2,1,0:T(8,128)(2,1)} %param.17) | copy-start | bytes 1572868
  (48 other events, 190.4 us)
Sparse Core Ops, SparseCore 0:
  9.6 55.4 all-gather.10
  92.2 61.1 all-gather.6
  154.9 90.8 all-gather.12
  281.2 54.6 all-gather.8
  346.8 86.4 reduce-scatter.6
  435.8 54.6 reduce-scatter.4
  493.6 54.8 reduce-scatter.8
  551.3 97.5 reduce-scatter.10

commit v7 on v6

--- a/solution.py
+++ b/solution.py
@@ -1464,6 +1464,50 @@
     )
 
 
+def gate_back_kernel(upstream, scale, gate_up, weight_out, grads, scaled):
+    low = jnp.bfloat16
+    half = gate_up.shape[1] // 2
+    scaled[...] = (scale[...] * upstream[...].astype(jnp.float32)).astype(low)
+    grad_unit = turned_dot(scaled[...], weight_out[...])
+    gate, up = gate_up[:, :half], gate_up[:, half:]
+    sigmoid = 1.0 / (1.0 + jnp.exp(-gate))
+    grad_gate = grad_unit * up * (sigmoid * (1.0 + gate * (1.0 - sigmoid)))
+    grad_up = grad_unit * (gate * sigmoid)
+    grads[...] = jnp.concatenate([grad_gate.astype(low), grad_up.astype(low)], axis=1)
+
+
+def gate_back(upstream, scale, gate_up, weight_out):
+    rows, width = upstream.shape
+    hidden = weight_out.shape[0]
+    low = jnp.bfloat16
+
+    def block(columns):
+        return pl.BlockSpec((SPAN, columns), lambda i: (i, 0))
+
+    return pl.pallas_call(
+        gate_back_kernel,
+        grid=(rows // SPAN,),
+        out_shape=[
+            jax.ShapeDtypeStruct((rows, 2 * hidden), low),
+            jax.ShapeDtypeStruct((rows, width), low),
+        ],
+        in_specs=[
+            block(width),
+            block(1),
+            block(2 * hidden),
+            pl.BlockSpec((hidden, width), lambda i: (0, 0)),
+        ],
+        out_specs=[block(2 * hidden), block(width)],
+        compiler_params=pltpu.CompilerParams(vmem_limit_bytes=48 * 2**20),
+        cost_estimate=pl.CostEstimate(
+            flops=2 * rows * width * hidden,
+            bytes_accessed=rows * (12 * hidden + 4 * width) + 2 * hidden * width,
+            transcendentals=rows * hidden,
+        ),
+        name="gate_back",
+    )(upstream, scale, gate_up, weight_out)
+
+
 def deal_kernel(pieces, weight, dealt):
     ctx_count = dealt.shape[0]
     width = dealt.shape[2] // pieces
@@ -1636,11 +1680,9 @@
     row_seg = numbers[:, number_count - 1].reshape(row_len)
     routed_here = jnp.any(numbers[:, : number_count - 1] == ctx_rank, axis=1).reshape(row_len)
 
+    shared_in_weight, numbers = lax.optimization_barrier((shared_in_weight, numbers))
     expert_outer = over("fsdp", expert_out_weight[0])
-    shared_in_weight, early_grad, numbers, expert_outer = lax.optimization_barrier(
-        (shared_in_weight, out_grad, numbers, expert_outer)
-    )
-    early_upstream = over("ctx", early_grad.reshape(tokens_dev, width)[:, :early])
+    early_upstream = over("ctx", out_grad.reshape(tokens_dev, width)[:, :early])
     inner_parts = deal_columns(shared_in_weight, ctx_count, 2 * fsdp_count)
     expert_inner = over("fsdp", expert_in_weight[0])
     inner_parts = exchange(inner_parts)
@@ -1675,8 +1717,8 @@
         key_marks,
         out_c,
     )
-    branch_part, inner_parts, early_upstream = lax.optimization_barrier(
-        (branch_part, inner_parts, early_upstream)
+    branch_part, inner_parts, early_upstream, expert_outer = lax.optimization_barrier(
+        (branch_part, inner_parts, early_upstream, expert_outer)
     )
     branch = line_scatter(ctx_count, 2, branch_part.reshape(ctx_count, tokens_dev, width))
     middle = inputs + branch
@@ -1709,28 +1751,23 @@
     shared_hidden = swiglu_mix(shared_gu, shared_width).astype(low)
     shared_out = matmul_low(shared_hidden, outer_c)
     shared_out, late_upstream = lax.optimization_barrier((shared_out, late_upstream))
-    upstream_row = jnp.concatenate([early_upstream, late_upstream], axis=1).astype(full)
+    row_upstream = lax.optimization_barrier(
+        jnp.concatenate([early_upstream, late_upstream], axis=1)
+    )
+    upstream_row = row_upstream.astype(full)
     out_part = (row_gate[:, None] * shared_out + here[:, None] * expert_result).astype(low)
     gate_dot = jnp.sum(upstream_row * shared_out, axis=1)
     expert_dot = jnp.where(routed_here, jnp.sum(upstream_row * expert_result, axis=1), 0.0)
     out_landed = reduce_over("ctx", out_part)
 
-    upstream_row, out_part = lax.optimization_barrier((upstream_row, out_part))
-    grad_buffers = (here[:, None] * upstream_row).astype(low)
+    row_upstream, out_part = lax.optimization_barrier((row_upstream, out_part))
+    grad_expert_gu, grad_buffers = gate_back(row_upstream, here[:, None], expert_gu, expert_outer)
     sum_expert_outer = reduce_over("fsdp", transposed_dot(expert_hidden, grad_buffers).astype(low))
-    grad_expert_hidden = dot_transposed(grad_buffers, expert_outer)
-    unused_mix, expert_pull = jax.vjp(
-        functools.partial(swiglu_mix, hidden_width=expert_width), expert_gu
-    )
-    grad_expert_gu = expert_pull(grad_expert_hidden)[0].astype(low)
     grad_rows = dot_transposed(grad_expert_gu, expert_inner).astype(low)
-    upstream_row, grad_rows = lax.optimization_barrier((upstream_row, grad_rows))
-    grad_shared_out = (row_gate[:, None] * upstream_row).astype(low)
-    grad_hidden = dot_transposed(grad_shared_out, outer_c)
-    unused_mix, mix_pull = jax.vjp(
-        functools.partial(swiglu_mix, hidden_width=shared_width), shared_gu
-    )
-    grad_shared_gu = mix_pull(grad_hidden)[0].astype(low)
+    row_upstream, grad_rows = lax.optimization_barrier((row_upstream, grad_rows))
+    grad_shared_gu, grad_shared_out = gate_back(
+        row_upstream, row_gate[:, None], shared_gu, outer_c
+    )
     grad_inner = transposed_dot(row_ffn, grad_shared_gu).astype(low)
     sum_inner_c = reduce_over("fsdp", grad_inner)
     grad_ffn_part = (

time: 737 us -> 723 us (0.981)
  Pallas kernels: 446 us -> 481 us
  matrix products: 125 us -> 97 us
  waiting for transfers between devices: 26.7 us -> 9.46 us
  other arithmetic: 54 us -> 37 us
  starting transfers between devices: 7.69 us -> 18.9 us
    dot_general x6 -> x4, matrix products: 61.4 us -> 34.9 us  [dot_transposed(): lax.dot_general(left, right, (((1,), (1,)), ((), ())), preferred_element_...]
    pallas_call x0 -> x2, Pallas kernels: none -> 23.5 us  [gate_back(): pl.pallas_call(gate_back_kernel, grid=(rows // SPAN,), out_shape=[jax.Sha...]
    pallas_call x1, Pallas kernels: 75.8 us -> 95 us  [opening(): pl.pallas_call(functools.partial(opening_kernel, ctx_count), out_shape=[o...]
    pallas_call x1, Pallas kernels: 70.2 us -> 53.8 us  [line_gather(): pl.pallas_call(functools.partial(gather_kernel, ctx_count // 2 - 1, count...]
    all_to_all x2, waiting for transfers between devices: 21.1 us -> 4.8 us  [exchange(): return lax.all_to_all(array, 'ctx', split_axis=0, concat_axis=0, tiled=True)]
    convert_element_type x3 -> x0, other arithmetic: 15 us -> none  [the longest x1 7.5 us: split_plan(): grad_expert_gu = expert_pull(grad_expert_hidden)[0].astype(low)]
    all_to_all x2, starting transfers between devices: 7.15 us -> 18.3 us  [exchange(): return lax.all_to_all(array, 'ctx', split_axis=0, concat_axis=0, tiled=True)]
    unnamed x131 -> x114, local copies, waits for them, and re-layouts: 34.9 us -> 32.7 us
  transfers between devices with their start and end apart: 10 -> 10, of which waited for: 3 -> 3; matrix products, arithmetic and copies ran while one was open for 25% -> 19% of each run, Pallas kernels for 61% -> 68%
where the time goes in v7:
time: 723 us; the launch traced here: 709 us
  Pallas kernels  481 us (67%)
  matrix products  97 us (13%)
  local copies, waits for them, and re-layouts  50.1 us (7%)
  other arithmetic  37 us (5%)
  starting transfers between devices  18.9 us (3%)
  between operations  15.5 us (2%)
  waiting for transfers between devices  9.46 us (1%)
    pallas_call x1, Pallas kernels, opening(): pl.pallas_call(functools.partial(opening_kernel, ctx_count), out_shape=[o...  95 us
    pallas_call x1, Pallas kernels, closing(): pl.pallas_call(functools.partial(closing_kernel, ctx_count), out_shape=[j...  84.7 us
    pallas_call x1, Pallas kernels, line_scatter(): pl.pallas_call(functools.partial(scatter_kernel, ctx_count), out_shape=[t...  60.3 us
    pallas_call x1, Pallas kernels, line_gather(): pl.pallas_call(functools.partial(gather_kernel, ctx_count // 2 - 1, count...  53.8 us
    pallas_call x1, Pallas kernels, product_gather(): pl.pallas_call(functools.partial(product_kernel, ctx_count // 2 - 1), out...  49.7 us
    pallas_call x1, Pallas kernels, line_scatter(): pl.pallas_call(functools.partial(line_scatter_kernel, half - 1), out_shap...  48.9 us
    dot_general x5, matrix products, matmul_low(): return jnp.dot(left, right, preferred_element_type=jnp.float32)  44.4 us
    pallas_call x1, Pallas kernels, attend_back(): pl.pallas_call(attend_back_kernel, out_shape=[shape((rows, width), low),...  38.4 us
  transfers between devices with their start and end apart: 10, of which 3 were waited for; matrix products, arithmetic and copies ran while one was open for 19% of the time, Pallas kernels for 68%

profile of v7, /device:TPU:0, one launch (start us, length us, event | category | flops | bytes accessed | tf_op | source)
XLA Modules:
  0.0 709.1 jit_solution(7571371927928182796)
XLA Ops:
  15.9 95.0 %opening.1 = (bf16[8,128,2048]{2,1,0:T(8,128)(2,1)}, bf16[4,8,64,768]{3,2,1,0:T(8,128)(2,1)}, bf16[4,2,64,2048]{3,2,1,0:T(8,128)(2,1)}, bf16[4,8,16,128]{3,2,1,0:T(8,128)(2,1)}, s32[8,8,128]{2,1,0:T(8,128)}) custom-call(bf16[128,2048]{1,0:T(8,128)(2,1)} %bitcast.153, bf16[8,64,768]{2,1,0:T(8,128)(2,1)} %reshape.359.qkv_own, bf16[64,2048]{1,0:T(8,128)(2,1)} %out_own.1, ...), custom_call_target="tpu_custom_call" | custom-call | tf_op jit(solution)/shard_map/opening/pallas_call | solution.py:1014
  114.0 12.5 %all-to-all-start = ((bf16[8,64,1408]{2,1,0:T(8,128)(2,1)}), bf16[8,64,1408]{2,1,0:T(8,128)(2,1)S(1)}, u32[]{:S(2)}, u32[]{:S(2)}) async-start(bf16[8,64,1408]{2,1,0:T(8,128)(2,1)} %deal_columns.1), calls=%async_computation | async-start | bytes 2883584 | tf_op jit(solution)/shard_map/all_to_all | solution.py:1584
  132.8 17.6 %attend.1 = (bf16[1024,2048]{1,0:T(8,128)(2,1)S(1)}, bf16[1024,256]{1,0:T(8,128)(2,1)S(1)}, bf16[1024,256]{1,0:T(8,128)(2,1)S(1)}, bf16[1024,256]{1,0:T(8,128)(2...) custom-call(bf16[1024,2048]{1,0:T(8,128)(2,1)} %bitcast.194, ...), custom_call_target="tpu_custom_call" | custom-call | flops 5368709120 | bytes 20971520 | tf_op jit(solution)/shard_map/attend/pallas_call | solution.py:1287
  156.6 4.8 all-to-all-done
  164.1 48.9 %line_scatter.2 = f32[128,2048]{1,0:T(8,128)S(1)} custom-call(bf16[8,128,2048]{2,1,0:T(8,128)(2,1)S(1)} %bitcast.142), custom_call_target="tpu_custom_call" | custom-call | tf_op jit(solution)/shard_map/line_scatter/pallas_call | solution.py:704
  215.2 53.8 %line_gather.1 = (bf16[8,128,2048]{2,1,0:T(8,128)(2,1)}, bf16[4,512,1408]{2,1,0:T(8,128)(2,1)}, bf16[4,176,2048]{2,1,0:T(8,128)(2,1)}) custom-call(bf16[128,2048]{1,0:T(8,128)(2,1)} %multiply_convert_fusion.refs_0_, bf16[512,1408]{1,0:T(8,128)(2,1)} %bitcast.154, bf16[176,2048]{1,0:T(8,128)(2,1)} %refs_2_.1), custom_call_target="tpu_custom_call" | custom-call | tf_op jit(solution)/shard_map/line_gather/pallas_call | solution.py:883
  274.1 17.2 %fusion.2.gate_up = f32[1024,2816]{1,0:T(8,128)S(1)} fusion(bf16[1024,2048]{1,0:T(8,128)(2,1)} %bitcast.149, bf16[1,2048,2816]{2,1,0:T(8,128)(2,1)} %all-gather.13.cloned.1.call-done), kind=kOutput, calls=%fused_computation.3 | convolution fusion | flops 11811160064 | bytes 27262976 | tf_op jit(solution)/shard_map/dot_general | solution.py:49
  296.6 11.9 %convert_convert_fusion = f32[1024,2048]{1,0:T(8,128)} fusion(bf16[1024,1408]{1,0:T(8,128)(2,1)S(1)} %fusion.6, bf16[1408,2048]{1,0:T(8,128)(2,1)} %bitcast.155), kind=kOutput, calls=%fused_computation.16 | convolution fusion | flops 5909774336 | bytes 17039360 | tf_op jit(solution)/shard_map/dot_general | solution.py:49
  308.5 6.7 fusion.40.gate_up
  319.5 6.1 fusion.41
  334.0 6.8 fusion.4
  341.4 14.5 %gate_back.2 = (bf16[1024,2816]{1,0:T(8,128)(2,1)}, bf16[1024,2048]{1,0:T(8,128)(2,1)S(1)}) custom-call(bf16[1024,2048]{1,0:T(8,128)(2,1)} %copy-done.14, f32[1024,1]{1,0:T(8,128)S(1)} %bitcast_select_fusion.scale, f32[1024,2816]{1,0:T(8,128)} %copy-done.15, bf16[1408,2048]{1,0:T(8,128)(2,1)} %bitcast.156), custom_call_target="tpu_custom_call" | custom-call | flops 5905580032 | bytes 31457280 | tf_op jit(solution)/shard_map/gate_back/pallas_call | solution.py:1487
  356.0 8.0 %convolution_convert_fusion = bf16[1408,2048]{1,0:T(8,128)(2,1)} fusion(bf16[1024,1408]{1,0:T(8,128)(2,1)S(1)} %copy-done.30, bf16[1024,2048]{1,0:T(8,128)(2,1)S(1)} %get-tuple-element.97), kind=kOutput, calls=%fused_computation.11 | convolution fusion | flops 5908463616 | bytes 12845056 | tf_op jit(solution)/shard_map/dot_general | solution.py:1588
  364.0 18.5 %fusion.7 = bf16[1024,2048]{1,0:T(8,128)(2,1)} fusion(bf16[1024,2816]{1,0:T(8,128)(2,1)} %get-tuple-element.90.grads, bf16[1,2048,2816]{2,1,0:T(8,128)(2,1)} %all-gather.13.cloned.1.call-done), kind=kOutput, calls=%fused_computation.17 | convolution fusion | flops 11813257216 | bytes 21495808 | tf_op jit(solution)/shard_map/dot_general | solution.py:1594
  382.6 9.0 %gate_back.3 = (bf16[1024,1408]{1,0:T(8,128)(2,1)S(1)}, bf16[1024,2048]{1,0:T(8,128)(2,1)}) custom-call(bf16[1024,2048]{1,0:T(8,128)(2,1)} %copy-done.14, f32[1024,1]{1,0:T(8,128)S(1)} %get-tuple-element.132.scale, f32[1024,1408]{1,0:T(8,128)} %copy-done.18, bf16[704,2048]{1,0:T(8,128)(2,1)} %bitcast.167), custom_call_target="tpu_custom_call" | custom-call | flops 2952790016 | bytes 19922944 | tf_op jit(solution)/shard_map/gate_back/pallas_call | solution.py:1487
  393.1 8.6 %convolution_convert_fusion.1 = bf16[2048,1408]{1,0:T(8,128)(2,1)} fusion(bf16[1024,2048]{1,0:T(8,128)(2,1)S(1)} %bitcast.152, bf16[1024,1408]{1,0:T(8,128)(2,1)S(1)} %get-tuple-element.92), kind=kOutput, calls=%fused_computation.12 | convolution fusion | flops 5908463616 | bytes 12845056 | tf_op jit(solution)/shard_map/dot_general | solution.py:1588
  401.8 11.6 %add_convert_fusion = bf16[1024,2048]{1,0:T(8,128)(2,1)} fusion(bf16[1024,2048]{1,0:T(8,128)(2,1)} %fusion.7, bf16[1024,1408]{1,0:T(8,128)(2,1)} %copy-done.8, bf16[2048,1408]{1,0:T(8,128)(2,1)} %bitcast.190), kind=kOutput, calls=%fused_computation.9 | convolution fusion | flops 5911871488 | bytes 17039360 | tf_op jit(solution)/shard_map/dot_general | solution.py:1594
  414.1 60.3 %line_scatter.3 = (f32[128,2048]{1,0:T(8,128)}, f32[8,8,128]{2,1,0:T(8,128)}, bf16[2048,2816]{1,0:T(8,128)(2,1)}) custom-call(bf16[8,128,2048]{2,1,0:T(8,128)(2,1)} %bitcast.160, f32[8,8,128]{2,1,0:T(8,128)} %pad.18.small, bf16[1024,2048]{1,0:T(8,128)(2,1)} %bitcast.150, bf16[1024,2816]{1,0:T(8,128)(2,1)} %get-tuple-element.90.grads), custom_call_target="tpu_custom_call" | custom-call | tf_op jit(solution)/shard_map/line_scatter/pallas_call | solution.py:717
  488.4 49.7 %product_gather.1 = (bf16[8,128,2048]{2,1,0:T(8,128)(2,1)S(1)}, bf16[704,2048]{1,0:T(8,128)(2,1)S(1)}) custom-call(bf16[128,2048]{1,0:T(8,128)(2,1)S(1)} %get-tuple-element.99.own, bf16[1024,704]{1,0:T(8,128)(2,1)S(1)} %fusion.10.units, bf16[1024,2048]{1,0:T(8,128)(2,1)S(1)} %copy-done.1), custom_call_target="tpu_custom_call" | custom-call | tf_op jit(solution)/shard_map/product_gather/pallas_call | solution.py:864
  542.7 5.8 all-to-all-start.1
  548.5 38.4 %attend_back.1 = (bf16[1024,2048]{1,0:T(8,128)(2,1)}, bf16[2048,768]{1,0:T(8,128)(2,1)}, bf16[256,2048]{1,0:T(8,128)(2,1)}, f32[1,768]{1,0:T(1,128)}, f32[1,2048]{1,0:T(1,128)}) custom-call(bf16[1024,2048]{1,0:T(8,128)(2,1)} %bitcast.145, bf16[256,2048]{1,0:T(8,128)(2,1)} %copy-done.3, bf16[1024,256]{1,0:T(8,128)(2,1)} %copy-done.10, ...), custom_call_target="tpu_custom_call" | custom-call | flops 11274289152 | bytes 36700160 | tf_op jit(solution)/shard_map/attend_back/pallas_call | solution.py:1424
  596.5 3.5 collect_columns.1
  600.1 84.7 %closing.1 = (f32[128,2048]{1,0:T(8,128)}, bf16[8,64,768]{2,1,0:T(8,128)(2,1)}, f32[64,2048]{1,0:T(8,128)}, f32[176,2048]{1,0:T(8,128)}, f32[8,128]{1,0:T(8,128)}) custom-call(bf16[8,128,2048]{2,1,0:T(8,128)(2,1)} %bitcast.159, bf16[4,512,768]{2,1,0:T(8,128)(2,1)} %bitcast.166, bf16[4,128,2048]{2,1,0:T(8,128)(2,1)} %pad_maximum_fusion.1.pair, ...), custom_call_target="tpu_custom_call" | custom-call | tf_op jit(solution)/shard_map/closing/pallas_call | solution.py:1186
  695.0 4.9 bitcast_convert_fusion
  (238 shorter events, 94.8 us)
Async XLA Ops:
  7.2 154.2 %all-gather.7.cloned.1.call-start = ((), (), s32[]{:S(2)}) async-start(), calls=%async_computation.6 | async-start | bytes 1769472 | tf_op jit(solution)/shard_map/all_gather | solution.py:1576
  9.0 152.4 %all-gather.11.cloned.1.call-start = ((), (), s32[]{:S(2)}) async-start(), calls=%async_computation.12 | async-start | bytes 7208960 | tf_op jit(solution)/shard_map/all_gather | solution.py:1576
  9.7 264.4 %all-gather.13.cloned.1.call-start = ((), (), s32[]{:S(2)}) async-start(), calls=%async_computation.13 | async-start | bytes 14417920 | tf_op jit(solution)/shard_map/all_gather | solution.py:1576
  14.5 112.4 %copy-start.49 = (s32[16]{0:T(128)S(1)}, s32[16]{0:T(128)}, u32[]{:S(2)}) copy-start(s32[16]{0:T(128)} %param.19) | copy-start | bytes 196
  110.9 15.7 %copy-start.38 = (bf16[4,8,16,128]{3,2,1,0:T(8,128)(2,1)S(1)}, bf16[4,8,16,128]{3,2,1,0:T(8,128)(2,1)}, u32[]{:S(2)}) copy-start(bf16[4,8,16,128]{3,2,1,0:T(8,128)(2,1)} %get-tuple-element.70) | copy-start | bytes 393220
  110.9 16.1 %copy-start.40 = (s32[8,8,128]{2,1,0:T(8,128)S(1)}, s32[8,8,128]{2,1,0:T(8,128)}, u32[]{:S(2)}) copy-start(s32[8,8,128]{2,1,0:T(8,128)} %get-tuple-element.72) | copy-start | bytes 98308
  114.0 47.3 %all-to-all-start = ((bf16[8,64,1408]{2,1,0:T(8,128)(2,1)}), bf16[8,64,1408]{2,1,0:T(8,128)(2,1)S(1)}, u32[]{:S(2)}, u32[]{:S(2)}) async-start(bf16[8,64,1408]{2,1,0:T(8,128)(2,1)} %deal_columns.1), calls=%async_computation | async-start | bytes 2883584 | tf_op jit(solution)/shard_map/all_to_all | solution.py:1584
  126.6 201.2 %all-gather.9.cloned.1.call-start = ((), (), s32[]{:S(2)}) async-start(), calls=%async_computation.7 | async-start | bytes 2949120 | tf_op jit(solution)/shard_map/all_gather | solution.py:1576
  132.8 80.2 %copy-start.22 = (bf16[1,128,2048]{2,1,0:T(8,128)(2,1)S(1)}, bf16[1,128,2048]{2,1,0:T(8,128)(2,1)}, u32[]{:S(2)}) copy-start(bf16[1,128,2048]{2,1,0:T(8,128)(2,1)} %param.17) | copy-start | bytes 1572868
  161.4 53.8 %copy-start.26 = (bf16[8,64,1408]{2,1,0:T(8,128)(2,1)}, bf16[8,64,1408]{2,1,0:T(8,128)(2,1)S(1)}, u32[]{:S(2)}) copy-start(bf16[8,64,1408]{2,1,0:T(8,128)(2,1)S(1)} %all-to-all-done) | copy-start | bytes 4325380
  213.0 56.0 %copy-start.27 = (bf16[1,128,2048]{2,1,0:T(8,128)(2,1)S(1)}, bf16[1,128,2048]{2,1,0:T(8,128)(2,1)}, u32[]{:S(2)}) copy-start(bf16[1,128,2048]{2,1,0:T(8,128)(2,1)} %param.21) | copy-start | bytes 1572868
  273.8 209.7 %reduce-scatter.7.cloned.1.call-start = ((), (), s32[]{:S(2)}) async-start(), calls=%async_computation.9 | async-start | bytes 4718592 | tf_op jit(solution)/shard_map/reduce_scatter | solution.py:1580
  291.3 17.2 %slice-start = ((s8[5767168]{0:T(1024)(128)(4,1)}), s8[4194304]{0:T(1024)(128)(4,1)S(1)}, s32[]{:S(2)}) async-start(s8[5767168]{0:T(1024)(128)(4,1)} %bitcast.191), calls=%async_computation.14 | async-start | bytes 8388608
  296.6 11.9 %copy-start.29 = (bf16[1024,1408]{1,0:T(8,128)(2,1)}, bf16[1024,1408]{1,0:T(8,128)(2,1)S(1)}, u32[]{:S(2)}) copy-start(bf16[1024,1408]{1,0:T(8,128)(2,1)S(1)} %fusion.6) | copy-start | bytes 8650756
  296.6 11.9 %copy-start.19 = (bf16[8,128,2048]{2,1,0:T(8,128)(2,1)S(1)}, bf16[8,128,2048]{2,1,0:T(8,128)(2,1)}, u32[]{:S(2)}) copy-start(bf16[8,128,2048]{2,1,0:T(8,128)(2,1)} %get-tuple-element.79) | copy-start | bytes 12582916
  296.6 11.9 %slice-start.1 = ((s8[5767168]{0:T(1024)(128)(4,1)}), s8[1572864]{0:T(1024)(128)(4,1)S(1)}, s32[]{:S(2)}) async-start(s8[5767168]{0:T(1024)(128)(4,1)} %bitcast.191), calls=%async_computation.15 | async-start | bytes 3145728
  330.6 10.2 %copy-start.14 = (bf16[1024,2048]{1,0:T(8,128)(2,1)}, bf16[1024,2048]{1,0:T(8,128)(2,1)S(1)}, u32[]{:S(2)}) copy-start(bf16[1024,2048]{1,0:T(8,128)(2,1)S(1)} %pad_maximum_fusion.upstream) | copy-start | bytes 12582916
  340.8 145.4 %reduce-scatter.5.cloned.1.call-start = ((), (), s32[]{:S(2)}) async-start(), calls=%async_computation.8 | async-start | bytes 7208960 | tf_op jit(solution)/shard_map/reduce_scatter | solution.py:1580
  341.4 14.5 %copy-start.30 = (bf16[1024,1408]{1,0:T(8,128)(2,1)S(1)}, bf16[1024,1408]{1,0:T(8,128)(2,1)}, u32[]{:S(2)}) copy-start(bf16[1024,1408]{1,0:T(8,128)(2,1)} %copy-done.29) | copy-start | bytes 8650756
  364.0 178.7 %reduce-scatter.9.cloned.1.call-start = ((), (), s32[]{:S(2)}) async-start(), calls=%async_computation.10 | async-start | bytes 7208960 | tf_op jit(solution)/shard_map/reduce_scatter | solution.py:1580
  382.6 10.6 %copy-start.20 = (bf16[8,128,2048]{2,1,0:T(8,128)(2,1)S(1)}, bf16[8,128,2048]{2,1,0:T(8,128)(2,1)}, u32[]{:S(2)}) copy-start(bf16[8,128,2048]{2,1,0:T(8,128)(2,1)} %get-tuple-element.79) | copy-start | bytes 12582916
  401.7 293.3 %reduce-scatter.11.cloned.1.call-start = ((), (), s32[]{:S(2)}) async-start(), calls=%async_computation.11 | async-start | bytes 14417920 | tf_op jit(solution)/shard_map/reduce_scatter | solution.py:1580
  542.7 52.7 %all-to-all-start.1 = ((bf16[8,64,1408]{2,1,0:T(8,128)(2,1)}), bf16[8,64,1408]{2,1,0:T(8,128)(2,1)S(1)}, u32[]{:S(2)}, u32[]{:S(2)}) async-start(bf16[8,64,1408]{2,1,0:T(8,128)(2,1)} %bitcast.169), calls=%async_computation.4 | async-start | bytes 2883584 | tf_op jit(solution)/shard_map/all_to_all | solution.py:1584
  600.1 90.0 %copy-start.23 = (bf16[1,128,2048]{2,1,0:T(8,128)(2,1)S(1)}, bf16[1,128,2048]{2,1,0:T(8,128)(2,1)}, u32[]{:S(2)}) copy-start(bf16[1,128,2048]{2,1,0:T(8,128)(2,1)} %param.17) | copy-start | bytes 1572868
  (38 other events, 119.5 us)
Sparse Core Ops, SparseCore 0:
  10.8 61.8 all-gather.6
  74.2 47.0 all-gather.10
  122.9 86.0 all-gather.12
  273.9 53.8 all-gather.8
  340.9 87.3 reduce-scatter.6
  430.8 54.4 reduce-scatter.4
  487.8 54.8 reduce-scatter.8
  545.5 116.6 reduce-scatter.10

commit v8 on v7

--- a/solution.py
+++ b/solution.py
@@ -646,9 +646,15 @@
 
 
 def scatter_kernel(
-    ctx_count, part, small, tokens, grads, total, small_in, weight_grad, *refs
+    ctx_count, part, small, far_tokens, far_grads, total, small_in, weight_grad, *refs
 ):
-    *refs, product, store_sem = refs
+    *refs, product, store_sem, tokens, grads, load_sem = refs
+    loads = [
+        pltpu.make_async_copy(source, target, load_sem.at[i])
+        for i, (source, target) in enumerate(((far_tokens, tokens), (far_grads, grads)))
+    ]
+    for copy in loads:
+        copy.start()
     greet_all(ctx_count)
     here = lax.axis_index("ctx")
     starts, waits = spread(
@@ -662,6 +668,8 @@
     pieces = ctx_count // 2
     depth = tokens.shape[1] // pieces
     stores = []
+    for copy in loads:
+        copy.wait()
     for piece in range(pieces):
 
         @pl.loop(0, depth // SPAN)
@@ -712,7 +720,7 @@
         )(part)
     product = (tokens.shape[1], grads.shape[1])
     params = pltpu.CompilerParams(
-        collective_id=call_id, has_side_effects=True, vmem_limit_bytes=56 * 2**20
+        collective_id=call_id, has_side_effects=True, vmem_limit_bytes=40 * 2**20
     )
     return pl.pallas_call(
         functools.partial(scatter_kernel, ctx_count),
@@ -721,12 +729,17 @@
             jax.ShapeDtypeStruct(small.shape, small.dtype),
             jax.ShapeDtypeStruct(product, part.dtype),
         ],
-        in_specs=[VMEM] * 4,
+        in_specs=[VMEM] * 2 + [ANY] * 2,
         out_specs=[VMEM] * 2 + [ANY],
         scratch_shapes=[slots] * 4
         + [dma] * 5
         + [spread_dma] * 2
-        + [pltpu.VMEM(product, part.dtype), pltpu.SemaphoreType.DMA((half,))],
+        + [pltpu.VMEM(product, part.dtype), pltpu.SemaphoreType.DMA((half,))]
+        + [
+            pltpu.VMEM(tokens.shape, tokens.dtype),
+            pltpu.VMEM(grads.shape, grads.dtype),
+            pltpu.SemaphoreType.DMA((2,)),
+        ],
         compiler_params=params,
         name="line_scatter",
     )(part, small, tokens, grads)
@@ -1210,7 +1223,7 @@
         + [dma((ctx_count,))] * 4
         + [dma((4,))] * 2,
         compiler_params=pltpu.CompilerParams(
-            collective_id=call_id, has_side_effects=True, vmem_limit_bytes=56 * 2**20
+            collective_id=call_id, has_side_effects=True, vmem_limit_bytes=36 * 2**20
         ),
         name="closing",
     )(part, weight, pair, plain, small)
@@ -1313,9 +1326,9 @@
     sine,
     columns,
     lines,
-    inputs,
-    normed,
-    weight,
+    far_inputs,
+    far_normed,
+    far_weight,
     part,
     grad_weight,
     grad_out,
@@ -1326,12 +1339,24 @@
     grad_keys,
     grad_values,
     gain_sum,
+    inputs,
+    normed,
+    weight,
+    load_sem,
 ):
     rows, width = branch.shape
     low = jnp.bfloat16
     full = jnp.float32
     wide = queries.shape[1]
     heads = wide // HD
+    loads = [
+        pltpu.make_async_copy(source, target, load_sem.at[i])
+        for i, (source, target) in enumerate(
+            ((far_weight, weight), (far_inputs, inputs), (far_normed, normed))
+        )
+    ]
+    for copy in loads:
+        copy.start()
 
     @pl.loop(0, rows // SPAN)
     def into_heads(index):
@@ -1375,6 +1400,8 @@
 
     gain_sum[...] = jnp.zeros_like(gain_sum)
     grad_bias[...] = jnp.zeros_like(grad_bias)
+    for copy in loads:
+        copy.wait()
 
     @pl.loop(0, rows // SPAN)
     def project_back(index):
@@ -1430,7 +1457,7 @@
             shape((1, 3 * wide), full),
             shape((1, width), full),
         ],
-        in_specs=[VMEM] * 14,
+        in_specs=[VMEM] * 11 + [ANY] * 3,
         out_specs=[VMEM] * 5,
         scratch_shapes=[
             pltpu.VMEM((rows, 3 * wide), low),
@@ -1438,8 +1465,12 @@
             pltpu.VMEM((rows, HD), full),
             pltpu.VMEM((rows, HD), full),
             pltpu.VMEM((1, width), full),
+            pltpu.VMEM(inputs.shape, low),
+            pltpu.VMEM(normed.shape, low),
+            pltpu.VMEM(weight.shape, low),
+            pltpu.SemaphoreType.DMA((3,)),
         ],
-        compiler_params=pltpu.CompilerParams(vmem_limit_bytes=56 * 2**20),
+        compiler_params=pltpu.CompilerParams(vmem_limit_bytes=40 * 2**20),
         cost_estimate=pl.CostEstimate(
             flops=2 * rows * width * 8 * wide + 10 * rows * rows * wide,
             bytes_accessed=35 * 2**20,

time: 723 us -> 726 us (level)
  local copies, waits for them, and re-layouts: 50.1 us -> 66.1 us
  Pallas kernels: 481 us -> 468 us
  waiting for transfers between devices: 9.46 us -> 17.2 us
    unnamed x114 -> x140, local copies, waits for them, and re-layouts: 32.7 us -> 51.2 us
    pallas_call x1, Pallas kernels: 38.4 us -> 30.4 us  [attend_back(): pl.pallas_call(attend_back_kernel, out_shape=[shape((rows, width), low),...]
    reduce_scatter x4, waiting for transfers between devices: 0.93 us -> 8.59 us  [reduce_over(): return lax.psum_scatter(array, axis, scatter_dimension=dim, tiled=True)]
  transfers between devices with their start and end apart: 10 -> 10, of which waited for: 3 -> 4; matrix products, arithmetic and copies ran while one was open for 19% -> 18% of each run, Pallas kernels for 68% -> 65%
where the time goes in v8:
time: 726 us; the launch traced here: 715 us
  Pallas kernels  468 us (64%)
  matrix products  95.7 us (13%)
  local copies, waits for them, and re-layouts  66.1 us (9%)
  other arithmetic  33.8 us (5%)
  starting transfers between devices  18.9 us (3%)
  waiting for transfers between devices  17.2 us (2%)
  between operations  15.5 us (2%)
    pallas_call x1, Pallas kernels, opening(): pl.pallas_call(functools.partial(opening_kernel, ctx_count), out_shape=[o...  95 us
    pallas_call x1, Pallas kernels, closing(): pl.pallas_call(functools.partial(closing_kernel, ctx_count), out_shape=[j...  83.5 us
    pallas_call x1, Pallas kernels, line_scatter(): pl.pallas_call(functools.partial(scatter_kernel, ctx_count), out_shape=[t...  54.6 us
    pallas_call x1, Pallas kernels, line_gather(): pl.pallas_call(functools.partial(gather_kernel, ctx_count // 2 - 1, count...  53.8 us
    unnamed x140, local copies, waits for them, and re-layouts  51.2 us
    pallas_call x1, Pallas kernels, product_gather(): pl.pallas_call(functools.partial(product_kernel, ctx_count // 2 - 1), out...  50.7 us
    pallas_call x1, Pallas kernels, line_scatter(): pl.pallas_call(functools.partial(line_scatter_kernel, half - 1), out_shap...  48.8 us
    dot_general x5, matrix products, matmul_low(): return jnp.dot(left, right, preferred_element_type=jnp.float32)  44.2 us
  transfers between devices with their start and end apart: 10, of which 4 were waited for; matrix products, arithmetic and copies ran while one was open for 18% of the time, Pallas kernels for 65%

profile of v8, /device:TPU:0, one launch (start us, length us, event | category | flops | bytes accessed | tf_op | source)
XLA Modules:
  0.0 714.6 jit_solution(3405400392606483882)
XLA Ops:
  15.9 95.0 %opening.1 = (bf16[8,128,2048]{2,1,0:T(8,128)(2,1)}, bf16[4,8,64,768]{3,2,1,0:T(8,128)(2,1)}, bf16[4,2,64,2048]{3,2,1,0:T(8,128)(2,1)}, bf16[4,8,16,128]{3,2,1,0:T(8,128)(2,1)}, s32[8,8,128]{2,1,0:T(8,128)}) custom-call(bf16[128,2048]{1,0:T(8,128)(2,1)} %bitcast.158, bf16[8,64,768]{2,1,0:T(8,128)(2,1)} %reshape.359.qkv_own, bf16[64,2048]{1,0:T(8,128)(2,1)} %out_own.1, ...), custom_call_target="tpu_custom_call" | custom-call | tf_op jit(solution)/shard_map/opening/pallas_call | solution.py:1027
  114.0 12.5 %all-to-all-start = ((bf16[8,64,1408]{2,1,0:T(8,128)(2,1)}), bf16[8,64,1408]{2,1,0:T(8,128)(2,1)S(1)}, u32[]{:S(2)}, u32[]{:S(2)}) async-start(bf16[8,64,1408]{2,1,0:T(8,128)(2,1)} %deal_columns.1), calls=%async_computation | async-start | bytes 2883584 | tf_op jit(solution)/shard_map/all_to_all | solution.py:1615
  132.8 18.0 %attend.1 = (bf16[1024,2048]{1,0:T(8,128)(2,1)S(1)}, bf16[1024,256]{1,0:T(8,128)(2,1)S(1)}, bf16[1024,256]{1,0:T(8,128)(2,1)S(1)}, bf16[1024,256]{1,0:T(8,128)(2...) custom-call(bf16[1024,2048]{1,0:T(8,128)(2,1)} %bitcast.194, ...), custom_call_target="tpu_custom_call" | custom-call | flops 5368709120 | bytes 20971520 | tf_op jit(solution)/shard_map/attend/pallas_call | solution.py:1300
  156.9 4.5 all-to-all-done
  164.1 48.8 %line_scatter.2 = f32[128,2048]{1,0:T(8,128)S(1)} custom-call(bf16[8,128,2048]{2,1,0:T(8,128)(2,1)S(1)} %bitcast.149), custom_call_target="tpu_custom_call" | custom-call | tf_op jit(solution)/shard_map/line_scatter/pallas_call | solution.py:712
  215.1 53.8 %line_gather.1 = (bf16[8,128,2048]{2,1,0:T(8,128)(2,1)}, bf16[4,512,1408]{2,1,0:T(8,128)(2,1)}, bf16[4,176,2048]{2,1,0:T(8,128)(2,1)}) custom-call(bf16[128,2048]{1,0:T(8,128)(2,1)} %multiply_convert_fusion.refs_0_, bf16[512,1408]{1,0:T(8,128)(2,1)} %bitcast.159, bf16[176,2048]{1,0:T(8,128)(2,1)} %refs_2_.1), custom_call_target="tpu_custom_call" | custom-call | tf_op jit(solution)/shard_map/line_gather/pallas_call | solution.py:896
  274.0 17.2 %fusion.2.gate_up = f32[1024,2816]{1,0:T(8,128)S(1)} fusion(bf16[1024,2048]{1,0:T(8,128)(2,1)} %bitcast.143, bf16[1,2048,2816]{2,1,0:T(8,128)(2,1)} %all-gather.13.cloned.1.call-done), kind=kOutput, calls=%fused_computation.3 | convolution fusion | flops 11811160064 | bytes 27262976 | tf_op jit(solution)/shard_map/dot_general | solution.py:49
  296.5 11.7 %convert_convert_fusion = f32[1024,2048]{1,0:T(8,128)} fusion(bf16[1024,1408]{1,0:T(8,128)(2,1)S(1)} %fusion.6, bf16[1408,2048]{1,0:T(8,128)(2,1)} %bitcast.160), kind=kOutput, calls=%fused_computation.16 | convolution fusion | flops 5909774336 | bytes 17039360 | tf_op jit(solution)/shard_map/dot_general | solution.py:49
  308.3 6.7 fusion.40.gate_up
  319.3 6.0 fusion.41
  334.0 7.0 fusion.4
  341.7 14.5 %gate_back.2 = (bf16[1024,2816]{1,0:T(8,128)(2,1)}, bf16[1024,2048]{1,0:T(8,128)(2,1)S(1)}) custom-call(bf16[1024,2048]{1,0:T(8,128)(2,1)} %copy-done.35, f32[1024,1]{1,0:T(8,128)S(1)} %bitcast_select_fusion.scale, f32[1024,2816]{1,0:T(8,128)} %copy-done.36, bf16[1408,2048]{1,0:T(8,128)(2,1)} %bitcast.161), custom_call_target="tpu_custom_call" | custom-call | flops 5905580032 | bytes 31457280 | tf_op jit(solution)/shard_map/gate_back/pallas_call | solution.py:1518
  356.2 8.1 %convolution_convert_fusion = bf16[1408,2048]{1,0:T(8,128)(2,1)} fusion(bf16[1024,1408]{1,0:T(8,128)(2,1)S(1)} %copy-done.46, bf16[1024,2048]{1,0:T(8,128)(2,1)S(1)} %get-tuple-element.97), kind=kOutput, calls=%fused_computation.11 | convolution fusion | flops 5908463616 | bytes 12845056 | tf_op jit(solution)/shard_map/dot_general | solution.py:1619
  364.3 18.5 %fusion.7 = bf16[1024,2048]{1,0:T(8,128)(2,1)} fusion(bf16[1024,2816]{1,0:T(8,128)(2,1)} %get-tuple-element.90.far_grads, bf16[1,2048,2816]{2,1,0:T(8,128)(2,1)} %all-gather.13.cloned.1.call-done), kind=kOutput, calls=%fused_computation.17 | convolution fusion | flops 11813257216 | bytes 21495808 | tf_op jit(solution)/shard_map/dot_general | solution.py:1625
  382.8 9.0 %gate_back.3 = (bf16[1024,1408]{1,0:T(8,128)(2,1)S(1)}, bf16[1024,2048]{1,0:T(8,128)(2,1)}) custom-call(bf16[1024,2048]{1,0:T(8,128)(2,1)} %copy-done.35, f32[1024,1]{1,0:T(8,128)S(1)} %get-tuple-element.132.scale, f32[1024,1408]{1,0:T(8,128)} %copy-done.39, bf16[704,2048]{1,0:T(8,128)(2,1)} %bitcast.169), custom_call_target="tpu_custom_call" | custom-call | flops 2952790016 | bytes 19922944 | tf_op jit(solution)/shard_map/gate_back/pallas_call | solution.py:1518
  393.4 8.6 %convolution_convert_fusion.1 = bf16[2048,1408]{1,0:T(8,128)(2,1)} fusion(bf16[1024,2048]{1,0:T(8,128)(2,1)S(1)} %bitcast.145, bf16[1024,1408]{1,0:T(8,128)(2,1)S(1)} %get-tuple-element.92), kind=kOutput, calls=%fused_computation.12 | convolution fusion | flops 5908463616 | bytes 12845056 | tf_op jit(solution)/shard_map/dot_general | solution.py:1619
  402.1 10.4 %add_convert_fusion = bf16[1024,2048]{1,0:T(8,128)(2,1)S(1)} fusion(bf16[1024,2048]{1,0:T(8,128)(2,1)} %fusion.7, bf16[1024,1408]{1,0:T(8,128)(2,1)} %copy-done.25, bf16[2048,1408]{1,0:T(8,128)(2,1)} %bitcast.190), kind=kOutput, calls=%fused_computation.9 | convolution fusion | flops 5911871488 | bytes 17039360 | tf_op jit(solution)/shard_map/dot_general | solution.py:1625
  412.6 54.6 %line_scatter.3 = (f32[128,2048]{1,0:T(8,128)S(1)}, f32[8,8,128]{2,1,0:T(8,128)S(1)}, bf16[2048,2816]{1,0:T(8,128)(2,1)}) custom-call(bf16[8,128,2048]{2,1,0:T(8,128)(2,1)S(1)} %bitcast.148, f32[8,8,128]{2,1,0:T(8,128)S(1)} %pad.18.small, bf16[1024,2048]{1,0:T(8,128)(2,1)S(1)} %bitcast.146, bf16[1024,2816]{1,0:T(8,128)(2,1)} %get-tuple-element.90.far_grads), custom_call_target="tpu_custom_call" | custom-call | tf_op jit(solution)/shard_map/line_scatter/pallas_call | solution.py:725
  478.0 7.6 %reduce-scatter.5.cloned.1.call-done = bf16[352,2048]{1,0:T(8,128)(2,1)} async-done(((bf16[1408,2048]{1,0:T(8,128)(2,1)}), bf16[352,2048]{1,0:T(8,128)(2,1)}) %reduce-scatter.5.cloned.1.call-update) | async-done | bytes 1441808 | tf_op jit(solution)/shard_map/reduce_scatter | solution.py:1611
  487.8 50.7 %product_gather.1 = (bf16[8,128,2048]{2,1,0:T(8,128)(2,1)S(1)}, bf16[704,2048]{1,0:T(8,128)(2,1)S(1)}) custom-call(bf16[128,2048]{1,0:T(8,128)(2,1)S(1)} %get-tuple-element.99.own, bf16[1024,704]{1,0:T(8,128)(2,1)S(1)} %fusion.10.units, bf16[1024,2048]{1,0:T(8,128)(2,1)S(1)} %copy-done.5), custom_call_target="tpu_custom_call" | custom-call | tf_op jit(solution)/shard_map/product_gather/pallas_call | solution.py:877
  543.0 5.8 all-to-all-start.1
  558.8 30.4 %attend_back.1 = (bf16[1024,2048]{1,0:T(8,128)(2,1)}, bf16[2048,768]{1,0:T(8,128)(2,1)S(1)}, bf16[256,2048]{1,0:T(8,128)(2,1)S(1)}, f32[1,768]{1,0:T(1,128)S(1)}, f32[1,2048]{1,0:T(1,128)S(1)}) custom-call(bf16[1024,2048]{1,0:T(8,128)(2,1)} %bitcast.155, bf16[256,2048]{1,0:T(8,128)(2,1)S(1)} %copy-done.13, bf16[1024,256]{1,0:T(8,128)(2,1)S(1)} %copy-done.28, ...), custom_call_target="tpu_custom_call" | custom-call | flops 11274289152 | bytes 36700160 | tf_op jit(solution)/shard_map/attend_back/pallas_call | solution.py:1451
  605.5 83.5 %closing.1 = (f32[128,2048]{1,0:T(8,128)S(1)}, bf16[8,64,768]{2,1,0:T(8,128)(2,1)S(1)}, f32[64,2048]{1,0:T(8,128)S(1)}, f32[176,2048]{1,0:T(8,128)S(1)}, f32[8,128]{1,0:T(8,128)S(1)}) custom-call(bf16[8,128,2048]{2,1,0:T(8,128)(2,1)S(1)} %bitcast.147, bf16[4,512,768]{2,1,0:T(8,128)(2,1)S(1)} %bitcast.150, bf16[4,128,2048]{2,1,0:T(8,128)(2,1)S(1)} %pad_maximum_fusion.1.pair, ...), custom_call_target="tpu_custom_call" | custom-call | tf_op jit(solution)/shard_map/closing/pallas_call | solution.py:1199
  700.6 4.9 bitcast_convert_fusion
  (264 shorter events, 111.5 us)
Async XLA Ops:
  7.2 154.2 %all-gather.7.cloned.1.call-start = ((), (), s32[]{:S(2)}) async-start(), calls=%async_computation.6 | async-start | bytes 1769472 | tf_op jit(solution)/shard_map/all_gather | solution.py:1607
  9.0 152.4 %all-gather.11.cloned.1.call-start = ((), (), s32[]{:S(2)}) async-start(), calls=%async_computation.12 | async-start | bytes 7208960 | tf_op jit(solution)/shard_map/all_gather | solution.py:1607
  9.7 264.3 %all-gather.13.cloned.1.call-start = ((), (), s32[]{:S(2)}) async-start(), calls=%async_computation.13 | async-start | bytes 14417920 | tf_op jit(solution)/shard_map/all_gather | solution.py:1607
  14.5 112.4 %copy-start.62 = (s32[16]{0:T(128)S(1)}, s32[16]{0:T(128)}, u32[]{:S(2)}) copy-start(s32[16]{0:T(128)} %param.19) | copy-start | bytes 196
  110.9 15.7 %copy-start.51 = (bf16[4,8,16,128]{3,2,1,0:T(8,128)(2,1)S(1)}, bf16[4,8,16,128]{3,2,1,0:T(8,128)(2,1)}, u32[]{:S(2)}) copy-start(bf16[4,8,16,128]{3,2,1,0:T(8,128)(2,1)} %get-tuple-element.70) | copy-start | bytes 393220
  110.9 16.1 %copy-start.53 = (s32[8,8,128]{2,1,0:T(8,128)S(1)}, s32[8,8,128]{2,1,0:T(8,128)}, u32[]{:S(2)}) copy-start(s32[8,8,128]{2,1,0:T(8,128)} %get-tuple-element.72) | copy-start | bytes 98308
  114.0 47.3 %all-to-all-start = ((bf16[8,64,1408]{2,1,0:T(8,128)(2,1)}), bf16[8,64,1408]{2,1,0:T(8,128)(2,1)S(1)}, u32[]{:S(2)}, u32[]{:S(2)}) async-start(bf16[8,64,1408]{2,1,0:T(8,128)(2,1)} %deal_columns.1), calls=%async_computation | async-start | bytes 2883584 | tf_op jit(solution)/shard_map/all_to_all | solution.py:1615
  126.6 201.3 %all-gather.9.cloned.1.call-start = ((), (), s32[]{:S(2)}) async-start(), calls=%async_computation.7 | async-start | bytes 2949120 | tf_op jit(solution)/shard_map/all_gather | solution.py:1607
  132.8 80.1 %copy-start.41 = (bf16[1,128,2048]{2,1,0:T(8,128)(2,1)S(1)}, bf16[1,128,2048]{2,1,0:T(8,128)(2,1)}, u32[]{:S(2)}) copy-start(bf16[1,128,2048]{2,1,0:T(8,128)(2,1)} %param.17) | copy-start | bytes 1572868
  161.4 53.8 %copy-start.43 = (bf16[8,64,1408]{2,1,0:T(8,128)(2,1)}, bf16[8,64,1408]{2,1,0:T(8,128)(2,1)S(1)}, u32[]{:S(2)}) copy-start(bf16[8,64,1408]{2,1,0:T(8,128)(2,1)S(1)} %all-to-all-done) | copy-start | bytes 4325380
  212.9 56.0 %copy-start.44 = (bf16[1,128,2048]{2,1,0:T(8,128)(2,1)S(1)}, bf16[1,128,2048]{2,1,0:T(8,128)(2,1)}, u32[]{:S(2)}) copy-start(bf16[1,128,2048]{2,1,0:T(8,128)(2,1)} %param.21) | copy-start | bytes 1572868
  273.7 201.2 %reduce-scatter.7.cloned.1.call-start = ((), (), s32[]{:S(2)}) async-start(), calls=%async_computation.9 | async-start | bytes 4718592 | tf_op jit(solution)/shard_map/reduce_scatter | solution.py:1611
  291.2 17.1 %slice-start = ((s8[5767168]{0:T(1024)(128)(4,1)}), s8[4194304]{0:T(1024)(128)(4,1)S(1)}, s32[]{:S(2)}) async-start(s8[5767168]{0:T(1024)(128)(4,1)} %bitcast.191), calls=%async_computation.14 | async-start | bytes 8388608
  296.5 11.7 %copy-start.45 = (bf16[1024,1408]{1,0:T(8,128)(2,1)}, bf16[1024,1408]{1,0:T(8,128)(2,1)S(1)}, u32[]{:S(2)}) copy-start(bf16[1024,1408]{1,0:T(8,128)(2,1)S(1)} %fusion.6) | copy-start | bytes 8650756
  296.5 11.7 %copy-start = (bf16[8,128,2048]{2,1,0:T(8,128)(2,1)S(1)}, bf16[8,128,2048]{2,1,0:T(8,128)(2,1)}, u32[]{:S(2)}) copy-start(bf16[8,128,2048]{2,1,0:T(8,128)(2,1)} %get-tuple-element.79) | copy-start | bytes 12582916
  296.5 11.7 %slice-start.1 = ((s8[5767168]{0:T(1024)(128)(4,1)}), s8[1572864]{0:T(1024)(128)(4,1)S(1)}, s32[]{:S(2)}) async-start(s8[5767168]{0:T(1024)(128)(4,1)} %bitcast.191), calls=%async_computation.15 | async-start | bytes 3145728
  341.0 144.6 %reduce-scatter.5.cloned.1.call-start = ((), (), s32[]{:S(2)}) async-start(), calls=%async_computation.8 | async-start | bytes 7208960 | tf_op jit(solution)/shard_map/reduce_scatter | solution.py:1611
  341.6 14.5 %copy-start.46 = (bf16[1024,1408]{1,0:T(8,128)(2,1)S(1)}, bf16[1024,1408]{1,0:T(8,128)(2,1)}, u32[]{:S(2)}) copy-start(bf16[1024,1408]{1,0:T(8,128)(2,1)} %copy-done.45) | copy-start | bytes 8650756
  364.2 178.8 %reduce-scatter.9.cloned.1.call-start = ((), (), s32[]{:S(2)}) async-start(), calls=%async_computation.10 | async-start | bytes 7208960 | tf_op jit(solution)/shard_map/reduce_scatter | solution.py:1611
  382.8 10.6 %copy-start.1 = (bf16[8,128,2048]{2,1,0:T(8,128)(2,1)S(1)}, bf16[8,128,2048]{2,1,0:T(8,128)(2,1)}, u32[]{:S(2)}) copy-start(bf16[8,128,2048]{2,1,0:T(8,128)(2,1)} %get-tuple-element.79) | copy-start | bytes 12582916
  402.0 298.5 %reduce-scatter.11.cloned.1.call-start = ((), (), s32[]{:S(2)}) async-start(), calls=%async_computation.11 | async-start | bytes 14417920 | tf_op jit(solution)/shard_map/reduce_scatter | solution.py:1611
  402.1 10.5 %copy-start.2 = (bf16[8,128,2048]{2,1,0:T(8,128)(2,1)S(1)}, bf16[8,128,2048]{2,1,0:T(8,128)(2,1)}, u32[]{:S(2)}) copy-start(bf16[8,128,2048]{2,1,0:T(8,128)(2,1)} %get-tuple-element.79) | copy-start | bytes 12582916
  487.8 61.0 %copy-start.13 = (bf16[256,2048]{1,0:T(8,128)(2,1)S(1)}, bf16[256,2048]{1,0:T(8,128)(2,1)}, u32[]{:S(2)}) copy-start(bf16[256,2048]{1,0:T(8,128)(2,1)} %copy-done.12) | copy-start | bytes 3145732
  543.0 53.0 %all-to-all-start.1 = ((bf16[8,64,1408]{2,1,0:T(8,128)(2,1)}), bf16[8,64,1408]{2,1,0:T(8,128)(2,1)}, u32[]{:S(2)}, u32[]{:S(2)}) async-start(bf16[8,64,1408]{2,1,0:T(8,128)(2,1)} %bitcast.171), calls=%async_computation.4 | async-start | bytes 2883584 | tf_op jit(solution)/shard_map/all_to_all | solution.py:1615
  (51 other events, 135.3 us)
Sparse Core Ops, SparseCore 0:
  10.8 61.8 all-gather.6
  74.2 47.0 all-gather.10
  122.9 85.9 all-gather.12
  273.8 53.9 all-gather.8
  341.1 87.4 reduce-scatter.6
  431.2 54.3 reduce-scatter.4
  488.1 54.8 reduce-scatter.8
  545.8 114.5 reduce-scatter.10

commit v9 on v8

--- a/solution.py
+++ b/solution.py
@@ -720,7 +720,7 @@
         )(part)
     product = (tokens.shape[1], grads.shape[1])
     params = pltpu.CompilerParams(
-        collective_id=call_id, has_side_effects=True, vmem_limit_bytes=40 * 2**20
+        collective_id=call_id, has_side_effects=True, vmem_limit_bytes=56 * 2**20
     )
     return pl.pallas_call(
         functools.partial(scatter_kernel, ctx_count),
@@ -1223,7 +1223,7 @@
         + [dma((ctx_count,))] * 4
         + [dma((4,))] * 2,
         compiler_params=pltpu.CompilerParams(
-            collective_id=call_id, has_side_effects=True, vmem_limit_bytes=36 * 2**20
+            collective_id=call_id, has_side_effects=True, vmem_limit_bytes=56 * 2**20
         ),
         name="closing",
     )(part, weight, pair, plain, small)
@@ -1470,7 +1470,7 @@
             pltpu.VMEM(weight.shape, low),
             pltpu.SemaphoreType.DMA((3,)),
         ],
-        compiler_params=pltpu.CompilerParams(vmem_limit_bytes=40 * 2**20),
+        compiler_params=pltpu.CompilerParams(vmem_limit_bytes=56 * 2**20),
         cost_estimate=pl.CostEstimate(
             flops=2 * rows * width * 8 * wide + 10 * rows * rows * wide,
             bytes_accessed=35 * 2**20,
@@ -1711,9 +1711,10 @@
     row_seg = numbers[:, number_count - 1].reshape(row_len)
     routed_here = jnp.any(numbers[:, : number_count - 1] == ctx_rank, axis=1).reshape(row_len)
 
-    shared_in_weight, numbers = lax.optimization_barrier((shared_in_weight, numbers))
     expert_outer = over("fsdp", expert_out_weight[0])
-    early_upstream = over("ctx", out_grad.reshape(tokens_dev, width)[:, :early])
+    shared_in_weight, numbers, expert_outer = lax.optimization_barrier(
+        (shared_in_weight, numbers, expert_outer)
+    )
     inner_parts = deal_columns(shared_in_weight, ctx_count, 2 * fsdp_count)
     expert_inner = over("fsdp", expert_in_weight[0])
     inner_parts = exchange(inner_parts)
@@ -1748,12 +1749,14 @@
         key_marks,
         out_c,
     )
-    branch_part, inner_parts, early_upstream, expert_outer = lax.optimization_barrier(
-        (branch_part, inner_parts, early_upstream, expert_outer)
-    )
+    branch_part, inner_parts = lax.optimization_barrier((branch_part, inner_parts))
     branch = line_scatter(ctx_count, 2, branch_part.reshape(ctx_count, tokens_dev, width))
     middle = inputs + branch
     normed_ffn = rms_scale(middle, gain_ffn).astype(low)
+    normed_ffn, early_grad, expert_inner = lax.optimization_barrier(
+        (normed_ffn, out_grad, expert_inner)
+    )
+    early_upstream = over("ctx", early_grad.reshape(tokens_dev, width)[:, :early])
 
     row_ffn, inner_c, outer_c = line_gather(
         ctx_count,
@@ -1763,7 +1766,9 @@
         shared_out_weight,
     )
     row_ffn = row_ffn.reshape(row_len, width)
-    row_ffn, late_grad = lax.optimization_barrier((row_ffn, out_grad))
+    row_ffn, late_grad, early_upstream = lax.optimization_barrier(
+        (row_ffn, out_grad, early_upstream)
+    )
     late_upstream = over("ctx", late_grad.reshape(tokens_dev, width)[:, early:])
     inner_c = inner_c.reshape(width, 2 * shared_width)
     outer_c = outer_c.reshape(shared_width, width)
@@ -1832,9 +1837,7 @@
     grad_middle_norm, grad_gain_ffn = norm_pull(grad_normed)
     grad_middle = out_grad.reshape(tokens_dev, width).astype(full) + grad_middle_norm
 
-    grad_branch, sum_expert_outer, hidden_out = lax.optimization_barrier(
-        (grad_middle.astype(low), sum_expert_outer, hidden_out)
-    )
+    grad_branch, hidden_out = lax.optimization_barrier((grad_middle.astype(low), hidden_out))
     row_branch, grad_outer = product_gather(
         ctx_count, 3, grad_branch, shared_hidden, grad_shared_out
     )
@@ -1864,7 +1867,9 @@
     padded_out = jnp.concatenate(
         [jnp.where(side == p, grad_out_c, jnp.zeros_like(grad_out_c)) for p in range(2)], axis=0
     )
-    grad_attn_part, sum_inner = lax.optimization_barrier((grad_attn_part, sum_inner))
+    grad_attn_part, sum_inner, sum_expert_outer = lax.optimization_barrier(
+        (grad_attn_part, sum_inner, sum_expert_outer)
+    )
     grad_bias_c = grad_bias_c.reshape(3, 1, 2, HD)
     mine = (jnp.arange(ctx_count) == ctx_rank)[None, :, None, None]
     places_of = [head_order.index(h) for h in range(head_count)]

time: 726 us -> 737 us (1.015)
  waiting for transfers between devices: 17.2 us -> 40.3 us
  local copies, waits for them, and re-layouts: 66.1 us -> 46.6 us
  starting transfers between devices: 18.9 us -> 8.58 us
  Pallas kernels: 468 us -> 476 us
    all_gather x4, waiting for transfers between devices: 2.64 us -> 33.3 us  [over(): return lax.all_gather(array, axis, axis=dim, tiled=True)]
    unnamed x140 -> x112, local copies, waits for them, and re-layouts: 51.2 us -> 29.3 us
    pallas_call x1, Pallas kernels: 95 us -> 76.5 us  [opening(): pl.pallas_call(functools.partial(opening_kernel, ctx_count), out_shape=[o...]
    pallas_call x1, Pallas kernels: 83.5 us -> 98.8 us  [closing(): pl.pallas_call(functools.partial(closing_kernel, ctx_count), out_shape=[j...]
    pallas_call x1, Pallas kernels: 53.8 us -> 67.2 us  [line_gather(): pl.pallas_call(functools.partial(gather_kernel, ctx_count // 2 - 1, count...]
    all_to_all x2, starting transfers between devices: 18.3 us -> 7.15 us  [exchange(): return lax.all_to_all(array, 'ctx', split_axis=0, concat_axis=0, tiled=True)]
    reduce_scatter x4, waiting for transfers between devices: 8.59 us -> 0.02 us  [reduce_over(): return lax.psum_scatter(array, axis, scatter_dimension=dim, tiled=True)]
  transfers between devices with their start and end apart: 10 -> 10, of which waited for: 4 -> 2; matrix products, arithmetic and copies ran while one was open for 18% -> 16% of each run, Pallas kernels for 65% -> 65%
where the time goes in v9:
time: 737 us; the launch traced here: 727 us
  Pallas kernels  476 us (65%)
  matrix products  103 us (14%)
  local copies, waits for them, and re-layouts  46.6 us (6%)
  waiting for transfers between devices  40.3 us (5%)
  other arithmetic  38.1 us (5%)
  between operations  15.1 us (2%)
  starting transfers between devices  8.58 us (1%)
    pallas_call x1, Pallas kernels, closing(): pl.pallas_call(functools.partial(closing_kernel, ctx_count), out_shape=[j...  98.8 us
    pallas_call x1, Pallas kernels, opening(): pl.pallas_call(functools.partial(opening_kernel, ctx_count), out_shape=[o...  76.5 us
    pallas_call x1, Pallas kernels, line_gather(): pl.pallas_call(functools.partial(gather_kernel, ctx_count // 2 - 1, count...  67.2 us
    pallas_call x1, Pallas kernels, line_scatter(): pl.pallas_call(functools.partial(scatter_kernel, ctx_count), out_shape=[t...  57.8 us
    pallas_call x1, Pallas kernels, line_scatter(): pl.pallas_call(functools.partial(line_scatter_kernel, half - 1), out_shap...  48.9 us
    dot_general x5, matrix products, matmul_low(): return jnp.dot(left, right, preferred_element_type=jnp.float32)  47.4 us
    pallas_call x1, Pallas kernels, product_gather(): pl.pallas_call(functools.partial(product_kernel, ctx_count // 2 - 1), out...  44.8 us
    dot_general x4, matrix products, dot_transposed(): lax.dot_general(left, right, (((1,), (1,)), ((), ())), preferred_element_...  35.9 us
  transfers between devices with their start and end apart: 10, of which 2 were waited for; matrix products, arithmetic and copies ran while one was open for 16% of the time, Pallas kernels for 65%

profile of v9, /device:TPU:0, one launch (start us, length us, event | category | flops | bytes accessed | tf_op | source)
XLA Modules:
  0.0 727.4 jit_solution(10415127360184844260)
XLA Ops:
  14.1 76.5 %opening.1 = (bf16[8,128,2048]{2,1,0:T(8,128)(2,1)}, bf16[4,8,64,768]{3,2,1,0:T(8,128)(2,1)}, bf16[4,2,64,2048]{3,2,1,0:T(8,128)(2,1)}, bf16[4,8,16,128]{3,2,1,0:T(8,128)(2,1)}, s32[8,8,128]{2,1,0:T(8,128)}) custom-call(bf16[128,2048]{1,0:T(8,128)(2,1)} %bitcast.151, bf16[8,64,768]{2,1,0:T(8,128)(2,1)} %reshape.360.qkv_own, bf16[64,2048]{1,0:T(8,128)(2,1)} %out_own.1, ...), custom_call_target="tpu_custom_call" | custom-call | tf_op jit(solution)/shard_map/opening/pallas_call | solution.py:1027
  93.9 3.6 all-to-all-start
  103.2 17.6 %attend.1 = (bf16[1024,2048]{1,0:T(8,128)(2,1)S(1)}, bf16[1024,256]{1,0:T(8,128)(2,1)S(1)}, bf16[1024,256]{1,0:T(8,128)(2,1)S(1)}, bf16[1024,256]{1,0:T(8,128)(2...) custom-call(bf16[1024,2048]{1,0:T(8,128)(2,1)} %bitcast.192, ...), custom_call_target="tpu_custom_call" | custom-call | flops 5368709120 | bytes 20971520 | tf_op jit(solution)/shard_map/attend/pallas_call | solution.py:1300
  126.9 5.5 all-to-all-done
  135.2 48.9 %line_scatter.2 = f32[128,2048]{1,0:T(8,128)S(1)} custom-call(bf16[8,128,2048]{2,1,0:T(8,128)(2,1)S(1)} %bitcast.140), custom_call_target="tpu_custom_call" | custom-call | tf_op jit(solution)/shard_map/line_scatter/pallas_call | solution.py:712
  187.7 67.2 %line_gather.1 = (bf16[8,128,2048]{2,1,0:T(8,128)(2,1)}, bf16[4,512,1408]{2,1,0:T(8,128)(2,1)}, bf16[4,176,2048]{2,1,0:T(8,128)(2,1)}) custom-call(bf16[128,2048]{1,0:T(8,128)(2,1)} %multiply_convert_fusion.refs_0_, bf16[512,1408]{1,0:T(8,128)(2,1)} %bitcast.152, bf16[176,2048]{1,0:T(8,128)(2,1)} %refs_2_.1), custom_call_target="tpu_custom_call" | custom-call | tf_op jit(solution)/shard_map/line_gather/pallas_call | solution.py:896
  254.9 17.2 %fusion.33.gate_up = f32[1024,2816]{1,0:T(8,128)S(1)} fusion(bf16[1024,2048]{1,0:T(8,128)(2,1)} %bitcast.146, bf16[2048,2816]{1,0:T(8,128)(2,1)} %bitcast.188), kind=kOutput, calls=%fused_computation.119 | convolution fusion | flops 11811160064 | bytes 27262976 | tf_op jit(solution)/shard_map/dot_general | solution.py:49
  276.3 11.7 %convert_convert_fusion = f32[1024,2048]{1,0:T(8,128)} fusion(bf16[1024,1408]{1,0:T(8,128)(2,1)S(1)} %fusion.2, bf16[1408,2048]{1,0:T(8,128)(2,1)} %bitcast.153), kind=kOutput, calls=%fused_computation.12 | convolution fusion | flops 5909774336 | bytes 17039360 | tf_op jit(solution)/shard_map/dot_general | solution.py:49
  293.3 10.4 %fusion.34.gate_up = f32[1024,1408]{1,0:T(8,128)S(1)} fusion(bf16[1024,2048]{1,0:T(8,128)(2,1)} %bitcast.148, bf16[2048,1408]{1,0:T(8,128)(2,1)} %bitcast.190), kind=kOutput, calls=%fused_computation.120 | convolution fusion | flops 5905580032 | bytes 15728640 | tf_op jit(solution)/shard_map/dot_general | solution.py:49
  308.0 5.5 fusion.35
  313.5 33.3 %all-gather.9.cloned.1.call-done = bf16[1024,1280]{1,0:T(8,128)(2,1)} async-done(((bf16[128,1280]{1,0:T(8,128)(2,1)}), bf16[1024,1280]{1,0:T(8,128)(2,1)}) %all-gather.9.cloned.1.call-update) | async-done | bytes 2621456 | tf_op jit(solution)/shard_map/all_gather | solution.py:1607
  352.9 6.8 fusion
  362.4 14.7 %gate_back.2 = (bf16[1024,2816]{1,0:T(8,128)(2,1)}, bf16[1024,2048]{1,0:T(8,128)(2,1)S(1)}) custom-call(bf16[1024,2048]{1,0:T(8,128)(2,1)} %copy-done.15, f32[1024,1]{1,0:T(8,128)S(1)} %bitcast_select_fusion.scale, f32[1024,2816]{1,0:T(8,128)} %copy-done.16, bf16[1408,2048]{1,0:T(8,128)(2,1)} %bitcast.154), custom_call_target="tpu_custom_call" | custom-call | flops 5905580032 | bytes 31457280 | tf_op jit(solution)/shard_map/gate_back/pallas_call | solution.py:1518
  377.1 19.7 %convolution_convert_fusion.2 = bf16[1024,2048]{1,0:T(8,128)(2,1)} fusion(bf16[1024,2816]{1,0:T(8,128)(2,1)} %get-tuple-element.96.far_grads, bf16[2048,2816]{1,0:T(8,128)(2,1)} %bitcast.189), kind=kOutput, calls=%fused_computation.13 | convolution fusion | flops 11813257216 | bytes 21495808 | tf_op jit(solution)/shard_map/dot_general | solution.py:1625
  396.8 9.0 %gate_back.3 = (bf16[1024,1408]{1,0:T(8,128)(2,1)S(1)}, bf16[1024,2048]{1,0:T(8,128)(2,1)}) custom-call(bf16[1024,2048]{1,0:T(8,128)(2,1)} %copy-done.15, f32[1024,1]{1,0:T(8,128)S(1)} %get-tuple-element.138.scale, f32[1024,1408]{1,0:T(8,128)} %copy-done.19, bf16[704,2048]{1,0:T(8,128)(2,1)} %bitcast.165), custom_call_target="tpu_custom_call" | custom-call | flops 2952790016 | bytes 19922944 | tf_op jit(solution)/shard_map/gate_back/pallas_call | solution.py:1518
  407.3 8.6 %convolution_convert_fusion.1 = bf16[2048,1408]{1,0:T(8,128)(2,1)} fusion(bf16[1024,2048]{1,0:T(8,128)(2,1)S(1)} %bitcast.150, bf16[1024,1408]{1,0:T(8,128)(2,1)S(1)} %get-tuple-element.98), kind=kOutput, calls=%fused_computation.8 | convolution fusion | flops 5908463616 | bytes 12845056 | tf_op jit(solution)/shard_map/dot_general | solution.py:1619
  416.2 10.5 %convolution_convert_fusion = bf16[1408,2048]{1,0:T(8,128)(2,1)} fusion(bf16[1024,1408]{1,0:T(8,128)(2,1)} %copy-done.32, bf16[1024,2048]{1,0:T(8,128)(2,1)} %copy-done.7), kind=kOutput, calls=%fused_computation.7 | convolution fusion | flops 5908463616 | bytes 12845056 | tf_op jit(solution)/shard_map/dot_general | solution.py:1619
  426.7 11.6 %add_convert_fusion = bf16[1024,2048]{1,0:T(8,128)(2,1)} fusion(bf16[1024,2048]{1,0:T(8,128)(2,1)} %convolution_convert_fusion.2, bf16[1024,1408]{1,0:T(8,128)(2,1)} %copy-done.9, bf16[2048,1408]{1,0:T(8,128)(2,1)} %bitcast.191), kind=kOutput, calls=%fused_computation.5 | convolution fusion | flops 5911871488 | bytes 17039360 | tf_op jit(solution)/shard_map/dot_general | solution.py:1625
  439.0 57.8 %line_scatter.3 = (f32[128,2048]{1,0:T(8,128)}, f32[8,8,128]{2,1,0:T(8,128)}, bf16[2048,2816]{1,0:T(8,128)(2,1)}) custom-call(bf16[8,128,2048]{2,1,0:T(8,128)(2,1)} %bitcast.158, f32[8,8,128]{2,1,0:T(8,128)} %pad.18.small, bf16[1024,2048]{1,0:T(8,128)(2,1)} %bitcast.149, bf16[1024,2816]{1,0:T(8,128)(2,1)} %get-tuple-element.96.far_grads), custom_call_target="tpu_custom_call" | custom-call | tf_op jit(solution)/shard_map/line_scatter/pallas_call | solution.py:725
  507.1 44.8 %product_gather.1 = (bf16[8,128,2048]{2,1,0:T(8,128)(2,1)S(1)}, bf16[704,2048]{1,0:T(8,128)(2,1)S(1)}) custom-call(bf16[128,2048]{1,0:T(8,128)(2,1)S(1)} %get-tuple-element.104.own, bf16[1024,704]{1,0:T(8,128)(2,1)S(1)} %fusion.3.units, bf16[1024,2048]{1,0:T(8,128)(2,1)S(1)} %copy-done.1), custom_call_target="tpu_custom_call" | custom-call | tf_op jit(solution)/shard_map/product_gather/pallas_call | solution.py:877
  555.5 3.6 all-to-all-start.1
  559.7 31.7 %attend_back.1 = (bf16[1024,2048]{1,0:T(8,128)(2,1)}, bf16[2048,768]{1,0:T(8,128)(2,1)}, bf16[256,2048]{1,0:T(8,128)(2,1)}, f32[1,768]{1,0:T(1,128)}, f32[1,2048]{1,0:T(1,128)}) custom-call(bf16[1024,2048]{1,0:T(8,128)(2,1)} %bitcast.143, bf16[256,2048]{1,0:T(8,128)(2,1)} %copy-done.3, bf16[1024,256]{1,0:T(8,128)(2,1)} %copy-done.11, ...), custom_call_target="tpu_custom_call" | custom-call | flops 11274289152 | bytes 36700160 | tf_op jit(solution)/shard_map/attend_back/pallas_call | solution.py:1451
  602.4 98.8 %closing.1 = (f32[128,2048]{1,0:T(8,128)}, bf16[8,64,768]{2,1,0:T(8,128)(2,1)}, f32[64,2048]{1,0:T(8,128)}, f32[176,2048]{1,0:T(8,128)}, f32[8,128]{1,0:T(8,128)}) custom-call(bf16[8,128,2048]{2,1,0:T(8,128)(2,1)} %bitcast.157, bf16[4,512,768]{2,1,0:T(8,128)(2,1)} %bitcast.164, bf16[4,128,2048]{2,1,0:T(8,128)(2,1)} %pad_maximum_fusion.1.pair, ...), custom_call_target="tpu_custom_call" | custom-call | tf_op jit(solution)/shard_map/closing/pallas_call | solution.py:1199
  713.6 4.9 bitcast_convert_fusion
  (235 shorter events, 92.7 us)
Async XLA Ops:
  7.2 83.5 %all-gather.11.cloned.1.call-start = ((), (), s32[]{:S(2)}) async-start(), calls=%async_computation.12 | async-start | bytes 7208960 | tf_op jit(solution)/shard_map/all_gather | solution.py:1607
  7.9 178.3 %all-gather.13.cloned.1.call-start = ((), (), s32[]{:S(2)}) async-start(), calls=%async_computation.13 | async-start | bytes 14417920 | tf_op jit(solution)/shard_map/all_gather | solution.py:1607
  9.8 80.8 %copy-start.50 = (s32[16]{0:T(128)S(1)}, s32[16]{0:T(128)}, u32[]{:S(2)}) copy-start(s32[16]{0:T(128)} %param.19) | copy-start | bytes 196
  90.6 7.1 copy-start.39
  90.7 7.4 %copy-start.41 = (s32[8,8,128]{2,1,0:T(8,128)S(1)}, s32[8,8,128]{2,1,0:T(8,128)}, u32[]{:S(2)}) copy-start(s32[8,8,128]{2,1,0:T(8,128)} %get-tuple-element.75) | copy-start | bytes 98308
  93.9 38.6 %all-to-all-start = ((bf16[8,64,1408]{2,1,0:T(8,128)(2,1)}), bf16[8,64,1408]{2,1,0:T(8,128)(2,1)S(1)}, u32[]{:S(2)}, u32[]{:S(2)}) async-start(bf16[8,64,1408]{2,1,0:T(8,128)(2,1)} %deal_columns.1), calls=%async_computation | async-start | bytes 2883584 | tf_op jit(solution)/shard_map/all_to_all | solution.py:1615
  97.4 157.5 %all-gather.7.cloned.1.call-start = ((), (), s32[]{:S(2)}) async-start(), calls=%async_computation.6 | async-start | bytes 1769472 | tf_op jit(solution)/shard_map/all_gather | solution.py:1607
  103.2 80.9 %copy-start.22 = (bf16[1,128,2048]{2,1,0:T(8,128)(2,1)S(1)}, bf16[1,128,2048]{2,1,0:T(8,128)(2,1)}, u32[]{:S(2)}) copy-start(bf16[1,128,2048]{2,1,0:T(8,128)(2,1)} %param.17) | copy-start | bytes 1572868
  132.4 53.8 %copy-start.27 = (bf16[8,64,1408]{2,1,0:T(8,128)(2,1)}, bf16[8,64,1408]{2,1,0:T(8,128)(2,1)S(1)}, u32[]{:S(2)}) copy-start(bf16[8,64,1408]{2,1,0:T(8,128)(2,1)S(1)} %all-to-all-done) | copy-start | bytes 4325380
  135.2 51.1 %copy-start.28 = (bf16[1,128,2048]{2,1,0:T(8,128)(2,1)S(1)}, bf16[1,128,2048]{2,1,0:T(8,128)(2,1)}, u32[]{:S(2)}) copy-start(bf16[1,128,2048]{2,1,0:T(8,128)(2,1)} %param.21) | copy-start | bytes 1572868
  186.9 159.9 %all-gather.9.cloned.1.call-start = ((), (), s32[]{:S(2)}) async-start(), calls=%async_computation.7 | async-start | bytes 2949120 | tf_op jit(solution)/shard_map/all_gather | solution.py:1607
  276.3 11.7 %copy-start.32 = (bf16[1024,1408]{1,0:T(8,128)(2,1)}, bf16[1024,1408]{1,0:T(8,128)(2,1)S(1)}, u32[]{:S(2)}) copy-start(bf16[1024,1408]{1,0:T(8,128)(2,1)S(1)} %fusion.2) | copy-start | bytes 8650756
  288.7 215.6 %reduce-scatter.5.cloned.1.call-start = ((), (), s32[]{:S(2)}) async-start(), calls=%async_computation.8 | async-start | bytes 4718592 | tf_op jit(solution)/shard_map/reduce_scatter | solution.py:1611
  349.6 10.1 %copy-start.15 = (bf16[1024,2048]{1,0:T(8,128)(2,1)}, bf16[1024,2048]{1,0:T(8,128)(2,1)S(1)}, u32[]{:S(2)}) copy-start(bf16[1024,2048]{1,0:T(8,128)(2,1)S(1)} %pad_maximum_fusion.upstream) | copy-start | bytes 12582916
  359.7 195.8 %reduce-scatter.7.cloned.1.call-start = ((), (), s32[]{:S(2)}) async-start(), calls=%async_computation.9 | async-start | bytes 7208960 | tf_op jit(solution)/shard_map/reduce_scatter | solution.py:1611
  377.1 19.7 %copy-start.7 = (bf16[1024,2048]{1,0:T(8,128)(2,1)}, bf16[1024,2048]{1,0:T(8,128)(2,1)S(1)}, u32[]{:S(2)}) copy-start(bf16[1024,2048]{1,0:T(8,128)(2,1)S(1)} %get-tuple-element.116) | copy-start | bytes 12582916
  396.8 10.5 %copy-start.20 = (bf16[8,128,2048]{2,1,0:T(8,128)(2,1)S(1)}, bf16[8,128,2048]{2,1,0:T(8,128)(2,1)}, u32[]{:S(2)}) copy-start(bf16[8,128,2048]{2,1,0:T(8,128)(2,1)} %get-tuple-element.82) | copy-start | bytes 12582916
  415.9 186.5 %reduce-scatter.9.cloned.1.call-start = ((), (), s32[]{:S(2)}) async-start(), calls=%async_computation.10 | async-start | bytes 7208960 | tf_op jit(solution)/shard_map/reduce_scatter | solution.py:1611
  426.7 286.9 %reduce-scatter.11.cloned.1.call-start = ((), (), s32[]{:S(2)}) async-start(), calls=%async_computation.11 | async-start | bytes 14417920 | tf_op jit(solution)/shard_map/reduce_scatter | solution.py:1611
  507.1 52.0 %copy-start.24 = (bf16[128,2048]{1,0:T(8,128)(2,1)S(1)}, bf16[128,2048]{1,0:T(8,128)(2,1)}, u32[]{:S(2)}) copy-start(bf16[128,2048]{1,0:T(8,128)(2,1)} %multiply_convert_fusion.refs_0_) | copy-start | bytes 1572868
  555.5 42.3 %all-to-all-start.1 = ((bf16[8,64,1408]{2,1,0:T(8,128)(2,1)}), bf16[8,64,1408]{2,1,0:T(8,128)(2,1)S(1)}, u32[]{:S(2)}, u32[]{:S(2)}) async-start(bf16[8,64,1408]{2,1,0:T(8,128)(2,1)} %bitcast.167), calls=%async_computation.3 | async-start | bytes 2883584 | tf_op jit(solution)/shard_map/all_to_all | solution.py:1615
  602.4 104.2 %copy-start.23 = (bf16[1,128,2048]{2,1,0:T(8,128)(2,1)S(1)}, bf16[1,128,2048]{2,1,0:T(8,128)(2,1)}, u32[]{:S(2)}) copy-start(bf16[1,128,2048]{2,1,0:T(8,128)(2,1)} %param.17) | copy-start | bytes 1572868
  701.2 10.8 %copy-start.21 = (f32[128,2048]{1,0:T(8,128)S(1)}, f32[128,2048]{1,0:T(8,128)}, u32[]{:S(2)}) copy-start(f32[128,2048]{1,0:T(8,128)} %get-tuple-element.167) | copy-start | bytes 3145732
  701.2 10.8 %copy-start.30 = (bf16[1,128,2048]{2,1,0:T(8,128)(2,1)S(1)}, bf16[1,128,2048]{2,1,0:T(8,128)(2,1)}, u32[]{:S(2)}) copy-start(bf16[1,128,2048]{2,1,0:T(8,128)(2,1)} %param.21) | copy-start | bytes 1572868
  (37 other events, 107.6 us)
Sparse Core Ops, SparseCore 0:
  9.6 55.7 all-gather.10
  66.9 79.6 all-gather.12
  187.0 56.0 all-gather.6
  288.9 57.8 all-gather.8
  359.9 86.6 reduce-scatter.4
  449.1 55.1 reduce-scatter.6
  506.8 54.8 reduce-scatter.8
  564.5 131.9 reduce-scatter.10

commit v10 on v8

--- a/solution.py
+++ b/solution.py
@@ -720,7 +720,7 @@
         )(part)
     product = (tokens.shape[1], grads.shape[1])
     params = pltpu.CompilerParams(
-        collective_id=call_id, has_side_effects=True, vmem_limit_bytes=40 * 2**20
+        collective_id=call_id, has_side_effects=True, vmem_limit_bytes=56 * 2**20
     )
     return pl.pallas_call(
         functools.partial(scatter_kernel, ctx_count),
@@ -1223,7 +1223,7 @@
         + [dma((ctx_count,))] * 4
         + [dma((4,))] * 2,
         compiler_params=pltpu.CompilerParams(
-            collective_id=call_id, has_side_effects=True, vmem_limit_bytes=36 * 2**20
+            collective_id=call_id, has_side_effects=True, vmem_limit_bytes=56 * 2**20
         ),
         name="closing",
     )(part, weight, pair, plain, small)
@@ -1470,7 +1470,7 @@
             pltpu.VMEM(weight.shape, low),
             pltpu.SemaphoreType.DMA((3,)),
         ],
-        compiler_params=pltpu.CompilerParams(vmem_limit_bytes=40 * 2**20),
+        compiler_params=pltpu.CompilerParams(vmem_limit_bytes=56 * 2**20),
         cost_estimate=pl.CostEstimate(
             flops=2 * rows * width * 8 * wide + 10 * rows * rows * wide,
             bytes_accessed=35 * 2**20,
@@ -1654,7 +1654,7 @@
     ctx_rank = lax.axis_index("ctx")
     dev_count = ctx_count * fsdp_count
     row_len = ctx_count * tokens_dev
-    early = width * 3 // 8
+    early = width // 2
     head_count = width // HD
     shard = qkv_weight.shape[0]
     expert_count = router_weight.shape[1]
@@ -1832,9 +1832,7 @@
     grad_middle_norm, grad_gain_ffn = norm_pull(grad_normed)
     grad_middle = out_grad.reshape(tokens_dev, width).astype(full) + grad_middle_norm
 
-    grad_branch, sum_expert_outer, hidden_out = lax.optimization_barrier(
-        (grad_middle.astype(low), sum_expert_outer, hidden_out)
-    )
+    grad_branch, hidden_out = lax.optimization_barrier((grad_middle.astype(low), hidden_out))
     row_branch, grad_outer = product_gather(
         ctx_count, 3, grad_branch, shared_hidden, grad_shared_out
     )
@@ -1864,7 +1862,9 @@
     padded_out = jnp.concatenate(
         [jnp.where(side == p, grad_out_c, jnp.zeros_like(grad_out_c)) for p in range(2)], axis=0
     )
-    grad_attn_part, sum_inner = lax.optimization_barrier((grad_attn_part, sum_inner))
+    grad_attn_part, sum_inner, sum_expert_outer = lax.optimization_barrier(
+        (grad_attn_part, sum_inner, sum_expert_outer)
+    )
     grad_bias_c = grad_bias_c.reshape(3, 1, 2, HD)
     mine = (jnp.arange(ctx_count) == ctx_rank)[None, :, None, None]
     places_of = [head_order.index(h) for h in range(head_count)]

time: 726 us -> 715 us (0.985)
  Pallas kernels: 468 us -> 487 us
  local copies, waits for them, and re-layouts: 66.1 us -> 48.7 us
  waiting for transfers between devices: 17.2 us -> 4.95 us
  starting transfers between devices: 18.9 us -> 9.53 us
    unnamed x140 -> x118, local copies, waits for them, and re-layouts: 51.2 us -> 30.4 us
    pallas_call x1, Pallas kernels: 83.5 us -> 96.2 us  [closing(): pl.pallas_call(functools.partial(closing_kernel, ctx_count), out_shape=[j...]
    all_to_all x2, starting transfers between devices: 18.3 us -> 8.86 us  [exchange(): return lax.all_to_all(array, 'ctx', split_axis=0, concat_axis=0, tiled=True)]
    reduce_scatter x4, waiting for transfers between devices: 8.59 us -> 0.02 us  [reduce_over(): return lax.psum_scatter(array, axis, scatter_dimension=dim, tiled=True)]
  transfers between devices with their start and end apart: 10 -> 10, of which waited for: 4 -> 1; matrix products, arithmetic and copies ran while one was open for 18% -> 20% of each run, Pallas kernels for 65% -> 69%
where the time goes in v10:
time: 715 us; the launch traced here: 704 us
  Pallas kernels  487 us (68%)
  matrix products  100 us (14%)
  local copies, waits for them, and re-layouts  48.7 us (7%)
  other arithmetic  38.1 us (5%)
  between operations  15.2 us (2%)
  starting transfers between devices  9.53 us (1%)
    pallas_call x1, Pallas kernels, opening(): pl.pallas_call(functools.partial(opening_kernel, ctx_count), out_shape=[o...  100 us
    pallas_call x1, Pallas kernels, closing(): pl.pallas_call(functools.partial(closing_kernel, ctx_count), out_shape=[j...  96.2 us
    pallas_call x1, Pallas kernels, line_scatter(): pl.pallas_call(functools.partial(scatter_kernel, ctx_count), out_shape=[t...  58.5 us
    pallas_call x1, Pallas kernels, line_gather(): pl.pallas_call(functools.partial(gather_kernel, ctx_count // 2 - 1, count...  56.4 us
    pallas_call x1, Pallas kernels, line_scatter(): pl.pallas_call(functools.partial(line_scatter_kernel, half - 1), out_shap...  47.5 us
    pallas_call x1, Pallas kernels, product_gather(): pl.pallas_call(functools.partial(product_kernel, ctx_count // 2 - 1), out...  45.8 us
    dot_general x5, matrix products, matmul_low(): return jnp.dot(left, right, preferred_element_type=jnp.float32)  44.4 us
    dot_general x4, matrix products, dot_transposed(): lax.dot_general(left, right, (((1,), (1,)), ((), ())), preferred_element_...  36 us
  transfers between devices with their start and end apart: 10, of which 1 were waited for; matrix products, arithmetic and copies ran while one was open for 20% of the time, Pallas kernels for 69%

profile of v10, /device:TPU:0, one launch (start us, length us, event | category | flops | bytes accessed | tf_op | source)
XLA Modules:
  0.0 703.9 jit_solution(4274430485558245972)
XLA Ops:
  15.9 100.5 %opening.1 = (bf16[8,128,2048]{2,1,0:T(8,128)(2,1)}, bf16[4,8,64,768]{3,2,1,0:T(8,128)(2,1)}, bf16[4,2,64,2048]{3,2,1,0:T(8,128)(2,1)}, bf16[4,8,16,128]{3,2,1,0:T(8,128)(2,1)}, s32[8,8,128]{2,1,0:T(8,128)}) custom-call(bf16[128,2048]{1,0:T(8,128)(2,1)} %bitcast.153, bf16[8,64,768]{2,1,0:T(8,128)(2,1)} %reshape.359.qkv_own, bf16[64,2048]{1,0:T(8,128)(2,1)} %out_own.1, ...), custom_call_target="tpu_custom_call" | custom-call | tf_op jit(solution)/shard_map/opening/pallas_call | solution.py:1027
  119.5 5.3 all-to-all-start
  131.1 17.6 %attend.1 = (bf16[1024,2048]{1,0:T(8,128)(2,1)S(1)}, bf16[1024,256]{1,0:T(8,128)(2,1)S(1)}, bf16[1024,256]{1,0:T(8,128)(2,1)S(1)}, bf16[1024,256]{1,0:T(8,128)(2...) custom-call(bf16[1024,2048]{1,0:T(8,128)(2,1)} %bitcast.194, ...), custom_call_target="tpu_custom_call" | custom-call | flops 5368709120 | bytes 20971520 | tf_op jit(solution)/shard_map/attend/pallas_call | solution.py:1300
  161.0 47.5 %line_scatter.2 = f32[128,2048]{1,0:T(8,128)S(1)} custom-call(bf16[8,128,2048]{2,1,0:T(8,128)(2,1)S(1)} %bitcast.142), custom_call_target="tpu_custom_call" | custom-call | tf_op jit(solution)/shard_map/line_scatter/pallas_call | solution.py:712
  210.7 56.4 %line_gather.1 = (bf16[8,128,2048]{2,1,0:T(8,128)(2,1)}, bf16[4,512,1408]{2,1,0:T(8,128)(2,1)}, bf16[4,176,2048]{2,1,0:T(8,128)(2,1)}) custom-call(bf16[128,2048]{1,0:T(8,128)(2,1)} %multiply_convert_fusion.refs_0_, bf16[512,1408]{1,0:T(8,128)(2,1)} %bitcast.154, bf16[176,2048]{1,0:T(8,128)(2,1)} %refs_2_.1), custom_call_target="tpu_custom_call" | custom-call | tf_op jit(solution)/shard_map/line_gather/pallas_call | solution.py:896
  272.3 17.2 %fusion.2.gate_up = f32[1024,2816]{1,0:T(8,128)S(1)} fusion(bf16[1024,2048]{1,0:T(8,128)(2,1)} %bitcast.149, bf16[1,2048,2816]{2,1,0:T(8,128)(2,1)} %all-gather.13.cloned.1.call-done), kind=kOutput, calls=%fused_computation.3 | convolution fusion | flops 11811160064 | bytes 27262976 | tf_op jit(solution)/shard_map/dot_general | solution.py:49
  291.4 3.5 copy-done.16
  294.9 12.1 %convert_convert_fusion = f32[1024,2048]{1,0:T(8,128)} fusion(bf16[1024,1408]{1,0:T(8,128)(2,1)S(1)} %fusion.6, bf16[1408,2048]{1,0:T(8,128)(2,1)} %bitcast.155), kind=kOutput, calls=%fused_computation.16 | convolution fusion | flops 5909774336 | bytes 17039360 | tf_op jit(solution)/shard_map/dot_general | solution.py:49
  307.0 6.7 fusion.40.gate_up
  317.9 5.9 fusion.41
  329.9 6.8 fusion.4
  339.2 14.8 %gate_back.2 = (bf16[1024,2816]{1,0:T(8,128)(2,1)}, bf16[1024,2048]{1,0:T(8,128)(2,1)S(1)}) custom-call(bf16[1024,2048]{1,0:T(8,128)(2,1)} %copy-done.15, f32[1024,1]{1,0:T(8,128)S(1)} %bitcast_select_fusion.scale, f32[1024,2816]{1,0:T(8,128)} %copy-done.16, bf16[1408,2048]{1,0:T(8,128)(2,1)} %bitcast.156), custom_call_target="tpu_custom_call" | custom-call | flops 5905580032 | bytes 31457280 | tf_op jit(solution)/shard_map/gate_back/pallas_call | solution.py:1518
  354.0 19.7 %fusion.7 = bf16[1024,2048]{1,0:T(8,128)(2,1)} fusion(bf16[1024,2816]{1,0:T(8,128)(2,1)} %get-tuple-element.90.far_grads, bf16[1,2048,2816]{2,1,0:T(8,128)(2,1)} %all-gather.13.cloned.1.call-done), kind=kOutput, calls=%fused_computation.17 | convolution fusion | flops 11813257216 | bytes 21495808 | tf_op jit(solution)/shard_map/dot_general | solution.py:1625
  373.7 9.0 %gate_back.3 = (bf16[1024,1408]{1,0:T(8,128)(2,1)S(1)}, bf16[1024,2048]{1,0:T(8,128)(2,1)}) custom-call(bf16[1024,2048]{1,0:T(8,128)(2,1)} %copy-done.15, f32[1024,1]{1,0:T(8,128)S(1)} %get-tuple-element.132.scale, f32[1024,1408]{1,0:T(8,128)} %copy-done.19, bf16[704,2048]{1,0:T(8,128)(2,1)} %bitcast.167), custom_call_target="tpu_custom_call" | custom-call | flops 2952790016 | bytes 19922944 | tf_op jit(solution)/shard_map/gate_back/pallas_call | solution.py:1518
  384.2 8.6 %convolution_convert_fusion.1 = bf16[2048,1408]{1,0:T(8,128)(2,1)} fusion(bf16[1024,2048]{1,0:T(8,128)(2,1)S(1)} %bitcast.152, bf16[1024,1408]{1,0:T(8,128)(2,1)S(1)} %get-tuple-element.92), kind=kOutput, calls=%fused_computation.12 | convolution fusion | flops 5908463616 | bytes 12845056 | tf_op jit(solution)/shard_map/dot_general | solution.py:1619
  392.9 11.0 %convolution_convert_fusion = bf16[1408,2048]{1,0:T(8,128)(2,1)} fusion(bf16[1024,1408]{1,0:T(8,128)(2,1)} %copy-done.33, bf16[1024,2048]{1,0:T(8,128)(2,1)} %copy-done.7), kind=kOutput, calls=%fused_computation.11 | convolution fusion | flops 5908463616 | bytes 12845056 | tf_op jit(solution)/shard_map/dot_general | solution.py:1619
  403.9 11.6 %add_convert_fusion = bf16[1024,2048]{1,0:T(8,128)(2,1)} fusion(bf16[1024,2048]{1,0:T(8,128)(2,1)} %fusion.7, bf16[1024,1408]{1,0:T(8,128)(2,1)} %copy-done.9, bf16[2048,1408]{1,0:T(8,128)(2,1)} %bitcast.190), kind=kOutput, calls=%fused_computation.9 | convolution fusion | flops 5911871488 | bytes 17039360 | tf_op jit(solution)/shard_map/dot_general | solution.py:1625
  416.2 58.5 %line_scatter.3 = (f32[128,2048]{1,0:T(8,128)}, f32[8,8,128]{2,1,0:T(8,128)}, bf16[2048,2816]{1,0:T(8,128)(2,1)}) custom-call(bf16[8,128,2048]{2,1,0:T(8,128)(2,1)} %bitcast.160, f32[8,8,128]{2,1,0:T(8,128)} %pad.18.small, bf16[1024,2048]{1,0:T(8,128)(2,1)} %bitcast.150, bf16[1024,2816]{1,0:T(8,128)(2,1)} %get-tuple-element.90.far_grads), custom_call_target="tpu_custom_call" | custom-call | tf_op jit(solution)/shard_map/line_scatter/pallas_call | solution.py:725
  485.0 45.8 %product_gather.1 = (bf16[8,128,2048]{2,1,0:T(8,128)(2,1)S(1)}, bf16[704,2048]{1,0:T(8,128)(2,1)S(1)}) custom-call(bf16[128,2048]{1,0:T(8,128)(2,1)S(1)} %get-tuple-element.98.own, bf16[1024,704]{1,0:T(8,128)(2,1)S(1)} %fusion.10.units, bf16[1024,2048]{1,0:T(8,128)(2,1)S(1)} %copy-done.1), custom_call_target="tpu_custom_call" | custom-call | tf_op jit(solution)/shard_map/product_gather/pallas_call | solution.py:877
  534.4 3.6 all-to-all-start.1
  538.6 31.9 %attend_back.1 = (bf16[1024,2048]{1,0:T(8,128)(2,1)}, bf16[2048,768]{1,0:T(8,128)(2,1)}, bf16[256,2048]{1,0:T(8,128)(2,1)}, f32[1,768]{1,0:T(1,128)}, f32[1,2048]{1,0:T(1,128)}) custom-call(bf16[1024,2048]{1,0:T(8,128)(2,1)} %bitcast.145, bf16[256,2048]{1,0:T(8,128)(2,1)} %copy-done.3, bf16[1024,256]{1,0:T(8,128)(2,1)} %copy-done.11, ...), custom_call_target="tpu_custom_call" | custom-call | flops 11274289152 | bytes 36700160 | tf_op jit(solution)/shard_map/attend_back/pallas_call | solution.py:1451
  578.0 3.6 collect_columns.1
  581.5 96.2 %closing.1 = (f32[128,2048]{1,0:T(8,128)}, bf16[8,64,768]{2,1,0:T(8,128)(2,1)}, f32[64,2048]{1,0:T(8,128)}, f32[176,2048]{1,0:T(8,128)}, f32[8,128]{1,0:T(8,128)}) custom-call(bf16[8,128,2048]{2,1,0:T(8,128)(2,1)} %bitcast.159, bf16[4,512,768]{2,1,0:T(8,128)(2,1)} %bitcast.166, bf16[4,128,2048]{2,1,0:T(8,128)(2,1)} %pad_maximum_fusion.1.pair, ...), custom_call_target="tpu_custom_call" | custom-call | tf_op jit(solution)/shard_map/closing/pallas_call | solution.py:1199
  690.1 4.9 bitcast_convert_fusion
  (242 shorter events, 90.4 us)
Async XLA Ops:
  7.2 151.1 %all-gather.7.cloned.1.call-start = ((), (), s32[]{:S(2)}) async-start(), calls=%async_computation.6 | async-start | bytes 2359296 | tf_op jit(solution)/shard_map/all_gather | solution.py:1607
  9.0 149.3 %all-gather.11.cloned.1.call-start = ((), (), s32[]{:S(2)}) async-start(), calls=%async_computation.12 | async-start | bytes 7208960 | tf_op jit(solution)/shard_map/all_gather | solution.py:1607
  9.8 262.6 %all-gather.13.cloned.1.call-start = ((), (), s32[]{:S(2)}) async-start(), calls=%async_computation.13 | async-start | bytes 14417920 | tf_op jit(solution)/shard_map/all_gather | solution.py:1607
  14.5 110.6 %copy-start.51 = (s32[16]{0:T(128)S(1)}, s32[16]{0:T(128)}, u32[]{:S(2)}) copy-start(s32[16]{0:T(128)} %param.19) | copy-start | bytes 196
  119.5 38.8 %all-to-all-start = ((bf16[8,64,1408]{2,1,0:T(8,128)(2,1)}), bf16[8,64,1408]{2,1,0:T(8,128)(2,1)S(1)}, u32[]{:S(2)}, u32[]{:S(2)}) async-start(bf16[8,64,1408]{2,1,0:T(8,128)(2,1)} %deal_columns.1), calls=%async_computation | async-start | bytes 2883584 | tf_op jit(solution)/shard_map/all_to_all | solution.py:1615
  124.8 198.9 %all-gather.9.cloned.1.call-start = ((), (), s32[]{:S(2)}) async-start(), calls=%async_computation.7 | async-start | bytes 2359296 | tf_op jit(solution)/shard_map/all_gather | solution.py:1607
  131.1 77.5 %copy-start.23 = (bf16[1,128,2048]{2,1,0:T(8,128)(2,1)S(1)}, bf16[1,128,2048]{2,1,0:T(8,128)(2,1)}, u32[]{:S(2)}) copy-start(bf16[1,128,2048]{2,1,0:T(8,128)(2,1)} %param.17) | copy-start | bytes 1572868
  158.3 52.4 %copy-start.28 = (bf16[8,64,1408]{2,1,0:T(8,128)(2,1)}, bf16[8,64,1408]{2,1,0:T(8,128)(2,1)S(1)}, u32[]{:S(2)}) copy-start(bf16[8,64,1408]{2,1,0:T(8,128)(2,1)S(1)} %all-to-all-done) | copy-start | bytes 4325380
  208.6 58.6 %copy-start.29 = (bf16[1,128,2048]{2,1,0:T(8,128)(2,1)S(1)}, bf16[1,128,2048]{2,1,0:T(8,128)(2,1)}, u32[]{:S(2)}) copy-start(bf16[1,128,2048]{2,1,0:T(8,128)(2,1)} %param.21) | copy-start | bytes 1572868
  271.9 210.3 %reduce-scatter.5.cloned.1.call-start = ((), (), s32[]{:S(2)}) async-start(), calls=%async_computation.8 | async-start | bytes 4718592 | tf_op jit(solution)/shard_map/reduce_scatter | solution.py:1611
  289.5 17.4 %slice-start = ((s8[5767168]{0:T(1024)(128)(4,1)}), s8[4194304]{0:T(1024)(128)(4,1)S(1)}, s32[]{:S(2)}) async-start(s8[5767168]{0:T(1024)(128)(4,1)} %bitcast.191), calls=%async_computation.14 | async-start | bytes 8388608
  294.9 12.1 %copy-start.33 = (bf16[1024,1408]{1,0:T(8,128)(2,1)}, bf16[1024,1408]{1,0:T(8,128)(2,1)S(1)}, u32[]{:S(2)}) copy-start(bf16[1024,1408]{1,0:T(8,128)(2,1)S(1)} %fusion.6) | copy-start | bytes 8650756
  294.9 12.1 %copy-start.20 = (bf16[8,128,2048]{2,1,0:T(8,128)(2,1)S(1)}, bf16[8,128,2048]{2,1,0:T(8,128)(2,1)}, u32[]{:S(2)}) copy-start(bf16[8,128,2048]{2,1,0:T(8,128)(2,1)} %get-tuple-element.79) | copy-start | bytes 12582916
  294.9 12.1 %slice-start.1 = ((s8[5767168]{0:T(1024)(128)(4,1)}), s8[1572864]{0:T(1024)(128)(4,1)S(1)}, s32[]{:S(2)}) async-start(s8[5767168]{0:T(1024)(128)(4,1)} %bitcast.191), calls=%async_computation.15 | async-start | bytes 3145728
  336.7 197.7 %reduce-scatter.7.cloned.1.call-start = ((), (), s32[]{:S(2)}) async-start(), calls=%async_computation.9 | async-start | bytes 7208960 | tf_op jit(solution)/shard_map/reduce_scatter | solution.py:1611
  354.0 19.7 %copy-start.7 = (bf16[1024,2048]{1,0:T(8,128)(2,1)}, bf16[1024,2048]{1,0:T(8,128)(2,1)S(1)}, u32[]{:S(2)}) copy-start(bf16[1024,2048]{1,0:T(8,128)(2,1)S(1)} %get-tuple-element.110) | copy-start | bytes 12582916
  373.7 10.6 %copy-start.21 = (bf16[8,128,2048]{2,1,0:T(8,128)(2,1)S(1)}, bf16[8,128,2048]{2,1,0:T(8,128)(2,1)}, u32[]{:S(2)}) copy-start(bf16[8,128,2048]{2,1,0:T(8,128)(2,1)} %get-tuple-element.79) | copy-start | bytes 12582916
  392.8 188.7 %reduce-scatter.9.cloned.1.call-start = ((), (), s32[]{:S(2)}) async-start(), calls=%async_computation.10 | async-start | bytes 7208960 | tf_op jit(solution)/shard_map/reduce_scatter | solution.py:1611
  403.8 286.3 %reduce-scatter.11.cloned.1.call-start = ((), (), s32[]{:S(2)}) async-start(), calls=%async_computation.11 | async-start | bytes 14417920 | tf_op jit(solution)/shard_map/reduce_scatter | solution.py:1611
  485.0 53.0 %copy-start.25 = (bf16[128,2048]{1,0:T(8,128)(2,1)S(1)}, bf16[128,2048]{1,0:T(8,128)(2,1)}, u32[]{:S(2)}) copy-start(bf16[128,2048]{1,0:T(8,128)(2,1)} %multiply_convert_fusion.refs_0_) | copy-start | bytes 1572868
  534.4 42.5 %all-to-all-start.1 = ((bf16[8,64,1408]{2,1,0:T(8,128)(2,1)}), bf16[8,64,1408]{2,1,0:T(8,128)(2,1)S(1)}, u32[]{:S(2)}, u32[]{:S(2)}) async-start(bf16[8,64,1408]{2,1,0:T(8,128)(2,1)} %bitcast.169), calls=%async_computation.3 | async-start | bytes 2883584 | tf_op jit(solution)/shard_map/all_to_all | solution.py:1615
  581.5 101.6 %copy-start.24 = (bf16[1,128,2048]{2,1,0:T(8,128)(2,1)S(1)}, bf16[1,128,2048]{2,1,0:T(8,128)(2,1)}, u32[]{:S(2)}) copy-start(bf16[1,128,2048]{2,1,0:T(8,128)(2,1)} %param.17) | copy-start | bytes 1572868
  677.7 10.8 %copy-start.22 = (f32[128,2048]{1,0:T(8,128)S(1)}, f32[128,2048]{1,0:T(8,128)}, u32[]{:S(2)}) copy-start(f32[128,2048]{1,0:T(8,128)} %get-tuple-element.161) | copy-start | bytes 3145732
  677.8 10.8 %copy-start.31 = (bf16[1,128,2048]{2,1,0:T(8,128)(2,1)S(1)}, bf16[1,128,2048]{2,1,0:T(8,128)(2,1)}, u32[]{:S(2)}) copy-start(bf16[1,128,2048]{2,1,0:T(8,128)(2,1)} %param.21) | copy-start | bytes 1572868
  (40 other events, 140.2 us)
Sparse Core Ops, SparseCore 0:
  10.7 70.9 all-gather.6
  83.3 44.5 all-gather.10
  129.5 80.2 all-gather.12
  272.0 47.7 all-gather.8
  336.8 86.6 reduce-scatter.4
  426.1 54.6 reduce-scatter.6
  483.4 54.8 reduce-scatter.8
  541.0 128.6 reduce-scatter.10

commit v11 on v10

--- a/solution.py
+++ b/solution.py
@@ -565,14 +565,14 @@
             ctx=side,
         )
 
-    def rise(goal):
+    def rise(goal, target=side):
         return remote(
-            sums.at[goal], rising.at[goal], move_send.at[goal], rise_recv.at[goal], ctx=here + 2
+            sums.at[goal], rising.at[goal], move_send.at[goal], rise_recv.at[goal], ctx=target
         )
 
-    def fall(goal):
+    def fall(goal, target=side):
         return remote(
-            sums.at[goal], falling.at[goal], move_send.at[goal], fall_recv.at[goal], ctx=here - 2
+            sums.at[goal], falling.at[goal], move_send.at[goal], fall_recv.at[goal], ctx=target
         )
 
     for k in range(min(2, last + 1)):
@@ -596,7 +596,7 @@
             def first():
                 add_rows(sums.at[goal], (mine, crossed.at[goal]), row_count)
 
-            rise(goal).start()
+            rise(goal, here + 2).start()
 
         @pl.when(goal < level)
         def downward():
@@ -609,7 +609,7 @@
             def first():
                 add_rows(sums.at[goal], (mine, crossed.at[goal]), row_count)
 
-            fall(goal).start()
+            fall(goal, here - 2).start()
 
         @pl.when(goal == level)
         def here_at_last():

time: 715 us -> 715 us (level)
  no operation moved by 1% of the time
where the time goes in v11:
time: 715 us; the launch traced here: 704 us
  Pallas kernels  487 us (68%)
  matrix products  100 us (14%)
  local copies, waits for them, and re-layouts  48.7 us (7%)
  other arithmetic  38.1 us (5%)
  between operations  15.2 us (2%)
  starting transfers between devices  9.53 us (1%)
    pallas_call x1, Pallas kernels, opening(): pl.pallas_call(functools.partial(opening_kernel, ctx_count), out_shape=[o...  100 us
    pallas_call x1, Pallas kernels, closing(): pl.pallas_call(functools.partial(closing_kernel, ctx_count), out_shape=[j...  96.2 us
    pallas_call x1, Pallas kernels, line_scatter(): pl.pallas_call(functools.partial(scatter_kernel, ctx_count), out_shape=[t...  58.5 us
    pallas_call x1, Pallas kernels, line_gather(): pl.pallas_call(functools.partial(gather_kernel, ctx_count // 2 - 1, count...  56.4 us
    pallas_call x1, Pallas kernels, line_scatter(): pl.pallas_call(functools.partial(line_scatter_kernel, half - 1), out_shap...  47.5 us
    pallas_call x1, Pallas kernels, product_gather(): pl.pallas_call(functools.partial(product_kernel, ctx_count // 2 - 1), out...  45.8 us
    dot_general x5, matrix products, matmul_low(): return jnp.dot(left, right, preferred_element_type=jnp.float32)  44.4 us
    dot_general x4, matrix products, dot_transposed(): lax.dot_general(left, right, (((1,), (1,)), ((), ())), preferred_element_...  36 us
  transfers between devices with their start and end apart: 10, of which 1 were waited for; matrix products, arithmetic and copies ran while one was open for 20% of the time, Pallas kernels for 69%

profile of v11, /device:TPU:0, one launch (start us, length us, event | category | flops | bytes accessed | tf_op | source)
XLA Modules:
  0.0 703.9 jit_solution(4274430485558245972)
XLA Ops:
  15.9 100.5 %opening.1 = (bf16[8,128,2048]{2,1,0:T(8,128)(2,1)}, bf16[4,8,64,768]{3,2,1,0:T(8,128)(2,1)}, bf16[4,2,64,2048]{3,2,1,0:T(8,128)(2,1)}, bf16[4,8,16,128]{3,2,1,0:T(8,128)(2,1)}, s32[8,8,128]{2,1,0:T(8,128)}) custom-call(bf16[128,2048]{1,0:T(8,128)(2,1)} %bitcast.153, bf16[8,64,768]{2,1,0:T(8,128)(2,1)} %reshape.359.qkv_own, bf16[64,2048]{1,0:T(8,128)(2,1)} %out_own.1, ...), custom_call_target="tpu_custom_call" | custom-call | tf_op jit(solution)/shard_map/opening/pallas_call | solution.py:1027
  119.5 5.3 all-to-all-start
  131.1 17.6 %attend.1 = (bf16[1024,2048]{1,0:T(8,128)(2,1)S(1)}, bf16[1024,256]{1,0:T(8,128)(2,1)S(1)}, bf16[1024,256]{1,0:T(8,128)(2,1)S(1)}, bf16[1024,256]{1,0:T(8,128)(2...) custom-call(bf16[1024,2048]{1,0:T(8,128)(2,1)} %bitcast.194, ...), custom_call_target="tpu_custom_call" | custom-call | flops 5368709120 | bytes 20971520 | tf_op jit(solution)/shard_map/attend/pallas_call | solution.py:1300
  161.0 47.5 %line_scatter.2 = f32[128,2048]{1,0:T(8,128)S(1)} custom-call(bf16[8,128,2048]{2,1,0:T(8,128)(2,1)S(1)} %bitcast.142), custom_call_target="tpu_custom_call" | custom-call | tf_op jit(solution)/shard_map/line_scatter/pallas_call | solution.py:712
  210.7 56.4 %line_gather.1 = (bf16[8,128,2048]{2,1,0:T(8,128)(2,1)}, bf16[4,512,1408]{2,1,0:T(8,128)(2,1)}, bf16[4,176,2048]{2,1,0:T(8,128)(2,1)}) custom-call(bf16[128,2048]{1,0:T(8,128)(2,1)} %multiply_convert_fusion.refs_0_, bf16[512,1408]{1,0:T(8,128)(2,1)} %bitcast.154, bf16[176,2048]{1,0:T(8,128)(2,1)} %refs_2_.1), custom_call_target="tpu_custom_call" | custom-call | tf_op jit(solution)/shard_map/line_gather/pallas_call | solution.py:896
  272.3 17.2 %fusion.2.gate_up = f32[1024,2816]{1,0:T(8,128)S(1)} fusion(bf16[1024,2048]{1,0:T(8,128)(2,1)} %bitcast.149, bf16[1,2048,2816]{2,1,0:T(8,128)(2,1)} %all-gather.13.cloned.1.call-done), kind=kOutput, calls=%fused_computation.3 | convolution fusion | flops 11811160064 | bytes 27262976 | tf_op jit(solution)/shard_map/dot_general | solution.py:49
  291.4 3.5 copy-done.16
  294.9 12.1 %convert_convert_fusion = f32[1024,2048]{1,0:T(8,128)} fusion(bf16[1024,1408]{1,0:T(8,128)(2,1)S(1)} %fusion.6, bf16[1408,2048]{1,0:T(8,128)(2,1)} %bitcast.155), kind=kOutput, calls=%fused_computation.16 | convolution fusion | flops 5909774336 | bytes 17039360 | tf_op jit(solution)/shard_map/dot_general | solution.py:49
  307.0 6.7 fusion.40.gate_up
  317.9 5.9 fusion.41
  329.9 6.8 fusion.4
  339.2 14.8 %gate_back.2 = (bf16[1024,2816]{1,0:T(8,128)(2,1)}, bf16[1024,2048]{1,0:T(8,128)(2,1)S(1)}) custom-call(bf16[1024,2048]{1,0:T(8,128)(2,1)} %copy-done.15, f32[1024,1]{1,0:T(8,128)S(1)} %bitcast_select_fusion.scale, f32[1024,2816]{1,0:T(8,128)} %copy-done.16, bf16[1408,2048]{1,0:T(8,128)(2,1)} %bitcast.156), custom_call_target="tpu_custom_call" | custom-call | flops 5905580032 | bytes 31457280 | tf_op jit(solution)/shard_map/gate_back/pallas_call | solution.py:1518
  354.0 19.7 %fusion.7 = bf16[1024,2048]{1,0:T(8,128)(2,1)} fusion(bf16[1024,2816]{1,0:T(8,128)(2,1)} %get-tuple-element.90.far_grads, bf16[1,2048,2816]{2,1,0:T(8,128)(2,1)} %all-gather.13.cloned.1.call-done), kind=kOutput, calls=%fused_computation.17 | convolution fusion | flops 11813257216 | bytes 21495808 | tf_op jit(solution)/shard_map/dot_general | solution.py:1625
  373.7 9.0 %gate_back.3 = (bf16[1024,1408]{1,0:T(8,128)(2,1)S(1)}, bf16[1024,2048]{1,0:T(8,128)(2,1)}) custom-call(bf16[1024,2048]{1,0:T(8,128)(2,1)} %copy-done.15, f32[1024,1]{1,0:T(8,128)S(1)} %get-tuple-element.132.scale, f32[1024,1408]{1,0:T(8,128)} %copy-done.19, bf16[704,2048]{1,0:T(8,128)(2,1)} %bitcast.167), custom_call_target="tpu_custom_call" | custom-call | flops 2952790016 | bytes 19922944 | tf_op jit(solution)/shard_map/gate_back/pallas_call | solution.py:1518
  384.2 8.6 %convolution_convert_fusion.1 = bf16[2048,1408]{1,0:T(8,128)(2,1)} fusion(bf16[1024,2048]{1,0:T(8,128)(2,1)S(1)} %bitcast.152, bf16[1024,1408]{1,0:T(8,128)(2,1)S(1)} %get-tuple-element.92), kind=kOutput, calls=%fused_computation.12 | convolution fusion | flops 5908463616 | bytes 12845056 | tf_op jit(solution)/shard_map/dot_general | solution.py:1619
  392.9 11.0 %convolution_convert_fusion = bf16[1408,2048]{1,0:T(8,128)(2,1)} fusion(bf16[1024,1408]{1,0:T(8,128)(2,1)} %copy-done.33, bf16[1024,2048]{1,0:T(8,128)(2,1)} %copy-done.7), kind=kOutput, calls=%fused_computation.11 | convolution fusion | flops 5908463616 | bytes 12845056 | tf_op jit(solution)/shard_map/dot_general | solution.py:1619
  403.9 11.6 %add_convert_fusion = bf16[1024,2048]{1,0:T(8,128)(2,1)} fusion(bf16[1024,2048]{1,0:T(8,128)(2,1)} %fusion.7, bf16[1024,1408]{1,0:T(8,128)(2,1)} %copy-done.9, bf16[2048,1408]{1,0:T(8,128)(2,1)} %bitcast.190), kind=kOutput, calls=%fused_computation.9 | convolution fusion | flops 5911871488 | bytes 17039360 | tf_op jit(solution)/shard_map/dot_general | solution.py:1625
  416.2 58.5 %line_scatter.3 = (f32[128,2048]{1,0:T(8,128)}, f32[8,8,128]{2,1,0:T(8,128)}, bf16[2048,2816]{1,0:T(8,128)(2,1)}) custom-call(bf16[8,128,2048]{2,1,0:T(8,128)(2,1)} %bitcast.160, f32[8,8,128]{2,1,0:T(8,128)} %pad.18.small, bf16[1024,2048]{1,0:T(8,128)(2,1)} %bitcast.150, bf16[1024,2816]{1,0:T(8,128)(2,1)} %get-tuple-element.90.far_grads), custom_call_target="tpu_custom_call" | custom-call | tf_op jit(solution)/shard_map/line_scatter/pallas_call | solution.py:725
  485.0 45.8 %product_gather.1 = (bf16[8,128,2048]{2,1,0:T(8,128)(2,1)S(1)}, bf16[704,2048]{1,0:T(8,128)(2,1)S(1)}) custom-call(bf16[128,2048]{1,0:T(8,128)(2,1)S(1)} %get-tuple-element.98.own, bf16[1024,704]{1,0:T(8,128)(2,1)S(1)} %fusion.10.units, bf16[1024,2048]{1,0:T(8,128)(2,1)S(1)} %copy-done.1), custom_call_target="tpu_custom_call" | custom-call | tf_op jit(solution)/shard_map/product_gather/pallas_call | solution.py:877
  534.4 3.6 all-to-all-start.1
  538.6 31.9 %attend_back.1 = (bf16[1024,2048]{1,0:T(8,128)(2,1)}, bf16[2048,768]{1,0:T(8,128)(2,1)}, bf16[256,2048]{1,0:T(8,128)(2,1)}, f32[1,768]{1,0:T(1,128)}, f32[1,2048]{1,0:T(1,128)}) custom-call(bf16[1024,2048]{1,0:T(8,128)(2,1)} %bitcast.145, bf16[256,2048]{1,0:T(8,128)(2,1)} %copy-done.3, bf16[1024,256]{1,0:T(8,128)(2,1)} %copy-done.11, ...), custom_call_target="tpu_custom_call" | custom-call | flops 11274289152 | bytes 36700160 | tf_op jit(solution)/shard_map/attend_back/pallas_call | solution.py:1451
  578.0 3.6 collect_columns.1
  581.5 96.2 %closing.1 = (f32[128,2048]{1,0:T(8,128)}, bf16[8,64,768]{2,1,0:T(8,128)(2,1)}, f32[64,2048]{1,0:T(8,128)}, f32[176,2048]{1,0:T(8,128)}, f32[8,128]{1,0:T(8,128)}) custom-call(bf16[8,128,2048]{2,1,0:T(8,128)(2,1)} %bitcast.159, bf16[4,512,768]{2,1,0:T(8,128)(2,1)} %bitcast.166, bf16[4,128,2048]{2,1,0:T(8,128)(2,1)} %pad_maximum_fusion.1.pair, ...), custom_call_target="tpu_custom_call" | custom-call | tf_op jit(solution)/shard_map/closing/pallas_call | solution.py:1199
  690.1 4.9 bitcast_convert_fusion
  (242 shorter events, 90.4 us)
Async XLA Ops:
  7.2 151.1 %all-gather.7.cloned.1.call-start = ((), (), s32[]{:S(2)}) async-start(), calls=%async_computation.6 | async-start | bytes 2359296 | tf_op jit(solution)/shard_map/all_gather | solution.py:1607
  9.0 149.3 %all-gather.11.cloned.1.call-start = ((), (), s32[]{:S(2)}) async-start(), calls=%async_computation.12 | async-start | bytes 7208960 | tf_op jit(solution)/shard_map/all_gather | solution.py:1607
  9.8 262.6 %all-gather.13.cloned.1.call-start = ((), (), s32[]{:S(2)}) async-start(), calls=%async_computation.13 | async-start | bytes 14417920 | tf_op jit(solution)/shard_map/all_gather | solution.py:1607
  14.5 110.6 %copy-start.51 = (s32[16]{0:T(128)S(1)}, s32[16]{0:T(128)}, u32[]{:S(2)}) copy-start(s32[16]{0:T(128)} %param.19) | copy-start | bytes 196
  119.5 38.8 %all-to-all-start = ((bf16[8,64,1408]{2,1,0:T(8,128)(2,1)}), bf16[8,64,1408]{2,1,0:T(8,128)(2,1)S(1)}, u32[]{:S(2)}, u32[]{:S(2)}) async-start(bf16[8,64,1408]{2,1,0:T(8,128)(2,1)} %deal_columns.1), calls=%async_computation | async-start | bytes 2883584 | tf_op jit(solution)/shard_map/all_to_all | solution.py:1615
  124.8 198.9 %all-gather.9.cloned.1.call-start = ((), (), s32[]{:S(2)}) async-start(), calls=%async_computation.7 | async-start | bytes 2359296 | tf_op jit(solution)/shard_map/all_gather | solution.py:1607
  131.1 77.5 %copy-start.23 = (bf16[1,128,2048]{2,1,0:T(8,128)(2,1)S(1)}, bf16[1,128,2048]{2,1,0:T(8,128)(2,1)}, u32[]{:S(2)}) copy-start(bf16[1,128,2048]{2,1,0:T(8,128)(2,1)} %param.17) | copy-start | bytes 1572868
  158.3 52.4 %copy-start.28 = (bf16[8,64,1408]{2,1,0:T(8,128)(2,1)}, bf16[8,64,1408]{2,1,0:T(8,128)(2,1)S(1)}, u32[]{:S(2)}) copy-start(bf16[8,64,1408]{2,1,0:T(8,128)(2,1)S(1)} %all-to-all-done) | copy-start | bytes 4325380
  208.6 58.6 %copy-start.29 = (bf16[1,128,2048]{2,1,0:T(8,128)(2,1)S(1)}, bf16[1,128,2048]{2,1,0:T(8,128)(2,1)}, u32[]{:S(2)}) copy-start(bf16[1,128,2048]{2,1,0:T(8,128)(2,1)} %param.21) | copy-start | bytes 1572868
  271.9 210.3 %reduce-scatter.5.cloned.1.call-start = ((), (), s32[]{:S(2)}) async-start(), calls=%async_computation.8 | async-start | bytes 4718592 | tf_op jit(solution)/shard_map/reduce_scatter | solution.py:1611
  289.5 17.4 %slice-start = ((s8[5767168]{0:T(1024)(128)(4,1)}), s8[4194304]{0:T(1024)(128)(4,1)S(1)}, s32[]{:S(2)}) async-start(s8[5767168]{0:T(1024)(128)(4,1)} %bitcast.191), calls=%async_computation.14 | async-start | bytes 8388608
  294.9 12.1 %copy-start.33 = (bf16[1024,1408]{1,0:T(8,128)(2,1)}, bf16[1024,1408]{1,0:T(8,128)(2,1)S(1)}, u32[]{:S(2)}) copy-start(bf16[1024,1408]{1,0:T(8,128)(2,1)S(1)} %fusion.6) | copy-start | bytes 8650756
  294.9 12.1 %copy-start.20 = (bf16[8,128,2048]{2,1,0:T(8,128)(2,1)S(1)}, bf16[8,128,2048]{2,1,0:T(8,128)(2,1)}, u32[]{:S(2)}) copy-start(bf16[8,128,2048]{2,1,0:T(8,128)(2,1)} %get-tuple-element.79) | copy-start | bytes 12582916
  294.9 12.1 %slice-start.1 = ((s8[5767168]{0:T(1024)(128)(4,1)}), s8[1572864]{0:T(1024)(128)(4,1)S(1)}, s32[]{:S(2)}) async-start(s8[5767168]{0:T(1024)(128)(4,1)} %bitcast.191), calls=%async_computation.15 | async-start | bytes 3145728
  336.7 197.7 %reduce-scatter.7.cloned.1.call-start = ((), (), s32[]{:S(2)}) async-start(), calls=%async_computation.9 | async-start | bytes 7208960 | tf_op jit(solution)/shard_map/reduce_scatter | solution.py:1611
  354.0 19.7 %copy-start.7 = (bf16[1024,2048]{1,0:T(8,128)(2,1)}, bf16[1024,2048]{1,0:T(8,128)(2,1)S(1)}, u32[]{:S(2)}) copy-start(bf16[1024,2048]{1,0:T(8,128)(2,1)S(1)} %get-tuple-element.110) | copy-start | bytes 12582916
  373.7 10.6 %copy-start.21 = (bf16[8,128,2048]{2,1,0:T(8,128)(2,1)S(1)}, bf16[8,128,2048]{2,1,0:T(8,128)(2,1)}, u32[]{:S(2)}) copy-start(bf16[8,128,2048]{2,1,0:T(8,128)(2,1)} %get-tuple-element.79) | copy-start | bytes 12582916
  392.8 188.7 %reduce-scatter.9.cloned.1.call-start = ((), (), s32[]{:S(2)}) async-start(), calls=%async_computation.10 | async-start | bytes 7208960 | tf_op jit(solution)/shard_map/reduce_scatter | solution.py:1611
  403.8 286.3 %reduce-scatter.11.cloned.1.call-start = ((), (), s32[]{:S(2)}) async-start(), calls=%async_computation.11 | async-start | bytes 14417920 | tf_op jit(solution)/shard_map/reduce_scatter | solution.py:1611
  485.0 53.0 %copy-start.25 = (bf16[128,2048]{1,0:T(8,128)(2,1)S(1)}, bf16[128,2048]{1,0:T(8,128)(2,1)}, u32[]{:S(2)}) copy-start(bf16[128,2048]{1,0:T(8,128)(2,1)} %multiply_convert_fusion.refs_0_) | copy-start | bytes 1572868
  534.4 42.5 %all-to-all-start.1 = ((bf16[8,64,1408]{2,1,0:T(8,128)(2,1)}), bf16[8,64,1408]{2,1,0:T(8,128)(2,1)S(1)}, u32[]{:S(2)}, u32[]{:S(2)}) async-start(bf16[8,64,1408]{2,1,0:T(8,128)(2,1)} %bitcast.169), calls=%async_computation.3 | async-start | bytes 2883584 | tf_op jit(solution)/shard_map/all_to_all | solution.py:1615
  581.5 101.6 %copy-start.24 = (bf16[1,128,2048]{2,1,0:T(8,128)(2,1)S(1)}, bf16[1,128,2048]{2,1,0:T(8,128)(2,1)}, u32[]{:S(2)}) copy-start(bf16[1,128,2048]{2,1,0:T(8,128)(2,1)} %param.17) | copy-start | bytes 1572868
  677.7 10.8 %copy-start.22 = (f32[128,2048]{1,0:T(8,128)S(1)}, f32[128,2048]{1,0:T(8,128)}, u32[]{:S(2)}) copy-start(f32[128,2048]{1,0:T(8,128)} %get-tuple-element.161) | copy-start | bytes 3145732
  677.8 10.8 %copy-start.31 = (bf16[1,128,2048]{2,1,0:T(8,128)(2,1)S(1)}, bf16[1,128,2048]{2,1,0:T(8,128)(2,1)}, u32[]{:S(2)}) copy-start(bf16[1,128,2048]{2,1,0:T(8,128)(2,1)} %param.21) | copy-start | bytes 1572868
  (40 other events, 140.2 us)
Sparse Core Ops, SparseCore 0:
  10.7 70.9 all-gather.6
  83.3 44.5 all-gather.10
  129.5 80.2 all-gather.12
  272.0 47.7 all-gather.8
  336.8 86.6 reduce-scatter.4
  426.1 54.6 reduce-scatter.6
  483.4 54.8 reduce-scatter.8
  541.0 128.6 reduce-scatter.10
